TPU v7x, 32 devices: a whole 2x2x4 slice. The times are simulated.
32 devices in a mesh: body: 2 (over x), gx: 4 (over z), yz: 4 (over y, core).
Axes of the slice: x: 2, y: 2, z: 4, core: 2. Of those that a mesh axis runs over, the one named last changes fastest.
Arguments:
- displacement: float32 [2, 3, 64, 256, 128], P('body', None, 'gx', 'yz'), may hold values from -1.75 to 1.75
- velocity: float32 [2, 3, 64, 256, 128], P('body', None, 'gx', 'yz'), may hold values from -3 to 3
- material: int32 [2, 64, 256, 128], P('body', 'gx', 'yz'), may hold values from 0 to 7
- moduli: float32 [8], replicated, may hold values from 0.5 to 2
- density: float32 [8], replicated, may hold values from 1 to 4
- partner: int32 [256], replicated, may hold values from 0 to 255, as said below
- active: int32 [256], replicated, may hold values 0 or 1
Outputs:
- final_displacement: float32 [2, 3, 64, 256, 128], P('body', None, 'gx', 'yz')
- final_velocity: float32 [2, 3, 64, 256, 128], P('body', None, 'gx', 'yz')
Inputs may be any that keep to these rules, and one draw needn't show every extreme that they name: partner is a permutation of the rows of body 1's face; in every aligned block of 64 rows of partner, exactly 32 values lie in the same-numbered block of 64 rows and the others in the next block, the last block's next being the first.
All inputs are finite; a program needn't handle non-finite values.
Results may differ from a plain program's by a relative error of at most 0.0001.
Values sent between devices are 32-bit elements; how exact they have to be, the bound alone decides.
No kernel may reach another device: no remote copies, remote signals or barrier semaphores. Data moves between devices by JAX's collectives and lax.ppermute only.
A program may use at most 64 MiB of HBM per device.

v0:
```python
import math

import jax
import jax.numpy as jnp
from jax import lax
from jax.sharding import PartitionSpec as P

STEPS = 4


STEP_TIME = 0.2
YIELD_SPAN = 0.5
PENALTY = 4.0
SOFT_WIDTH = 0.1
KERNEL_WIDTH = 1.5


def passed_along(block, axis, distance):
    devices = range(lax.axis_size(axis))
    route = [(i - distance, i) for i in devices if i - distance in devices]
    return lax.ppermute(block, axis, route)


def padded(block, sides, width):
    for axis, dim in sides:
        count = lax.axis_size(axis)
        forward = [(i, i + 1) for i in range(count - 1)]
        backward = [(target, source) for source, target in forward]
        low = lax.ppermute(
            lax.slice_in_dim(block, block.shape[dim] - width, None, axis=dim), axis, forward
        )
        high = lax.ppermute(lax.slice_in_dim(block, 0, width, axis=dim), axis, backward)
        block = jnp.concatenate([low, block, high], axis=dim)
    return block


def shifted_2(value, axis, steps):
    count = lax.axis_size(axis)
    pairs = [(source, (source + steps) % count) for source in range(count)]
    return lax.ppermute(value, axis, pairs)


def tension(stretch):
    return YIELD_SPAN * jnp.tanh(stretch / YIELD_SPAN)


def pair_pressure(own_surface, far_surface):
    column = jnp.arange(own_surface.shape[-1]).astype(jnp.float32)
    opening = -own_surface[0][:, :, None] - far_surface[0][:, None, :]
    along_z = (column + own_surface[2])[:, :, None] - (column + far_surface[2])[:, None, :]
    along_y = own_surface[1][:, :, None] - far_surface[1][:, None, :]
    weight = jnp.exp(-(along_y * along_y + along_z * along_z) / (2.0 * KERNEL_WIDTH * KERNEL_WIDTH))
    return weight * (PENALTY * SOFT_WIDTH) * jax.nn.softplus(-opening / SOFT_WIDTH)


def axis_forces(displace, stiffness, dimension):
    extent = displace.shape[dimension]
    zero_plane = jnp.zeros_like(lax.slice_in_dim(displace, 0, 1, axis=dimension))
    ahead = jnp.concatenate(
        [lax.slice_in_dim(displace, 1, extent, axis=dimension), zero_plane], axis=dimension
    )
    pulls = stiffness * tension(ahead - displace)
    behind = jnp.concatenate(
        [zero_plane, lax.slice_in_dim(pulls, 0, extent - 1, axis=dimension)], axis=dimension
    )
    return pulls - behind


def lookup(material, values_table):
    result = jnp.zeros(material.shape, jnp.float32)
    for kind_id in range(values_table.shape[0]):
        result = jnp.where(material == kind_id, values_table[kind_id], result)
    return result


def paired_terms(own_rows_surface, far_rows_surface, live_rows):
    length_y, length_z = (own_rows_surface.shape[1], own_rows_surface.shape[2])
    group_rows = math.gcd(8, length_y)
    blocks = length_y // group_rows
    own_split = own_rows_surface.reshape(3, blocks, group_rows, length_z).transpose(1, 0, 2, 3)
    far_split = far_rows_surface.reshape(3, blocks, group_rows, length_z).transpose(1, 0, 2, 3)
    live_split = live_rows.reshape(blocks, group_rows)

    def per_block(pieces):
        own_piece, far_piece, live_piece = pieces
        pressure = pair_pressure(own_piece, far_piece)
        return (
            -jnp.sum(pressure, axis=2) * live_piece[:, None],
            -jnp.sum(pressure, axis=1) * live_piece[:, None],
        )

    pushed, reacted = lax.map(per_block, (own_split, far_split, live_split))
    return (pushed.reshape(length_y, length_z), reacted.reshape(length_y, length_z))


def contact_terms(surface, partner_pool, pool_rows, active_part):
    matched = jnp.take(partner_pool, pool_rows, axis=1)
    pushes, reaction = paired_terms(surface, matched, active_part)
    returned = (
        jnp.zeros((partner_pool.shape[1], surface.shape[2]), jnp.float32)
        .at[pool_rows]
        .add(reaction)
    )
    return (pushes, returned)


def spare_terms(surface, partner_pool, pool_rows, active_part):
    return (
        jnp.zeros((surface.shape[1], surface.shape[2]), jnp.float32),
        jnp.zeros((partner_pool.shape[1], surface.shape[2]), jnp.float32),
    )


def local(displacement, velocity, material, moduli, density, partner, active):
    length_x, length_y, length_z = (
        displacement.shape[2],
        displacement.shape[3],
        displacement.shape[4],
    )
    count_x = lax.axis_size("gx")
    count_y = lax.axis_size("yz")
    place_x = lax.axis_index("gx")
    place_y = lax.axis_index("yz")
    place_body = lax.axis_index("body")
    rows_all = length_y * count_y
    whole_x = place_x * length_x + jnp.arange(length_x)
    whole_y = place_y * length_y + jnp.arange(length_y)
    inside = (
        (whole_x < length_x * count_x - 1)[:, None, None]
        & (whole_y < rows_all - 1)[None, :, None]
        & (jnp.arange(length_z) < length_z - 1)[None, None, :]
    )
    elements = jnp.where(inside[None], lookup(material, moduli), 0.0)
    node_mass = lookup(material, density)[:, None]
    shifted = jnp.concatenate([jnp.zeros_like(elements[..., :1]), elements[..., :-1]], axis=3)
    paired = jnp.concatenate([elements, elements + shifted], axis=0)
    below_x = passed_along(paired[:, length_x - 1 :], "gx", 1)
    extended = jnp.concatenate([below_x, paired], axis=1)
    below_y = passed_along(extended[:, :, length_y - 1 :], "yz", 1)
    stiff_halo = jnp.concatenate([below_y, extended], axis=2)
    single = stiff_halo[0]
    summed = stiff_halo[1]
    stiff_x = 0.25 * (summed[: length_x + 1, 1 : length_y + 1] + summed[: length_x + 1, :length_y])
    stiff_y = 0.25 * (summed[1 : length_x + 1, : length_y + 1] + summed[:length_x, : length_y + 1])
    stiff_z = 0.25 * (
        single[1 : length_x + 1, 1 : length_y + 1]
        + single[:length_x, 1 : length_y + 1]
        + single[1 : length_x + 1, :length_y]
        + single[:length_x, :length_y]
    )
    own_rows = lax.dynamic_slice_in_dim(partner, place_y * length_y, length_y)
    active_part = lax.dynamic_slice_in_dim(active, place_y * length_y, length_y).astype(jnp.float32)
    is_face = place_x == count_x - 1
    is_contact = (place_body == 0) & is_face
    pool_rows = (own_rows - place_y * length_y) % rows_all
    for repeat in range(STEPS):
        widened = padded(displacement, (("gx", 2), ("yz", 3)), 1)
        surface = displacement[0, :, length_x - 1]
        pull_x = stiff_x * tension(widened[:, :, 1:, 1:-1] - widened[:, :, :-1, 1:-1])
        forces = pull_x[:, :, 1:] - pull_x[:, :, :-1]
        pull_y = stiff_y * tension(widened[:, :, 1:-1, 1:] - widened[:, :, 1:-1, :-1])
        forces = forces + (pull_y[:, :, :, 1:] - pull_y[:, :, :, :-1])
        forces = forces + axis_forces(displacement, stiff_z, 4)
        across = passed_along(surface, "body", -1)
        onward = shifted_2(across, "yz", -1)
        partner_pool = jnp.concatenate([across, onward], axis=1)
        pushes, returned = lax.cond(
            is_contact, contact_terms, spare_terms, surface, partner_pool, pool_rows, active_part
        )
        carried = shifted_2(returned[length_y:], "yz", 1)
        arriving = passed_along(returned[:length_y] + carried, "body", 1)
        contact = pushes + arriving
        forces = forces.at[0, 0, length_x - 1].add(contact)
        velocity = velocity + STEP_TIME * forces / node_mass
        displacement = displacement + STEP_TIME * velocity
    return (displacement, velocity)


def solution(mesh):
    in_specs = (
        P("body", None, "gx", "yz", None),
        P("body", None, "gx", "yz", None),
        P("body", "gx", "yz", None),
        P(),
        P(),
        P(),
        P(),
    )
    out_specs = (P("body", None, "gx", "yz", None), P("body", None, "gx", "yz", None))
    return jax.shard_map(local, mesh=mesh, in_specs=in_specs, out_specs=out_specs, check_vma=False)
```

profile of v0, /device:TPU:30, one launch (start us, length us, event | category | flops | bytes accessed | tf_op | source)
XLA Modules:
  0.0 184.8 jit_solution(13951790360902705441)
XLA Ops:
  2.4 6.9 %select_select_fusion = (f32[1,16,64,128]{3,2,1,0:T(8,128)S(1)}, pred[1,16,64,128]{3,2,1,0:T(8,128)(4,1)S(1)}, pred[1,16,64,128]{3,2,1,0:T(8,128)(4,1)S(1)}, pre...) fusion(f32[]{:T(128)} %bitcast.87, f32[]{:T(128)} %bitcast.86, ...), kind=kLoop, calls=%fused_computation.222 | loop fusion | flops 2359296 | bytes 2098336 | tf_op jit(solution)/shard_map/jit(_where)/select_n | solution.py:133
  12.3 5.2 %collective-permute-start = (f32[1,3,1,64,128]{4,3,2,1,0:T(8,128)S(1)}, f32[1,3,1,64,128]{4,3,2,1,0:T(8,128)S(1)}, u32[]{:S(2)}, u32[]{:S(2)}) collective-permute-start(f32[1,3,1,64,128]{4,3,2,1,0:T(8,128)S(1)} %get-tuple-element.455), channel_id=1, source_target_pairs={{4,0},{8,4},{12,8},{5,1},{9,5},{13,9},{6,2},{10,6},{14,10},{7,3},{... | collective-permute-start | bytes 294920 | tf_op jit(solution)/shard_map/ppermute | solution.py:32
  17.5 2.4 %collective-permute-start.6 = (f32[3,64,128]{2,1,0:T(8,128)S(1)}, f32[3,64,128]{2,1,0:T(8,128)S(1)}, u32[]{:S(2)}, u32[]{:S(2)}) collective-permute-start(f32[3,64,128]{2,1,0:T(8,128)S(1)} %get-tuple-element.453), channel_id=1, source_target_pairs={{16,0},{17,1},{18,2},{19,3},{20,4},{21,5},{22,6},{23,7},{24,8},{25... | collective-permute-start | bytes 294920 | tf_op jit(solution)/shard_map/ppermute | solution.py:21
  20.6 6.3 %select_bitcast_fusion.4 = f32[16,64,128]{2,1,0:T(8,128)} fusion(pred[1,16,64,128]{3,2,1,0:T(8,128)(4,1)S(1)} %get-tuple-element.395, pred[1,16,64,128]{3,2,1,0:T(8,128)(4,1)S(1)} %get-tuple-element.394, pred[1,16,64,128]{3,2,1,0:T(8,128)(4,1)S(1)} %get-tuple-element.393, pred[1,16,64,128]{3,2,1,0:T(8,128)(4,1)S(1)} %get-tuple-element.392, ...), kind=kLoop, calls=%fused_computation.220 | loop fusion | flops 1048576 | bytes 1572896 | tf_op jit(solution)/shard_map/div | solution.py:174
  26.9 1.9 %collective-permute-start.3 = (f32[2,17,1,128]{3,2,1,0:T(1,128)S(1)}, f32[2,17,1,128]{3,2,1,0:T(1,128)S(1)}, u32[]{:S(2)}, u32[]{:S(2)}) collective-permute-start(f32[2,17,1,128]{3,2,1,0:T(1,128)S(1)} %pad_maximum_fusion.34), channel_id=1, source_target_pairs={{0,1},{1,2},{2,3},{4,5},{5,6},{6,7},{8,9},{9,10},{10,11},{12,13},{... | collective-permute-start | bytes 52232 | tf_op jit(solution)/shard_map/ppermute | solution.py:21
  28.9 1.6 slice.551
  32.5 1.8 copy-done.33
  34.2 1.6 tanh_multiply_fusion.3
  35.9 2.2 %collective-permute-start.4 = (f32[1,3,18,1,128]{4,3,2,1,0:T(1,128)S(1)}, f32[1,3,18,1,128]{4,3,2,1,0:T(1,128)S(1)}, u32[]{:S(2)}, u32[]{:S(2)}) collective-permute-start(f32[1,3,18,1,128]{4,3,2,1,0:T(1,128)S(1)} %get-tuple-element.442), channel_id=1, source_target_pairs={{1,0},{2,1},{3,2},{5,4},{6,5},{7,6},{9,8},{10,9},{11,10},{13,12},{... | collective-permute-start | bytes 82952 | tf_op jit(solution)/shard_map/ppermute | solution.py:32
  38.2 2.1 %collective-permute-start.5 = (f32[1,3,18,1,128]{4,3,2,1,0:T(1,128)S(1)}, f32[1,3,18,1,128]{4,3,2,1,0:T(1,128)S(1)}, u32[]{:S(2)}, u32[]{:S(2)}) collective-permute-start(f32[1,3,18,1,128]{4,3,2,1,0:T(1,128)S(1)} %get-tuple-element.443), channel_id=1, source_target_pairs={{0,1},{1,2},{2,3},{4,5},{5,6},{6,7},{8,9},{9,10},{10,11},{12,13},{... | collective-permute-start | bytes 82952 | tf_op jit(solution)/shard_map/ppermute | solution.py:29
  44.9 2.4 %fusion.63 = f32[1,3,16,65,128]{4,3,2,1,0:T(8,128)S(1)} fusion(f32[1,3,18,64,128]{4,3,2,1,0:T(8,128)} %copy-done.34, f32[1,3,18,1,128]{4,3,2,1,0:T(1,128)S(1)} %collective-permute-done.5, f32[1,3,18,1,128]{4,3,2,1,0:T(1,128)S(1)} %collective-permute-done.4, f32[16,65,128]{2,1,0:T(8,128)S(1)} %fusion.85), kind=kLoop, calls=%fused_computation.162 | loop fusion | flops 1996800 | bytes 3954688 | tf_op jit(solution)/shard_map/mul | solution.py:161
  50.3 13.1 %collective-permute-done.9 = f32[64,128]{1,0:T(8,128)S(1)} collective-permute-done((f32[64,128]{1,0:T(8,128)S(1)}, f32[64,128]{1,0:T(8,128)S(1)}, u32[]{:S(2)}, u32[]{:S(2)}) %collective-permute-start.9) | collective-permute-done | bytes 32800 | tf_op jit(solution)/shard_map/ppermute | solution.py:21
  65.9 1.6 collective-permute-start.14
  71.7 3.7 %collective-permute-done.11 = f32[1,3,1,64,128]{4,3,2,1,0:T(8,128)S(1)} collective-permute-done((f32[1,3,1,64,128]{4,3,2,1,0:T(8,128)S(1)}, f32[1,3,1,64,128]{4,3,2,1,0:T(8,128)S(1)}, u32[]{:S(2)}, u32[]{:S(2)}) %collective-permute-start.11) | collective-permute-done | bytes 98336 | tf_op jit(solution)/shard_map/ppermute | solution.py:29
  75.4 1.9 %collective-permute-start.12 = (f32[1,3,18,1,128]{4,3,2,1,0:T(1,128)S(1)}, f32[1,3,18,1,128]{4,3,2,1,0:T(1,128)S(1)}, u32[]{:S(2)}, u32[]{:S(2)}) collective-permute-start(f32[1,3,18,1,128]{4,3,2,1,0:T(1,128)S(1)} %get-tuple-element.440), channel_id=1, source_target_pairs={{1,0},{2,1},{3,2},{5,4},{6,5},{7,6},{9,8},{10,9},{11,10},{13,12},{... | collective-permute-start | bytes 82952 | tf_op jit(solution)/shard_map/ppermute | solution.py:32
  77.3 2.4 %collective-permute-start.13 = (f32[1,3,18,1,128]{4,3,2,1,0:T(1,128)S(1)}, f32[1,3,18,1,128]{4,3,2,1,0:T(1,128)S(1)}, u32[]{:S(2)}, u32[]{:S(2)}) collective-permute-start(f32[1,3,18,1,128]{4,3,2,1,0:T(1,128)S(1)} %get-tuple-element.441), channel_id=1, source_target_pairs={{0,1},{1,2},{2,3},{4,5},{5,6},{6,7},{8,9},{9,10},{10,11},{12,13},{... | collective-permute-start | bytes 82952 | tf_op jit(solution)/shard_map/ppermute | solution.py:29
  84.7 2.7 %collective-permute-done.16 = f32[64,128]{1,0:T(8,128)S(1)} collective-permute-done((f32[64,128]{1,0:T(8,128)S(1)}, f32[64,128]{1,0:T(8,128)S(1)}, u32[]{:S(2)}, u32[]{:S(2)}) %collective-permute-start.16) | collective-permute-done | bytes 32800 | tf_op jit(solution)/shard_map/ppermute | solution.py:40
  89.6 12.9 %collective-permute-done.17 = f32[64,128]{1,0:T(8,128)S(1)} collective-permute-done((f32[64,128]{1,0:T(8,128)S(1)}, f32[64,128]{1,0:T(8,128)S(1)}, u32[]{:S(2)}, u32[]{:S(2)}) %collective-permute-start.17) | collective-permute-done | bytes 32800 | tf_op jit(solution)/shard_map/ppermute | solution.py:21
  103.3 2.0 %multiply_add_fusion.2 = (f32[1,3,16,64,128]{4,3,2,1,0:T(8,128)S(1)}, f32[1,3,16,64,128]{4,3,2,1,0:T(8,128)}) fusion(f32[1,3,16,64,128]{4,3,2,1,0:T(8,128)S(1)} %multiply_add_fusion.3, f32[1,3,16,64,128]{4,3,2,1,0:T(8,128)S(1)} %fusion.90, f32[1,3,16,64,128]{4,3,2,1,0:T(8,128)S(1)} %copy-done.32, f32[16,64,128]{2,1,0:T(8,128)S(1)} %copy-done.28, ...), kind=kLoop, calls=%fused_computation.202 | loop fusion | flops 3145728 | bytes 9961472 | tf_op jit(solution)/shard_map/add | solution.py:175
  105.8 1.6 collective-permute-start.22
  111.6 3.7 %collective-permute-done.19 = f32[1,3,1,64,128]{4,3,2,1,0:T(8,128)S(1)} collective-permute-done((f32[1,3,1,64,128]{4,3,2,1,0:T(8,128)S(1)}, f32[1,3,1,64,128]{4,3,2,1,0:T(8,128)S(1)}, u32[]{:S(2)}, u32[]{:S(2)}) %collective-permute-start.19) | collective-permute-done | bytes 98336 | tf_op jit(solution)/shard_map/ppermute | solution.py:29
  115.3 1.9 %collective-permute-start.20 = (f32[1,3,18,1,128]{4,3,2,1,0:T(1,128)S(1)}, f32[1,3,18,1,128]{4,3,2,1,0:T(1,128)S(1)}, u32[]{:S(2)}, u32[]{:S(2)}) collective-permute-start(f32[1,3,18,1,128]{4,3,2,1,0:T(1,128)S(1)} %get-tuple-element.438), channel_id=1, source_target_pairs={{1,0},{2,1},{3,2},{5,4},{6,5},{7,6},{9,8},{10,9},{11,10},{13,12},{... | collective-permute-start | bytes 82952 | tf_op jit(solution)/shard_map/ppermute | solution.py:32
  117.2 2.4 %collective-permute-start.21 = (f32[1,3,18,1,128]{4,3,2,1,0:T(1,128)S(1)}, f32[1,3,18,1,128]{4,3,2,1,0:T(1,128)S(1)}, u32[]{:S(2)}, u32[]{:S(2)}) collective-permute-start(f32[1,3,18,1,128]{4,3,2,1,0:T(1,128)S(1)} %get-tuple-element.439), channel_id=1, source_target_pairs={{0,1},{1,2},{2,3},{4,5},{5,6},{6,7},{8,9},{9,10},{10,11},{12,13},{... | collective-permute-start | bytes 82952 | tf_op jit(solution)/shard_map/ppermute | solution.py:29
  124.6 2.7 %collective-permute-done.24 = f32[64,128]{1,0:T(8,128)S(1)} collective-permute-done((f32[64,128]{1,0:T(8,128)S(1)}, f32[64,128]{1,0:T(8,128)S(1)}, u32[]{:S(2)}, u32[]{:S(2)}) %collective-permute-start.24) | collective-permute-done | bytes 32800 | tf_op jit(solution)/shard_map/ppermute | solution.py:40
  129.3 13.1 %collective-permute-done.25 = f32[64,128]{1,0:T(8,128)S(1)} collective-permute-done((f32[64,128]{1,0:T(8,128)S(1)}, f32[64,128]{1,0:T(8,128)S(1)}, u32[]{:S(2)}, u32[]{:S(2)}) %collective-permute-start.25) | collective-permute-done | bytes 32800 | tf_op jit(solution)/shard_map/ppermute | solution.py:21
  144.9 1.6 collective-permute-start.30
  150.7 3.7 %collective-permute-done.27 = f32[1,3,1,64,128]{4,3,2,1,0:T(8,128)S(1)} collective-permute-done((f32[1,3,1,64,128]{4,3,2,1,0:T(8,128)S(1)}, f32[1,3,1,64,128]{4,3,2,1,0:T(8,128)S(1)}, u32[]{:S(2)}, u32[]{:S(2)}) %collective-permute-start.27) | collective-permute-done | bytes 98336 | tf_op jit(solution)/shard_map/ppermute | solution.py:29
  154.4 1.9 %collective-permute-start.28 = (f32[1,3,18,1,128]{4,3,2,1,0:T(1,128)S(1)}, f32[1,3,18,1,128]{4,3,2,1,0:T(1,128)S(1)}, u32[]{:S(2)}, u32[]{:S(2)}) collective-permute-start(f32[1,3,18,1,128]{4,3,2,1,0:T(1,128)S(1)} %get-tuple-element.436), channel_id=1, source_target_pairs={{1,0},{2,1},{3,2},{5,4},{6,5},{7,6},{9,8},{10,9},{11,10},{13,12},{... | collective-permute-start | bytes 82952 | tf_op jit(solution)/shard_map/ppermute | solution.py:32
  156.3 2.4 %collective-permute-start.29 = (f32[1,3,18,1,128]{4,3,2,1,0:T(1,128)S(1)}, f32[1,3,18,1,128]{4,3,2,1,0:T(1,128)S(1)}, u32[]{:S(2)}, u32[]{:S(2)}) collective-permute-start(f32[1,3,18,1,128]{4,3,2,1,0:T(1,128)S(1)} %get-tuple-element.437), channel_id=1, source_target_pairs={{0,1},{1,2},{2,3},{4,5},{5,6},{6,7},{8,9},{9,10},{10,11},{12,13},{... | collective-permute-start | bytes 82952 | tf_op jit(solution)/shard_map/ppermute | solution.py:29
  163.7 2.7 %collective-permute-done.32 = f32[64,128]{1,0:T(8,128)S(1)} collective-permute-done((f32[64,128]{1,0:T(8,128)S(1)}, f32[64,128]{1,0:T(8,128)S(1)}, u32[]{:S(2)}, u32[]{:S(2)}) %collective-permute-start.32) | collective-permute-done | bytes 32800 | tf_op jit(solution)/shard_map/ppermute | solution.py:40
  168.4 13.1 %collective-permute-done.33 = f32[64,128]{1,0:T(8,128)S(1)} collective-permute-done((f32[64,128]{1,0:T(8,128)S(1)}, f32[64,128]{1,0:T(8,128)S(1)}, u32[]{:S(2)}, u32[]{:S(2)}) %collective-permute-start.33) | collective-permute-done | bytes 32800 | tf_op jit(solution)/shard_map/ppermute | solution.py:21
  182.3 2.5 %multiply_add_fusion = (f32[1,3,16,64,128]{4,3,2,1,0:T(8,128)}, f32[1,3,16,64,128]{4,3,2,1,0:T(8,128)}) fusion(f32[1,3,16,64,128]{4,3,2,1,0:T(8,128)S(1)} %multiply_add_fusion.1, f32[1,3,16,64,128]{4,3,2,1,0:T(8,128)S(1)} %fusion.88, f32[1,3,16,64,128]{4,3,2,1,0:T(8,128)S(1)} %copy-done.10, f32[16,64,128]{2,1,0:T(8,128)S(1)} %copy-done.30, ...), kind=kLoop, calls=%fused_computation.196 | loop fusion | flops 3145728 | bytes 9961472 | tf_op jit(solution)/shard_map/add | solution.py:175
  (191 shorter events, 57.7 us)
Async XLA Ops:
  9.5 17.4 %collective-permute-start.2 = (f32[2,1,64,128]{3,2,1,0:T(8,128)S(1)}, f32[2,1,64,128]{3,2,1,0:T(8,128)S(1)}, u32[]{:S(2)}, u32[]{:S(2)}) collective-permute-start(f32[2,1,64,128]{3,2,1,0:T(8,128)S(1)} %pad_maximum_fusion.24), channel_id=1, source_target_pairs={{0,4},{4,8},{8,12},{1,5},{5,9},{9,13},{2,6},{6,10},{10,14},{3,7},{... | collective-permute-start | bytes 196616 | tf_op jit(solution)/shard_map/ppermute | solution.py:21
  11.0 21.5 %collective-permute-start.1 = (f32[1,3,1,64,128]{4,3,2,1,0:T(8,128)S(1)}, f32[1,3,1,64,128]{4,3,2,1,0:T(8,128)S(1)}, u32[]{:S(2)}, u32[]{:S(2)}) collective-permute-start(f32[1,3,1,64,128]{4,3,2,1,0:T(8,128)S(1)} %get-tuple-element.454), channel_id=1, source_target_pairs={{0,4},{4,8},{8,12},{1,5},{5,9},{9,13},{2,6},{6,10},{10,14},{3,7},{... | collective-permute-start | bytes 294920 | tf_op jit(solution)/shard_map/ppermute | solution.py:29
  12.3 23.6 %collective-permute-start = (f32[1,3,1,64,128]{4,3,2,1,0:T(8,128)S(1)}, f32[1,3,1,64,128]{4,3,2,1,0:T(8,128)S(1)}, u32[]{:S(2)}, u32[]{:S(2)}) collective-permute-start(f32[1,3,1,64,128]{4,3,2,1,0:T(8,128)S(1)} %get-tuple-element.455), channel_id=1, source_target_pairs={{4,0},{8,4},{12,8},{5,1},{9,5},{13,9},{6,2},{10,6},{14,10},{7,3},{... | collective-permute-start | bytes 294920 | tf_op jit(solution)/shard_map/ppermute | solution.py:32
  17.5 22.8 %collective-permute-start.6 = (f32[3,64,128]{2,1,0:T(8,128)S(1)}, f32[3,64,128]{2,1,0:T(8,128)S(1)}, u32[]{:S(2)}, u32[]{:S(2)}) collective-permute-start(f32[3,64,128]{2,1,0:T(8,128)S(1)} %get-tuple-element.453), channel_id=1, source_target_pairs={{16,0},{17,1},{18,2},{19,3},{20,4},{21,5},{22,6},{23,7},{24,8},{25... | collective-permute-start | bytes 294920 | tf_op jit(solution)/shard_map/ppermute | solution.py:21
  26.9 5.1 %collective-permute-start.3 = (f32[2,17,1,128]{3,2,1,0:T(1,128)S(1)}, f32[2,17,1,128]{3,2,1,0:T(1,128)S(1)}, u32[]{:S(2)}, u32[]{:S(2)}) collective-permute-start(f32[2,17,1,128]{3,2,1,0:T(1,128)S(1)} %pad_maximum_fusion.34), channel_id=1, source_target_pairs={{0,1},{1,2},{2,3},{4,5},{5,6},{6,7},{8,9},{9,10},{10,11},{12,13},{... | collective-permute-start | bytes 52232 | tf_op jit(solution)/shard_map/ppermute | solution.py:21
  35.9 8.9 %collective-permute-start.4 = (f32[1,3,18,1,128]{4,3,2,1,0:T(1,128)S(1)}, f32[1,3,18,1,128]{4,3,2,1,0:T(1,128)S(1)}, u32[]{:S(2)}, u32[]{:S(2)}) collective-permute-start(f32[1,3,18,1,128]{4,3,2,1,0:T(1,128)S(1)} %get-tuple-element.442), channel_id=1, source_target_pairs={{1,0},{2,1},{3,2},{5,4},{6,5},{7,6},{9,8},{10,9},{11,10},{13,12},{... | collective-permute-start | bytes 82952 | tf_op jit(solution)/shard_map/ppermute | solution.py:32
  38.2 6.7 %collective-permute-start.5 = (f32[1,3,18,1,128]{4,3,2,1,0:T(1,128)S(1)}, f32[1,3,18,1,128]{4,3,2,1,0:T(1,128)S(1)}, u32[]{:S(2)}, u32[]{:S(2)}) collective-permute-start(f32[1,3,18,1,128]{4,3,2,1,0:T(1,128)S(1)} %get-tuple-element.443), channel_id=1, source_target_pairs={{0,1},{1,2},{2,3},{4,5},{5,6},{6,7},{8,9},{9,10},{10,11},{12,13},{... | collective-permute-start | bytes 82952 | tf_op jit(solution)/shard_map/ppermute | solution.py:29
  40.3 3.8 %collective-permute-start.7 = (f32[3,64,128]{2,1,0:T(8,128)S(1)}, f32[3,64,128]{2,1,0:T(8,128)S(1)}, u32[]{:S(2)}, u32[]{:S(2)}) collective-permute-start(f32[3,64,128]{2,1,0:T(8,128)S(1)} %collective-permute-done.6), channel_id=1, source_target_pairs={{0,3},{1,0},{2,1},{3,2},{4,7},{5,4},{6,5},{7,6},{8,11},{9,8},{10,9... | collective-permute-start | bytes 294920 | tf_op jit(solution)/shard_map/ppermute | solution.py:40
  44.8 3.5 %collective-permute-start.8 = (f32[64,128]{1,0:T(8,128)S(1)}, f32[64,128]{1,0:T(8,128)S(1)}, u32[]{:S(2)}, u32[]{:S(2)}) collective-permute-start(f32[64,128]{1,0:T(8,128)S(1)} %slice.560), channel_id=1, source_target_pairs={{0,1},{1,2},{2,3},{3,0},{4,5},{5,6},{6,7},{7,4},{8,9},{9,10},{10,1... | collective-permute-start | bytes 98312 | tf_op jit(solution)/shard_map/ppermute | solution.py:40
  48.3 15.2 %collective-permute-start.9 = (f32[64,128]{1,0:T(8,128)S(1)}, f32[64,128]{1,0:T(8,128)S(1)}, u32[]{:S(2)}, u32[]{:S(2)}) collective-permute-start(f32[64,128]{1,0:T(8,128)S(1)} %slice_add_fusion.12), channel_id=1, source_target_pairs={{0,16},{1,17},{2,18},{3,19},{4,20},{5,21},{6,22},{7,23},{8,24},{9,... | collective-permute-start | bytes 98312 | tf_op jit(solution)/shard_map/ppermute | solution.py:21
  65.9 13.8 %collective-permute-start.14 = (f32[3,64,128]{2,1,0:T(8,128)S(1)}, f32[3,64,128]{2,1,0:T(8,128)S(1)}, u32[]{:S(2)}, u32[]{:S(2)}) collective-permute-start(f32[3,64,128]{2,1,0:T(8,128)S(1)} %get-tuple-element.450), channel_id=1, source_target_pairs={{16,0},{17,1},{18,2},{19,3},{20,4},{21,5},{22,6},{23,7},{24,8},{25... | collective-permute-start | bytes 294920 | tf_op jit(solution)/shard_map/ppermute | solution.py:21
  67.5 4.2 %collective-permute-start.10 = (f32[1,3,1,64,128]{4,3,2,1,0:T(8,128)S(1)}, f32[1,3,1,64,128]{4,3,2,1,0:T(8,128)S(1)}, u32[]{:S(2)}, u32[]{:S(2)}) collective-permute-start(f32[1,3,1,64,128]{4,3,2,1,0:T(8,128)S(1)} %get-tuple-element.452), channel_id=1, source_target_pairs={{4,0},{8,4},{12,8},{5,1},{9,5},{13,9},{6,2},{10,6},{14,10},{7,3},{... | collective-permute-start | bytes 294920 | tf_op jit(solution)/shard_map/ppermute | solution.py:32
  68.8 6.5 %collective-permute-start.11 = (f32[1,3,1,64,128]{4,3,2,1,0:T(8,128)S(1)}, f32[1,3,1,64,128]{4,3,2,1,0:T(8,128)S(1)}, u32[]{:S(2)}, u32[]{:S(2)}) collective-permute-start(f32[1,3,1,64,128]{4,3,2,1,0:T(8,128)S(1)} %get-tuple-element.451), channel_id=1, source_target_pairs={{0,4},{4,8},{8,12},{1,5},{5,9},{9,13},{2,6},{6,10},{10,14},{3,7},{... | collective-permute-start | bytes 294920 | tf_op jit(solution)/shard_map/ppermute | solution.py:29
  75.4 8.7 %collective-permute-start.12 = (f32[1,3,18,1,128]{4,3,2,1,0:T(1,128)S(1)}, f32[1,3,18,1,128]{4,3,2,1,0:T(1,128)S(1)}, u32[]{:S(2)}, u32[]{:S(2)}) collective-permute-start(f32[1,3,18,1,128]{4,3,2,1,0:T(1,128)S(1)} %get-tuple-element.440), channel_id=1, source_target_pairs={{1,0},{2,1},{3,2},{5,4},{6,5},{7,6},{9,8},{10,9},{11,10},{13,12},{... | collective-permute-start | bytes 82952 | tf_op jit(solution)/shard_map/ppermute | solution.py:32
  77.3 6.8 %collective-permute-start.13 = (f32[1,3,18,1,128]{4,3,2,1,0:T(1,128)S(1)}, f32[1,3,18,1,128]{4,3,2,1,0:T(1,128)S(1)}, u32[]{:S(2)}, u32[]{:S(2)}) collective-permute-start(f32[1,3,18,1,128]{4,3,2,1,0:T(1,128)S(1)} %get-tuple-element.441), channel_id=1, source_target_pairs={{0,1},{1,2},{2,3},{4,5},{5,6},{6,7},{8,9},{9,10},{10,11},{12,13},{... | collective-permute-start | bytes 82952 | tf_op jit(solution)/shard_map/ppermute | solution.py:29
  79.7 3.5 %collective-permute-start.15 = (f32[3,64,128]{2,1,0:T(8,128)S(1)}, f32[3,64,128]{2,1,0:T(8,128)S(1)}, u32[]{:S(2)}, u32[]{:S(2)}) collective-permute-start(f32[3,64,128]{2,1,0:T(8,128)S(1)} %collective-permute-done.14), channel_id=1, source_target_pairs={{0,3},{1,0},{2,1},{3,2},{4,7},{5,4},{6,5},{7,6},{8,11},{9,8},{10,9... | collective-permute-start | bytes 294920 | tf_op jit(solution)/shard_map/ppermute | solution.py:40
  83.9 3.5 %collective-permute-start.16 = (f32[64,128]{1,0:T(8,128)S(1)}, f32[64,128]{1,0:T(8,128)S(1)}, u32[]{:S(2)}, u32[]{:S(2)}) collective-permute-start(f32[64,128]{1,0:T(8,128)S(1)} %slice.583), channel_id=1, source_target_pairs={{0,1},{1,2},{2,3},{3,0},{4,5},{5,6},{6,7},{7,4},{8,9},{9,10},{10,1... | collective-permute-start | bytes 98312 | tf_op jit(solution)/shard_map/ppermute | solution.py:40
  87.4 15.1 %collective-permute-start.17 = (f32[64,128]{1,0:T(8,128)S(1)}, f32[64,128]{1,0:T(8,128)S(1)}, u32[]{:S(2)}, u32[]{:S(2)}) collective-permute-start(f32[64,128]{1,0:T(8,128)S(1)} %slice_add_fusion.11), channel_id=1, source_target_pairs={{0,16},{1,17},{2,18},{3,19},{4,20},{5,21},{6,22},{7,23},{8,24},{9,... | collective-permute-start | bytes 98312 | tf_op jit(solution)/shard_map/ppermute | solution.py:21
  105.8 13.8 %collective-permute-start.22 = (f32[3,64,128]{2,1,0:T(8,128)S(1)}, f32[3,64,128]{2,1,0:T(8,128)S(1)}, u32[]{:S(2)}, u32[]{:S(2)}) collective-permute-start(f32[3,64,128]{2,1,0:T(8,128)S(1)} %get-tuple-element.447), channel_id=1, source_target_pairs={{16,0},{17,1},{18,2},{19,3},{20,4},{21,5},{22,6},{23,7},{24,8},{25... | collective-permute-start | bytes 294920 | tf_op jit(solution)/shard_map/ppermute | solution.py:21
  107.4 4.2 %collective-permute-start.18 = (f32[1,3,1,64,128]{4,3,2,1,0:T(8,128)S(1)}, f32[1,3,1,64,128]{4,3,2,1,0:T(8,128)S(1)}, u32[]{:S(2)}, u32[]{:S(2)}) collective-permute-start(f32[1,3,1,64,128]{4,3,2,1,0:T(8,128)S(1)} %get-tuple-element.449), channel_id=1, source_target_pairs={{4,0},{8,4},{12,8},{5,1},{9,5},{13,9},{6,2},{10,6},{14,10},{7,3},{... | collective-permute-start | bytes 294920 | tf_op jit(solution)/shard_map/ppermute | solution.py:32
  108.7 6.5 %collective-permute-start.19 = (f32[1,3,1,64,128]{4,3,2,1,0:T(8,128)S(1)}, f32[1,3,1,64,128]{4,3,2,1,0:T(8,128)S(1)}, u32[]{:S(2)}, u32[]{:S(2)}) collective-permute-start(f32[1,3,1,64,128]{4,3,2,1,0:T(8,128)S(1)} %get-tuple-element.448), channel_id=1, source_target_pairs={{0,4},{4,8},{8,12},{1,5},{5,9},{9,13},{2,6},{6,10},{10,14},{3,7},{... | collective-permute-start | bytes 294920 | tf_op jit(solution)/shard_map/ppermute | solution.py:29
  115.3 8.7 %collective-permute-start.20 = (f32[1,3,18,1,128]{4,3,2,1,0:T(1,128)S(1)}, f32[1,3,18,1,128]{4,3,2,1,0:T(1,128)S(1)}, u32[]{:S(2)}, u32[]{:S(2)}) collective-permute-start(f32[1,3,18,1,128]{4,3,2,1,0:T(1,128)S(1)} %get-tuple-element.438), channel_id=1, source_target_pairs={{1,0},{2,1},{3,2},{5,4},{6,5},{7,6},{9,8},{10,9},{11,10},{13,12},{... | collective-permute-start | bytes 82952 | tf_op jit(solution)/shard_map/ppermute | solution.py:32
  117.2 6.8 %collective-permute-start.21 = (f32[1,3,18,1,128]{4,3,2,1,0:T(1,128)S(1)}, f32[1,3,18,1,128]{4,3,2,1,0:T(1,128)S(1)}, u32[]{:S(2)}, u32[]{:S(2)}) collective-permute-start(f32[1,3,18,1,128]{4,3,2,1,0:T(1,128)S(1)} %get-tuple-element.439), channel_id=1, source_target_pairs={{0,1},{1,2},{2,3},{4,5},{5,6},{6,7},{8,9},{9,10},{10,11},{12,13},{... | collective-permute-start | bytes 82952 | tf_op jit(solution)/shard_map/ppermute | solution.py:29
  119.6 3.5 %collective-permute-start.23 = (f32[3,64,128]{2,1,0:T(8,128)S(1)}, f32[3,64,128]{2,1,0:T(8,128)S(1)}, u32[]{:S(2)}, u32[]{:S(2)}) collective-permute-start(f32[3,64,128]{2,1,0:T(8,128)S(1)} %collective-permute-done.22), channel_id=1, source_target_pairs={{0,3},{1,0},{2,1},{3,2},{4,7},{5,4},{6,5},{7,6},{8,11},{9,8},{10,9... | collective-permute-start | bytes 294920 | tf_op jit(solution)/shard_map/ppermute | solution.py:40
  127.3 15.1 %collective-permute-start.25 = (f32[64,128]{1,0:T(8,128)S(1)}, f32[64,128]{1,0:T(8,128)S(1)}, u32[]{:S(2)}, u32[]{:S(2)}) collective-permute-start(f32[64,128]{1,0:T(8,128)S(1)} %slice_add_fusion.10), channel_id=1, source_target_pairs={{0,16},{1,17},{2,18},{3,19},{4,20},{5,21},{6,22},{7,23},{8,24},{9,... | collective-permute-start | bytes 98312 | tf_op jit(solution)/shard_map/ppermute | solution.py:21
  144.9 13.8 %collective-permute-start.30 = (f32[3,64,128]{2,1,0:T(8,128)S(1)}, f32[3,64,128]{2,1,0:T(8,128)S(1)}, u32[]{:S(2)}, u32[]{:S(2)}) collective-permute-start(f32[3,64,128]{2,1,0:T(8,128)S(1)} %get-tuple-element.444), channel_id=1, source_target_pairs={{16,0},{17,1},{18,2},{19,3},{20,4},{21,5},{22,6},{23,7},{24,8},{25... | collective-permute-start | bytes 294920 | tf_op jit(solution)/shard_map/ppermute | solution.py:21
  146.5 4.2 %collective-permute-start.26 = (f32[1,3,1,64,128]{4,3,2,1,0:T(8,128)S(1)}, f32[1,3,1,64,128]{4,3,2,1,0:T(8,128)S(1)}, u32[]{:S(2)}, u32[]{:S(2)}) collective-permute-start(f32[1,3,1,64,128]{4,3,2,1,0:T(8,128)S(1)} %get-tuple-element.446), channel_id=1, source_target_pairs={{4,0},{8,4},{12,8},{5,1},{9,5},{13,9},{6,2},{10,6},{14,10},{7,3},{... | collective-permute-start | bytes 294920 | tf_op jit(solution)/shard_map/ppermute | solution.py:32
  147.8 6.5 %collective-permute-start.27 = (f32[1,3,1,64,128]{4,3,2,1,0:T(8,128)S(1)}, f32[1,3,1,64,128]{4,3,2,1,0:T(8,128)S(1)}, u32[]{:S(2)}, u32[]{:S(2)}) collective-permute-start(f32[1,3,1,64,128]{4,3,2,1,0:T(8,128)S(1)} %get-tuple-element.445), channel_id=1, source_target_pairs={{0,4},{4,8},{8,12},{1,5},{5,9},{9,13},{2,6},{6,10},{10,14},{3,7},{... | collective-permute-start | bytes 294920 | tf_op jit(solution)/shard_map/ppermute | solution.py:29
  154.4 8.7 %collective-permute-start.28 = (f32[1,3,18,1,128]{4,3,2,1,0:T(1,128)S(1)}, f32[1,3,18,1,128]{4,3,2,1,0:T(1,128)S(1)}, u32[]{:S(2)}, u32[]{:S(2)}) collective-permute-start(f32[1,3,18,1,128]{4,3,2,1,0:T(1,128)S(1)} %get-tuple-element.436), channel_id=1, source_target_pairs={{1,0},{2,1},{3,2},{5,4},{6,5},{7,6},{9,8},{10,9},{11,10},{13,12},{... | collective-permute-start | bytes 82952 | tf_op jit(solution)/shard_map/ppermute | solution.py:32
  156.3 6.8 %collective-permute-start.29 = (f32[1,3,18,1,128]{4,3,2,1,0:T(1,128)S(1)}, f32[1,3,18,1,128]{4,3,2,1,0:T(1,128)S(1)}, u32[]{:S(2)}, u32[]{:S(2)}) collective-permute-start(f32[1,3,18,1,128]{4,3,2,1,0:T(1,128)S(1)} %get-tuple-element.437), channel_id=1, source_target_pairs={{0,1},{1,2},{2,3},{4,5},{5,6},{6,7},{8,9},{9,10},{10,11},{12,13},{... | collective-permute-start | bytes 82952 | tf_op jit(solution)/shard_map/ppermute | solution.py:29
  158.7 3.5 %collective-permute-start.31 = (f32[3,64,128]{2,1,0:T(8,128)S(1)}, f32[3,64,128]{2,1,0:T(8,128)S(1)}, u32[]{:S(2)}, u32[]{:S(2)}) collective-permute-start(f32[3,64,128]{2,1,0:T(8,128)S(1)} %collective-permute-done.30), channel_id=1, source_target_pairs={{0,3},{1,0},{2,1},{3,2},{4,7},{5,4},{6,5},{7,6},{8,11},{9,8},{10,9... | collective-permute-start | bytes 294920 | tf_op jit(solution)/shard_map/ppermute | solution.py:40
  166.4 15.1 %collective-permute-start.33 = (f32[64,128]{1,0:T(8,128)S(1)}, f32[64,128]{1,0:T(8,128)S(1)}, u32[]{:S(2)}, u32[]{:S(2)}) collective-permute-start(f32[64,128]{1,0:T(8,128)S(1)} %slice_add_fusion.9), channel_id=1, source_target_pairs={{0,16},{1,17},{2,18},{3,19},{4,20},{5,21},{6,22},{7,23},{8,24},{9,... | collective-permute-start | bytes 98312 | tf_op jit(solution)/shard_map/ppermute | solution.py:21
  (40 other events, 325.0 us)
where the time goes:
time: 186 us; the launch traced here: 185 us
  waiting for transfers between devices  76.9 us (41%)
  starting transfers between devices  53.5 us (29%)
  other arithmetic  41 us (22%)
  local copies, waits for them, and re-layouts  11.8 us (6%)
    ppermute x10, waiting for transfers between devices, passed_along(): return lax.ppermute(block, axis, route)  53.8 us
    ppermute x8, starting transfers between devices, padded(): lax.ppermute(lax.slice_in_dim(block, 0, width, axis=dim), axis, backward)  17.1 us
    ppermute x10, starting transfers between devices, passed_along(): return lax.ppermute(block, axis, route)  15.9 us
    ppermute x8, starting transfers between devices, padded(): lax.ppermute(lax.slice_in_dim(block, block.shape[dim] - width, None, axis...  14.5 us
    ppermute x8, waiting for transfers between devices, shifted_2(): return lax.ppermute(value, axis, pairs)  12.1 us
    ppermute x8, waiting for transfers between devices, padded(): lax.ppermute(lax.slice_in_dim(block, block.shape[dim] - width, None, axis...  11 us
    select_n x1, other arithmetic, local(): elements = jnp.where(inside[None], lookup(material, moduli), 0.0)  6.85 us
    mul x5, other arithmetic, axis_forces(): pulls = stiffness * tension(ahead - displace)  6.36 us
  transfers between devices with their start and end apart: 34, of which 16 were waited for; matrix products, arithmetic and copies ran while one was open for 16% of the time, Pallas kernels for 0%

commit v1 on v0

v1 whole, which is shorter than its diff:
```python
import functools
import math

import jax
import jax.numpy as jnp
from jax import lax
from jax.experimental import pallas as pl
from jax.experimental.pallas import tpu as pltpu
from jax.sharding import PartitionSpec as P

STEPS = 4
STEP_TIME = 0.2
YIELD_SPAN = 0.5
PENALTY = 4.0
SOFT_WIDTH = 0.1
KERNEL_WIDTH = 1.5

U_SCALE = 1.0 / YIELD_SPAN
W_SCALE = STEP_TIME / YIELD_SPAN
KICK = STEP_TIME * STEP_TIME / YIELD_SPAN
LOG2E = math.log2(math.e)
GAP_SCALE = YIELD_SPAN / SOFT_WIDTH * LOG2E
SPAN = math.sqrt(LOG2E / (2.0 * KERNEL_WIDTH * KERNEL_WIDTH))
PRESSURE_SCALE = PENALTY * SOFT_WIDTH / LOG2E

AXES = ("body", "gx", "yz")
VMEM_LIMIT = 48 * 1024 * 1024


def vmem(shape):
    return pltpu.VMEM(shape, jnp.float32)


def call(kernel, outs, args, spaces=None, aliases=None, scratch=(), flops=0, moved=0):
    spaces = spaces or [None] * len(args)
    specs, placed = [], []
    for arg, space in zip(args, spaces):
        if space is None:
            placed.append(pltpu.with_memory_space_constraint(arg, pltpu.VMEM))
            specs.append(pl.BlockSpec(memory_space=pltpu.VMEM))
        else:
            placed.append(arg)
            specs.append(pl.BlockSpec(memory_space=space))
    return pl.pallas_call(
        kernel,
        out_shape=outs,
        in_specs=specs,
        out_specs=[pl.BlockSpec(memory_space=pltpu.VMEM)] * len(outs),
        input_output_aliases=aliases or {},
        scratch_shapes=list(scratch),
        compiler_params=pltpu.CompilerParams(vmem_limit_bytes=VMEM_LIMIT),
        cost_estimate=pl.CostEstimate(flops=flops, bytes_accessed=moved, transcendentals=0),
    )(*placed)


def prepare_kernel(d_ref, v_ref, mat_ref, moduli_ref, density_ref, place_ref, u_ref, w_ref, el_ref, kick_ref):
    planes, rows, cols = mat_ref.shape
    last_x = place_ref[0] == place_ref[1] - 1
    last_y = place_ref[2] == place_ref[3] - 1
    row = lax.broadcasted_iota(jnp.int32, (rows, cols), 0)
    col = lax.broadcasted_iota(jnp.int32, (rows, cols), 1)
    inside = (col < cols - 1) & ((row < rows - 1) | jnp.logical_not(last_y))

    @pl.loop(0, planes)
    def _(i):
        for c in range(3):
            u_ref[c, i] = d_ref[c, i] * U_SCALE
            w_ref[c, i] = v_ref[c, i] * W_SCALE
        kinds = mat_ref[i]
        stiff = jnp.zeros((rows, cols), jnp.float32)
        mass = jnp.ones((rows, cols), jnp.float32)
        for m in range(moduli_ref.shape[0]):
            hit = kinds == m
            stiff = jnp.where(hit, moduli_ref[m], stiff)
            mass = jnp.where(hit, density_ref[m], mass)
        keep = inside & ((i < planes - 1) | jnp.logical_not(last_x))
        el_ref[i] = jnp.where(keep, stiff, 0.0)
        kick_ref[i] = KICK / mass


def stiffness_kernel(
    el_ref, kick_ref, ra_ref, rb_ref, rc_ref, rd_ref, corner_ref, moduli_ref, place_ref, contact_ref,
    kx_ref, ky_ref, kz_ref, xlow_ref, xhigh_ref, ylow_ref, yhigh_ref, push_ref,
):
    planes, rows, cols = el_ref.shape
    even_x = place_ref[0] % 2 == 0
    even_y = place_ref[2] % 2 == 0
    inner_x = place_ref[0] > 0
    inner_y = place_ref[2] > 0
    factor = 0.25 * YIELD_SPAN

    def looked_up(kinds, keep):
        stiff = jnp.zeros(kinds.shape, jnp.float32)
        for m in range(moduli_ref.shape[0]):
            stiff = jnp.where(kinds == m, moduli_ref[m], stiff)
        col = lax.broadcasted_iota(jnp.int32, kinds.shape, 1)
        return jnp.where((col < cols - 1) & keep, stiff, 0.0)

    def with_behind(value):
        return value + pltpu.roll(value, 1, 1)

    row = lax.broadcasted_iota(jnp.int32, (rows, cols), 0)
    last_y = place_ref[2] == place_ref[3] - 1
    last_x = place_ref[0] == place_ref[1] - 1
    below_x = looked_up(
        jnp.where(even_x, rb_ref[3], ra_ref[3]), inner_x & ((row < rows - 1) | jnp.logical_not(last_y))
    )
    below_y = looked_up(jnp.where(even_y, rd_ref[3], rc_ref[3]), inner_y)
    plane_of = lax.broadcasted_iota(jnp.int32, (planes, cols), 0)
    below_y = jnp.where((plane_of < planes - 1) | jnp.logical_not(last_x), below_y, 0.0)
    corner = looked_up(corner_ref[...], inner_x & inner_y)[:1]

    def row_behind(value, first):
        return jnp.where(row == 0, first, pltpu.roll(value, 1, 0))

    def one_plane(i, value, first, earlier, earlier_first):
        s, s_first = with_behind(value), with_behind(first)
        t, t_first = with_behind(earlier), with_behind(earlier_first)
        z, z_first = value + earlier, first + earlier_first
        kx = factor * (s + row_behind(s, s_first))
        ky = factor * (s + t)
        kx_ref[i] = kx
        kz_ref[i] = factor * (z + row_behind(z, z_first))
        kick = kick_ref[i]
        ylow_ref[pl.ds(i, 1)] = kick[0:1] * factor * (s_first + t_first)
        yhigh_ref[pl.ds(i, 1)] = kick[rows - 1 : rows] * ky[rows - 1 : rows]
        ky_ref[i] = jnp.where(row < rows - 1, ky, 0.0)

    s, s_first = with_behind(below_x), with_behind(corner)
    xlow_ref[...] = kick_ref[0] * factor * (s + row_behind(s, s_first))
    earlier, earlier_first = below_x, corner
    for i in range(planes):
        value, first = el_ref[i], below_y[i : i + 1]
        one_plane(i, value, first, earlier, earlier_first)
        earlier, earlier_first = value, first
    xhigh_ref[...] = kick_ref[planes - 1] * kx_ref[planes - 1]
    push_ref[...] = contact_ref[...] * kick_ref[planes - 1] * (-PRESSURE_SCALE)


def interior_kernel(first, *refs):
    if first:
        u_in, w_in, kx_ref, ky_ref, kz_ref, kick_ref, u_ref, w_ref, y0_ref, y1_ref = refs
    else:
        (u_in, w_in, kx_ref, ky_ref, kz_ref, kick_ref, dx0_ref, dx1_ref, dy0_ref, dy1_ref,
         u_ref, w_ref, y0_ref, y1_ref) = refs
    _, planes, rows, cols = u_ref.shape
    if not first:
        patch(u_ref, w_ref, dx0_ref, dx1_ref, dy0_ref, dy1_ref)

    def plane(i, c, carried, ahead):
        here = u_ref[c, i]
        force = -carried
        pull_x = None
        if ahead is not None:
            pull_x = kx_ref[i] * jnp.tanh(ahead - here)
            force = force + pull_x
        pull_y = ky_ref[i] * jnp.tanh(pltpu.roll(here, rows - 1, 0) - here)
        force = force + (pull_y - pltpu.roll(pull_y, 1, 0))
        pull_z = kz_ref[i] * jnp.tanh(pltpu.roll(here, cols - 1, 1) - here)
        force = force + (pull_z - pltpu.roll(pull_z, 1, 1))
        w = w_ref[c, i] + kick_ref[i] * force
        u = here + w
        w_ref[c, i] = w
        u_ref[c, i] = u
        y0_ref[c, pl.ds(i, 1)] = u[0:1]
        y1_ref[c, pl.ds(i, 1)] = u[rows - 1 : rows]
        return pull_x

    def step(i, carried):
        return tuple(plane(i, c, carried[c], u_ref[c, i + 1]) for c in range(3))

    zero = jnp.zeros((rows, cols), jnp.float32)
    carried = lax.fori_loop(0, planes - 1, step, (zero, zero, zero))
    for c in range(3):
        plane(planes - 1, c, carried[c], None)


def patch(u_ref, w_ref, dx0_ref, dx1_ref, dy0_ref, dy1_ref):
    _, planes, rows, cols = u_ref.shape
    tile = math.gcd(8, rows)
    row = lax.broadcasted_iota(jnp.int32, (tile, cols), 0)
    low = jnp.where(row == 0, 1.0, 0.0)
    high = jnp.where(row == tile - 1, 1.0, 0.0)
    for ref in (u_ref, w_ref):
        ref[:, 0] += dx0_ref[...]
        ref[:, planes - 1] += dx1_ref[...]
        for c in range(3):
            for i in range(planes):
                ref[c, i, 0:tile] += low * dy0_ref[c, i : i + 1]
                ref[c, i, rows - tile : rows] += high * dy1_ref[c, i : i + 1]


def contact_kernel(scale, own_ref, near_ref, far_ref, pick_ref, push_ref, face_ref, out_ref, fx_ref, fy_ref, fz_ref):
    rows, cols = out_ref.shape
    lanes = pick_ref.shape[1]
    parts = lanes // rows
    deep = cols // parts
    is_face = face_ref[0] != 0

    @pl.when(jnp.logical_not(is_face))
    def _():
        out_ref[...] = jnp.zeros_like(out_ref)

    @pl.when(is_face)
    def _():
        pick = pick_ref[...]

        def matched(c):
            pool = jnp.concatenate([near_ref[c], far_ref[c]], axis=0)
            return lax.dot_general(
                pool, pick, (((0,), (0,)), ((), ())),
                precision=lax.Precision.HIGHEST, preferred_element_type=jnp.float32,
            )

        def own(c):
            turned = own_ref[c].T
            return jnp.concatenate([turned[h * deep : (h + 1) * deep] for h in range(parts)], axis=1)

        gap = scale * GAP_SCALE
        along = scale * YIELD_SPAN * SPAN
        fx_ref[...] = matched(0) * gap
        fy_ref[...] = matched(1) * along
        spot = lax.broadcasted_iota(jnp.int32, (cols, lanes), 0).astype(jnp.float32)
        fz_ref[...] = matched(2) * along + spot * SPAN
        lane = lax.broadcasted_iota(jnp.int32, (deep, lanes), 1)
        depth = lax.broadcasted_iota(jnp.int32, (deep, lanes), 0)
        mine = (depth + lane // rows * deep).astype(jnp.float32)
        ox = own(0) * gap
        oy = own(1) * along
        oz = own(2) * along + mine * SPAN

        def term(m, total):
            t = ox + fx_ref[pl.ds(m, 1)]
            dy = oy - fy_ref[pl.ds(m, 1)]
            dz = oz - fz_ref[pl.ds(m, 1)]
            weight = jnp.exp2(-(dy * dy + dz * dz))
            soft = jnp.maximum(t, 0.0) + jnp.log2(1.0 + jnp.exp2(-jnp.abs(t)))
            return total + weight * soft

        total = lax.fori_loop(0, cols, term, jnp.zeros((deep, lanes), jnp.float32), unroll=2)
        turned = jnp.concatenate([total[:, h * rows : (h + 1) * rows] for h in range(parts)], axis=0)
        out_ref[...] = turned.T * push_ref[...]


def boundary_kernel(
    scale, u_ref, y0_ref, y1_ref, sa_ref, sb_ref, sc_ref, sd_ref, ra_ref, rb_ref, rc_ref, rd_ref,
    xlow_ref, xhigh_ref, ylow_ref, yhigh_ref, push_ref, place_ref,
    na_ref, nb_ref, nc_ref, nd_ref, dx0_ref, dx1_ref, dy0_ref, dy1_ref,
):
    _, planes, rows, cols = u_ref.shape

    def halves(place, sent_a, sent_b, got_a, got_b, low_ref, high_ref):
        even = place % 2 == 0
        for c in range(3):
            a, b, x, y = sent_a[c], sent_b[c], got_a[c], got_b[c]
            first, last = jnp.where(even, b, a), jnp.where(even, a, b)
            before, after = jnp.where(even, y, x), jnp.where(even, x, y)
            yield (
                c,
                low_ref[...] * jnp.tanh((before - first) * scale),
                high_ref[...] * jnp.tanh((after - last) * scale),
            )

    for c, low, high in halves(place_ref[0], sa_ref, sb_ref, ra_ref, rb_ref, xlow_ref, xhigh_ref):
        if c == 0:
            high = high + push_ref[...]
        dx0_ref[c], dx1_ref[c] = low, high
    for c, low, high in halves(place_ref[2], sc_ref, sd_ref, rc_ref, rd_ref, ylow_ref, yhigh_ref):
        dy0_ref[c], dy1_ref[c] = low, high

    def send(first_ref, last_ref, side_first, side_last):
        for c in range(3):
            first_ref[c] = u_ref[c, 0] + dx0_ref[c]
            last_ref[c] = u_ref[c, planes - 1] + dx1_ref[c]
            side_first[c] = y0_ref[c] + dy0_ref[c]
            side_last[c] = y1_ref[c] + dy1_ref[c]
            for ref, i in ((first_ref, 0), (last_ref, planes - 1)):
                ref[c, 0:1] += dy0_ref[c, i : i + 1]
                ref[c, rows - 1 : rows] += dy1_ref[c, i : i + 1]
            for ref, j in ((side_first, 0), (side_last, rows - 1)):
                ref[c, 0:1] += dx0_ref[c, j : j + 1]
                ref[c, planes - 1 : planes] += dx1_ref[c, j : j + 1]

    even_x = place_ref[0] % 2 == 0
    even_y = place_ref[2] % 2 == 0
    for flag_x in (True, False):
        for flag_y in (True, False):

            @pl.when((even_x == flag_x) & (even_y == flag_y))
            def _(flag_x=flag_x, flag_y=flag_y):
                xs = (nb_ref, na_ref) if flag_x else (na_ref, nb_ref)
                ys = (nd_ref, nc_ref) if flag_y else (nc_ref, nd_ref)
                send(*xs, *ys)


def finish_kernel(u_in, w_in, dx0_ref, dx1_ref, dy0_ref, dy1_ref, d_ref, v_ref, u_ref, w_ref):
    planes = u_in.shape[1]
    patch(u_ref, w_ref, dx0_ref, dx1_ref, dy0_ref, dy1_ref)

    @pl.loop(0, planes)
    def _(i):
        for c in range(3):
            d_ref[c, i] = u_ref[c, i] * (1.0 / U_SCALE)
            v_ref[c, i] = w_ref[c, i] * (1.0 / W_SCALE)


def routes(count_body, count_x, count_y):
    def number(b, g, y):
        return (b * count_x + g) * count_y + y

    every = [(b, g, y) for b in range(count_body) for g in range(count_x) for y in range(count_y)]

    def pairs(target):
        return [(number(*at), number(*target(*at))) for at in every]

    def outer_x(b, g, y):
        if g in (0, count_x - 1):
            return 1 - b, g, y
        return b, (g + 1 if g % 2 else g - 1), y

    return {
        "a": pairs(lambda b, g, y: (b, g ^ 1, y)),
        "b": pairs(outer_x),
        "c": pairs(lambda b, g, y: (b, g, y ^ 1)),
        "d": pairs(lambda b, g, y: (b, g, (y + 1 if y % 2 else y - 1) % count_y)),
        "e": pairs(lambda b, g, y: (1 - b, g, (y - 1 if b else y + 1) % count_y)),
        "corner": pairs(lambda b, g, y: (b, (g + 1) % count_x, (y + 1) % count_y)),
    }


def contact_tables(partner, active, place_body, place_y, rows, rows_all, lanes):
    own = place_y * rows + jnp.arange(rows)
    index = jnp.arange(2 * rows)
    turn = jnp.where(place_body == 0, 1, -1)
    block = (place_y + turn * (index // rows)) % (rows_all // rows)
    pool = block * rows + index % rows
    both = jnp.concatenate([partner, partner])
    live = active.astype(jnp.float32)
    both_live = jnp.concatenate([live, live])

    def rows_of(table, first):
        return lax.dynamic_slice_in_dim(table, first, rows)

    start = place_y * rows
    other = (place_y + turn) % (rows_all // rows) * rows
    own_partner = rows_of(both, start)
    pool_partner = jnp.concatenate([own_partner, rows_of(both, other)])
    own_live = rows_of(both_live, start)
    pool_live = jnp.concatenate([own_live, rows_of(both_live, other)])
    near = own_partner[None, :] == pool[:, None]
    far = pool_partner[:, None] == own[None, :]
    match = jnp.where(place_body == 0, near, far).astype(jnp.float32)
    by_row = jnp.where(place_body == 0, own_live, jnp.sum(match * pool_live[:, None], axis=0))
    pick = jnp.concatenate([match] * (lanes // rows), axis=1)
    return pick, by_row


def local(displacement, velocity, material, moduli, density, partner, active):
    planes, rows, cols = displacement.shape[2:]
    count_x, count_y = lax.axis_size("gx"), lax.axis_size("yz")
    place_x, place_y, place_body = lax.axis_index("gx"), lax.axis_index("yz"), lax.axis_index("body")
    route = routes(lax.axis_size("body"), count_x, count_y)
    lanes = 128
    shape = (3, planes, rows, cols)
    d, v, kinds = displacement[0], velocity[0], material[0]
    place = jnp.stack([place_x, jnp.int32(count_x), place_y, jnp.int32(count_y)])
    face = jnp.stack([(place_x == count_x - 1).astype(jnp.int32)])
    smem = pltpu.SMEM

    def passed(block, name):
        return lax.ppermute(block, AXES, route[name])

    def packed(block, kind):
        return jnp.concatenate([block, kind[None].astype(jnp.float32)], axis=0)

    even_x, even_y = place_x % 2 == 0, place_y % 2 == 0
    first_x, last_x = packed(d[:, 0], kinds[0]), packed(d[:, planes - 1], kinds[planes - 1])
    first_y, last_y = packed(d[:, :, 0], kinds[:, 0]), packed(d[:, :, rows - 1], kinds[:, rows - 1])
    sent = [
        jnp.where(even_x, last_x, first_x),
        jnp.where(even_x, first_x, last_x),
        jnp.where(even_y, last_y, first_y),
        jnp.where(even_y, first_y, last_y),
    ]
    corner = kinds[planes - 1, rows - 1 :].astype(jnp.float32)

    def exchange(sent):
        got_e = passed(sent[1][:3], "e")
        got_b = passed(sent[1], "b")
        got_c = passed(sent[2], "c")
        got_d = passed(sent[3], "d")
        got_a = passed(sent[0], "a")
        return got_a, got_b, got_c, got_d, got_e

    got = exchange(sent)
    corner = passed(corner, "corner")
    pick, by_row = contact_tables(partner, active, place_body, place_y, rows, rows * count_y, lanes)
    by_node = jnp.broadcast_to(by_row[:, None], (rows, cols))

    u, w, el, kick = call(
        prepare_kernel,
        [vmem(shape), vmem(shape), vmem(shape[1:]), vmem(shape[1:])],
        [d, v, kinds, moduli, density, place],
        [pltpu.VMEM] * 3 + [smem] * 3,
        flops=8_000_000, moved=0,
    )
    kx, ky, kz, xlow, xhigh, ylow, yhigh, push_scale = call(
        stiffness_kernel,
        [vmem(shape[1:])] * 3 + [vmem((rows, cols))] * 2 + [vmem((planes, cols))] * 2 + [vmem((rows, cols))],
        [el, kick, *got[:4], corner, moduli, place, by_node],
        [None] * 7 + [smem] * 2 + [None],
    )
    edges = [xlow, xhigh, ylow, yhigh]
    fixes = []
    for step in range(STEPS):
        scale = U_SCALE if step == 0 else 1.0
        if step:
            got = exchange(sent)
        u, w, y0, y1 = call(
            functools.partial(interior_kernel, step == 0),
            [vmem(shape), vmem(shape), vmem((3, planes, cols)), vmem((3, planes, cols))],
            [u, w, kx, ky, kz, kick, *fixes],
            aliases={0: 0, 1: 1},
            flops=20_000_000,
        )
        (push,) = call(
            functools.partial(contact_kernel, scale),
            [vmem((rows, cols))],
            [sent[1], got[1], got[4], pick, push_scale, face],
            [None] * 5 + [smem],
            scratch=[vmem((cols, lanes))] * 3,
            flops=20_000_000,
        )
        *sent, dx0, dx1, dy0, dy1 = call(
            functools.partial(boundary_kernel, scale),
            [vmem((3, rows, cols))] * 2 + [vmem((3, planes, cols))] * 2
            + [vmem((3, rows, cols))] * 2 + [vmem((3, planes, cols))] * 2,
            [u, y0, y1, *sent, *got[:4], *edges, push, place],
            [None] * 16 + [smem],
        )
        fixes = [dx0, dx1, dy0, dy1]
    d, v, _, _ = call(
        finish_kernel,
        [jax.ShapeDtypeStruct(shape, jnp.float32)] * 2 + [vmem(shape)] * 2,
        [u, w, *fixes],
        aliases={0: 2, 1: 3},
    )
    return d[None], v[None]


def solution(mesh):
    in_specs = (
        P("body", None, "gx", "yz", None),
        P("body", None, "gx", "yz", None),
        P("body", "gx", "yz", None),
        P(),
        P(),
        P(),
        P(),
    )
    out_specs = (P("body", None, "gx", "yz", None), P("body", None, "gx", "yz", None))
    return jax.shard_map(local, mesh=mesh, in_specs=in_specs, out_specs=out_specs, check_vma=False)
```

time: 186 us -> 60.8 us (0.33)
  the two profiles are of different devices: /device:TPU:30 before, /device:TPU:27 now
where the time goes in v1:
time: 60.8 us; the launch traced here: 60.6 us
  Pallas kernels  35.9 us (59%)
  starting transfers between devices  15.9 us (26%)
  local copies, waits for them, and re-layouts  4.19 us (7%)
  waiting for transfers between devices  3.16 us (5%)
  between operations  1 us (2%)
    pallas_call x15, Pallas kernels, call(): pl.pallas_call(kernel, out_shape=outs, in_specs=specs, out_specs=[pl.Bloc...  35.9 us
    ppermute x21, starting transfers between devices, passed(): return lax.ppermute(block, AXES, route[name])  15.9 us
    unnamed x13, local copies, waits for them, and re-layouts  3.78 us
    ppermute x21, waiting for transfers between devices, passed(): return lax.ppermute(block, AXES, route[name])  3.16 us
  transfers between devices with their start and end apart: 21, of which 3 were waited for; matrix products, arithmetic and copies ran while one was open for 5% of the time, Pallas kernels for 44%

profile of v1, /device:TPU:27, one launch (start us, length us, event | category | flops | bytes accessed | tf_op | source)
XLA Modules:
  0.0 60.6 jit_solution(527970645522633086)
XLA Ops:
  0.6 1.4 %copy.61 = s32[1,16,64,128]{3,1,2,0:T(8,128)S(1)} copy(s32[1,16,64,128]{3,2,1,0:T(8,128)} %param.9) | data formatting | bytes 1048576 | tf_op args[2]
  2.0 1.5 %collective-permute-start.4 = (f32[1,128]{1,0:T(1,128)S(1)}, f32[1,128]{1,0:T(1,128)S(1)}, u32[]{:S(2)}, u32[]{:S(2)}) collective-permute-start(f32[1,128]{1,0:T(1,128)S(1)} %fusion.11), channel_id=1, source_target_pairs={{0,5},{1,6},{2,7},{3,4},{4,9},{5,10},{6,11},{7,8},{8,13},{9,14},{1... | collective-permute-start | bytes 1544 | tf_op jit(solution)/shard_map/ppermute | solution.py:371
  3.5 2.4 %copy.60 = f32[1,3,16,64,128]{4,2,1,3,0:T(8,128)S(1)} copy(f32[1,3,16,64,128]{4,3,2,1,0:T(8,128)} %param.7) | data formatting | bytes 3145728 | tf_op args[0]
  6.0 0.5 collective-permute-start.3
  6.9 1.6 %collective-permute-start = (f32[4,64,128]{2,1,0:T(8,128)S(1)}, f32[4,64,128]{2,1,0:T(8,128)S(1)}, u32[]{:S(2)}, u32[]{:S(2)}) collective-permute-start(f32[4,64,128]{2,1,0:T(8,128)S(1)} %get-tuple-element.129.sa_ref), channel_id=1, source_target_pairs={{0,4},{1,5},{2,6},{3,7},{4,0},{5,1},{6,2},{7,3},{8,12},{9,13},{10,... | collective-permute-start | bytes 393224 | tf_op jit(solution)/shard_map/ppermute | solution.py:371
  9.4 1.7 %collective-permute-start.5 = (f32[3,64,128]{2,1,0:T(8,128)S(1)}, f32[3,64,128]{2,1,0:T(8,128)S(1)}, u32[]{:S(2)}, u32[]{:S(2)}) collective-permute-start(f32[3,64,128]{2,1,0:T(8,128)S(1)} %slice.49), channel_id=1, source_target_pairs={{0,17},{1,18},{2,19},{3,16},{4,21},{5,22},{6,23},{7,20},{8,25},{9,... | collective-permute-start | bytes 294920 | tf_op jit(solution)/shard_map/ppermute | solution.py:371
  11.2 2.9 %shard_map.86 = (f32[3,16,64,128]{3,2,1,0:T(8,128)S(1)}, f32[3,16,64,128]{3,2,1,0:T(8,128)S(1)}, f32[16,64,128]{2,1,0:T(8,128)S(1)}, f32[16,64,128]{2,1,0:T(8,128)S(1)}) custom-call(f32[3,16,64,128]{3,2,1,0:T(8,128)} %bitcast.33, f32[3,16,64,128]{3,2,1,0:T(8,128)} %bitcast.36, s32[16,64,128]{2,1,0:T(8,128)S(1)} %bitcast.32, f32[8]{0:T(128)S(1)} %copy-done.1, ...), custom_call_target="tpu_custom_call" | custom-call | flops 8000000 | tf_op jit(solution)/shard_map/pallas_call | solution.py:44
  14.2 0.8 %shard_map.87 = (f32[16,64,128]{2,1,0:T(8,128)S(1)}, f32[16,64,128]{2,1,0:T(8,128)S(1)}, f32[16,64,128]{2,1,0:T(8,128)S(1)}, f32[64,128]{1,0:T(8,128)S(1)}, f32[...) custom-call(f32[16,64,128]{2,1,0:T(8,128)S(1)} %get-tuple-element.62.el_ref, ...), custom_call_target="tpu_custom_call" | custom-call | tf_op jit(solution)/shard_map/pallas_call | solution.py:44
  15.0 2.8 %shard_map.88 = (f32[3,16,64,128]{3,2,1,0:T(8,128)S(1)}, f32[3,16,64,128]{3,2,1,0:T(8,128)S(1)}, f32[3,16,128]{2,1,0:T(8,128)S(1)}, f32[3,16,128]{2,1,0:T(8,128)S(1)}) custom-call(f32[3,16,64,128]{3,2,1,0:T(8,128)S(1)} %get-tuple-element.60.refs_0_, f32[3,16,64,128]{3,2,1,0:T(8,128)S(1)} %get-tuple-element.61.refs_1_, ...), custom_call_target="tpu_custom_call", output_to_operand_aliasing={{0}: (0, {}), {1}: (1, {})} | custom-call | flops 20000000 | tf_op jit(solution)/shard_map/pallas_call | solution.py:44
  17.8 3.8 %shard_map.89.push_ref = f32[64,128]{1,0:T(8,128)S(1)} custom-call(f32[4,64,128]{2,1,0:T(8,128)S(1)} %get-tuple-element.128.own_ref.sb_ref, f32[4,64,128]{2,1,0:T(8,128)S(1)} %collective-permute-done.1.rb_ref.near_ref, f32[3,64,128]{2,1,0:T(8,128)S(1)} %collective-permute-done.5.far_ref, f32[128,128]{1,0:T(8,128)S(1)} %add_convert_fusion.pick_ref, ...), custom_call_target="tpu_custom_call" | custom-call | flops 20000000 | tf_op jit(solution)/shard_map/pallas_call | solution.py:44
  21.6 0.7 %shard_map.90 = (f32[3,64,128]{2,1,0:T(8,128)S(1)}, f32[3,64,128]{2,1,0:T(8,128)S(1)}, f32[3,16,128]{2,1,0:T(8,128)S(1)}, f32[3,16,128]{2,1,0:T(8,128)S(1)}, f32...) custom-call(f32[3,16,64,128]{3,2,1,0:T(8,128)S(1)} %get-tuple-element, ...), custom_call_target="tpu_custom_call" | custom-call | tf_op jit(solution)/shard_map/pallas_call | solution.py:44
  22.3 0.9 %collective-permute-start.10 = (f32[3,64,128]{2,1,0:T(8,128)S(1)}, f32[3,64,128]{2,1,0:T(8,128)S(1)}, u32[]{:S(2)}, u32[]{:S(2)}) collective-permute-start(f32[3,64,128]{2,1,0:T(8,128)S(1)} %get-tuple-element.85.own_ref.sb_ref), channel_id=1, source_target_pairs={{0,17},{1,18},{2,19},{3,16},{4,21},{5,22},{6,23},{7,20},{8,25},{9,... | collective-permute-start | bytes 294920 | tf_op jit(solution)/shard_map/ppermute | solution.py:371
  23.2 2.5 %collective-permute-start.7 = (f32[3,64,128]{2,1,0:T(8,128)S(1)}, f32[3,64,128]{2,1,0:T(8,128)S(1)}, u32[]{:S(2)}, u32[]{:S(2)}) collective-permute-start(f32[3,64,128]{2,1,0:T(8,128)S(1)} %get-tuple-element.85.own_ref.sb_ref), channel_id=1, source_target_pairs={{0,16},{1,17},{2,18},{3,19},{4,8},{5,9},{6,10},{7,11},{8,4},{9,5},... | collective-permute-start | bytes 294920 | tf_op jit(solution)/shard_map/ppermute | solution.py:371
  25.7 0.5 collective-permute-start.9
  26.2 2.9 %shard_map.91 = (f32[3,16,64,128]{3,2,1,0:T(8,128)S(1)}, f32[3,16,64,128]{3,2,1,0:T(8,128)S(1)}, f32[3,16,128]{2,1,0:T(8,128)S(1)}, f32[3,16,128]{2,1,0:T(8,128)S(1)}) custom-call(f32[3,16,64,128]{3,2,1,0:T(8,128)S(1)} %get-tuple-element.67.u_ref.refs_0_, ...), custom_call_target="tpu_custom_call", output_to_operand_aliasing={{0}: (0, {}), {1}: (1, {})} | custom-call | flops 20000000 | tf_op jit(solution)/shard_map/pallas_call | solution.py:44
  29.1 0.6 %collective-permute-done.7.near_ref.rb_ref = f32[3,64,128]{2,1,0:T(8,128)S(1)} collective-permute-done((f32[3,64,128]{2,1,0:T(8,128)S(1)}, f32[3,64,128]{2,1,0:T(8,128)S(1)}, u32[]{:S(2)}, u32[]{:S(2)}) %collective-permute-start.7) | collective-permute-done | bytes 98336 | tf_op jit(solution)/shard_map/ppermute | solution.py:371
  29.8 3.8 %shard_map.92.push_ref = f32[64,128]{1,0:T(8,128)S(1)} custom-call(f32[3,64,128]{2,1,0:T(8,128)S(1)} %get-tuple-element.85.own_ref.sb_ref, f32[3,64,128]{2,1,0:T(8,128)S(1)} %collective-permute-done.7.near_ref.rb_ref, f32[3,64,128]{2,1,0:T(8,128)S(1)} %collective-permute-done.10.far_ref, f32[128,128]{1,0:T(8,128)S(1)} %add_convert_fusion.pick_ref, ...), custom_call_target="tpu_custom_call" | custom-call | flops 20000000 | tf_op jit(solution)/shard_map/pallas_call | solution.py:44
  33.6 0.7 %shard_map.93 = (f32[3,64,128]{2,1,0:T(8,128)S(1)}, f32[3,64,128]{2,1,0:T(8,128)S(1)}, f32[3,16,128]{2,1,0:T(8,128)S(1)}, f32[3,16,128]{2,1,0:T(8,128)S(1)}, f32...) custom-call(f32[3,16,64,128]{3,2,1,0:T(8,128)S(1)} %get-tuple-element, ...), custom_call_target="tpu_custom_call" | custom-call | tf_op jit(solution)/shard_map/pallas_call | solution.py:44
  34.3 0.4 collective-permute-start.15
  34.7 2.2 %collective-permute-start.12 = (f32[3,64,128]{2,1,0:T(8,128)S(1)}, f32[3,64,128]{2,1,0:T(8,128)S(1)}, u32[]{:S(2)}, u32[]{:S(2)}) collective-permute-start(f32[3,64,128]{2,1,0:T(8,128)S(1)} %get-tuple-element.97.own_ref.sb_ref), channel_id=1, source_target_pairs={{0,16},{1,17},{2,18},{3,19},{4,8},{5,9},{6,10},{7,11},{8,4},{9,5},... | collective-permute-start | bytes 294920 | tf_op jit(solution)/shard_map/ppermute | solution.py:371
  36.9 0.6 collective-permute-start.14
  37.5 2.9 %shard_map.94 = (f32[3,16,64,128]{3,2,1,0:T(8,128)S(1)}, f32[3,16,64,128]{3,2,1,0:T(8,128)S(1)}, f32[3,16,128]{2,1,0:T(8,128)S(1)}, f32[3,16,128]{2,1,0:T(8,128)S(1)}) custom-call(f32[3,16,64,128]{3,2,1,0:T(8,128)S(1)} %get-tuple-element.80.u_ref.refs_0_, ...), custom_call_target="tpu_custom_call", output_to_operand_aliasing={{0}: (0, {}), {1}: (1, {})} | custom-call | flops 20000000 | tf_op jit(solution)/shard_map/pallas_call | solution.py:44
  40.5 1.2 %collective-permute-done.12.near_ref.rb_ref = f32[3,64,128]{2,1,0:T(8,128)S(1)} collective-permute-done((f32[3,64,128]{2,1,0:T(8,128)S(1)}, f32[3,64,128]{2,1,0:T(8,128)S(1)}, u32[]{:S(2)}, u32[]{:S(2)}) %collective-permute-start.12) | collective-permute-done | bytes 98336 | tf_op jit(solution)/shard_map/ppermute | solution.py:371
  41.7 3.8 %shard_map.95.push_ref = f32[64,128]{1,0:T(8,128)S(1)} custom-call(f32[3,64,128]{2,1,0:T(8,128)S(1)} %get-tuple-element.97.own_ref.sb_ref, f32[3,64,128]{2,1,0:T(8,128)S(1)} %collective-permute-done.12.near_ref.rb_ref, f32[3,64,128]{2,1,0:T(8,128)S(1)} %collective-permute-done.15.far_ref, f32[128,128]{1,0:T(8,128)S(1)} %add_convert_fusion.pick_ref, ...), custom_call_target="tpu_custom_call" | custom-call | flops 20000000 | tf_op jit(solution)/shard_map/pallas_call | solution.py:44
  45.5 0.7 %shard_map.96 = (f32[3,64,128]{2,1,0:T(8,128)S(1)}, f32[3,64,128]{2,1,0:T(8,128)S(1)}, f32[3,16,128]{2,1,0:T(8,128)S(1)}, f32[3,16,128]{2,1,0:T(8,128)S(1)}, f32...) custom-call(f32[3,16,64,128]{3,2,1,0:T(8,128)S(1)} %get-tuple-element, ...), custom_call_target="tpu_custom_call" | custom-call | tf_op jit(solution)/shard_map/pallas_call | solution.py:44
  46.3 1.8 %collective-permute-start.17 = (f32[3,64,128]{2,1,0:T(8,128)S(1)}, f32[3,64,128]{2,1,0:T(8,128)S(1)}, u32[]{:S(2)}, u32[]{:S(2)}) collective-permute-start(f32[3,64,128]{2,1,0:T(8,128)S(1)} %get-tuple-element.109.own_ref.sb_ref), channel_id=1, source_target_pairs={{0,16},{1,17},{2,18},{3,19},{4,8},{5,9},{6,10},{7,11},{8,4},{9,5},... | collective-permute-start | bytes 294920 | tf_op jit(solution)/shard_map/ppermute | solution.py:371
  48.4 0.8 %collective-permute-start.19 = (f32[3,16,128]{2,1,0:T(8,128)S(1)}, f32[3,16,128]{2,1,0:T(8,128)S(1)}, u32[]{:S(2)}, u32[]{:S(2)}) collective-permute-start(f32[3,16,128]{2,1,0:T(8,128)S(1)} %get-tuple-element.111.sd_ref), channel_id=1, source_target_pairs={{0,3},{1,2},{2,1},{3,0},{4,7},{5,6},{6,5},{7,4},{8,11},{9,10},{10,... | collective-permute-start | bytes 73736 | tf_op jit(solution)/shard_map/ppermute | solution.py:371
  49.2 3.0 %shard_map.97 = (f32[3,16,64,128]{3,2,1,0:T(8,128)S(1)}, f32[3,16,64,128]{3,2,1,0:T(8,128)S(1)}, f32[3,16,128]{2,1,0:T(8,128)S(1)}, f32[3,16,128]{2,1,0:T(8,128)S(1)}) custom-call(f32[3,16,64,128]{3,2,1,0:T(8,128)S(1)} %get-tuple-element.92.u_ref.refs_0_, ...), custom_call_target="tpu_custom_call", output_to_operand_aliasing={{0}: (0, {}), {1}: (1, {})} | custom-call | flops 20000000 | tf_op jit(solution)/shard_map/pallas_call | solution.py:44
  52.1 1.2 %collective-permute-done.17.near_ref.rb_ref = f32[3,64,128]{2,1,0:T(8,128)S(1)} collective-permute-done((f32[3,64,128]{2,1,0:T(8,128)S(1)}, f32[3,64,128]{2,1,0:T(8,128)S(1)}, u32[]{:S(2)}, u32[]{:S(2)}) %collective-permute-start.17) | collective-permute-done | bytes 98336 | tf_op jit(solution)/shard_map/ppermute | solution.py:371
  53.4 3.8 %shard_map.98.push_ref = f32[64,128]{1,0:T(8,128)S(1)} custom-call(f32[3,64,128]{2,1,0:T(8,128)S(1)} %get-tuple-element.109.own_ref.sb_ref, f32[3,64,128]{2,1,0:T(8,128)S(1)} %collective-permute-done.17.near_ref.rb_ref, f32[3,64,128]{2,1,0:T(8,128)S(1)} %collective-permute-done.20.far_ref, f32[128,128]{1,0:T(8,128)S(1)} %add_convert_fusion.pick_ref, ...), custom_call_target="tpu_custom_call" | custom-call | flops 20000000 | tf_op jit(solution)/shard_map/pallas_call | solution.py:44
  57.2 1.4 %shard_map.99 = (f32[3,64,128]{2,1,0:T(8,128)}, f32[3,64,128]{2,1,0:T(8,128)}, f32[3,16,128]{2,1,0:T(8,128)}, f32[3,16,128]{2,1,0:T(8,128)}, f32[3,64,128]{2,1,0...) custom-call(f32[3,16,64,128]{3,2,1,0:T(8,128)S(1)} %get-tuple-element.104.u_ref.u_in,, ...), custom_call_target="tpu_custom_call" | custom-call | tf_op jit(solution)/shard_map/pallas_call | solution.py:44
  58.6 2.1 %shard_map.100 = (f32[3,16,64,128]{3,2,1,0:T(8,128)}, f32[3,16,64,128]{3,2,1,0:T(8,128)}, f32[3,16,64,128]{3,2,1,0:T(8,128)S(1)}, f32[3,16,64,128]{3,2,1,0:T(8,128)S(1)}) custom-call(f32[3,16,64,128]{3,2,1,0:T(8,128)S(1)} %get-tuple-element.104.u_ref.u_in, ...), custom_call_target="tpu_custom_call", output_to_operand_aliasing={{2}: (0, {}), {3}: (1, {})} | custom-call | tf_op jit(solution)/shard_map/pallas_call | solution.py:44
  (61 shorter events, 1.9 us)
Async XLA Ops:
  2.0 7.4 %collective-permute-start.4 = (f32[1,128]{1,0:T(1,128)S(1)}, f32[1,128]{1,0:T(1,128)S(1)}, u32[]{:S(2)}, u32[]{:S(2)}) collective-permute-start(f32[1,128]{1,0:T(1,128)S(1)} %fusion.11), channel_id=1, source_target_pairs={{0,5},{1,6},{2,7},{3,4},{4,9},{5,10},{6,11},{7,8},{8,13},{9,14},{1... | collective-permute-start | bytes 1544 | tf_op jit(solution)/shard_map/ppermute | solution.py:371
  3.5 3.2 %copy-start = (s32[1,16,64,128]{3,2,1,0:T(8,128)S(1)}, s32[1,16,64,128]{3,2,1,0:T(8,128)}, u32[]{:S(2)}) copy-start(s32[1,16,64,128]{3,2,1,0:T(8,128)} %param.9) | copy-start | bytes 1572868
  5.9 2.8 %copy-start.4 = (s32[256]{0:T(256)S(1)}, s32[256]{0:T(256)}, u32[]{:S(2)}) copy-start(s32[256]{0:T(256)} %param.13) | copy-start | bytes 3076
  5.9 2.8 %copy-start.3 = (s32[256]{0:T(256)S(1)}, s32[256]{0:T(256)}, u32[]{:S(2)}) copy-start(s32[256]{0:T(256)} %param.12) | copy-start | bytes 3076
  5.9 5.3 %copy-start.1 = (f32[8]{0:T(128)S(1)}, f32[8]{0:T(128)}, u32[]{:S(2)}) copy-start(f32[8]{0:T(128)} %moduli_ref.3) | copy-start | bytes 100
  5.9 5.2 %copy-start.2 = (f32[8]{0:T(128)S(1)}, f32[8]{0:T(128)}, u32[]{:S(2)}) copy-start(f32[8]{0:T(128)} %density_ref.1) | copy-start | bytes 100
  6.0 8.1 %collective-permute-start.3 = (f32[4,16,128]{2,1,0:T(8,128)S(1)}, f32[4,16,128]{2,1,0:T(8,128)S(1)}, u32[]{:S(2)}, u32[]{:S(2)}) collective-permute-start(f32[4,16,128]{2,1,0:T(8,128)S(1)} %get-tuple-element.130.sd_ref), channel_id=1, source_target_pairs={{0,3},{1,2},{2,1},{3,0},{4,7},{5,6},{6,5},{7,4},{8,11},{9,10},{10,... | collective-permute-start | bytes 98312 | tf_op jit(solution)/shard_map/ppermute | solution.py:371
  6.4 7.6 %collective-permute-start.2 = (f32[4,16,128]{2,1,0:T(8,128)S(1)}, f32[4,16,128]{2,1,0:T(8,128)S(1)}, u32[]{:S(2)}, u32[]{:S(2)}) collective-permute-start(f32[4,16,128]{2,1,0:T(8,128)S(1)} %get-tuple-element.131.sc_ref), channel_id=1, source_target_pairs={{0,1},{1,0},{2,3},{3,2},{4,5},{5,4},{6,7},{7,6},{8,9},{9,8},{10,11... | collective-permute-start | bytes 98312 | tf_op jit(solution)/shard_map/ppermute | solution.py:371
  6.9 7.2 %collective-permute-start = (f32[4,64,128]{2,1,0:T(8,128)S(1)}, f32[4,64,128]{2,1,0:T(8,128)S(1)}, u32[]{:S(2)}, u32[]{:S(2)}) collective-permute-start(f32[4,64,128]{2,1,0:T(8,128)S(1)} %get-tuple-element.129.sa_ref), channel_id=1, source_target_pairs={{0,4},{1,5},{2,6},{3,7},{4,0},{5,1},{6,2},{7,3},{8,12},{9,13},{10,... | collective-permute-start | bytes 393224 | tf_op jit(solution)/shard_map/ppermute | solution.py:371
  8.5 5.6 %collective-permute-start.1 = (f32[4,64,128]{2,1,0:T(8,128)S(1)}, f32[4,64,128]{2,1,0:T(8,128)S(1)}, u32[]{:S(2)}, u32[]{:S(2)}) collective-permute-start(f32[4,64,128]{2,1,0:T(8,128)S(1)} %get-tuple-element.128.own_ref.sb_ref), channel_id=1, source_target_pairs={{0,16},{1,17},{2,18},{3,19},{4,8},{5,9},{6,10},{7,11},{8,4},{9,5},... | collective-permute-start | bytes 393224 | tf_op jit(solution)/shard_map/ppermute | solution.py:371
  9.4 8.4 %collective-permute-start.5 = (f32[3,64,128]{2,1,0:T(8,128)S(1)}, f32[3,64,128]{2,1,0:T(8,128)S(1)}, u32[]{:S(2)}, u32[]{:S(2)}) collective-permute-start(f32[3,64,128]{2,1,0:T(8,128)S(1)} %slice.49), channel_id=1, source_target_pairs={{0,17},{1,18},{2,19},{3,16},{4,21},{5,22},{6,23},{7,20},{8,25},{9,... | collective-permute-start | bytes 294920 | tf_op jit(solution)/shard_map/ppermute | solution.py:371
  22.3 6.9 %collective-permute-start.10 = (f32[3,64,128]{2,1,0:T(8,128)S(1)}, f32[3,64,128]{2,1,0:T(8,128)S(1)}, u32[]{:S(2)}, u32[]{:S(2)}) collective-permute-start(f32[3,64,128]{2,1,0:T(8,128)S(1)} %get-tuple-element.85.own_ref.sb_ref), channel_id=1, source_target_pairs={{0,17},{1,18},{2,19},{3,16},{4,21},{5,22},{6,23},{7,20},{8,25},{9,... | collective-permute-start | bytes 294920 | tf_op jit(solution)/shard_map/ppermute | solution.py:371
  23.2 6.6 %collective-permute-start.7 = (f32[3,64,128]{2,1,0:T(8,128)S(1)}, f32[3,64,128]{2,1,0:T(8,128)S(1)}, u32[]{:S(2)}, u32[]{:S(2)}) collective-permute-start(f32[3,64,128]{2,1,0:T(8,128)S(1)} %get-tuple-element.85.own_ref.sb_ref), channel_id=1, source_target_pairs={{0,16},{1,17},{2,18},{3,19},{4,8},{5,9},{6,10},{7,11},{8,4},{9,5},... | collective-permute-start | bytes 294920 | tf_op jit(solution)/shard_map/ppermute | solution.py:371
  25.7 7.9 %collective-permute-start.6 = (f32[3,64,128]{2,1,0:T(8,128)S(1)}, f32[3,64,128]{2,1,0:T(8,128)S(1)}, u32[]{:S(2)}, u32[]{:S(2)}) collective-permute-start(f32[3,64,128]{2,1,0:T(8,128)S(1)} %get-tuple-element.84.sa_ref), channel_id=1, source_target_pairs={{0,4},{1,5},{2,6},{3,7},{4,0},{5,1},{6,2},{7,3},{8,12},{9,13},{10,... | collective-permute-start | bytes 294920 | tf_op jit(solution)/shard_map/ppermute | solution.py:371
  25.7 7.9 %collective-permute-start.8 = (f32[3,16,128]{2,1,0:T(8,128)S(1)}, f32[3,16,128]{2,1,0:T(8,128)S(1)}, u32[]{:S(2)}, u32[]{:S(2)}) collective-permute-start(f32[3,16,128]{2,1,0:T(8,128)S(1)} %get-tuple-element.86.sc_ref), channel_id=1, source_target_pairs={{0,1},{1,0},{2,3},{3,2},{4,5},{5,4},{6,7},{7,6},{8,9},{9,8},{10,11... | collective-permute-start | bytes 73736 | tf_op jit(solution)/shard_map/ppermute | solution.py:371
  25.7 7.9 %collective-permute-start.9 = (f32[3,16,128]{2,1,0:T(8,128)S(1)}, f32[3,16,128]{2,1,0:T(8,128)S(1)}, u32[]{:S(2)}, u32[]{:S(2)}) collective-permute-start(f32[3,16,128]{2,1,0:T(8,128)S(1)} %get-tuple-element.87.sd_ref), channel_id=1, source_target_pairs={{0,3},{1,2},{2,1},{3,0},{4,7},{5,6},{6,5},{7,4},{8,11},{9,10},{10,... | collective-permute-start | bytes 73736 | tf_op jit(solution)/shard_map/ppermute | solution.py:371
  34.3 6.2 %collective-permute-start.15 = (f32[3,64,128]{2,1,0:T(8,128)S(1)}, f32[3,64,128]{2,1,0:T(8,128)S(1)}, u32[]{:S(2)}, u32[]{:S(2)}) collective-permute-start(f32[3,64,128]{2,1,0:T(8,128)S(1)} %get-tuple-element.97.own_ref.sb_ref), channel_id=1, source_target_pairs={{0,17},{1,18},{2,19},{3,16},{4,21},{5,22},{6,23},{7,20},{8,25},{9,... | collective-permute-start | bytes 294920 | tf_op jit(solution)/shard_map/ppermute | solution.py:371
  34.7 7.0 %collective-permute-start.12 = (f32[3,64,128]{2,1,0:T(8,128)S(1)}, f32[3,64,128]{2,1,0:T(8,128)S(1)}, u32[]{:S(2)}, u32[]{:S(2)}) collective-permute-start(f32[3,64,128]{2,1,0:T(8,128)S(1)} %get-tuple-element.97.own_ref.sb_ref), channel_id=1, source_target_pairs={{0,16},{1,17},{2,18},{3,19},{4,8},{5,9},{6,10},{7,11},{8,4},{9,5},... | collective-permute-start | bytes 294920 | tf_op jit(solution)/shard_map/ppermute | solution.py:371
  36.9 8.6 %collective-permute-start.11 = (f32[3,64,128]{2,1,0:T(8,128)S(1)}, f32[3,64,128]{2,1,0:T(8,128)S(1)}, u32[]{:S(2)}, u32[]{:S(2)}) collective-permute-start(f32[3,64,128]{2,1,0:T(8,128)S(1)} %get-tuple-element.96.sa_ref), channel_id=1, source_target_pairs={{0,4},{1,5},{2,6},{3,7},{4,0},{5,1},{6,2},{7,3},{8,12},{9,13},{10,... | collective-permute-start | bytes 294920 | tf_op jit(solution)/shard_map/ppermute | solution.py:371
  36.9 8.5 %collective-permute-start.13 = (f32[3,16,128]{2,1,0:T(8,128)S(1)}, f32[3,16,128]{2,1,0:T(8,128)S(1)}, u32[]{:S(2)}, u32[]{:S(2)}) collective-permute-start(f32[3,16,128]{2,1,0:T(8,128)S(1)} %get-tuple-element.98.sc_ref), channel_id=1, source_target_pairs={{0,1},{1,0},{2,3},{3,2},{4,5},{5,4},{6,7},{7,6},{8,9},{9,8},{10,11... | collective-permute-start | bytes 73736 | tf_op jit(solution)/shard_map/ppermute | solution.py:371
  36.9 8.6 %collective-permute-start.14 = (f32[3,16,128]{2,1,0:T(8,128)S(1)}, f32[3,16,128]{2,1,0:T(8,128)S(1)}, u32[]{:S(2)}, u32[]{:S(2)}) collective-permute-start(f32[3,16,128]{2,1,0:T(8,128)S(1)} %get-tuple-element.99.sd_ref), channel_id=1, source_target_pairs={{0,3},{1,2},{2,1},{3,0},{4,7},{5,6},{6,5},{7,4},{8,11},{9,10},{10,... | collective-permute-start | bytes 73736 | tf_op jit(solution)/shard_map/ppermute | solution.py:371
  46.2 5.9 %collective-permute-start.20 = (f32[3,64,128]{2,1,0:T(8,128)S(1)}, f32[3,64,128]{2,1,0:T(8,128)S(1)}, u32[]{:S(2)}, u32[]{:S(2)}) collective-permute-start(f32[3,64,128]{2,1,0:T(8,128)S(1)} %get-tuple-element.109.own_ref.sb_ref), channel_id=1, source_target_pairs={{0,17},{1,18},{2,19},{3,16},{4,21},{5,22},{6,23},{7,20},{8,25},{9,... | collective-permute-start | bytes 294920 | tf_op jit(solution)/shard_map/ppermute | solution.py:371
  46.3 7.1 %collective-permute-start.17 = (f32[3,64,128]{2,1,0:T(8,128)S(1)}, f32[3,64,128]{2,1,0:T(8,128)S(1)}, u32[]{:S(2)}, u32[]{:S(2)}) collective-permute-start(f32[3,64,128]{2,1,0:T(8,128)S(1)} %get-tuple-element.109.own_ref.sb_ref), channel_id=1, source_target_pairs={{0,16},{1,17},{2,18},{3,19},{4,8},{5,9},{6,10},{7,11},{8,4},{9,5},... | collective-permute-start | bytes 294920 | tf_op jit(solution)/shard_map/ppermute | solution.py:371
  48.1 9.1 %collective-permute-start.16 = (f32[3,64,128]{2,1,0:T(8,128)S(1)}, f32[3,64,128]{2,1,0:T(8,128)S(1)}, u32[]{:S(2)}, u32[]{:S(2)}) collective-permute-start(f32[3,64,128]{2,1,0:T(8,128)S(1)} %get-tuple-element.108.sa_ref), channel_id=1, source_target_pairs={{0,4},{1,5},{2,6},{3,7},{4,0},{5,1},{6,2},{7,3},{8,12},{9,13},{10,... | collective-permute-start | bytes 294920 | tf_op jit(solution)/shard_map/ppermute | solution.py:371
  48.1 9.0 %collective-permute-start.18 = (f32[3,16,128]{2,1,0:T(8,128)S(1)}, f32[3,16,128]{2,1,0:T(8,128)S(1)}, u32[]{:S(2)}, u32[]{:S(2)}) collective-permute-start(f32[3,16,128]{2,1,0:T(8,128)S(1)} %get-tuple-element.110.sc_ref), channel_id=1, source_target_pairs={{0,1},{1,0},{2,3},{3,2},{4,5},{5,4},{6,7},{7,6},{8,9},{9,8},{10,11... | collective-permute-start | bytes 73736 | tf_op jit(solution)/shard_map/ppermute | solution.py:371
  48.4 8.8 %collective-permute-start.19 = (f32[3,16,128]{2,1,0:T(8,128)S(1)}, f32[3,16,128]{2,1,0:T(8,128)S(1)}, u32[]{:S(2)}, u32[]{:S(2)}) collective-permute-start(f32[3,16,128]{2,1,0:T(8,128)S(1)} %get-tuple-element.111.sd_ref), channel_id=1, source_target_pairs={{0,3},{1,2},{2,1},{3,0},{4,7},{5,6},{6,5},{7,4},{8,11},{9,10},{10,... | collective-permute-start | bytes 73736 | tf_op jit(solution)/shard_map/ppermute | solution.py:371

commit v2 on v1

v2 whole, which is shorter than its diff:
```python
import functools
import math

import jax
import jax.numpy as jnp
from jax import lax
from jax.experimental import pallas as pl
from jax.experimental.pallas import tpu as pltpu
from jax.sharding import PartitionSpec as P

STEPS = 4
STEP_TIME = 0.2
YIELD_SPAN = 0.5
PENALTY = 4.0
SOFT_WIDTH = 0.1
KERNEL_WIDTH = 1.5

U_SCALE = 1.0 / YIELD_SPAN
W_SCALE = STEP_TIME / YIELD_SPAN
KICK = STEP_TIME * STEP_TIME / YIELD_SPAN
LOG2E = math.log2(math.e)
GAP_SCALE = YIELD_SPAN / SOFT_WIDTH * LOG2E
SPAN = math.sqrt(LOG2E / (2.0 * KERNEL_WIDTH * KERNEL_WIDTH))
PRESSURE_SCALE = PENALTY * SOFT_WIDTH / LOG2E
STIFF = 0.25 * YIELD_SPAN
TOP = 2.0**126

AXES = ("body", "gx", "yz")
VMEM_LIMIT = 48 * 1024 * 1024


def vmem(shape):
    return pltpu.VMEM(shape, jnp.float32)


def call(kernel, outs, args, spaces=None, aliases=None, scratch=(), flops=0, moved=0, hbm_outs=0):
    spaces = spaces or [None] * len(args)
    specs, placed = [], []
    for arg, space in zip(args, spaces):
        if space is None:
            placed.append(pltpu.with_memory_space_constraint(arg, pltpu.VMEM))
            specs.append(pl.BlockSpec(memory_space=pltpu.VMEM))
        else:
            placed.append(pltpu.with_memory_space_constraint(arg, space) if space == pltpu.HBM else arg)
            specs.append(pl.BlockSpec(memory_space=space))
    return pl.pallas_call(
        kernel,
        out_shape=outs,
        in_specs=specs,
        out_specs=[
            pl.BlockSpec(memory_space=pl.ANY if n < hbm_outs else getattr(out, "memory_space", pltpu.VMEM))
            for n, out in enumerate(outs)
        ],
        input_output_aliases=aliases or {},
        scratch_shapes=list(scratch),
        compiler_params=pltpu.CompilerParams(vmem_limit_bytes=VMEM_LIMIT),
        cost_estimate=pl.CostEstimate(flops=flops, bytes_accessed=moved, transcendentals=0),
    )(*placed)


def pack_kernel(
    d_ref, mat_ref, partner_ref, place_ref, sa_ref, sb_ref, sc_ref, sd_ref, inverse_ref,
    plane_ref, rows_ref, kinds_ref, sems,
):
    planes, rows, cols = mat_ref.shape
    ia, ib, jc, jd = links(place_ref, planes, rows)
    tile = rows_ref.shape[3]
    tile_c, tile_d = jc // tile * tile, jd // tile * tile
    copies = []
    for n, (ref, i) in enumerate(((sa_ref, ia), (sb_ref, ib))):
        copies.append(pltpu.make_async_copy(d_ref.at[:, i], ref.at[0:3], sems.at[n]))
        copies.append(pltpu.make_async_copy(mat_ref.at[i], plane_ref.at[n], sems.at[2 + n]))
    for n, at in enumerate((tile_c, tile_d)):
        some = pl.ds(pl.multiple_of(at, tile), tile)
        copies.append(pltpu.make_async_copy(d_ref.at[:, :, some], rows_ref.at[n], sems.at[4 + n]))
        copies.append(pltpu.make_async_copy(mat_ref.at[:, some], kinds_ref.at[n], sems.at[6 + n]))
    for copy in copies:
        copy.start()

    @pl.loop(0, partner_ref.shape[0], unroll=8)
    def _(b):
        inverse_ref[partner_ref[b]] = b

    for copy in copies:
        copy.wait()
    sa_ref[3] = plane_ref[0].astype(jnp.float32)
    sb_ref[3] = plane_ref[1].astype(jnp.float32)
    for n, (ref, j) in enumerate(((sc_ref, jc - tile_c), (sd_ref, jd - tile_d))):
        for i in range(planes):
            for c in range(3):
                ref[c, i : i + 1] = rows_ref[n, c, i, pl.ds(j, 1)]
            ref[3, i : i + 1] = kinds_ref[n, i, pl.ds(j, 1)].astype(jnp.float32)


def links(place_ref, planes, rows):
    ia = jnp.where(place_ref[0] % 2 == 0, planes - 1, 0)
    jc = jnp.where(place_ref[2] % 2 == 0, rows - 1, 0)
    return ia, planes - 1 - ia, jc, rows - 1 - jc


def prepare_kernel(
    d_ref, v_ref, mat_ref, moduli_ref, density_ref, partner_ref, inverse_ref, active_ref, place_ref,
    u_ref, w_ref, kx_ref, ky_ref, kz_ref, kick_ref, row_kick_ref, high_ky_ref, push_ref, yc_ref, yd_ref,
    pick_ref, half_ref, chosen_ref, kinds_ref, turned_ref, slot_ref, sems,
):
    planes, rows, cols = kinds_ref.shape
    last_x = place_ref[0] == place_ref[1] - 1
    last_y = place_ref[2] == place_ref[3] - 1
    row = lax.broadcasted_iota(jnp.int32, (rows, cols), 0)
    col = lax.broadcasted_iota(jnp.int32, (rows, cols), 1)
    inside = (col < cols - 1) & ((row < rows - 1) | jnp.logical_not(last_y))

    def copies(i):
        return (
            pltpu.make_async_copy(d_ref.at[:, i], u_ref.at[:, i], sems.at[0, i]),
            pltpu.make_async_copy(mat_ref.at[i], kinds_ref.at[i], sems.at[1, i]),
            pltpu.make_async_copy(v_ref.at[:, i], w_ref.at[:, i], sems.at[2, i]),
        )

    for i in range(planes):
        for copy in copies(i):
            copy.start()

    body, blocks = place_ref[4], place_ref[3]
    start = place_ref[2] * rows
    other = jnp.where(body == 0, place_ref[2] + 1, place_ref[2] + blocks - 1) % blocks * rows

    def met(q):
        return jnp.where(body == 0, inverse_ref[q], partner_ref[q])

    def arrive(q, slot):
        r = met(other + q) - start
        here = (r >= 0) & (r < rows)
        slot_ref[jnp.where(here, r, rows)] = rows + slot
        return slot + here.astype(jnp.int32)

    lax.fori_loop(0, rows, arrive, jnp.int32(0), unroll=4)
    lane = lax.broadcasted_iota(jnp.int32, (1, turned_ref.shape[2]), 1)

    def leave(r, count):
        q = jnp.where(body == 0, partner_ref[start + r], inverse_ref[start + r])
        beside = (q >= start) & (q < start + rows)
        whole = jnp.where(beside, q - start, rows + q - other)
        half = jnp.where(beside, q - start, slot_ref[r])
        for n in range(turned_ref.shape[1] // rows):
            turned_ref[0, pl.ds(n * rows + r, 1)] = jnp.where(lane == whole, 1.0, 0.0)
            turned_ref[1, pl.ds(n * rows + r, 1)] = jnp.where(lane == half, 1.0, 0.0)
        live = active_ref[jnp.where(body == 0, start + r, q)]
        push_ref[pl.ds(r, 1)] = jnp.where(lane[:, :cols] >= 0, live.astype(jnp.float32) * (-PRESSURE_SCALE), 0.0)
        chosen_ref[jnp.where(beside, rows, count)] = r
        return count + 1 - beside.astype(jnp.int32)

    lax.fori_loop(0, rows, leave, jnp.int32(0), unroll=4)
    pick_ref[...] = turned_ref[0].T
    half_ref[...] = turned_ref[1].T[: half_ref.shape[0]]

    for copy in copies(0):
        copy.wait()

    def elements(i):
        kinds = kinds_ref[i]
        stiff = jnp.zeros((rows, cols), jnp.float32)
        mass = jnp.ones((rows, cols), jnp.float32)
        for m in range(moduli_ref.shape[0]):
            hit = kinds == m
            stiff = jnp.where(hit, moduli_ref[m] * STIFF, stiff)
            mass = jnp.where(hit, density_ref[m], mass)
        keep = inside & ((i < planes - 1) | jnp.logical_not(last_x))
        kick = KICK / mass
        kick_ref[i] = kick
        row_kick_ref[0, pl.ds(i, 1)] = kick[0:1]
        row_kick_ref[1, pl.ds(i, 1)] = kick[rows - 1 : rows]
        return jnp.where(keep, stiff, 0.0)

    even_y = place_ref[2] % 2 == 0

    def plane(i, earlier, carried, ahead):
        here = elements(i)
        s = here + pltpu.roll(here, 1, 1)
        both = here + earlier
        kx = s + rows_behind(s, row)
        ky = both + pltpu.roll(both, 1, 1)
        kz = both + rows_behind(both, row)
        high_ky_ref[pl.ds(i, 1)] = ky[rows - 1 : rows]
        ky = jnp.where(row < rows - 1, ky, 0.0)
        kx_ref[i], ky_ref[i], kz_ref[i] = kx, ky, kz
        pulls = []
        for c in range(3):
            pulls.append(advance_plane(
                c, i, u_ref[c, i] * U_SCALE, ahead and u_ref[c, i + 1] * U_SCALE, w_ref[c, i] * W_SCALE, carried[c],
                kx, ky, kz, kick_ref[i], u_ref, w_ref, yc_ref, yd_ref, even_y,
            ))
        return here, pulls

    def step(i, state):
        for copy in copies(i + 1):
            copy.wait()
        here, pulls = plane(i, state[0], state[1:], True)
        return (here, *pulls)

    zero = jnp.zeros((rows, cols), jnp.float32)
    state = lax.fori_loop(0, planes - 1, step, (zero,) * 4, unroll=math.gcd(3, planes - 1))
    plane(planes - 1, state[0], state[1:], False)
    push_ref[...] = push_ref[...] * kick_ref[planes - 1]


def rows_behind(value, row, first=0.0):
    return jnp.where(row == 0, first, pltpu.roll(value, 1, 0))


def edge_kernel(
    sa_ref, sb_ref, sc_ref, sd_ref, ra_ref, rb_ref, rc_ref, rd_ref, corner_ref,
    kick_ref, row_kick_ref, high_ky_ref, kx_in, ky_in, kz_in, moduli_ref, place_ref,
    kx_ref, ky_ref, kz_ref, ka_ref, kb_ref, kc_ref, kd_ref, ea_ref, eb_ref, ec_ref, ed_ref,
):
    planes, rows, cols = kick_ref.shape
    even_x, even_y = place_ref[0] % 2 == 0, place_ref[2] % 2 == 0
    inner_x, inner_y = place_ref[0] > 0, place_ref[2] > 0
    last_x = place_ref[0] == place_ref[1] - 1
    last_y = place_ref[2] == place_ref[3] - 1
    row = lax.broadcasted_iota(jnp.int32, (rows, cols), 0)
    plane = lax.broadcasted_iota(jnp.int32, (planes, cols), 0)

    def looked_up(kinds, keep):
        stiff = jnp.zeros(kinds.shape, jnp.float32)
        for m in range(moduli_ref.shape[0]):
            stiff = jnp.where(kinds == m, moduli_ref[m] * STIFF, stiff)
        col = lax.broadcasted_iota(jnp.int32, kinds.shape, 1)
        return jnp.where((col < cols - 1) & keep, stiff, 0.0)

    def with_behind(value):
        return value + pltpu.roll(value, 1, 1)

    below_x = looked_up(
        jnp.where(even_x, rb_ref[3], ra_ref[3]), inner_x & ((row < rows - 1) | jnp.logical_not(last_y))
    )
    below_y = looked_up(
        jnp.where(even_y, rd_ref[3], rc_ref[3]), inner_y & ((plane < planes - 1) | jnp.logical_not(last_x))
    )
    corner = looked_up(corner_ref[...], inner_x & inner_y)
    s_x, s_y, s_corner = with_behind(below_x), with_behind(below_y), with_behind(corner)

    x_low = kick_ref[0] * (s_x + rows_behind(s_x, row, s_corner))
    y_low = row_kick_ref[0] * (s_y + rows_behind(s_y, plane, s_corner))
    plane_ky = jnp.where(row < rows - 1, s_x, 0.0)
    plane_kz = below_x + rows_behind(below_x, row, corner)
    rows_kx = jnp.where(plane < planes - 1, s_y, 0.0)
    rows_kz = below_y + rows_behind(below_y, plane)

    ky_ref[0] += plane_ky
    kz_ref[0] += plane_kz
    for i in range(planes):
        kx_ref[i, 0:1] += s_y[i : i + 1]
        kz_ref[i, 0:1] += rows_kz[i : i + 1]
    x_high = kick_ref[planes - 1] * kx_ref[planes - 1]
    y_high = (high_ky_ref[...] + jnp.where(plane == 0, s_x[rows - 1 : rows], 0.0)) * row_kick_ref[1]
    ka_ref[...] = jnp.where(even_x, x_high, x_low)
    kb_ref[...] = jnp.where(even_x, x_low, x_high)
    kc_ref[...] = jnp.where(even_y, y_high, y_low)
    kd_ref[...] = jnp.where(even_y, y_low, y_high)

    for c in range(3):
        u = jnp.where(even_x, sb_ref[c], sa_ref[c]) * U_SCALE
        pull_y = plane_ky * jnp.tanh(pltpu.roll(u, rows - 1, 0) - u)
        pull_z = plane_kz * jnp.tanh(pltpu.roll(u, cols - 1, 1) - u)
        extra = kick_ref[0] * (pull_y - pltpu.roll(pull_y, 1, 0) + (pull_z - pltpu.roll(pull_z, 1, 1)))
        ea_ref[c] = jnp.where(even_x, 0.0, extra)
        eb_ref[c] = jnp.where(even_x, extra, 0.0)
        u = jnp.where(even_y, sd_ref[c], sc_ref[c]) * U_SCALE
        pull_x = rows_kx * jnp.tanh(pltpu.roll(u, planes - 1, 0) - u)
        pull_z = rows_kz * jnp.tanh(pltpu.roll(u, cols - 1, 1) - u)
        extra = row_kick_ref[0] * (pull_x - pltpu.roll(pull_x, 1, 0) + (pull_z - pltpu.roll(pull_z, 1, 1)))
        ec_ref[c] = jnp.where(even_y, 0.0, extra)
        ed_ref[c] = jnp.where(even_y, extra, 0.0)


def interior_kernel(
    u_in, w_in, kx_ref, ky_ref, kz_ref, kick_ref, da_ref, db_ref, dc_ref, dd_ref, place_ref,
    u_ref, w_ref, yc_ref, yd_ref,
):
    patch(u_ref, w_ref, da_ref, db_ref, dc_ref, dd_ref, place_ref)
    advance(u_ref, w_ref, kx_ref, ky_ref, kz_ref, kick_ref, yc_ref, yd_ref, place_ref)


def advance(u_ref, w_ref, kx_ref, ky_ref, kz_ref, kick_ref, yc_ref, yd_ref, place_ref):
    _, planes, rows, cols = u_ref.shape
    even_y = place_ref[2] % 2 == 0

    def plane(i, carried, ahead):
        return tuple(
            advance_plane(
                c, i, u_ref[c, i], ahead and u_ref[c, i + 1], w_ref[c, i], carried[c],
                kx_ref[i], ky_ref[i], kz_ref[i], kick_ref[i], u_ref, w_ref, yc_ref, yd_ref, even_y,
            )
            for c in range(3)
        )

    zero = jnp.zeros((rows, cols), jnp.float32)
    carried = lax.fori_loop(
        0, planes - 1, lambda i, carried: plane(i, carried, True), (zero,) * 3, unroll=math.gcd(3, planes - 1)
    )
    plane(planes - 1, carried, False)


def advance_plane(c, i, here, ahead, w, carried, kx, ky, kz, kick, u_ref, w_ref, yc_ref, yd_ref, even_y):
    rows, cols = here.shape
    force = -carried
    pull_x = None
    if ahead is not False:
        pull_x = kx * jnp.tanh(ahead - here)
        force = force + pull_x
    pull_y = ky * jnp.tanh(pltpu.roll(here, rows - 1, 0) - here)
    force = force + (pull_y - pltpu.roll(pull_y, 1, 0))
    pull_z = kz * jnp.tanh(pltpu.roll(here, cols - 1, 1) - here)
    force = force + (pull_z - pltpu.roll(pull_z, 1, 1))
    w = w + kick * force
    u = here + w
    w_ref[c, i] = w
    u_ref[c, i] = u
    first, last = u[0:1], u[rows - 1 : rows]
    yc_ref[c, pl.ds(i, 1)] = jnp.where(even_y, last, first)
    yd_ref[c, pl.ds(i, 1)] = jnp.where(even_y, first, last)
    return pull_x


def patch(u_ref, w_ref, da_ref, db_ref, dc_ref, dd_ref, place_ref):
    _, planes, rows, cols = u_ref.shape
    even_x, even_y = place_ref[0] % 2 == 0, place_ref[2] % 2 == 0
    tile = math.gcd(8, rows)
    row = lax.broadcasted_iota(jnp.int32, (tile, cols), 0)
    for c in range(3):
        da, db, dc, dd = da_ref[c], db_ref[c], dc_ref[c], dd_ref[c]
        x_low, x_high = jnp.where(even_x, db, da), jnp.where(even_x, da, db)
        y_low, y_high = jnp.where(even_y, dd, dc), jnp.where(even_y, dc, dd)
        for ref in (u_ref, w_ref):
            ref[c, 0] += x_low
            ref[c, planes - 1] += x_high
            for i in range(planes):
                ref[c, i, 0:tile] += jnp.where(row == 0, y_low[i : i + 1], 0.0)
                ref[c, i, rows - tile : rows] += jnp.where(row == tile - 1, y_high[i : i + 1], 0.0)


def contact_kernel(
    scale, own_ref, near_ref, far_ref, pick_ref, push_ref, face_ref,
    out_ref, fx_ref, fp_ref, fy_ref, fz_ref,
):
    rows, cols = out_ref.shape
    lanes = pick_ref.shape[1]
    parts = lanes // rows
    deep = cols // parts
    is_face = face_ref[0] != 0

    @pl.when(jnp.logical_not(is_face))
    def _():
        out_ref[...] = jnp.zeros_like(out_ref)

    @pl.when(is_face)
    def _():
        pick = pick_ref[...]

        def matched(c):
            pool = jnp.concatenate([near_ref[c], far_ref[c]], axis=0)
            return lax.dot_general(
                pool, pick, (((0,), (0,)), ((), ())),
                precision=lax.Precision.HIGHEST, preferred_element_type=jnp.float32,
            )

        def own(c):
            turned = own_ref[c].T
            return jnp.concatenate([turned[h * deep : (h + 1) * deep] for h in range(parts)], axis=1)

        gap = scale * GAP_SCALE
        along = scale * YIELD_SPAN * SPAN
        fx = matched(0) * gap
        fx_ref[...] = fx
        fp_ref[...] = jnp.exp2(fx)
        fy_ref[...] = matched(1) * along
        spot = lax.broadcasted_iota(jnp.int32, (cols, lanes), 0).astype(jnp.float32)
        fz_ref[...] = matched(2) * along + spot * SPAN
        lane = lax.broadcasted_iota(jnp.int32, (deep, lanes), 1)
        depth = lax.broadcasted_iota(jnp.int32, (deep, lanes), 0)
        mine = (depth + lane // rows * deep).astype(jnp.float32)
        ox = own(0) * gap
        op = jnp.exp2(ox)
        oy = own(1) * along
        oz = own(2) * along + mine * SPAN

        def term(m, total):
            at = pl.ds(m, 1)
            dy = oy - fy_ref[at]
            dz = oz - fz_ref[at]
            weight = jnp.exp2(-(dy * dy + dz * dz))
            soft = jnp.maximum(ox + fx_ref[at], jnp.log2(1.0 + jnp.minimum(op * fp_ref[at], TOP)))
            return total + weight * soft

        total = lax.fori_loop(0, cols, term, jnp.zeros((deep, lanes), jnp.float32), unroll=math.gcd(16, cols))
        turned = jnp.concatenate([total[:, h * rows : (h + 1) * rows] for h in range(parts)], axis=0)
        out_ref[...] = turned.T * push_ref[...]


def link_moves(scale, extra, sent, got, edges, push_ref, c):
    moves = []
    for n in range(4):
        stretch = got[n][c] - sent[n][c]
        if scale != 1.0:
            stretch = stretch * scale
        move = edges[n][...] * jnp.tanh(stretch)
        moves.append(move + extra[n][c] if extra else move)
    if c == 0:
        moves[1] = moves[1] + push_ref[...]
    return moves


def boundary_kernel(scale, n_extra, *refs):
    extra, refs = refs[:n_extra], refs[n_extra:]
    u_ref, yc_ref, yd_ref, *refs = refs
    sent, got, edges, refs = refs[:4], refs[4:8], refs[8:12], refs[12:]
    (push_ref, place_ref, chosen_ref, na_ref, nb_ref, nc_ref, nd_ref, ne_ref,
     da_ref, db_ref, dc_ref, dd_ref) = refs
    _, planes, rows, cols = u_ref.shape
    even_x, even_y = place_ref[0] % 2 == 0, place_ref[2] % 2 == 0
    row = lax.broadcasted_iota(jnp.int32, (rows, cols), 0)
    plane = lax.broadcasted_iota(jnp.int32, (planes, cols), 0)

    def ends(value, index, low, high):
        value = jnp.where(index == 0, value + low, value)
        return jnp.where(index == value.shape[0] - 1, value + high, value)

    for c in range(3):
        da, db, dc, dd = link_moves(scale, extra, sent, got, edges, push_ref, c)
        da_ref[c], db_ref[c], dc_ref[c], dd_ref[c] = da, db, dc, dd
        x_low, x_high = jnp.where(even_x, db, da), jnp.where(even_x, da, db)
        y_low, y_high = jnp.where(even_y, dd, dc), jnp.where(even_y, dc, dd)
        low = u_ref[c, 0] + x_low
        low = ends(low, row, y_low[0:1], y_high[0:1])
        high = u_ref[c, planes - 1] + x_high
        high = ends(high, row, y_low[planes - 1 : planes], y_high[planes - 1 : planes])
        na_ref[c], nb_ref[c] = jnp.where(even_x, high, low), jnp.where(even_x, low, high)
        for new, rows_ref, move, at_even in ((nc_ref, yc_ref, dc, rows - 1), (nd_ref, yd_ref, dd, 0)):
            at_odd = rows - 1 - at_even
            side_low = jnp.where(even_y, x_low[at_even : at_even + 1], x_low[at_odd : at_odd + 1])
            side_high = jnp.where(even_y, x_high[at_even : at_even + 1], x_high[at_odd : at_odd + 1])
            new[c] = ends(rows_ref[c] + move, plane, side_low, side_high)
    for r in range(ne_ref.shape[1]):
        at = chosen_ref[r]
        for c in range(3):
            ne_ref[c, r : r + 1] = nb_ref[c, pl.ds(at, 1)]


def finish_kernel(*refs):
    u_in, w_in, *refs = refs
    sent, got, edges, refs = refs[:4], refs[4:8], refs[8:12], refs[12:]
    push_ref, place_ref, d_ref, v_ref, u_ref, w_ref, da_ref, db_ref, dc_ref, dd_ref, sems = refs
    planes = u_in.shape[1]
    for c in range(3):
        da_ref[c], db_ref[c], dc_ref[c], dd_ref[c] = link_moves(1.0, (), sent, got, edges, push_ref, c)
    patch(u_ref, w_ref, da_ref, db_ref, dc_ref, dd_ref, place_ref)

    def copies(i):
        return (
            pltpu.make_async_copy(u_ref.at[:, i], d_ref.at[:, i], sems.at[0, i]),
            pltpu.make_async_copy(w_ref.at[:, i], v_ref.at[:, i], sems.at[1, i]),
        )

    for i in range(planes):
        for c in range(3):
            u_ref[c, i] = u_ref[c, i] * (1.0 / U_SCALE)
            w_ref[c, i] = w_ref[c, i] * (1.0 / W_SCALE)
        for copy in copies(i):
            copy.start()
    for i in range(planes):
        for copy in copies(i):
            copy.wait()


def routes(count_body, count_x, count_y):
    def number(b, g, y):
        return (b * count_x + g) * count_y + y

    every = [(b, g, y) for b in range(count_body) for g in range(count_x) for y in range(count_y)]

    def pairs(target):
        return [(number(*at), number(*target(*at))) for at in every]

    def outer_x(b, g, y):
        if g in (0, count_x - 1):
            return 1 - b, g, y
        return b, (g + 1 if g % 2 else g - 1), y

    return {
        "a": pairs(lambda b, g, y: (b, g ^ 1, y)),
        "b": pairs(outer_x),
        "c": pairs(lambda b, g, y: (b, g, y ^ 1)),
        "d": pairs(lambda b, g, y: (b, g, (y + 1 if y % 2 else y - 1) % count_y)),
        "e": pairs(lambda b, g, y: (1 - b, g, (y - 1 if b else y + 1) % count_y)),
        "corner": pairs(lambda b, g, y: (b, (g + 1) % count_x, (y + 1) % count_y)),
    }


def local(displacement, velocity, material, moduli, density, partner, active):
    planes, rows, cols = displacement.shape[2:]
    count_x, count_y = lax.axis_size("gx"), lax.axis_size("yz")
    place_x, place_y, place_body = lax.axis_index("gx"), lax.axis_index("yz"), lax.axis_index("body")
    route = routes(lax.axis_size("body"), count_x, count_y)
    lanes = max(cols, 2 * rows)
    tile = math.gcd(8, rows)
    block, face_shape, side = (planes, rows, cols), (rows, cols), (planes, cols)
    state, face3, side3 = (3, *block), (3, *face_shape), (3, *side)
    d, v, kinds = displacement[0], velocity[0], material[0]
    place = jnp.stack([place_x, jnp.int32(count_x), place_y, jnp.int32(count_y), place_body])
    face = jnp.stack([(place_x == count_x - 1).astype(jnp.int32)])
    smem, hbm = pltpu.SMEM, pltpu.HBM

    def exchange(a, b, c, d, e):
        e = lax.ppermute(e, AXES, route["e"])
        b = lax.ppermute(b, AXES, route["b"])
        a = lax.ppermute(a, AXES, route["a"])
        c = lax.ppermute(c, AXES, route["c"])
        d = lax.ppermute(d, AXES, route["d"])
        return [a, b, c, d], e

    corner = lax.ppermute(kinds[planes - 1, rows - 1 :].astype(jnp.float32), AXES, route["corner"])
    *sent, inverse = call(
        pack_kernel,
        [vmem((4, *face_shape))] * 2 + [vmem((4, *side))] * 2 + [pltpu.SMEM(partner.shape, jnp.int32)],
        [d, kinds, partner, place],
        [hbm, hbm, smem, smem],
        scratch=[
            pltpu.VMEM((2, *face_shape), jnp.int32),
            vmem((2, 3, planes, tile, cols)),
            pltpu.VMEM((2, planes, tile, cols), jnp.int32),
            pltpu.SemaphoreType.DMA((8,)),
        ],
    )
    got, got_e = exchange(*sent, sent[1])
    u, w, kx, ky, kz, kick, row_kick, high_ky, push_scale, yc, yd, pick, pick_half, chosen = call(
        prepare_kernel,
        [vmem(state)] * 2 + [vmem(block)] * 4 + [vmem((2, *side)), vmem(side), vmem(face_shape)] + [vmem(side3)] * 2
        + [vmem((lanes, lanes)), vmem((rows + rows // 2, lanes)), pltpu.SMEM((rows + 1,), jnp.int32)],
        [d, v, kinds, moduli, density, partner, inverse, active, place],
        [hbm] * 3 + [smem] * 6,
        scratch=[
            pltpu.VMEM(block, jnp.int32),
            vmem((2, lanes, lanes)),
            pltpu.SMEM((rows + 1,), jnp.int32),
            pltpu.SemaphoreType.DMA((3, planes)),
        ],
        flops=20_000_000,
    )
    for step in range(STEPS):
        first = step == 0
        scale = U_SCALE if first else 1.0
        if not first:
            got, got_e = exchange(*sent, spare)
            u, w, yc, yd = call(
                interior_kernel,
                [vmem(state)] * 2 + [vmem(side3)] * 2,
                [u, w, kx, ky, kz, kick, *moves, place],
                [None] * 10 + [smem],
                aliases={0: 0, 1: 1},
                flops=20_000_000,
            )
        (push,) = call(
            functools.partial(contact_kernel, scale),
            [vmem(face_shape)],
            [sent[1], got[1], got_e, pick if first else pick_half, push_scale, face],
            [None] * 5 + [smem],
            scratch=[vmem((cols, lanes))] * 4,
            flops=20_000_000,
        )
        extra = []
        if first:
            kx, ky, kz, *rest = call(
                edge_kernel,
                [vmem(block)] * 3 + [vmem(face_shape)] * 2 + [vmem(side)] * 2 + [vmem(face3)] * 2 + [vmem(side3)] * 2,
                [*sent, *got, corner, kick, row_kick, high_ky, kx, ky, kz, moduli, place],
                [None] * 15 + [smem] * 2,
                aliases={12: 0, 13: 1, 14: 2},
            )
            edges, extra = rest[:4], rest[4:]
        if step < STEPS - 1:
            *sent, spare, da, db, dc, dd = call(
                functools.partial(boundary_kernel, scale, len(extra)),
                [vmem(face3)] * 2 + [vmem(side3)] * 2 + [vmem((3, rows // 2, cols))]
                + [vmem(face3)] * 2 + [vmem(side3)] * 2,
                [*extra, u, yc, yd, *sent, *got, *edges, push, place, chosen],
                [None] * (16 + len(extra)) + [smem] * 2,
            )
            moves = [da, db, dc, dd]
    d, v, _, _ = call(
        finish_kernel,
        [jax.ShapeDtypeStruct(state, jnp.float32)] * 2 + [vmem(state)] * 2,
        [u, w, *sent, *got, *edges, push, place],
        [None] * 15 + [smem],
        aliases={0: 2, 1: 3},
        scratch=[vmem(face3)] * 2 + [vmem(side3)] * 2 + [pltpu.SemaphoreType.DMA((2, planes))],
        hbm_outs=2,
    )
    return d[None], v[None]


def solution(mesh):
    in_specs = (
        P("body", None, "gx", "yz", None),
        P("body", None, "gx", "yz", None),
        P("body", "gx", "yz", None),
        P(),
        P(),
        P(),
        P(),
    )
    out_specs = (P("body", None, "gx", "yz", None), P("body", None, "gx", "yz", None))
    return jax.shard_map(local, mesh=mesh, in_specs=in_specs, out_specs=out_specs, check_vma=False)
```

time: 60.8 us -> 52 us (0.86)
  the two profiles are of different devices: /device:TPU:27 before, /device:TPU:25 now
where the time goes in v2:
time: 52 us; the launch traced here: 51.8 us
  Pallas kernels  32.1 us (62%)
  starting transfers between devices  16.5 us (32%)
  between operations  0.9 us (2%)
  local copies, waits for them, and re-layouts  0.78 us (2%)
  waiting for transfers between devices  0.78 us (2%)
  other arithmetic  0.69 us (1%)
    pallas_call x14, Pallas kernels, call(): pl.pallas_call(kernel, out_shape=outs, in_specs=specs, out_specs=[pl.Bloc...  32.1 us
    ppermute x4, starting transfers between devices, exchange(): e = lax.ppermute(e, AXES, route['e'])  7.41 us
    ppermute x4, starting transfers between devices, exchange(): d = lax.ppermute(d, AXES, route['d'])  4.1 us
    ppermute x1, starting transfers between devices, local(): lax.ppermute(kinds[planes - 1, rows - 1:].astype(jnp.float32), AXES, rout...  3.37 us
    ppermute x4, starting transfers between devices, exchange(): b = lax.ppermute(b, AXES, route['b'])  1.11 us
  transfers between devices with their start and end apart: 21, of which 1 were waited for; matrix products, arithmetic and copies ran while one was open for 1% of the time, Pallas kernels for 48%

profile of v2, /device:TPU:25, one launch (start us, length us, event | category | flops | bytes accessed | tf_op | source)
XLA Modules:
  0.0 51.8 jit_solution(9489368556516910690)
XLA Ops:
  0.7 0.1 stack.20.place_ref.refs_20_.refs_16_.refs_15_
  0.8 0.7 %copy-done = s32[256]{0:T(256)S(1)} copy-done((s32[256]{0:T(256)S(1)}, s32[256]{0:T(256)}, u32[]{:S(2)}) %copy-start) | copy-done | bytes 1048
  1.4 1.9 %shard_map.86 = (f32[4,64,128]{2,1,0:T(8,128)S(1)}, f32[4,64,128]{2,1,0:T(8,128)S(1)}, f32[4,16,128]{2,1,0:T(8,128)S(1)}, f32[4,16,128]{2,1,0:T(8,128)S(1)}, s32[256]{0:T(256)S(4)}) custom-call(f32[3,16,64,128]{3,2,1,0:T(8,128)} %bitcast.11, s32[16,64,128]{2,1,0:T(8,128)} %bitcast.13, s32[256]{0:T(256)S(1)} %copy-done, ...), custom_call_target="tpu_custom_call" | custom-call | tf_op jit(solution)/shard_map/pallas_call | solution.py:46
  3.3 2.8 %collective-permute-start.5 = (f32[4,64,128]{2,1,0:T(8,128)S(1)}, f32[4,64,128]{2,1,0:T(8,128)S(1)}, u32[]{:S(2)}, u32[]{:S(2)}) collective-permute-start(f32[4,64,128]{2,1,0:T(8,128)S(1)} %get-tuple-element.75.sb_ref.own_ref.refs_8_), channel_id=1, source_target_pairs={{0,17},{1,18},{2,19},{3,16},{4,21},{5,22},{6,23},{7,20},{8,25},{9,... | collective-permute-start | bytes 393224 | tf_op jit(solution)/shard_map/ppermute | solution.py:515
  6.1 0.4 collective-permute-start.2
  6.5 0.6 %collective-permute-start.3 = (f32[4,16,128]{2,1,0:T(8,128)S(1)}, f32[4,16,128]{2,1,0:T(8,128)S(1)}, u32[]{:S(2)}, u32[]{:S(2)}) collective-permute-start(f32[4,16,128]{2,1,0:T(8,128)S(1)} %get-tuple-element.77.sd_ref.refs_10_), channel_id=1, source_target_pairs={{0,3},{1,2},{2,1},{3,0},{4,7},{5,6},{6,5},{7,4},{8,11},{9,10},{10,... | collective-permute-start | bytes 98312 | tf_op jit(solution)/shard_map/ppermute | solution.py:519
  7.1 0.7 %fusion = f32[1,128]{1,0:T(1,128)S(1)} fusion(s32[16,64,128]{2,1,0:T(8,128)} %bitcast.14), kind=kLoop, calls=%fused_computation.1 | loop fusion | flops 128 | bytes 1024 | tf_op jit(solution)/shard_map/convert_element_type | solution.py:522
  7.8 5.2 %shard_map.87 = (f32[3,16,64,128]{3,2,1,0:T(8,128)S(1)}, f32[3,16,64,128]{3,2,1,0:T(8,128)S(1)}, f32[16,64,128]{2,1,0:T(8,128)S(1)}, f32[16,64,128]{2,1,0:T(8,12...) custom-call(f32[3,16,64,128]{3,2,1,0:T(8,128)} %bitcast.12, ...), custom_call_target="tpu_custom_call" | custom-call | flops 20000000 | tf_op jit(solution)/shard_map/pallas_call | solution.py:46
  13.0 3.4 %collective-permute-start.4 = (f32[1,128]{1,0:T(1,128)S(1)}, f32[1,128]{1,0:T(1,128)S(1)}, u32[]{:S(2)}, u32[]{:S(2)}) collective-permute-start(f32[1,128]{1,0:T(1,128)S(1)} %fusion), channel_id=1, source_target_pairs={{0,5},{1,6},{2,7},{3,4},{4,9},{5,10},{6,11},{7,8},{8,13},{9,14},{1... | collective-permute-start | bytes 1544 | tf_op jit(solution)/shard_map/ppermute | solution.py:522
  16.4 2.9 %shard_map.89.refs_19_ = f32[64,128]{1,0:T(8,128)S(1)} custom-call(f32[4,64,128]{2,1,0:T(8,128)S(1)} %get-tuple-element.75.sb_ref.own_ref.refs_8_, f32[4,64,128]{2,1,0:T(8,128)S(1)} %collective-permute-done.1.rb_ref.near_ref.refs_12_, f32[4,64,128]{2,1,0:T(8,128)S(1)} %collective-permute-done.5.far_ref, f32[128,128]{1,0:T(8,128)S(1)} %get-tuple-element.97.pick_ref, ...), custom_call_target="tpu_custom_call" | custom-call | flops 20000000 | tf_op jit(solution)/shard_map/pallas_call | solution.py:46
  19.3 0.8 %shard_map.88 = (f32[16,64,128]{2,1,0:T(8,128)S(1)}, f32[16,64,128]{2,1,0:T(8,128)S(1)}, f32[16,64,128]{2,1,0:T(8,128)S(1)}, f32[64,128]{1,0:T(8,128)S(1)}, f32[...) custom-call(f32[4,64,128]{2,1,0:T(8,128)S(1)} %get-tuple-element.74., ...), custom_call_target="tpu_custom_call", output_to_operand_aliasing={{0}: (12, {}), {1}: (13, {}), {2}: (14, {})} | custom-call | tf_op jit(solution)/shard_map/pallas_call | solution.py:46
  20.0 0.7 %shard_map.90 = (f32[3,64,128]{2,1,0:T(8,128)S(1)}, f32[3,64,128]{2,1,0:T(8,128)S(1)}, f32[3,16,128]{2,1,0:T(8,128)S(1)}, f32[3,16,128]{2,1,0:T(8,128)S(1)}, f32...) custom-call(f32[3,64,128]{2,1,0:T(8,128)S(1)} %get-tuple-element.87., ...), custom_call_target="tpu_custom_call" | custom-call | tf_op jit(solution)/shard_map/pallas_call | solution.py:46
  20.8 0.4 collective-permute-start.7
  21.2 1.5 %collective-permute-start.10 = (f32[3,32,128]{2,1,0:T(8,128)S(1)}, f32[3,32,128]{2,1,0:T(8,128)S(1)}, u32[]{:S(2)}, u32[]{:S(2)}) collective-permute-start(f32[3,32,128]{2,1,0:T(8,128)S(1)} %get-tuple-element.112), channel_id=1, source_target_pairs={{0,17},{1,18},{2,19},{3,16},{4,21},{5,22},{6,23},{7,20},{8,25},{9,... | collective-permute-start | bytes 147464 | tf_op jit(solution)/shard_map/ppermute | solution.py:515
  22.7 0.6 %collective-permute-start.9 = (f32[3,16,128]{2,1,0:T(8,128)S(1)}, f32[3,16,128]{2,1,0:T(8,128)S(1)}, u32[]{:S(2)}, u32[]{:S(2)}) collective-permute-start(f32[3,16,128]{2,1,0:T(8,128)S(1)} %get-tuple-element.111.refs_6_), channel_id=1, source_target_pairs={{0,3},{1,2},{2,1},{3,0},{4,7},{5,6},{6,5},{7,4},{8,11},{9,10},{10,... | collective-permute-start | bytes 73736 | tf_op jit(solution)/shard_map/ppermute | solution.py:519
  23.3 2.5 %shard_map.91 = (f32[3,16,64,128]{3,2,1,0:T(8,128)S(1)}, f32[3,16,64,128]{3,2,1,0:T(8,128)S(1)}, f32[3,16,128]{2,1,0:T(8,128)S(1)}, f32[3,16,128]{2,1,0:T(8,128)S(1)}) custom-call(f32[3,16,64,128]{3,2,1,0:T(8,128)S(1)} %get-tuple-element.72.refs_4_.u_in, ...), custom_call_target="tpu_custom_call", output_to_operand_aliasing={{0}: (0, {}), {1}: (1, {})} | custom-call | flops 20000000 | tf_op jit(solution)/shard_map/pallas_call | solution.py:46
  25.9 0.7 %collective-permute-done.10.far_ref = f32[3,32,128]{2,1,0:T(8,128)S(1)} collective-permute-done((f32[3,32,128]{2,1,0:T(8,128)S(1)}, f32[3,32,128]{2,1,0:T(8,128)S(1)}, u32[]{:S(2)}, u32[]{:S(2)}) %collective-permute-start.10) | collective-permute-done | bytes 49184 | tf_op jit(solution)/shard_map/ppermute | solution.py:515
  26.6 2.9 %shard_map.92.refs_15_ = f32[64,128]{1,0:T(8,128)S(1)} custom-call(f32[3,64,128]{2,1,0:T(8,128)S(1)} %get-tuple-element.109.own_ref.refs_4_, f32[3,64,128]{2,1,0:T(8,128)S(1)} %collective-permute-done.7.near_ref.refs_8_, f32[3,32,128]{2,1,0:T(8,128)S(1)} %collective-permute-done.10.far_ref, f32[96,128]{1,0:T(8,128)S(1)} %get-tuple-element.113.pick_ref, ...), custom_call_target="tpu_custom_call" | custom-call | flops 20000000 | tf_op jit(solution)/shard_map/pallas_call | solution.py:46
  29.5 0.7 %shard_map.93 = (f32[3,64,128]{2,1,0:T(8,128)S(1)}, f32[3,64,128]{2,1,0:T(8,128)S(1)}, f32[3,16,128]{2,1,0:T(8,128)S(1)}, f32[3,16,128]{2,1,0:T(8,128)S(1)}, f32...) custom-call(f32[3,16,64,128]{3,2,1,0:T(8,128)S(1)} %get-tuple-elemen, ...), custom_call_target="tpu_custom_call" | custom-call | tf_op jit(solution)/shard_map/pallas_call | solution.py:46
  30.2 0.2 collective-permute-start.12
  30.4 1.8 %collective-permute-start.15 = (f32[3,32,128]{2,1,0:T(8,128)S(1)}, f32[3,32,128]{2,1,0:T(8,128)S(1)}, u32[]{:S(2)}, u32[]{:S(2)}) collective-permute-start(f32[3,32,128]{2,1,0:T(8,128)S(1)} %get-tuple-element.126), channel_id=1, source_target_pairs={{0,17},{1,18},{2,19},{3,16},{4,21},{5,22},{6,23},{7,20},{8,25},{9,... | collective-permute-start | bytes 147464 | tf_op jit(solution)/shard_map/ppermute | solution.py:515
  32.1 1.6 %collective-permute-start.14 = (f32[3,16,128]{2,1,0:T(8,128)S(1)}, f32[3,16,128]{2,1,0:T(8,128)S(1)}, u32[]{:S(2)}, u32[]{:S(2)}) collective-permute-start(f32[3,16,128]{2,1,0:T(8,128)S(1)} %get-tuple-element.125.refs_6_), channel_id=1, source_target_pairs={{0,3},{1,2},{2,1},{3,0},{4,7},{5,6},{6,5},{7,4},{8,11},{9,10},{10,... | collective-permute-start | bytes 73736 | tf_op jit(solution)/shard_map/ppermute | solution.py:519
  33.7 2.5 %shard_map.94 = (f32[3,16,64,128]{3,2,1,0:T(8,128)S(1)}, f32[3,16,64,128]{3,2,1,0:T(8,128)S(1)}, f32[3,16,128]{2,1,0:T(8,128)S(1)}, f32[3,16,128]{2,1,0:T(8,128)S(1)}) custom-call(f32[3,16,64,128]{3,2,1,0:T(8,128)S(1)} %get-tuple-element.104.refs_0_.u_in, ...), custom_call_target="tpu_custom_call", output_to_operand_aliasing={{0}: (0, {}), {1}: (1, {})} | custom-call | flops 20000000 | tf_op jit(solution)/shard_map/pallas_call | solution.py:46
  36.2 2.9 %shard_map.95.refs_15_ = f32[64,128]{1,0:T(8,128)S(1)} custom-call(f32[3,64,128]{2,1,0:T(8,128)S(1)} %get-tuple-element.123.own_ref.refs_4_, f32[3,64,128]{2,1,0:T(8,128)S(1)} %collective-permute-done.12.near_ref.refs_8_, f32[3,32,128]{2,1,0:T(8,128)S(1)} %collective-permute-done.15.far_ref, f32[96,128]{1,0:T(8,128)S(1)} %get-tuple-element.113.pick_ref, ...), custom_call_target="tpu_custom_call" | custom-call | flops 20000000 | tf_op jit(solution)/shard_map/pallas_call | solution.py:46
  39.1 0.7 %shard_map.96 = (f32[3,64,128]{2,1,0:T(8,128)S(1)}, f32[3,64,128]{2,1,0:T(8,128)S(1)}, f32[3,16,128]{2,1,0:T(8,128)S(1)}, f32[3,16,128]{2,1,0:T(8,128)S(1)}, f32...) custom-call(f32[3,16,64,128]{3,2,1,0:T(8,128)S(1)} %get-tuple-elemen, ...), custom_call_target="tpu_custom_call" | custom-call | tf_op jit(solution)/shard_map/pallas_call | solution.py:46
  39.8 0.5 collective-permute-start.17
  40.3 1.3 %collective-permute-start.20 = (f32[3,32,128]{2,1,0:T(8,128)S(1)}, f32[3,32,128]{2,1,0:T(8,128)S(1)}, u32[]{:S(2)}, u32[]{:S(2)}) collective-permute-start(f32[3,32,128]{2,1,0:T(8,128)S(1)} %get-tuple-element.137), channel_id=1, source_target_pairs={{0,17},{1,18},{2,19},{3,16},{4,21},{5,22},{6,23},{7,20},{8,25},{9,... | collective-permute-start | bytes 147464 | tf_op jit(solution)/shard_map/ppermute | solution.py:515
  41.7 0.1 collective-permute-start.18
  41.8 1.4 %collective-permute-start.19 = (f32[3,16,128]{2,1,0:T(8,128)S(1)}, f32[3,16,128]{2,1,0:T(8,128)S(1)}, u32[]{:S(2)}, u32[]{:S(2)}) collective-permute-start(f32[3,16,128]{2,1,0:T(8,128)S(1)} %get-tuple-element.136.refs_5_), channel_id=1, source_target_pairs={{0,3},{1,2},{2,1},{3,0},{4,7},{5,6},{6,5},{7,4},{8,11},{9,10},{10,... | collective-permute-start | bytes 73736 | tf_op jit(solution)/shard_map/ppermute | solution.py:519
  43.1 3.1 %shard_map.97 = (f32[3,16,64,128]{3,2,1,0:T(8,128)S(1)}, f32[3,16,64,128]{3,2,1,0:T(8,128)S(1)}, f32[3,16,128]{2,1,0:T(8,128)}, f32[3,16,128]{2,1,0:T(8,128)}) custom-call(f32[3,16,64,128]{3,2,1,0:T(8,128)S(1)} %get-tuple-element.118.refs_0_.u_in, f32[3,16,64,128]{3,2,1,0:T(8,128)S(1)} %get-tuple-element.119.w_in, ...), custom_call_target="tpu_custom_call", output_to_operand_aliasing={{0}: (0, {}), {1}: (1, {})} | custom-call | flops 20000000 | tf_op jit(solution)/shard_map/pallas_call | solution.py:46
  46.2 2.9 %shard_map.98.refs_14_ = f32[64,128]{1,0:T(8,128)S(1)} custom-call(f32[3,64,128]{2,1,0:T(8,128)S(1)} %get-tuple-element.134.own_ref.refs_3_, f32[3,64,128]{2,1,0:T(8,128)S(1)} %collective-permute-done.17.near_ref.refs_7_, f32[3,32,128]{2,1,0:T(8,128)S(1)} %collective-permute-done.20.far_ref, f32[96,128]{1,0:T(8,128)S(1)} %get-tuple-element.113.pick_ref, ...), custom_call_target="tpu_custom_call" | custom-call | flops 20000000 | tf_op jit(solution)/shard_map/pallas_call | solution.py:46
  49.1 2.6 %shard_map.99 = (f32[3,16,64,128]{3,2,1,0:T(8,128)}, f32[3,16,64,128]{3,2,1,0:T(8,128)}, f32[3,16,64,128]{3,2,1,0:T(8,128)S(1)}, f32[3,16,64,128]{3,2,1,0:T(8,128)S(1)}) custom-call(f32[3,16,64,128]{3,2,1,0:T(8,128)S(1)} %get-tuple-element.131.refs_0_, ...), custom_call_target="tpu_custom_call", output_to_operand_aliasing={{2}: (0, {}), {3}: (1, {})} | custom-call | tf_op jit(solution)/shard_map/pallas_call | solution.py:46
  (36 shorter events, 0.1 us)
Async XLA Ops:
  0.6 7.2 %copy-start.1 = (s32[256]{0:T(256)S(1)}, s32[256]{0:T(256)}, u32[]{:S(2)}) copy-start(s32[256]{0:T(256)} %partner_ref.3) | copy-start | bytes 3076
  0.6 7.1 %copy-start.2 = (f32[8]{0:T(128)S(1)}, f32[8]{0:T(128)}, u32[]{:S(2)}) copy-start(f32[8]{0:T(128)} %moduli_ref.3) | copy-start | bytes 100
  0.7 7.1 %copy-start.3 = (s32[256]{0:T(256)S(1)}, s32[256]{0:T(256)}, u32[]{:S(2)}) copy-start(s32[256]{0:T(256)} %active_ref.1) | copy-start | bytes 3076
  0.7 7.1 %copy-start.4 = (f32[8]{0:T(128)S(1)}, f32[8]{0:T(128)}, u32[]{:S(2)}) copy-start(f32[8]{0:T(128)} %density_ref.1) | copy-start | bytes 100
  0.8 0.7 %copy-start = (s32[256]{0:T(256)S(1)}, s32[256]{0:T(256)}, u32[]{:S(2)}) copy-start(s32[256]{0:T(256)} %partner_ref.3) | copy-start | bytes 3076
  3.3 9.6 %collective-permute-start.5 = (f32[4,64,128]{2,1,0:T(8,128)S(1)}, f32[4,64,128]{2,1,0:T(8,128)S(1)}, u32[]{:S(2)}, u32[]{:S(2)}) collective-permute-start(f32[4,64,128]{2,1,0:T(8,128)S(1)} %get-tuple-element.75.sb_ref.own_ref.refs_8_), channel_id=1, source_target_pairs={{0,17},{1,18},{2,19},{3,16},{4,21},{5,22},{6,23},{7,20},{8,25},{9,... | collective-permute-start | bytes 393224 | tf_op jit(solution)/shard_map/ppermute | solution.py:515
  6.1 10.2 %collective-permute-start.1 = (f32[4,64,128]{2,1,0:T(8,128)S(1)}, f32[4,64,128]{2,1,0:T(8,128)S(1)}, u32[]{:S(2)}, u32[]{:S(2)}) collective-permute-start(f32[4,64,128]{2,1,0:T(8,128)S(1)} %get-tuple-element.75.sb_ref.own_ref.refs_8_), channel_id=1, source_target_pairs={{0,16},{1,17},{2,18},{3,19},{4,8},{5,9},{6,10},{7,11},{8,4},{9,5},... | collective-permute-start | bytes 393224 | tf_op jit(solution)/shard_map/ppermute | solution.py:516
  6.1 13.1 %collective-permute-start.2 = (f32[4,16,128]{2,1,0:T(8,128)S(1)}, f32[4,16,128]{2,1,0:T(8,128)S(1)}, u32[]{:S(2)}, u32[]{:S(2)}) collective-permute-start(f32[4,16,128]{2,1,0:T(8,128)S(1)} %get-tuple-element.76.sc_ref.refs_9_), channel_id=1, source_target_pairs={{0,1},{1,0},{2,3},{3,2},{4,5},{5,4},{6,7},{7,6},{8,9},{9,8},{10,11... | collective-permute-start | bytes 98312 | tf_op jit(solution)/shard_map/ppermute | solution.py:518
  6.5 12.7 %collective-permute-start.3 = (f32[4,16,128]{2,1,0:T(8,128)S(1)}, f32[4,16,128]{2,1,0:T(8,128)S(1)}, u32[]{:S(2)}, u32[]{:S(2)}) collective-permute-start(f32[4,16,128]{2,1,0:T(8,128)S(1)} %get-tuple-element.77.sd_ref.refs_10_), channel_id=1, source_target_pairs={{0,3},{1,2},{2,1},{3,0},{4,7},{5,6},{6,5},{7,4},{8,11},{9,10},{10,... | collective-permute-start | bytes 98312 | tf_op jit(solution)/shard_map/ppermute | solution.py:519
  7.1 12.2 %collective-permute-start = (f32[4,64,128]{2,1,0:T(8,128)S(1)}, f32[4,64,128]{2,1,0:T(8,128)S(1)}, u32[]{:S(2)}, u32[]{:S(2)}) collective-permute-start(f32[4,64,128]{2,1,0:T(8,128)S(1)} %get-tuple-element.74.sa_ref.refs_7_), channel_id=1, source_target_pairs={{0,4},{1,5},{2,6},{3,7},{4,0},{5,1},{6,2},{7,3},{8,12},{9,13},{10,... | collective-permute-start | bytes 393224 | tf_op jit(solution)/shard_map/ppermute | solution.py:517
  13.0 6.2 %collective-permute-start.4 = (f32[1,128]{1,0:T(1,128)S(1)}, f32[1,128]{1,0:T(1,128)S(1)}, u32[]{:S(2)}, u32[]{:S(2)}) collective-permute-start(f32[1,128]{1,0:T(1,128)S(1)} %fusion), channel_id=1, source_target_pairs={{0,5},{1,6},{2,7},{3,4},{4,9},{5,10},{6,11},{7,8},{8,13},{9,14},{1... | collective-permute-start | bytes 1544 | tf_op jit(solution)/shard_map/ppermute | solution.py:522
  20.8 5.8 %collective-permute-start.7 = (f32[3,64,128]{2,1,0:T(8,128)S(1)}, f32[3,64,128]{2,1,0:T(8,128)S(1)}, u32[]{:S(2)}, u32[]{:S(2)}) collective-permute-start(f32[3,64,128]{2,1,0:T(8,128)S(1)} %get-tuple-element.109.own_ref.refs_4_), channel_id=1, source_target_pairs={{0,16},{1,17},{2,18},{3,19},{4,8},{5,9},{6,10},{7,11},{8,4},{9,5},... | collective-permute-start | bytes 294920 | tf_op jit(solution)/shard_map/ppermute | solution.py:516
  21.2 8.3 %collective-permute-start.6 = (f32[3,64,128]{2,1,0:T(8,128)S(1)}, f32[3,64,128]{2,1,0:T(8,128)S(1)}, u32[]{:S(2)}, u32[]{:S(2)}) collective-permute-start(f32[3,64,128]{2,1,0:T(8,128)S(1)} %get-tuple-element.108.refs_3_), channel_id=1, source_target_pairs={{0,4},{1,5},{2,6},{3,7},{4,0},{5,1},{6,2},{7,3},{8,12},{9,13},{10,... | collective-permute-start | bytes 294920 | tf_op jit(solution)/shard_map/ppermute | solution.py:517
  21.2 5.4 %collective-permute-start.10 = (f32[3,32,128]{2,1,0:T(8,128)S(1)}, f32[3,32,128]{2,1,0:T(8,128)S(1)}, u32[]{:S(2)}, u32[]{:S(2)}) collective-permute-start(f32[3,32,128]{2,1,0:T(8,128)S(1)} %get-tuple-element.112), channel_id=1, source_target_pairs={{0,17},{1,18},{2,19},{3,16},{4,21},{5,22},{6,23},{7,20},{8,25},{9,... | collective-permute-start | bytes 147464 | tf_op jit(solution)/shard_map/ppermute | solution.py:515
  22.7 6.7 %collective-permute-start.8 = (f32[3,16,128]{2,1,0:T(8,128)S(1)}, f32[3,16,128]{2,1,0:T(8,128)S(1)}, u32[]{:S(2)}, u32[]{:S(2)}) collective-permute-start(f32[3,16,128]{2,1,0:T(8,128)S(1)} %get-tuple-element.110.refs_5_), channel_id=1, source_target_pairs={{0,1},{1,0},{2,3},{3,2},{4,5},{5,4},{6,7},{7,6},{8,9},{9,8},{10,11... | collective-permute-start | bytes 73736 | tf_op jit(solution)/shard_map/ppermute | solution.py:518
  22.7 6.7 %collective-permute-start.9 = (f32[3,16,128]{2,1,0:T(8,128)S(1)}, f32[3,16,128]{2,1,0:T(8,128)S(1)}, u32[]{:S(2)}, u32[]{:S(2)}) collective-permute-start(f32[3,16,128]{2,1,0:T(8,128)S(1)} %get-tuple-element.111.refs_6_), channel_id=1, source_target_pairs={{0,3},{1,2},{2,1},{3,0},{4,7},{5,6},{6,5},{7,4},{8,11},{9,10},{10,... | collective-permute-start | bytes 73736 | tf_op jit(solution)/shard_map/ppermute | solution.py:519
  30.2 6.0 %collective-permute-start.12 = (f32[3,64,128]{2,1,0:T(8,128)S(1)}, f32[3,64,128]{2,1,0:T(8,128)S(1)}, u32[]{:S(2)}, u32[]{:S(2)}) collective-permute-start(f32[3,64,128]{2,1,0:T(8,128)S(1)} %get-tuple-element.123.own_ref.refs_4_), channel_id=1, source_target_pairs={{0,16},{1,17},{2,18},{3,19},{4,8},{5,9},{6,10},{7,11},{8,4},{9,5},... | collective-permute-start | bytes 294920 | tf_op jit(solution)/shard_map/ppermute | solution.py:516
  30.4 8.8 %collective-permute-start.11 = (f32[3,64,128]{2,1,0:T(8,128)S(1)}, f32[3,64,128]{2,1,0:T(8,128)S(1)}, u32[]{:S(2)}, u32[]{:S(2)}) collective-permute-start(f32[3,64,128]{2,1,0:T(8,128)S(1)} %get-tuple-element.122.refs_3_), channel_id=1, source_target_pairs={{0,4},{1,5},{2,6},{3,7},{4,0},{5,1},{6,2},{7,3},{8,12},{9,13},{10,... | collective-permute-start | bytes 294920 | tf_op jit(solution)/shard_map/ppermute | solution.py:517
  30.4 5.8 %collective-permute-start.15 = (f32[3,32,128]{2,1,0:T(8,128)S(1)}, f32[3,32,128]{2,1,0:T(8,128)S(1)}, u32[]{:S(2)}, u32[]{:S(2)}) collective-permute-start(f32[3,32,128]{2,1,0:T(8,128)S(1)} %get-tuple-element.126), channel_id=1, source_target_pairs={{0,17},{1,18},{2,19},{3,16},{4,21},{5,22},{6,23},{7,20},{8,25},{9,... | collective-permute-start | bytes 147464 | tf_op jit(solution)/shard_map/ppermute | solution.py:515
  32.1 7.0 %collective-permute-start.13 = (f32[3,16,128]{2,1,0:T(8,128)S(1)}, f32[3,16,128]{2,1,0:T(8,128)S(1)}, u32[]{:S(2)}, u32[]{:S(2)}) collective-permute-start(f32[3,16,128]{2,1,0:T(8,128)S(1)} %get-tuple-element.124.refs_5_), channel_id=1, source_target_pairs={{0,1},{1,0},{2,3},{3,2},{4,5},{5,4},{6,7},{7,6},{8,9},{9,8},{10,11... | collective-permute-start | bytes 73736 | tf_op jit(solution)/shard_map/ppermute | solution.py:518
  32.1 7.0 %collective-permute-start.14 = (f32[3,16,128]{2,1,0:T(8,128)S(1)}, f32[3,16,128]{2,1,0:T(8,128)S(1)}, u32[]{:S(2)}, u32[]{:S(2)}) collective-permute-start(f32[3,16,128]{2,1,0:T(8,128)S(1)} %get-tuple-element.125.refs_6_), channel_id=1, source_target_pairs={{0,3},{1,2},{2,1},{3,0},{4,7},{5,6},{6,5},{7,4},{8,11},{9,10},{10,... | collective-permute-start | bytes 73736 | tf_op jit(solution)/shard_map/ppermute | solution.py:519
  39.8 6.4 %collective-permute-start.17 = (f32[3,64,128]{2,1,0:T(8,128)S(1)}, f32[3,64,128]{2,1,0:T(8,128)S(1)}, u32[]{:S(2)}, u32[]{:S(2)}) collective-permute-start(f32[3,64,128]{2,1,0:T(8,128)S(1)} %get-tuple-element.134.own_ref.refs_3_), channel_id=1, source_target_pairs={{0,16},{1,17},{2,18},{3,19},{4,8},{5,9},{6,10},{7,11},{8,4},{9,5},... | collective-permute-start | bytes 294920 | tf_op jit(solution)/shard_map/ppermute | solution.py:516
  40.3 8.8 %collective-permute-start.16 = (f32[3,64,128]{2,1,0:T(8,128)S(1)}, f32[3,64,128]{2,1,0:T(8,128)S(1)}, u32[]{:S(2)}, u32[]{:S(2)}) collective-permute-start(f32[3,64,128]{2,1,0:T(8,128)S(1)} %get-tuple-element.133.refs_2_), channel_id=1, source_target_pairs={{0,4},{1,5},{2,6},{3,7},{4,0},{5,1},{6,2},{7,3},{8,12},{9,13},{10,... | collective-permute-start | bytes 294920 | tf_op jit(solution)/shard_map/ppermute | solution.py:517
  40.3 5.9 %collective-permute-start.20 = (f32[3,32,128]{2,1,0:T(8,128)S(1)}, f32[3,32,128]{2,1,0:T(8,128)S(1)}, u32[]{:S(2)}, u32[]{:S(2)}) collective-permute-start(f32[3,32,128]{2,1,0:T(8,128)S(1)} %get-tuple-element.137), channel_id=1, source_target_pairs={{0,17},{1,18},{2,19},{3,16},{4,21},{5,22},{6,23},{7,20},{8,25},{9,... | collective-permute-start | bytes 147464 | tf_op jit(solution)/shard_map/ppermute | solution.py:515
  41.7 7.4 %collective-permute-start.18 = (f32[3,16,128]{2,1,0:T(8,128)S(1)}, f32[3,16,128]{2,1,0:T(8,128)S(1)}, u32[]{:S(2)}, u32[]{:S(2)}) collective-permute-start(f32[3,16,128]{2,1,0:T(8,128)S(1)} %get-tuple-element.135.refs_4_), channel_id=1, source_target_pairs={{0,1},{1,0},{2,3},{3,2},{4,5},{5,4},{6,7},{7,6},{8,9},{9,8},{10,11... | collective-permute-start | bytes 73736 | tf_op jit(solution)/shard_map/ppermute | solution.py:518
  41.8 7.3 %collective-permute-start.19 = (f32[3,16,128]{2,1,0:T(8,128)S(1)}, f32[3,16,128]{2,1,0:T(8,128)S(1)}, u32[]{:S(2)}, u32[]{:S(2)}) collective-permute-start(f32[3,16,128]{2,1,0:T(8,128)S(1)} %get-tuple-element.136.refs_5_), channel_id=1, source_target_pairs={{0,3},{1,2},{2,1},{3,0},{4,7},{5,6},{6,5},{7,4},{8,11},{9,10},{10,... | collective-permute-start | bytes 73736 | tf_op jit(solution)/shard_map/ppermute | solution.py:519

commit v3 on v2

v3 whole, which is shorter than its diff:
```python
import functools
import math

import jax
import jax.numpy as jnp
from jax import lax
from jax.experimental import pallas as pl
from jax.experimental.pallas import tpu as pltpu
from jax.sharding import PartitionSpec as P

STEPS = 4
STEP_TIME = 0.2
YIELD_SPAN = 0.5
PENALTY = 4.0
SOFT_WIDTH = 0.1
KERNEL_WIDTH = 1.5

U_SCALE = 1.0 / YIELD_SPAN
W_SCALE = STEP_TIME / YIELD_SPAN
KICK = STEP_TIME * STEP_TIME / YIELD_SPAN
LOG2E = math.log2(math.e)
GAP_SCALE = YIELD_SPAN / SOFT_WIDTH * LOG2E
SPAN = math.sqrt(LOG2E / (2.0 * KERNEL_WIDTH * KERNEL_WIDTH))
PRESSURE_SCALE = PENALTY * SOFT_WIDTH / LOG2E
STIFF = 0.25 * YIELD_SPAN
BIAS = 32.0

AXES = ("body", "gx", "yz")
VMEM_LIMIT = 48 * 1024 * 1024


def vmem(shape):
    return pltpu.VMEM(shape, jnp.float32)


def call(kernel, outs, args, spaces=None, aliases=None, scratch=(), flops=0, moved=0, hbm_outs=0):
    spaces = spaces or [None] * len(args)
    specs, placed = [], []
    for arg, space in zip(args, spaces):
        if space is None:
            placed.append(pltpu.with_memory_space_constraint(arg, pltpu.VMEM))
            specs.append(pl.BlockSpec(memory_space=pltpu.VMEM))
        else:
            placed.append(pltpu.with_memory_space_constraint(arg, space) if space == pltpu.HBM else arg)
            specs.append(pl.BlockSpec(memory_space=space))
    return pl.pallas_call(
        kernel,
        out_shape=outs,
        in_specs=specs,
        out_specs=[
            pl.BlockSpec(memory_space=pl.ANY if n < hbm_outs else getattr(out, "memory_space", pltpu.VMEM))
            for n, out in enumerate(outs)
        ],
        input_output_aliases=aliases or {},
        scratch_shapes=list(scratch),
        compiler_params=pltpu.CompilerParams(vmem_limit_bytes=VMEM_LIMIT),
        cost_estimate=pl.CostEstimate(flops=flops, bytes_accessed=moved, transcendentals=0),
    )(*placed)


def here_in_mesh():
    return (
        lax.axis_index("gx"), lax.axis_size("gx"), lax.axis_index("yz"), lax.axis_size("yz"), lax.axis_index("body")
    )


def pack_kernel(
    d_ref, mat_ref, sa_ref, sb_ref, sc_ref, sd_ref, corner_ref, plane_ref, rows_ref, kinds_ref, sems,
):
    planes, rows, cols = mat_ref.shape
    place = here_in_mesh()
    ia, ib, jc, jd = links(place, planes, rows)
    tile = rows_ref.shape[3]
    tile_c, tile_d = jc // tile * tile, jd // tile * tile
    copies = []
    for n, (ref, i) in enumerate(((sa_ref, ia), (sb_ref, ib))):
        copies.append(pltpu.make_async_copy(d_ref.at[:, i], ref.at[0:3], sems.at[n]))
        copies.append(pltpu.make_async_copy(mat_ref.at[i], plane_ref.at[n], sems.at[2 + n]))
    for n, at in enumerate((tile_c, tile_d)):
        some = pl.ds(pl.multiple_of(at, tile), tile)
        copies.append(pltpu.make_async_copy(d_ref.at[:, :, some], rows_ref.at[n], sems.at[4 + n]))
        copies.append(pltpu.make_async_copy(mat_ref.at[:, some], kinds_ref.at[n], sems.at[6 + n]))
    for copy in copies:
        copy.start()
    for copy in copies:
        copy.wait()
    kinds_a, kinds_b = plane_ref[0].astype(jnp.float32), plane_ref[1].astype(jnp.float32)
    sa_ref[3], sb_ref[3] = kinds_a, kinds_b
    corner_ref[...] = jnp.where(place[0] % 2 == 0, kinds_a[rows - 1 :], kinds_b[rows - 1 :])
    for n, (ref, j) in enumerate(((sc_ref, jc - tile_c), (sd_ref, jd - tile_d))):
        for i in range(planes):
            for c in range(3):
                ref[c, i : i + 1] = rows_ref[n, c, i, pl.ds(j, 1)]
            ref[3, i : i + 1] = kinds_ref[n, i, pl.ds(j, 1)].astype(jnp.float32)


def links(place, planes, rows):
    ia = jnp.where(place[0] % 2 == 0, planes - 1, 0)
    jc = jnp.where(place[2] % 2 == 0, rows - 1, 0)
    return ia, planes - 1 - ia, jc, rows - 1 - jc


def setup_kernel(
    mat_ref, moduli_ref, density_ref, partner_ref, active_ref,
    kx_ref, ky_ref, kz_ref, kick_ref, row_kick_ref, high_ky_ref, push_ref, pick_ref, half_ref, chosen_ref,
    kinds_ref, turned_ref, inverse_ref, slot_ref, sems,
):
    planes, rows, cols = kinds_ref.shape
    place = here_in_mesh()
    last_x = place[0] == place[1] - 1
    last_y = place[2] == place[3] - 1
    row = lax.broadcasted_iota(jnp.int32, (rows, cols), 0)
    col = lax.broadcasted_iota(jnp.int32, (rows, cols), 1)
    inside = (col < cols - 1) & ((row < rows - 1) | jnp.logical_not(last_y))

    def copy(i):
        return pltpu.make_async_copy(mat_ref.at[i], kinds_ref.at[i], sems.at[i])

    for i in range(planes):
        copy(i).start()

    body, blocks = place[4], place[3]
    start = place[2] * rows
    other = jnp.where(body == 0, place[2] + 1, place[2] + blocks - 1) % blocks * rows

    @pl.when(last_x)
    def _():
        def invert(b, _):
            inverse_ref[partner_ref[b]] = b
            return 0

        lax.fori_loop(0, partner_ref.shape[0], invert, 0, unroll=8)

        def arrive(q, slot):
            q = other + q
            r = jnp.where(body == 0, inverse_ref[q], partner_ref[q]) - start
            here = (r >= 0) & (r < rows)
            slot_ref[jnp.where(here, r, rows)] = rows + slot
            return slot + here.astype(jnp.int32)

        lax.fori_loop(0, rows, arrive, jnp.int32(0), unroll=4)
        lane = lax.broadcasted_iota(jnp.int32, (1, turned_ref.shape[2]), 1)

        def leave(r, count):
            q = jnp.where(body == 0, partner_ref[start + r], inverse_ref[start + r])
            beside = (q >= start) & (q < start + rows)
            whole = jnp.where(beside, q - start, rows + q - other)
            half = jnp.where(beside, q - start, slot_ref[r])
            for n in range(turned_ref.shape[1] // rows):
                turned_ref[0, pl.ds(n * rows + r, 1)] = jnp.where(lane == whole, 1.0, 0.0)
                turned_ref[1, pl.ds(n * rows + r, 1)] = jnp.where(lane == half, 1.0, 0.0)
            live = active_ref[jnp.where(body == 0, start + r, q)].astype(jnp.float32)
            push_ref[pl.ds(r, 1)] = jnp.where(lane[:, :cols] >= 0, live * (-PRESSURE_SCALE), 0.0)
            chosen_ref[jnp.where(beside, rows, count)] = r
            return count + 1 - beside.astype(jnp.int32)

        lax.fori_loop(0, rows, leave, jnp.int32(0), unroll=4)
        pick_ref[...] = turned_ref[0].T
        half_ref[...] = turned_ref[1].T[: half_ref.shape[0]]

    @pl.when(jnp.logical_not(last_x))
    def _():
        push_ref[...] = jnp.zeros_like(push_ref)
        pick_ref[...] = jnp.zeros_like(pick_ref)
        half_ref[...] = jnp.zeros_like(half_ref)

        def any_row(r, _):
            chosen_ref[r] = 0
            return 0

        lax.fori_loop(0, rows + 1, any_row, 0, unroll=8)

    def plane(i, earlier):
        copy(i).wait()
        kinds = kinds_ref[i]
        stiff = jnp.zeros((rows, cols), jnp.float32)
        mass = jnp.ones((rows, cols), jnp.float32)
        for m in range(moduli_ref.shape[0]):
            hit = kinds == m
            stiff = jnp.where(hit, moduli_ref[m] * STIFF, stiff)
            mass = jnp.where(hit, density_ref[m], mass)
        keep = inside & ((i < planes - 1) | jnp.logical_not(last_x))
        here = jnp.where(keep, stiff, 0.0)
        kick = KICK / mass
        kick_ref[i] = kick
        row_kick_ref[0, pl.ds(i, 1)] = kick[0:1]
        row_kick_ref[1, pl.ds(i, 1)] = kick[rows - 1 : rows]
        s = here + pltpu.roll(here, 1, 1)
        both = here + earlier
        ky = both + pltpu.roll(both, 1, 1)
        high_ky_ref[pl.ds(i, 1)] = ky[rows - 1 : rows]
        kx_ref[i] = s + rows_behind(s, row)
        ky_ref[i] = jnp.where(row < rows - 1, ky, 0.0)
        kz_ref[i] = both + rows_behind(both, row)
        return here

    lax.fori_loop(0, planes, plane, jnp.zeros((rows, cols), jnp.float32), unroll=math.gcd(4, planes))
    push_ref[...] = push_ref[...] * kick_ref[planes - 1]


def rows_behind(value, row, first=0.0):
    return jnp.where(row == 0, first, pltpu.roll(value, 1, 0))


def first_kernel(
    d_ref, v_ref, kx_ref, ky_ref, kz_ref, kick_ref, u_ref, w_ref, yc_ref, yd_ref, sems,
):
    _, planes, rows, cols = u_ref.shape
    even_y = lax.axis_index("yz") % 2 == 0

    def copies(i):
        return (
            pltpu.make_async_copy(d_ref.at[:, i], u_ref.at[:, i], sems.at[0, i]),
            pltpu.make_async_copy(v_ref.at[:, i], w_ref.at[:, i], sems.at[1, i]),
        )

    for i in range(planes):
        for copy in copies(i):
            copy.start()
    for copy in copies(0):
        copy.wait()

    def plane(i, carried, ahead):
        if ahead:
            for copy in copies(i + 1):
                copy.wait()
        return tuple(
            advance_plane(
                c, i, u_ref[c, i] * U_SCALE, ahead and u_ref[c, i + 1] * U_SCALE, w_ref[c, i] * W_SCALE, carried[c],
                kx_ref[i], ky_ref[i], kz_ref[i], kick_ref[i], u_ref, w_ref, yc_ref, yd_ref, even_y,
            )
            for c in range(3)
        )

    zero = jnp.zeros((rows, cols), jnp.float32)
    carried = lax.fori_loop(
        0, planes - 1, lambda i, carried: plane(i, carried, True), (zero,) * 3, unroll=math.gcd(3, planes - 1)
    )
    plane(planes - 1, carried, False)


def edge_kernel(
    sa_ref, sb_ref, sc_ref, sd_ref, ra_ref, rb_ref, rc_ref, rd_ref, corner_ref,
    kick_ref, row_kick_ref, high_ky_ref, kx_in, ky_in, kz_in, moduli_ref,
    kx_ref, ky_ref, kz_ref, ka_ref, kb_ref, kc_ref, kd_ref, ex_ref, ey_ref,
):
    planes, rows, cols = kick_ref.shape
    place = here_in_mesh()
    even_x, even_y = place[0] % 2 == 0, place[2] % 2 == 0
    inner_x, inner_y = place[0] > 0, place[2] > 0
    last_x = place[0] == place[1] - 1
    last_y = place[2] == place[3] - 1
    row = lax.broadcasted_iota(jnp.int32, (rows, cols), 0)
    plane = lax.broadcasted_iota(jnp.int32, (planes, cols), 0)

    def looked_up(kinds, keep):
        stiff = jnp.zeros(kinds.shape, jnp.float32)
        for m in range(moduli_ref.shape[0]):
            stiff = jnp.where(kinds == m, moduli_ref[m] * STIFF, stiff)
        col = lax.broadcasted_iota(jnp.int32, kinds.shape, 1)
        return jnp.where((col < cols - 1) & keep, stiff, 0.0)

    def with_behind(value):
        return value + pltpu.roll(value, 1, 1)

    below_x = looked_up(
        jnp.where(even_x, rb_ref[3], ra_ref[3]), inner_x & ((row < rows - 1) | jnp.logical_not(last_y))
    )
    below_y = looked_up(
        jnp.where(even_y, rd_ref[3], rc_ref[3]), inner_y & ((plane < planes - 1) | jnp.logical_not(last_x))
    )
    corner = looked_up(corner_ref[...], inner_x & inner_y)
    s_x, s_y, s_corner = with_behind(below_x), with_behind(below_y), with_behind(corner)

    x_low = kick_ref[0] * (s_x + rows_behind(s_x, row, s_corner))
    y_low = row_kick_ref[0] * (s_y + rows_behind(s_y, plane, s_corner))
    plane_ky = jnp.where(row < rows - 1, s_x, 0.0)
    plane_kz = below_x + rows_behind(below_x, row, corner)
    rows_kx = jnp.where(plane < planes - 1, s_y, 0.0)
    rows_kz = below_y + rows_behind(below_y, plane)

    ky_ref[0] += plane_ky
    kz_ref[0] += plane_kz
    for i in range(planes):
        kx_ref[i, 0:1] += s_y[i : i + 1]
        kz_ref[i, 0:1] += rows_kz[i : i + 1]
    x_high = kick_ref[planes - 1] * kx_ref[planes - 1]
    y_high = (high_ky_ref[...] + jnp.where(plane == 0, s_x[rows - 1 : rows], 0.0)) * row_kick_ref[1]
    ka_ref[...] = jnp.where(even_x, x_high, x_low)
    kb_ref[...] = jnp.where(even_x, x_low, x_high)
    kc_ref[...] = jnp.where(even_y, y_high, y_low)
    kd_ref[...] = jnp.where(even_y, y_low, y_high)

    for c in range(3):
        u = jnp.where(even_x, sb_ref[c], sa_ref[c]) * U_SCALE
        pull_y = plane_ky * jnp.tanh(pltpu.roll(u, rows - 1, 0) - u)
        pull_z = plane_kz * jnp.tanh(pltpu.roll(u, cols - 1, 1) - u)
        ex_ref[c] = kick_ref[0] * (pull_y - pltpu.roll(pull_y, 1, 0) + (pull_z - pltpu.roll(pull_z, 1, 1)))
        u = jnp.where(even_y, sd_ref[c], sc_ref[c]) * U_SCALE
        pull_x = rows_kx * jnp.tanh(pltpu.roll(u, planes - 1, 0) - u)
        pull_z = rows_kz * jnp.tanh(pltpu.roll(u, cols - 1, 1) - u)
        ey_ref[c] = row_kick_ref[0] * (pull_x - pltpu.roll(pull_x, 1, 0) + (pull_z - pltpu.roll(pull_z, 1, 1)))


def interior_kernel(
    u_scale, w_scale, u_in, w_in, kx_ref, ky_ref, kz_ref, kick_ref, xl_ref, xh_ref, yl_ref, yh_ref,
    u_ref, w_ref, yc_ref, yd_ref,
):
    _, planes, rows, cols = u_ref.shape
    even_y = lax.axis_index("yz") % 2 == 0
    for ref in (u_ref, w_ref):
        for c in range(3):
            ref[c, 0] += xl_ref[c]
            ref[c, planes - 1] += xh_ref[c]

    def fixed(ref, c, i):
        return with_sides(ref[c, i], yl_ref[c, pl.ds(i, 1)], yh_ref[c, pl.ds(i, 1)])

    def plane(i, carried, ahead):
        return tuple(
            advance_plane(
                c, i, fixed(u_ref, c, i), ahead and fixed(u_ref, c, i + 1), fixed(w_ref, c, i), carried[c],
                kx_ref[i], ky_ref[i], kz_ref[i], kick_ref[i], u_ref, w_ref, yc_ref, yd_ref, even_y, u_scale, w_scale,
            )
            for c in range(3)
        )

    zero = jnp.zeros((rows, cols), jnp.float32)
    carried = lax.fori_loop(
        0, planes - 1, lambda i, carried: plane(i, carried, True), (zero,) * 3, unroll=math.gcd(3, planes - 1)
    )
    plane(planes - 1, carried, False)


def with_sides(value, low, high):
    rows, cols = value.shape
    tile = math.gcd(8, rows)
    row = lax.broadcasted_iota(jnp.int32, (tile, cols), 0)
    low, high = jnp.where(row == 0, low, 0.0), jnp.where(row == tile - 1, high, 0.0)
    if rows == tile:
        return value + (low + high)
    middle = [value[tile : rows - tile]] if rows > 2 * tile else []
    return jnp.concatenate([value[0:tile] + low, *middle, value[rows - tile :] + high], axis=0)


def advance_plane(
    c, i, here, ahead, w, carried, kx, ky, kz, kick, u_ref, w_ref, yc_ref, yd_ref, even_y, u_scale=1.0, w_scale=1.0
):
    rows, cols = here.shape
    force = -carried
    pull_x = None
    if ahead is not False:
        pull_x = kx * jnp.tanh(ahead - here)
        force = force + pull_x
    pull_y = ky * jnp.tanh(pltpu.roll(here, rows - 1, 0) - here)
    force = force + (pull_y - pltpu.roll(pull_y, 1, 0))
    pull_z = kz * jnp.tanh(pltpu.roll(here, cols - 1, 1) - here)
    force = force + (pull_z - pltpu.roll(pull_z, 1, 1))
    w = w + kick * force
    u = here + w
    if u_scale != 1.0:
        u, w = u * u_scale, w * w_scale
    w_ref[c, i] = w
    u_ref[c, i] = u
    first, last = u[0:1], u[rows - 1 : rows]
    yc_ref[c, pl.ds(i, 1)] = jnp.where(even_y, last, first)
    yd_ref[c, pl.ds(i, 1)] = jnp.where(even_y, first, last)
    return pull_x


def contact_kernel(
    scale, own_ref, near_ref, far_ref, pick_ref, push_ref, out_ref, fp_ref, fy_ref, fz_ref,
):
    rows, cols = out_ref.shape
    lanes = pick_ref.shape[1]
    parts = lanes // rows
    deep = cols // parts
    is_face = lax.axis_index("gx") == lax.axis_size("gx") - 1

    @pl.when(jnp.logical_not(is_face))
    def _():
        out_ref[...] = jnp.zeros_like(out_ref)

    @pl.when(is_face)
    def _():
        pick = pick_ref[...]

        def matched(c):
            pool = jnp.concatenate([near_ref[c], far_ref[c]], axis=0)
            return lax.dot_general(
                pool, pick, (((0,), (0,)), ((), ())),
                precision=lax.Precision.HIGHEST, preferred_element_type=jnp.float32,
            )

        def own(c):
            turned = own_ref[c].T
            return jnp.concatenate([turned[h * deep : (h + 1) * deep] for h in range(parts)], axis=1)

        gap = scale * GAP_SCALE
        along = scale * YIELD_SPAN * SPAN
        fp_ref[...] = jnp.exp2(matched(0) * gap - BIAS / 2.0)
        fy_ref[...] = matched(1) * along
        spot = lax.broadcasted_iota(jnp.int32, (cols, lanes), 0).astype(jnp.float32)
        fz_ref[...] = matched(2) * along + spot * SPAN
        lane = lax.broadcasted_iota(jnp.int32, (deep, lanes), 1)
        depth = lax.broadcasted_iota(jnp.int32, (deep, lanes), 0)
        mine = (depth + lane // rows * deep).astype(jnp.float32)
        op = jnp.exp2(own(0) * gap - BIAS / 2.0)
        oy = own(1) * along
        oz = own(2) * along + mine * SPAN

        def term(m, total):
            at = pl.ds(m, 1)
            dy = oy - fy_ref[at]
            dz = oz - fz_ref[at]
            weight = jnp.exp2(-(dy * dy + dz * dz))
            soft = jnp.log2(op * fp_ref[at] + 2.0**-BIAS) + BIAS
            return total + weight * soft

        total = lax.fori_loop(0, cols, term, jnp.zeros((deep, lanes), jnp.float32), unroll=math.gcd(16, cols))
        turned = jnp.concatenate([total[:, h * rows : (h + 1) * rows] for h in range(parts)], axis=0)
        out_ref[...] = turned.T * push_ref[...]


def last_contact_kernel(
    own_ref, near_ref, far_ref, pick_ref, push_ref, u_ref, w_ref, d_ref, v_ref, out_ref, fp_ref, fy_ref, fz_ref, sems,
):
    copies = [
        pltpu.make_async_copy(u_ref, d_ref, sems.at[0]),
        pltpu.make_async_copy(w_ref, v_ref, sems.at[1]),
    ]
    for copy in copies:
        copy.start()
    contact_kernel(1.0, own_ref, near_ref, far_ref, pick_ref, push_ref, out_ref, fp_ref, fy_ref, fz_ref)
    for copy in copies:
        copy.wait()


def link_moves(scale, extra, sent, got, edges, push_ref, c):
    moves = []
    for n in range(4):
        stretch = got[n][c] - sent[n][c]
        if scale != 1.0:
            stretch = stretch * scale
        moves.append(edges[n][...] * jnp.tanh(stretch))
    if c == 0:
        moves[1] = moves[1] + push_ref[...]
    a, b, c_, d = moves
    even_x, even_y = lax.axis_index("gx") % 2 == 0, lax.axis_index("yz") % 2 == 0
    moves = [jnp.where(even_x, b, a), jnp.where(even_x, a, b), jnp.where(even_y, d, c_), jnp.where(even_y, c_, d)]
    if extra:
        moves[0] = moves[0] + extra[0][c]
        moves[2] = moves[2] + extra[1][c]
    return moves


def boundary_kernel(scale, n_extra, *refs):
    extra, refs = refs[:n_extra], refs[n_extra:]
    u_ref, yc_ref, yd_ref, *refs = refs
    sent, got, edges, refs = refs[:4], refs[4:8], refs[8:12], refs[12:]
    push_ref, chosen_ref, na_ref, nb_ref, nc_ref, nd_ref, ne_ref, xl_ref, xh_ref, yl_ref, yh_ref = refs
    _, planes, rows, cols = u_ref.shape
    even_x, even_y = lax.axis_index("gx") % 2 == 0, lax.axis_index("yz") % 2 == 0
    for c in range(3):
        xl, xh, yl, yh = link_moves(scale, extra, sent, got, edges, push_ref, c)
        xl_ref[c], xh_ref[c], yl_ref[c], yh_ref[c] = xl, xh, yl, yh
        low = with_sides(u_ref[c, 0] + xl, yl[0:1], yh[0:1])
        high = with_sides(u_ref[c, planes - 1] + xh, yl[planes - 1 :], yh[planes - 1 :])
        na_ref[c], nb_ref[c] = jnp.where(even_x, high, low), jnp.where(even_x, low, high)
        first = xl[0:1], xh[0:1]
        last = xl[rows - 1 :], xh[rows - 1 :]
        c_low, c_high = (jnp.where(even_y, y, x) for x, y in zip(first, last))
        d_low, d_high = (jnp.where(even_y, x, y) for x, y in zip(first, last))
        nc_ref[c] = with_sides(yc_ref[c] + jnp.where(even_y, yh, yl), c_low, c_high)
        nd_ref[c] = with_sides(yd_ref[c] + jnp.where(even_y, yl, yh), d_low, d_high)
    for r in range(ne_ref.shape[1]):
        at = chosen_ref[r]
        for c in range(3):
            ne_ref[c, r : r + 1] = nb_ref[c, pl.ds(at, 1)]


def finish_kernel(*refs):
    u_ref, w_ref, _, _, *refs = refs
    sent, got, edges, refs = refs[:4], refs[4:8], refs[8:12], refs[12:]
    push_ref, d_ref, v_ref, planes_ref, rows_ref, sems = refs
    _, planes, rows, cols = u_ref.shape
    tile = rows_ref.shape[4]
    inner = slice(1, planes - 1)
    copies = []
    moves = [link_moves(1.0, (), sent, got, edges, push_ref, c) for c in range(3)]
    results = ((u_ref, d_ref, 1.0 / U_SCALE), (w_ref, v_ref, 1.0 / W_SCALE))
    for n, (ref, out, scale) in enumerate(results):
        for side, at in ((0, 0), (1, rows - tile)):
            for c in range(3):
                fix = moves[c][2 + side] * scale
                for i in range(1, planes - 1):
                    value = ref[c, i, at : at + tile]
                    line = fix[i : i + 1]
                    row = lax.broadcasted_iota(jnp.int32, (tile, cols), 0)
                    rows_ref[n, side, c, i - 1] = value + jnp.where(row == (tile - 1 if side else 0), line, 0.0)
            copies.append(
                pltpu.make_async_copy(
                    rows_ref.at[n, side], out.at[:, inner, at : at + tile], sems.at[len(copies)]
                )
            )
            copies[-1].start()
    for n, (ref, out, scale) in enumerate(results):
        for side, i in ((0, 0), (1, planes - 1)):
            for c in range(3):
                xl, xh, yl, yh = moves[c]
                value = ref[c, i] + (xh if side else xl) * scale
                planes_ref[n, side, c] = with_sides(value, yl[i : i + 1] * scale, yh[i : i + 1] * scale)
            copies.append(pltpu.make_async_copy(planes_ref.at[n, side], out.at[:, i], sems.at[len(copies)]))
            copies[-1].start()
    for copy in copies:
        copy.wait()


def routes(count_body, count_x, count_y):
    def number(b, g, y):
        return (b * count_x + g) * count_y + y

    every = [(b, g, y) for b in range(count_body) for g in range(count_x) for y in range(count_y)]

    def pairs(target):
        return [(number(*at), number(*target(*at))) for at in every]

    def outer_x(b, g, y):
        if g in (0, count_x - 1):
            return 1 - b, g, y
        return b, (g + 1 if g % 2 else g - 1), y

    return {
        "a": pairs(lambda b, g, y: (b, g ^ 1, y)),
        "b": pairs(outer_x),
        "c": pairs(lambda b, g, y: (b, g, y ^ 1)),
        "d": pairs(lambda b, g, y: (b, g, (y + 1 if y % 2 else y - 1) % count_y)),
        "e": pairs(lambda b, g, y: (1 - b, g, (y - 1 if b else y + 1) % count_y)),
        "corner": pairs(lambda b, g, y: (b, (g + 1) % count_x, (y + 1) % count_y)),
    }


def local(displacement, velocity, material, moduli, density, partner, active):
    planes, rows, cols = displacement.shape[2:]
    route = routes(lax.axis_size("body"), lax.axis_size("gx"), lax.axis_size("yz"))
    lanes = max(cols, 2 * rows)
    tile = math.gcd(8, rows)
    block, face, side = (planes, rows, cols), (rows, cols), (planes, cols)
    state, face3, side3 = (3, *block), (3, *face), (3, *side)
    d, v, kinds = displacement[0], velocity[0], material[0]
    smem, hbm = pltpu.SMEM, pltpu.HBM

    def exchange(a, b, c, d, e):
        e = lax.ppermute(e, AXES, route["e"])
        b = lax.ppermute(b, AXES, route["b"])
        a = lax.ppermute(a, AXES, route["a"])
        c = lax.ppermute(c, AXES, route["c"])
        d = lax.ppermute(d, AXES, route["d"])
        return [a, b, c, d], e

    *sent, corner = call(
        pack_kernel,
        [vmem((4, *face))] * 2 + [vmem((4, *side))] * 2 + [vmem((1, cols))],
        [d, kinds],
        [hbm, hbm],
        scratch=[
            pltpu.VMEM((2, *face), jnp.int32),
            vmem((2, 3, planes, tile, cols)),
            pltpu.VMEM((2, planes, tile, cols), jnp.int32),
            pltpu.SemaphoreType.DMA((8,)),
        ],
    )
    got, got_e = exchange(*sent, sent[1])
    kx, ky, kz, kick, row_kick, high_ky, push_scale, pick, pick_half, chosen = call(
        setup_kernel,
        [vmem(block)] * 4 + [vmem((2, *side)), vmem(side), vmem(face)]
        + [vmem((lanes, lanes)), vmem((rows + rows // 2, lanes)), pltpu.SMEM((rows + 1,), jnp.int32)],
        [kinds, moduli, density, partner, active],
        [hbm] + [smem] * 4,
        scratch=[
            pltpu.VMEM(block, jnp.int32),
            vmem((2, lanes, lanes)),
            pltpu.SMEM(partner.shape, jnp.int32),
            pltpu.SMEM((rows + 1,), jnp.int32),
            pltpu.SemaphoreType.DMA((planes,)),
        ],
        flops=8_000_000,
    )
    pair_scratch = [vmem((cols, lanes))] * 3
    for step in range(STEPS):
        first, last = step == 0, step == STEPS - 1
        scale = U_SCALE if first else 1.0
        if not first:
            got, got_e = exchange(*sent, spare)
            u, w, yc, yd = call(
                functools.partial(interior_kernel, *((1.0 / U_SCALE, 1.0 / W_SCALE) if last else (1.0, 1.0))),
                [vmem(state)] * 2 + [vmem(side3)] * 2,
                [u, w, kx, ky, kz, kick, *moves],
                aliases={0: 0, 1: 1},
                flops=20_000_000,
            )
        meet = [sent[1], got[1], got_e, pick if first else pick_half, push_scale]
        if last:
            d, v, push = call(
                last_contact_kernel,
                [jax.ShapeDtypeStruct(state, jnp.float32)] * 2 + [vmem(face)],
                [*meet, u, w],
                scratch=pair_scratch + [pltpu.SemaphoreType.DMA((2,))],
                hbm_outs=2,
                flops=20_000_000,
            )
            break
        (push,) = call(
            functools.partial(contact_kernel, scale), [vmem(face)], meet, scratch=pair_scratch, flops=20_000_000
        )
        extra = []
        if first:
            corner, push = lax.optimization_barrier((corner, push))
            corner = lax.ppermute(corner, AXES, route["corner"])
            u, w, yc, yd = call(
                first_kernel,
                [vmem(state)] * 2 + [vmem(side3)] * 2,
                [d, v, kx, ky, kz, kick],
                [hbm] * 2 + [None] * 4,
                scratch=[pltpu.SemaphoreType.DMA((2, planes))],
                flops=20_000_000,
            )
            kx, ky, kz, *rest = call(
                edge_kernel,
                [vmem(block)] * 3 + [vmem(face)] * 2 + [vmem(side)] * 2 + [vmem(face3), vmem(side3)],
                [*sent, *got, corner, kick, row_kick, high_ky, kx, ky, kz, moduli],
                [None] * 15 + [smem],
                aliases={12: 0, 13: 1, 14: 2},
            )
            edges, extra = rest[:4], rest[4:]
        *sent, spare, xl, xh, yl, yh = call(
            functools.partial(boundary_kernel, scale, len(extra)),
            [vmem(face3)] * 2 + [vmem(side3)] * 2 + [vmem((3, rows // 2, cols))]
            + [vmem(face3)] * 2 + [vmem(side3)] * 2,
            [*extra, u, yc, yd, *sent, *got, *edges, push, chosen],
            [None] * (16 + len(extra)) + [smem],
        )
        moves = [xl, xh, yl, yh]
    d, v = call(
        finish_kernel,
        [jax.ShapeDtypeStruct(state, jnp.float32)] * 2,
        [u, w, d, v, *sent, *got, *edges, push],
        [None, None, hbm, hbm] + [None] * 13,
        aliases={2: 0, 3: 1},
        scratch=[vmem((2, 2, *face3)), vmem((2, 2, 3, planes - 2, tile, cols)), pltpu.SemaphoreType.DMA((8,))],
        hbm_outs=2,
    )
    return d[None], v[None]


def solution(mesh):
    in_specs = (
        P("body", None, "gx", "yz", None),
        P("body", None, "gx", "yz", None),
        P("body", "gx", "yz", None),
        P(),
        P(),
        P(),
        P(),
    )
    out_specs = (P("body", None, "gx", "yz", None), P("body", None, "gx", "yz", None))
    return jax.shard_map(local, mesh=mesh, in_specs=in_specs, out_specs=out_specs, check_vma=False)
```

time: 52 us -> 47.9 us (0.921)
  the two profiles are of different devices: /device:TPU:25 before, /device:TPU:1 now
where the time goes in v3:
time: 47.9 us; the launch traced here: 47.7 us
  starting transfers between devices  23.9 us (50%)
  Pallas kernels  19.2 us (40%)
  waiting for transfers between devices  3.73 us (8%)
  between operations  0.83 us (2%)
    pallas_call x15, Pallas kernels, call(): pl.pallas_call(kernel, out_shape=outs, in_specs=specs, out_specs=[pl.Bloc...  19.2 us
    ppermute x4, starting transfers between devices, exchange(): a = lax.ppermute(a, AXES, route['a'])  10.1 us
    ppermute x4, starting transfers between devices, exchange(): e = lax.ppermute(e, AXES, route['e'])  9.33 us
    ppermute x4, starting transfers between devices, exchange(): d = lax.ppermute(d, AXES, route['d'])  2.81 us
    ppermute x1, waiting for transfers between devices, local(): corner = lax.ppermute(corner, AXES, route['corner'])  1.61 us
    ppermute x4, waiting for transfers between devices, exchange(): d = lax.ppermute(d, AXES, route['d'])  1.43 us
  transfers between devices with their start and end apart: 21, of which 5 were waited for; matrix products, arithmetic and copies ran while one was open for 0% of the time, Pallas kernels for 33%

profile of v3, /device:TPU:1, one launch (start us, length us, event | category | flops | bytes accessed | tf_op | source)
XLA Modules:
  0.0 47.7 jit_solution(5850580044940218719)
XLA Ops:
  0.7 1.3 %shard_map.88 = (f32[4,64,128]{2,1,0:T(8,128)S(1)}, f32[4,64,128]{2,1,0:T(8,128)S(1)}, f32[4,16,128]{2,1,0:T(8,128)S(1)}, f32[4,16,128]{2,1,0:T(8,128)S(1)}, f32[1,128]{1,0:T(1,128)S(1)}) custom-call(f32[3,16,64,128]{3,2,1,0:T(8,128)} %bitcast.5, s32[16,64,128]{2,1,0:T(8,128)} %bitcast.7), custom_call_target="tpu_custom_call" | custom-call | tf_op jit(solution)/shard_map/pallas_call | solution.py:46
  2.0 3.6 %collective-permute-start.4 = (f32[4,64,128]{2,1,0:T(8,128)S(1)}, f32[4,64,128]{2,1,0:T(8,128)S(1)}, u32[]{:S(2)}, u32[]{:S(2)}) collective-permute-start(f32[4,64,128]{2,1,0:T(8,128)S(1)} %get-tuple-element.81.own_ref.sb_ref.refs_6_), channel_id=1, source_target_pairs={{0,17},{1,18},{2,19},{3,16},{4,21},{5,22},{6,23},{7,20},{8,25},{9,... | collective-permute-start | bytes 393224 | tf_op jit(solution)/shard_map/ppermute | solution.py:554
  5.6 2.6 %collective-permute-start = (f32[4,64,128]{2,1,0:T(8,128)S(1)}, f32[4,64,128]{2,1,0:T(8,128)S(1)}, u32[]{:S(2)}, u32[]{:S(2)}) collective-permute-start(f32[4,64,128]{2,1,0:T(8,128)S(1)} %get-tuple-element.80.sa_ref.refs_5_), channel_id=1, source_target_pairs={{0,4},{1,5},{2,6},{3,7},{4,0},{5,1},{6,2},{7,3},{8,12},{9,13},{10,... | collective-permute-start | bytes 393224 | tf_op jit(solution)/shard_map/ppermute | solution.py:556
  8.2 0.6 %collective-permute-start.3 = (f32[4,16,128]{2,1,0:T(8,128)S(1)}, f32[4,16,128]{2,1,0:T(8,128)S(1)}, u32[]{:S(2)}, u32[]{:S(2)}) collective-permute-start(f32[4,16,128]{2,1,0:T(8,128)S(1)} %get-tuple-element.83.sd_ref.refs_8_), channel_id=1, source_target_pairs={{0,3},{1,2},{2,1},{3,0},{4,7},{5,6},{6,5},{7,4},{8,11},{9,10},{10,... | collective-permute-start | bytes 98312 | tf_op jit(solution)/shard_map/ppermute | solution.py:558
  8.9 3.3 %shard_map.86 = (f32[16,64,128]{2,1,0:T(8,128)S(1)}, f32[16,64,128]{2,1,0:T(8,128)S(1)}, f32[16,64,128]{2,1,0:T(8,128)S(1)}, f32[16,64,128]{2,1,0:T(8,128)S(1)},...) custom-call(s32[16,64,128]{2,1,0:T(8,128)} %bitcast.8, ...), custom_call_target="tpu_custom_call" | custom-call | flops 8000000 | tf_op jit(solution)/shard_map/pallas_call | solution.py:46
  12.3 0.9 %collective-permute-start.5 = (f32[1,128]{1,0:T(1,128)S(1)}, f32[1,128]{1,0:T(1,128)S(1)}, u32[]{:S(2)}, u32[]{:S(2)}) collective-permute-start(f32[1,128]{1,0:T(1,128)S(1)} %get-tuple-element.87), channel_id=1, source_target_pairs={{0,5},{1,6},{2,7},{3,4},{4,9},{5,10},{6,11},{7,8},{8,13},{9,14},{1... | collective-permute-start | bytes 1544 | tf_op jit(solution)/shard_map/ppermute | solution.py:619
  13.2 4.3 %shard_map.87 = (f32[3,16,64,128]{3,2,1,0:T(8,128)S(1)}, f32[3,16,64,128]{3,2,1,0:T(8,128)S(1)}, f32[3,16,128]{2,1,0:T(8,128)S(1)}, f32[3,16,128]{2,1,0:T(8,128)S(1)}) custom-call(f32[3,16,64,128]{3,2,1,0:T(8,128)} %bitcast.6, f32[3,16,64,128]{3,2,1,0:T(8,128)} %bitcast.9, f32[16,64,128]{2,1,0:T(8,128)S(1)} %get-tuple-element.74.kx_ref.kx_in, ...), custom_call_target="tpu_custom_call" | custom-call | flops 20000000 | tf_op jit(solution)/shard_map/pallas_call | solution.py:46
  17.5 1.6 %collective-permute-done.5.corner_ref = f32[1,128]{1,0:T(1,128)S(1)} collective-permute-done((f32[1,128]{1,0:T(1,128)S(1)}, f32[1,128]{1,0:T(1,128)S(1)}, u32[]{:S(2)}, u32[]{:S(2)}) %collective-permute-start.5) | collective-permute-done | bytes 544 | tf_op jit(solution)/shard_map/ppermute | solution.py:619
  19.1 0.7 %shard_map.90 = (f32[16,64,128]{2,1,0:T(8,128)S(1)}, f32[16,64,128]{2,1,0:T(8,128)S(1)}, f32[16,64,128]{2,1,0:T(8,128)S(1)}, f32[64,128]{1,0:T(8,128)S(1)}, f32[...) custom-call(f32[4,64,128]{2,1,0:T(8,128)S(1)} %get-tuple-element.80., ...), custom_call_target="tpu_custom_call", output_to_operand_aliasing={{0}: (12, {}), {1}: (13, {}), {2}: (14, {})} | custom-call | tf_op jit(solution)/shard_map/pallas_call | solution.py:46
  19.9 0.2 shard_map.91
  20.0 0.4 collective-permute-start.7
  20.4 4.4 %collective-permute-start.6 = (f32[3,64,128]{2,1,0:T(8,128)S(1)}, f32[3,64,128]{2,1,0:T(8,128)S(1)}, u32[]{:S(2)}, u32[]{:S(2)}) collective-permute-start(f32[3,64,128]{2,1,0:T(8,128)S(1)} %get-tuple-element.111.refs_3_), channel_id=1, source_target_pairs={{0,4},{1,5},{2,6},{3,7},{4,0},{5,1},{6,2},{7,3},{8,12},{9,13},{10,... | collective-permute-start | bytes 294920 | tf_op jit(solution)/shard_map/ppermute | solution.py:556
  24.7 1.6 %collective-permute-start.10 = (f32[3,32,128]{2,1,0:T(8,128)S(1)}, f32[3,32,128]{2,1,0:T(8,128)S(1)}, u32[]{:S(2)}, u32[]{:S(2)}) collective-permute-start(f32[3,32,128]{2,1,0:T(8,128)S(1)} %get-tuple-element.115), channel_id=1, source_target_pairs={{0,17},{1,18},{2,19},{3,16},{4,21},{5,22},{6,23},{7,20},{8,25},{9,... | collective-permute-start | bytes 147464 | tf_op jit(solution)/shard_map/ppermute | solution.py:554
  26.4 0.5 collective-permute-start.9
  26.9 1.8 %shard_map.92 = (f32[3,16,64,128]{3,2,1,0:T(8,128)S(1)}, f32[3,16,64,128]{3,2,1,0:T(8,128)S(1)}, f32[3,16,128]{2,1,0:T(8,128)S(1)}, f32[3,16,128]{2,1,0:T(8,128)S(1)}) custom-call(f32[3,16,64,128]{3,2,1,0:T(8,128)S(1)} %get-tuple-element.78.refs_2_.u_in, ...), custom_call_target="tpu_custom_call", output_to_operand_aliasing={{0}: (0, {}), {1}: (1, {})} | custom-call | flops 20000000 | tf_op jit(solution)/shard_map/pallas_call | solution.py:46
  28.7 0.4 collective-permute-done.10.far_ref
  29.2 0.7 %collective-permute-done.9.refs_10_ = f32[3,16,128]{2,1,0:T(8,128)S(1)} collective-permute-done((f32[3,16,128]{2,1,0:T(8,128)S(1)}, f32[3,16,128]{2,1,0:T(8,128)S(1)}, u32[]{:S(2)}, u32[]{:S(2)}) %collective-permute-start.9) | collective-permute-done | bytes 24608 | tf_op jit(solution)/shard_map/ppermute | solution.py:558
  29.8 0.1 shard_map.94
  30.1 0.5 collective-permute-start.11
  30.6 2.1 %collective-permute-start.15 = (f32[3,32,128]{2,1,0:T(8,128)S(1)}, f32[3,32,128]{2,1,0:T(8,128)S(1)}, u32[]{:S(2)}, u32[]{:S(2)}) collective-permute-start(f32[3,32,128]{2,1,0:T(8,128)S(1)} %get-tuple-element.129), channel_id=1, source_target_pairs={{0,17},{1,18},{2,19},{3,16},{4,21},{5,22},{6,23},{7,20},{8,25},{9,... | collective-permute-start | bytes 147464 | tf_op jit(solution)/shard_map/ppermute | solution.py:554
  32.7 0.9 %collective-permute-start.14 = (f32[3,16,128]{2,1,0:T(8,128)S(1)}, f32[3,16,128]{2,1,0:T(8,128)S(1)}, u32[]{:S(2)}, u32[]{:S(2)}) collective-permute-start(f32[3,16,128]{2,1,0:T(8,128)S(1)} %get-tuple-element.128.refs_6_), channel_id=1, source_target_pairs={{0,3},{1,2},{2,1},{3,0},{4,7},{5,6},{6,5},{7,4},{8,11},{9,10},{10,... | collective-permute-start | bytes 73736 | tf_op jit(solution)/shard_map/ppermute | solution.py:558
  33.7 1.8 %shard_map.95 = (f32[3,16,64,128]{3,2,1,0:T(8,128)S(1)}, f32[3,16,64,128]{3,2,1,0:T(8,128)S(1)}, f32[3,16,128]{2,1,0:T(8,128)S(1)}, f32[3,16,128]{2,1,0:T(8,128)S(1)}) custom-call(f32[3,16,64,128]{3,2,1,0:T(8,128)S(1)} %get-tuple-element.107.refs_0_.u_in, ...), custom_call_target="tpu_custom_call", output_to_operand_aliasing={{0}: (0, {}), {1}: (1, {})} | custom-call | flops 20000000 | tf_op jit(solution)/shard_map/pallas_call | solution.py:46
  35.5 0.2 collective-permute-done.15.far_ref
  35.7 0.8 %collective-permute-done.14.refs_10_ = f32[3,16,128]{2,1,0:T(8,128)S(1)} collective-permute-done((f32[3,16,128]{2,1,0:T(8,128)S(1)}, f32[3,16,128]{2,1,0:T(8,128)S(1)}, u32[]{:S(2)}, u32[]{:S(2)}) %collective-permute-start.14) | collective-permute-done | bytes 24608 | tf_op jit(solution)/shard_map/ppermute | solution.py:558
  36.5 0.1 shard_map.97
  36.6 0.3 collective-permute-start.16
  36.9 2.6 %collective-permute-start.18 = (f32[3,64,128]{2,1,0:T(8,128)S(1)}, f32[3,64,128]{2,1,0:T(8,128)S(1)}, u32[]{:S(2)}, u32[]{:S(2)}) collective-permute-start(f32[3,64,128]{2,1,0:T(8,128)S(1)} %get-tuple-element.140.refs_4_), channel_id=1, source_target_pairs={{0,4},{1,5},{2,6},{3,7},{4,0},{5,1},{6,2},{7,3},{8,12},{9,13},{10,... | collective-permute-start | bytes 294920 | tf_op jit(solution)/shard_map/ppermute | solution.py:556
  39.6 2.0 %collective-permute-start.17 = (f32[3,32,128]{2,1,0:T(8,128)S(1)}, f32[3,32,128]{2,1,0:T(8,128)S(1)}, u32[]{:S(2)}, u32[]{:S(2)}) collective-permute-start(f32[3,32,128]{2,1,0:T(8,128)S(1)} %get-tuple-element.137), channel_id=1, source_target_pairs={{0,17},{1,18},{2,19},{3,16},{4,21},{5,22},{6,23},{7,20},{8,25},{9,... | collective-permute-start | bytes 147464 | tf_op jit(solution)/shard_map/ppermute | solution.py:554
  41.5 0.8 %collective-permute-start.20 = (f32[3,16,128]{2,1,0:T(8,128)S(1)}, f32[3,16,128]{2,1,0:T(8,128)S(1)}, u32[]{:S(2)}, u32[]{:S(2)}) collective-permute-start(f32[3,16,128]{2,1,0:T(8,128)S(1)} %get-tuple-element.142.refs_7_), channel_id=1, source_target_pairs={{0,3},{1,2},{2,1},{3,0},{4,7},{5,6},{6,5},{7,4},{8,11},{9,10},{10,... | collective-permute-start | bytes 73736 | tf_op jit(solution)/shard_map/ppermute | solution.py:558
  42.3 2.6 %shard_map.98 = (f32[3,16,64,128]{3,2,1,0:T(8,128)S(1)}, f32[3,16,64,128]{3,2,1,0:T(8,128)S(1)}, f32[3,16,128]{2,1,0:T(8,128)}, f32[3,16,128]{2,1,0:T(8,128)}) custom-call(f32[3,16,64,128]{3,2,1,0:T(8,128)S(1)} %get-tuple-element.121.refs_0_.u_in, f32[3,16,64,128]{3,2,1,0:T(8,128)S(1)} %get-tuple-element.122.w_in, ...), custom_call_target="tpu_custom_call", output_to_operand_aliasing={{0}: (0, {}), {1}: (1, {})} | custom-call | flops 20000000 | tf_op jit(solution)/shard_map/pallas_call | solution.py:46
  44.9 1.7 %shard_map.99 = (f32[3,16,64,128]{3,2,1,0:T(8,128)}, f32[3,16,64,128]{3,2,1,0:T(8,128)}, f32[64,128]{1,0:T(8,128)S(1)}) custom-call(f32[3,64,128]{2,1,0:T(8,128)S(1)} %get-tuple-element.136.own_ref.refs_5_, f32[3,64,128]{2,1,0:T(8,128)S(1)} %collective-permute-done.16.near_ref.refs_9_, f32[3,32,128]{2,1,0:T(8,128)S(1)} %collective-permute-done.17.far_ref, ...), custom_call_target="tpu_custom_call" | custom-call | flops 20000000 | tf_op jit(solution)/shard_map/pallas_call | solution.py:46
  46.6 1.1 %shard_map.100 = (f32[3,16,64,128]{3,2,1,0:T(8,128)}, f32[3,16,64,128]{3,2,1,0:T(8,128)}) custom-call(f32[3,16,64,128]{3,2,1,0:T(8,128)S(1)} %get-tuple-element.134.u_ref.refs_0_, f32[3,16,64,128]{3,2,1,0:T(8,128)S(1)} %get-tuple-element.135.w_ref.refs_1_, ...), custom_call_target="tpu_custom_call", output_to_operand_aliasing={{0}: (2, {}), {1}: (3, {})} | custom-call | tf_op jit(solution)/shard_map/pallas_call | solution.py:46
  (33 shorter events, 0.2 us)
Async XLA Ops:
  0.6 8.2 %copy-start = (f32[8]{0:T(128)S(1)}, f32[8]{0:T(128)}, u32[]{:S(2)}) copy-start(f32[8]{0:T(128)} %moduli_ref.3) | copy-start | bytes 100
  0.6 8.2 %copy-start.2 = (s32[256]{0:T(256)S(1)}, s32[256]{0:T(256)}, u32[]{:S(2)}) copy-start(s32[256]{0:T(256)} %active_ref.1) | copy-start | bytes 3076
  0.7 8.2 %copy-start.1 = (s32[256]{0:T(256)S(1)}, s32[256]{0:T(256)}, u32[]{:S(2)}) copy-start(s32[256]{0:T(256)} %partner_ref.1) | copy-start | bytes 3076
  0.7 8.2 %copy-start.3 = (f32[8]{0:T(128)S(1)}, f32[8]{0:T(128)}, u32[]{:S(2)}) copy-start(f32[8]{0:T(128)} %density_ref.1) | copy-start | bytes 100
  2.0 10.2 %collective-permute-start.4 = (f32[4,64,128]{2,1,0:T(8,128)S(1)}, f32[4,64,128]{2,1,0:T(8,128)S(1)}, u32[]{:S(2)}, u32[]{:S(2)}) collective-permute-start(f32[4,64,128]{2,1,0:T(8,128)S(1)} %get-tuple-element.81.own_ref.sb_ref.refs_6_), channel_id=1, source_target_pairs={{0,17},{1,18},{2,19},{3,16},{4,21},{5,22},{6,23},{7,20},{8,25},{9,... | collective-permute-start | bytes 393224 | tf_op jit(solution)/shard_map/ppermute | solution.py:554
  5.6 6.6 %collective-permute-start.1 = (f32[4,64,128]{2,1,0:T(8,128)S(1)}, f32[4,64,128]{2,1,0:T(8,128)S(1)}, u32[]{:S(2)}, u32[]{:S(2)}) collective-permute-start(f32[4,64,128]{2,1,0:T(8,128)S(1)} %get-tuple-element.81.own_ref.sb_ref.refs_6_), channel_id=1, source_target_pairs={{0,16},{1,17},{2,18},{3,19},{4,8},{5,9},{6,10},{7,11},{8,4},{9,5},... | collective-permute-start | bytes 393224 | tf_op jit(solution)/shard_map/ppermute | solution.py:555
  5.6 11.9 %collective-permute-start = (f32[4,64,128]{2,1,0:T(8,128)S(1)}, f32[4,64,128]{2,1,0:T(8,128)S(1)}, u32[]{:S(2)}, u32[]{:S(2)}) collective-permute-start(f32[4,64,128]{2,1,0:T(8,128)S(1)} %get-tuple-element.80.sa_ref.refs_5_), channel_id=1, source_target_pairs={{0,4},{1,5},{2,6},{3,7},{4,0},{5,1},{6,2},{7,3},{8,12},{9,13},{10,... | collective-permute-start | bytes 393224 | tf_op jit(solution)/shard_map/ppermute | solution.py:556
  8.2 9.2 %collective-permute-start.2 = (f32[4,16,128]{2,1,0:T(8,128)S(1)}, f32[4,16,128]{2,1,0:T(8,128)S(1)}, u32[]{:S(2)}, u32[]{:S(2)}) collective-permute-start(f32[4,16,128]{2,1,0:T(8,128)S(1)} %get-tuple-element.82.sc_ref.refs_7_), channel_id=1, source_target_pairs={{0,1},{1,0},{2,3},{3,2},{4,5},{5,4},{6,7},{7,6},{8,9},{9,8},{10,11... | collective-permute-start | bytes 98312 | tf_op jit(solution)/shard_map/ppermute | solution.py:557
  8.2 9.2 %collective-permute-start.3 = (f32[4,16,128]{2,1,0:T(8,128)S(1)}, f32[4,16,128]{2,1,0:T(8,128)S(1)}, u32[]{:S(2)}, u32[]{:S(2)}) collective-permute-start(f32[4,16,128]{2,1,0:T(8,128)S(1)} %get-tuple-element.83.sd_ref.refs_8_), channel_id=1, source_target_pairs={{0,3},{1,2},{2,1},{3,0},{4,7},{5,6},{6,5},{7,4},{8,11},{9,10},{10,... | collective-permute-start | bytes 98312 | tf_op jit(solution)/shard_map/ppermute | solution.py:558
  12.3 6.8 %collective-permute-start.5 = (f32[1,128]{1,0:T(1,128)S(1)}, f32[1,128]{1,0:T(1,128)S(1)}, u32[]{:S(2)}, u32[]{:S(2)}) collective-permute-start(f32[1,128]{1,0:T(1,128)S(1)} %get-tuple-element.87), channel_id=1, source_target_pairs={{0,5},{1,6},{2,7},{3,4},{4,9},{5,10},{6,11},{7,8},{8,13},{9,14},{1... | collective-permute-start | bytes 1544 | tf_op jit(solution)/shard_map/ppermute | solution.py:619
  20.0 9.1 %collective-permute-start.7 = (f32[3,64,128]{2,1,0:T(8,128)S(1)}, f32[3,64,128]{2,1,0:T(8,128)S(1)}, u32[]{:S(2)}, u32[]{:S(2)}) collective-permute-start(f32[3,64,128]{2,1,0:T(8,128)S(1)} %get-tuple-element.112.own_ref.refs_4_), channel_id=1, source_target_pairs={{0,16},{1,17},{2,18},{3,19},{4,8},{5,9},{6,10},{7,11},{8,4},{9,5},... | collective-permute-start | bytes 294920 | tf_op jit(solution)/shard_map/ppermute | solution.py:555
  20.4 9.5 %collective-permute-start.6 = (f32[3,64,128]{2,1,0:T(8,128)S(1)}, f32[3,64,128]{2,1,0:T(8,128)S(1)}, u32[]{:S(2)}, u32[]{:S(2)}) collective-permute-start(f32[3,64,128]{2,1,0:T(8,128)S(1)} %get-tuple-element.111.refs_3_), channel_id=1, source_target_pairs={{0,4},{1,5},{2,6},{3,7},{4,0},{5,1},{6,2},{7,3},{8,12},{9,13},{10,... | collective-permute-start | bytes 294920 | tf_op jit(solution)/shard_map/ppermute | solution.py:556
  24.7 4.4 %collective-permute-start.10 = (f32[3,32,128]{2,1,0:T(8,128)S(1)}, f32[3,32,128]{2,1,0:T(8,128)S(1)}, u32[]{:S(2)}, u32[]{:S(2)}) collective-permute-start(f32[3,32,128]{2,1,0:T(8,128)S(1)} %get-tuple-element.115), channel_id=1, source_target_pairs={{0,17},{1,18},{2,19},{3,16},{4,21},{5,22},{6,23},{7,20},{8,25},{9,... | collective-permute-start | bytes 147464 | tf_op jit(solution)/shard_map/ppermute | solution.py:554
  26.4 2.8 %collective-permute-start.8 = (f32[3,16,128]{2,1,0:T(8,128)S(1)}, f32[3,16,128]{2,1,0:T(8,128)S(1)}, u32[]{:S(2)}, u32[]{:S(2)}) collective-permute-start(f32[3,16,128]{2,1,0:T(8,128)S(1)} %get-tuple-element.113.refs_5_), channel_id=1, source_target_pairs={{0,1},{1,0},{2,3},{3,2},{4,5},{5,4},{6,7},{7,6},{8,9},{9,8},{10,11... | collective-permute-start | bytes 73736 | tf_op jit(solution)/shard_map/ppermute | solution.py:557
  26.4 3.4 %collective-permute-start.9 = (f32[3,16,128]{2,1,0:T(8,128)S(1)}, f32[3,16,128]{2,1,0:T(8,128)S(1)}, u32[]{:S(2)}, u32[]{:S(2)}) collective-permute-start(f32[3,16,128]{2,1,0:T(8,128)S(1)} %get-tuple-element.114.refs_6_), channel_id=1, source_target_pairs={{0,3},{1,2},{2,1},{3,0},{4,7},{5,6},{6,5},{7,4},{8,11},{9,10},{10,... | collective-permute-start | bytes 73736 | tf_op jit(solution)/shard_map/ppermute | solution.py:558
  30.0 5.7 %collective-permute-start.12 = (f32[3,64,128]{2,1,0:T(8,128)S(1)}, f32[3,64,128]{2,1,0:T(8,128)S(1)}, u32[]{:S(2)}, u32[]{:S(2)}) collective-permute-start(f32[3,64,128]{2,1,0:T(8,128)S(1)} %get-tuple-element.126.own_ref.refs_4_), channel_id=1, source_target_pairs={{0,16},{1,17},{2,18},{3,19},{4,8},{5,9},{6,10},{7,11},{8,4},{9,5},... | collective-permute-start | bytes 294920 | tf_op jit(solution)/shard_map/ppermute | solution.py:555
  30.1 6.4 %collective-permute-start.11 = (f32[3,64,128]{2,1,0:T(8,128)S(1)}, f32[3,64,128]{2,1,0:T(8,128)S(1)}, u32[]{:S(2)}, u32[]{:S(2)}) collective-permute-start(f32[3,64,128]{2,1,0:T(8,128)S(1)} %get-tuple-element.125.refs_3_), channel_id=1, source_target_pairs={{0,4},{1,5},{2,6},{3,7},{4,0},{5,1},{6,2},{7,3},{8,12},{9,13},{10,... | collective-permute-start | bytes 294920 | tf_op jit(solution)/shard_map/ppermute | solution.py:556
  30.6 5.1 %collective-permute-start.15 = (f32[3,32,128]{2,1,0:T(8,128)S(1)}, f32[3,32,128]{2,1,0:T(8,128)S(1)}, u32[]{:S(2)}, u32[]{:S(2)}) collective-permute-start(f32[3,32,128]{2,1,0:T(8,128)S(1)} %get-tuple-element.129), channel_id=1, source_target_pairs={{0,17},{1,18},{2,19},{3,16},{4,21},{5,22},{6,23},{7,20},{8,25},{9,... | collective-permute-start | bytes 147464 | tf_op jit(solution)/shard_map/ppermute | solution.py:554
  32.7 3.0 %collective-permute-start.13 = (f32[3,16,128]{2,1,0:T(8,128)S(1)}, f32[3,16,128]{2,1,0:T(8,128)S(1)}, u32[]{:S(2)}, u32[]{:S(2)}) collective-permute-start(f32[3,16,128]{2,1,0:T(8,128)S(1)} %get-tuple-element.127.refs_5_), channel_id=1, source_target_pairs={{0,1},{1,0},{2,3},{3,2},{4,5},{5,4},{6,7},{7,6},{8,9},{9,8},{10,11... | collective-permute-start | bytes 73736 | tf_op jit(solution)/shard_map/ppermute | solution.py:557
  32.7 3.8 %collective-permute-start.14 = (f32[3,16,128]{2,1,0:T(8,128)S(1)}, f32[3,16,128]{2,1,0:T(8,128)S(1)}, u32[]{:S(2)}, u32[]{:S(2)}) collective-permute-start(f32[3,16,128]{2,1,0:T(8,128)S(1)} %get-tuple-element.128.refs_6_), channel_id=1, source_target_pairs={{0,3},{1,2},{2,1},{3,0},{4,7},{5,6},{6,5},{7,4},{8,11},{9,10},{10,... | collective-permute-start | bytes 73736 | tf_op jit(solution)/shard_map/ppermute | solution.py:558
  36.6 8.2 %collective-permute-start.16 = (f32[3,64,128]{2,1,0:T(8,128)S(1)}, f32[3,64,128]{2,1,0:T(8,128)S(1)}, u32[]{:S(2)}, u32[]{:S(2)}) collective-permute-start(f32[3,64,128]{2,1,0:T(8,128)S(1)} %get-tuple-element.136.own_ref.refs_5_), channel_id=1, source_target_pairs={{0,16},{1,17},{2,18},{3,19},{4,8},{5,9},{6,10},{7,11},{8,4},{9,5},... | collective-permute-start | bytes 294920 | tf_op jit(solution)/shard_map/ppermute | solution.py:555
  36.9 9.7 %collective-permute-start.18 = (f32[3,64,128]{2,1,0:T(8,128)S(1)}, f32[3,64,128]{2,1,0:T(8,128)S(1)}, u32[]{:S(2)}, u32[]{:S(2)}) collective-permute-start(f32[3,64,128]{2,1,0:T(8,128)S(1)} %get-tuple-element.140.refs_4_), channel_id=1, source_target_pairs={{0,4},{1,5},{2,6},{3,7},{4,0},{5,1},{6,2},{7,3},{8,12},{9,13},{10,... | collective-permute-start | bytes 294920 | tf_op jit(solution)/shard_map/ppermute | solution.py:556
  39.6 5.3 %collective-permute-start.17 = (f32[3,32,128]{2,1,0:T(8,128)S(1)}, f32[3,32,128]{2,1,0:T(8,128)S(1)}, u32[]{:S(2)}, u32[]{:S(2)}) collective-permute-start(f32[3,32,128]{2,1,0:T(8,128)S(1)} %get-tuple-element.137), channel_id=1, source_target_pairs={{0,17},{1,18},{2,19},{3,16},{4,21},{5,22},{6,23},{7,20},{8,25},{9,... | collective-permute-start | bytes 147464 | tf_op jit(solution)/shard_map/ppermute | solution.py:554
  41.5 5.0 %collective-permute-start.19 = (f32[3,16,128]{2,1,0:T(8,128)S(1)}, f32[3,16,128]{2,1,0:T(8,128)S(1)}, u32[]{:S(2)}, u32[]{:S(2)}) collective-permute-start(f32[3,16,128]{2,1,0:T(8,128)S(1)} %get-tuple-element.141.refs_6_), channel_id=1, source_target_pairs={{0,1},{1,0},{2,3},{3,2},{4,5},{5,4},{6,7},{7,6},{8,9},{9,8},{10,11... | collective-permute-start | bytes 73736 | tf_op jit(solution)/shard_map/ppermute | solution.py:557
  41.5 5.1 %collective-permute-start.20 = (f32[3,16,128]{2,1,0:T(8,128)S(1)}, f32[3,16,128]{2,1,0:T(8,128)S(1)}, u32[]{:S(2)}, u32[]{:S(2)}) collective-permute-start(f32[3,16,128]{2,1,0:T(8,128)S(1)} %get-tuple-element.142.refs_7_), channel_id=1, source_target_pairs={{0,3},{1,2},{2,1},{3,0},{4,7},{5,6},{6,5},{7,4},{8,11},{9,10},{10,... | collective-permute-start | bytes 73736 | tf_op jit(solution)/shard_map/ppermute | solution.py:558

commit v4 on v3

--- a/solution.py
+++ b/solution.py
@@ -65,7 +65,7 @@
 
 
 def pack_kernel(
-    d_ref, mat_ref, sa_ref, sb_ref, sc_ref, sd_ref, corner_ref, plane_ref, rows_ref, kinds_ref, sems,
+    d_ref, mat_ref, sa_ref, sb_ref, sc_ref, sd_ref, se_ref, corner_ref, plane_ref, rows_ref, kinds_ref, sems,
 ):
     planes, rows, cols = mat_ref.shape
     place = here_in_mesh()
@@ -86,6 +86,8 @@
         copy.wait()
     kinds_a, kinds_b = plane_ref[0].astype(jnp.float32), plane_ref[1].astype(jnp.float32)
     sa_ref[3], sb_ref[3] = kinds_a, kinds_b
+    for c in range(3):
+        se_ref[c] = sb_ref[c]
     corner_ref[...] = jnp.where(place[0] % 2 == 0, kinds_a[rows - 1 :], kinds_b[rows - 1 :])
     for n, (ref, j) in enumerate(((sc_ref, jc - tile_c), (sd_ref, jd - tile_d))):
         for i in range(planes):
@@ -101,9 +103,9 @@
 
 
 def setup_kernel(
-    mat_ref, moduli_ref, density_ref, partner_ref, active_ref,
-    kx_ref, ky_ref, kz_ref, kick_ref, row_kick_ref, high_ky_ref, push_ref, pick_ref, half_ref, chosen_ref,
-    kinds_ref, turned_ref, inverse_ref, slot_ref, sems,
+    kinds_ref, v_ref, moduli_ref, density_ref, partner_ref, active_ref,
+    kx_ref, ky_ref, kz_ref, kick_ref, row_kick_ref, high_ky_ref, push_ref, pick_ref, half_ref, chosen_ref, held_ref,
+    turned_ref, inverse_ref, slot_ref, sem,
 ):
     planes, rows, cols = kinds_ref.shape
     place = here_in_mesh()
@@ -113,11 +115,8 @@
     col = lax.broadcasted_iota(jnp.int32, (rows, cols), 1)
     inside = (col < cols - 1) & ((row < rows - 1) | jnp.logical_not(last_y))
 
-    def copy(i):
-        return pltpu.make_async_copy(mat_ref.at[i], kinds_ref.at[i], sems.at[i])
-
-    for i in range(planes):
-        copy(i).start()
+    velocities = pltpu.make_async_copy(v_ref, held_ref, sem)
+    velocities.start()
 
     body, blocks = place[4], place[3]
     start = place[2] * rows
@@ -171,7 +170,6 @@
         lax.fori_loop(0, rows + 1, any_row, 0, unroll=8)
 
     def plane(i, earlier):
-        copy(i).wait()
         kinds = kinds_ref[i]
         stiff = jnp.zeros((rows, cols), jnp.float32)
         mass = jnp.ones((rows, cols), jnp.float32)
@@ -196,37 +194,21 @@
 
     lax.fori_loop(0, planes, plane, jnp.zeros((rows, cols), jnp.float32), unroll=math.gcd(4, planes))
     push_ref[...] = push_ref[...] * kick_ref[planes - 1]
+    velocities.wait()
 
 
 def rows_behind(value, row, first=0.0):
     return jnp.where(row == 0, first, pltpu.roll(value, 1, 0))
 
 
-def first_kernel(
-    d_ref, v_ref, kx_ref, ky_ref, kz_ref, kick_ref, u_ref, w_ref, yc_ref, yd_ref, sems,
-):
+def first_kernel(d_ref, v_ref, kx_ref, ky_ref, kz_ref, kick_ref, u_ref, w_ref, yc_ref, yd_ref):
     _, planes, rows, cols = u_ref.shape
     even_y = lax.axis_index("yz") % 2 == 0
 
-    def copies(i):
-        return (
-            pltpu.make_async_copy(d_ref.at[:, i], u_ref.at[:, i], sems.at[0, i]),
-            pltpu.make_async_copy(v_ref.at[:, i], w_ref.at[:, i], sems.at[1, i]),
-        )
-
-    for i in range(planes):
-        for copy in copies(i):
-            copy.start()
-    for copy in copies(0):
-        copy.wait()
-
     def plane(i, carried, ahead):
-        if ahead:
-            for copy in copies(i + 1):
-                copy.wait()
         return tuple(
             advance_plane(
-                c, i, u_ref[c, i] * U_SCALE, ahead and u_ref[c, i + 1] * U_SCALE, w_ref[c, i] * W_SCALE, carried[c],
+                c, i, d_ref[c, i] * U_SCALE, ahead and d_ref[c, i + 1] * U_SCALE, v_ref[c, i] * W_SCALE, carried[c],
                 kx_ref[i], ky_ref[i], kz_ref[i], kick_ref[i], u_ref, w_ref, yc_ref, yd_ref, even_y,
             )
             for c in range(3)
@@ -526,16 +508,21 @@
         return [(number(*at), number(*target(*at))) for at in every]
 
     def outer_x(b, g, y):
-        if g in (0, count_x - 1):
+        if g == count_x - 1:
             return 1 - b, g, y
-        return b, (g + 1 if g % 2 else g - 1), y
+        return (b, (g + 1 if g % 2 else g - 1), y) if g else (b, g, y ^ 1)
+
+    def diagonal(b, g, y):
+        if g == count_x - 1:
+            return 1 - b, g, (y - 1 if b else y + 1) % count_y
+        return b, g, y ^ 1
 
     return {
         "a": pairs(lambda b, g, y: (b, g ^ 1, y)),
         "b": pairs(outer_x),
         "c": pairs(lambda b, g, y: (b, g, y ^ 1)),
         "d": pairs(lambda b, g, y: (b, g, (y + 1 if y % 2 else y - 1) % count_y)),
-        "e": pairs(lambda b, g, y: (1 - b, g, (y - 1 if b else y + 1) % count_y)),
+        "e": pairs(diagonal),
         "corner": pairs(lambda b, g, y: (b, (g + 1) % count_x, (y + 1) % count_y)),
     }
 
@@ -550,17 +537,12 @@
     d, v, kinds = displacement[0], velocity[0], material[0]
     smem, hbm = pltpu.SMEM, pltpu.HBM
 
-    def exchange(a, b, c, d, e):
-        e = lax.ppermute(e, AXES, route["e"])
-        b = lax.ppermute(b, AXES, route["b"])
-        a = lax.ppermute(a, AXES, route["a"])
-        c = lax.ppermute(c, AXES, route["c"])
-        d = lax.ppermute(d, AXES, route["d"])
-        return [a, b, c, d], e
-
-    *sent, corner = call(
+    def passed(block, name):
+        return lax.ppermute(block, AXES, route[name])
+
+    *sent, spare, corner = call(
         pack_kernel,
-        [vmem((4, *face))] * 2 + [vmem((4, *side))] * 2 + [vmem((1, cols))],
+        [vmem((4, *face))] * 2 + [vmem((4, *side))] * 2 + [vmem(face3), vmem((1, cols))],
         [d, kinds],
         [hbm, hbm],
         scratch=[
@@ -570,19 +552,20 @@
             pltpu.SemaphoreType.DMA((8,)),
         ],
     )
-    got, got_e = exchange(*sent, sent[1])
-    kx, ky, kz, kick, row_kick, high_ky, push_scale, pick, pick_half, chosen = call(
+    got_e = passed(spare, "e")
+    got = [passed(block, name) for block, name in zip(sent, "abcd")]
+    kx, ky, kz, kick, row_kick, high_ky, push_scale, pick, pick_half, chosen, v = call(
         setup_kernel,
         [vmem(block)] * 4 + [vmem((2, *side)), vmem(side), vmem(face)]
-        + [vmem((lanes, lanes)), vmem((rows + rows // 2, lanes)), pltpu.SMEM((rows + 1,), jnp.int32)],
-        [kinds, moduli, density, partner, active],
-        [hbm] + [smem] * 4,
+        + [vmem((lanes, lanes)), vmem((rows + rows // 2, lanes)), pltpu.SMEM((rows + 1,), jnp.int32)]
+        + [vmem(state)],
+        [kinds, v, moduli, density, partner, active],
+        [None, hbm] + [smem] * 4,
         scratch=[
-            pltpu.VMEM(block, jnp.int32),
             vmem((2, lanes, lanes)),
             pltpu.SMEM(partner.shape, jnp.int32),
             pltpu.SMEM((rows + 1,), jnp.int32),
-            pltpu.SemaphoreType.DMA((planes,)),
+            pltpu.SemaphoreType.DMA,
         ],
         flops=8_000_000,
     )
@@ -590,8 +573,18 @@
     for step in range(STEPS):
         first, last = step == 0, step == STEPS - 1
         scale = U_SCALE if first else 1.0
-        if not first:
-            got, got_e = exchange(*sent, spare)
+        if first:
+            u, w, yc, yd = call(
+                first_kernel,
+                [vmem(state)] * 2 + [vmem(side3)] * 2,
+                [d, v, kx, ky, kz, kick],
+                flops=20_000_000,
+            )
+            corner, push_scale, yc = lax.optimization_barrier((corner, push_scale, yc))
+            corner = passed(corner, "corner")
+        else:
+            got_e = passed(spare, "e")
+            got = [passed(block, name) for block, name in zip(sent, "abcd")]
             u, w, yc, yd = call(
                 functools.partial(interior_kernel, *((1.0 / U_SCALE, 1.0 / W_SCALE) if last else (1.0, 1.0))),
                 [vmem(state)] * 2 + [vmem(side3)] * 2,
@@ -611,20 +604,11 @@
             )
             break
         (push,) = call(
-            functools.partial(contact_kernel, scale), [vmem(face)], meet, scratch=pair_scratch, flops=20_000_000
+            functools.partial(contact_kernel, scale), [vmem(face)], meet, scratch=pair_scratch,
+            flops=0 if first else 20_000_000,
         )
         extra = []
         if first:
-            corner, push = lax.optimization_barrier((corner, push))
-            corner = lax.ppermute(corner, AXES, route["corner"])
-            u, w, yc, yd = call(
-                first_kernel,
-                [vmem(state)] * 2 + [vmem(side3)] * 2,
-                [d, v, kx, ky, kz, kick],
-                [hbm] * 2 + [None] * 4,
-                scratch=[pltpu.SemaphoreType.DMA((2, planes))],
-                flops=20_000_000,
-            )
             kx, ky, kz, *rest = call(
                 edge_kernel,
                 [vmem(block)] * 3 + [vmem(face)] * 2 + [vmem(side)] * 2 + [vmem(face3), vmem(side3)],

time: 47.9 us -> 43.1 us (0.90)
  the two profiles are of different devices: /device:TPU:1 before, /device:TPU:25 now
where the time goes in v4:
time: 43.1 us; the launch traced here: 42.9 us
  Pallas kernels  24.5 us (57%)
  starting transfers between devices  14.5 us (34%)
  waiting for transfers between devices  3.06 us (7%)
  between operations  0.91 us (2%)
    pallas_call x15, Pallas kernels, call(): pl.pallas_call(kernel, out_shape=outs, in_specs=specs, out_specs=[pl.Bloc...  24.5 us
    ppermute x21, starting transfers between devices, passed(): return lax.ppermute(block, AXES, route[name])  14.5 us
    ppermute x21, waiting for transfers between devices, passed(): return lax.ppermute(block, AXES, route[name])  3.06 us
  transfers between devices with their start and end apart: 21, of which 3 were waited for; matrix products, arithmetic and copies ran while one was open for 0% of the time, Pallas kernels for 48%

profile of v4, /device:TPU:25, one launch (start us, length us, event | category | flops | bytes accessed | tf_op | source)
XLA Modules:
  0.0 42.9 jit_solution(4542176756390421288)
XLA Ops:
  0.7 1.4 %shard_map.88 = (f32[4,64,128]{2,1,0:T(8,128)S(1)}, f32[4,64,128]{2,1,0:T(8,128)S(1)}, f32[4,16,128]{2,1,0:T(8,128)S(1)}, f32[4,16,128]{2,1,0:T(8,128)S(1)}, f32...) custom-call(f32[3,16,64,128]{3,2,1,0:T(8,128)} %bitcast.5, s32[16,64,128]{2,1,0:T(8,128)} %bitcast.7), custom_call_target="tpu_custom_call" | custom-call | tf_op jit(solution)/shard_map/pallas_call | solution.py:46
  2.1 1.3 %collective-permute-start.1 = (f32[4,64,128]{2,1,0:T(8,128)S(1)}, f32[4,64,128]{2,1,0:T(8,128)S(1)}, u32[]{:S(2)}, u32[]{:S(2)}) collective-permute-start(f32[4,64,128]{2,1,0:T(8,128)S(1)} %get-tuple-element.85.sb_ref.own_ref.refs_6_), channel_id=1, source_target_pairs={{0,1},{1,0},{2,3},{3,2},{4,8},{5,9},{6,10},{7,11},{8,4},{9,5},{10,... | collective-permute-start | bytes 393224 | tf_op jit(solution)/shard_map/ppermute | solution.py:541
  3.4 2.4 %collective-permute-start.5 = (f32[3,64,128]{2,1,0:T(8,128)S(1)}, f32[3,64,128]{2,1,0:T(8,128)S(1)}, u32[]{:S(2)}, u32[]{:S(2)}) collective-permute-start(f32[3,64,128]{2,1,0:T(8,128)S(1)} %get-tuple-element.105), channel_id=1, source_target_pairs={{0,1},{1,0},{2,3},{3,2},{4,5},{5,4},{6,7},{7,6},{8,9},{9,8},{10,11... | collective-permute-start | bytes 294920 | tf_op jit(solution)/shard_map/ppermute | solution.py:541
  5.8 0.6 %collective-permute-start.3 = (f32[4,16,128]{2,1,0:T(8,128)S(1)}, f32[4,16,128]{2,1,0:T(8,128)S(1)}, u32[]{:S(2)}, u32[]{:S(2)}) collective-permute-start(f32[4,16,128]{2,1,0:T(8,128)S(1)} %get-tuple-element.87.sd_ref.refs_8_), channel_id=1, source_target_pairs={{0,3},{1,2},{2,1},{3,0},{4,7},{5,6},{6,5},{7,4},{8,11},{9,10},{10,... | collective-permute-start | bytes 98312 | tf_op jit(solution)/shard_map/ppermute | solution.py:541
  6.4 2.9 %shard_map.86 = (f32[16,64,128]{2,1,0:T(8,128)S(1)}, f32[16,64,128]{2,1,0:T(8,128)S(1)}, f32[16,64,128]{2,1,0:T(8,128)S(1)}, f32[16,64,128]{2,1,0:T(8,128)S(1)},...) custom-call(s32[16,64,128]{2,1,0:T(8,128)S(1)} %bitcast.8, ...), custom_call_target="tpu_custom_call" | custom-call | flops 8000000 | tf_op jit(solution)/shard_map/pallas_call | solution.py:46
  9.4 2.0 %shard_map.87 = (f32[3,16,64,128]{3,2,1,0:T(8,128)S(1)}, f32[3,16,64,128]{3,2,1,0:T(8,128)S(1)}, f32[3,16,128]{2,1,0:T(8,128)S(1)}, f32[3,16,128]{2,1,0:T(8,128)S(1)}) custom-call(f32[3,16,64,128]{3,2,1,0:T(8,128)S(1)} %bitcast.6, f32[3,16,64,128]{3,2,1,0:T(8,128)S(1)} %get-tuple-element.77.v_ref, f32[16,64,128]{2,1,0:T(8,128)S(1)} %get-tuple-element.78.kx_ref.kx_in, ...), custom_call_target="tpu_custom_call" | custom-call | flops 20000000 | tf_op jit(solution)/shard_map/pallas_call | solution.py:46
  11.4 0.1 collective-permute-start.4
  11.5 2.4 %shard_map.90.refs_17_ = f32[64,128]{1,0:T(8,128)S(1)} custom-call(f32[4,64,128]{2,1,0:T(8,128)S(1)} %get-tuple-element.85.sb_ref.own_ref.refs_6_, f32[4,64,128]{2,1,0:T(8,128)S(1)} %collective-permute-done.1.rb_ref.near_ref.refs_10_, f32[3,64,128]{2,1,0:T(8,128)S(1)} %collective-permute-done.5.far_ref, f32[128,128]{1,0:T(8,128)S(1)} %get-tuple-element.106.pick_ref, ...), custom_call_target="tpu_custom_call" | custom-call | tf_op jit(solution)/shard_map/pallas_call | solution.py:46
  13.9 0.5 %collective-permute-done.4.corner_ref = f32[1,128]{1,0:T(1,128)S(1)} collective-permute-done((f32[1,128]{1,0:T(1,128)S(1)}, f32[1,128]{1,0:T(1,128)S(1)}, u32[]{:S(2)}, u32[]{:S(2)}) %collective-permute-start.4) | collective-permute-done | bytes 544 | tf_op jit(solution)/shard_map/ppermute | solution.py:541
  14.4 0.8 %shard_map.89 = (f32[16,64,128]{2,1,0:T(8,128)S(1)}, f32[16,64,128]{2,1,0:T(8,128)S(1)}, f32[16,64,128]{2,1,0:T(8,128)S(1)}, f32[64,128]{1,0:T(8,128)S(1)}, f32[...) custom-call(f32[4,64,128]{2,1,0:T(8,128)S(1)} %get-tuple-element.84., ...), custom_call_target="tpu_custom_call", output_to_operand_aliasing={{0}: (12, {}), {1}: (13, {}), {2}: (14, {})} | custom-call | tf_op jit(solution)/shard_map/pallas_call | solution.py:46
  15.2 0.2 shard_map.91
  15.4 1.0 %collective-permute-start.7 = (f32[3,64,128]{2,1,0:T(8,128)S(1)}, f32[3,64,128]{2,1,0:T(8,128)S(1)}, u32[]{:S(2)}, u32[]{:S(2)}) collective-permute-start(f32[3,64,128]{2,1,0:T(8,128)S(1)} %get-tuple-element.118.own_ref.refs_4_), channel_id=1, source_target_pairs={{0,1},{1,0},{2,3},{3,2},{4,8},{5,9},{6,10},{7,11},{8,4},{9,5},{10,... | collective-permute-start | bytes 294920 | tf_op jit(solution)/shard_map/ppermute | solution.py:541
  16.3 2.6 %collective-permute-start.10 = (f32[3,32,128]{2,1,0:T(8,128)S(1)}, f32[3,32,128]{2,1,0:T(8,128)S(1)}, u32[]{:S(2)}, u32[]{:S(2)}) collective-permute-start(f32[3,32,128]{2,1,0:T(8,128)S(1)} %get-tuple-element.121), channel_id=1, source_target_pairs={{0,1},{1,0},{2,3},{3,2},{4,5},{5,4},{6,7},{7,6},{8,9},{9,8},{10,11... | collective-permute-start | bytes 147464 | tf_op jit(solution)/shard_map/ppermute | solution.py:541
  18.9 0.6 %collective-permute-start.9 = (f32[3,16,128]{2,1,0:T(8,128)S(1)}, f32[3,16,128]{2,1,0:T(8,128)S(1)}, u32[]{:S(2)}, u32[]{:S(2)}) collective-permute-start(f32[3,16,128]{2,1,0:T(8,128)S(1)} %get-tuple-element.120.refs_6_), channel_id=1, source_target_pairs={{0,3},{1,2},{2,1},{3,0},{4,7},{5,6},{6,5},{7,4},{8,11},{9,10},{10,... | collective-permute-start | bytes 73736 | tf_op jit(solution)/shard_map/ppermute | solution.py:541
  19.6 1.8 %shard_map.92 = (f32[3,16,64,128]{3,2,1,0:T(8,128)S(1)}, f32[3,16,64,128]{3,2,1,0:T(8,128)S(1)}, f32[3,16,128]{2,1,0:T(8,128)S(1)}, f32[3,16,128]{2,1,0:T(8,128)S(1)}) custom-call(f32[3,16,64,128]{3,2,1,0:T(8,128)S(1)} %get-tuple-element.82.refs_2_.u_in, ...), custom_call_target="tpu_custom_call", output_to_operand_aliasing={{0}: (0, {}), {1}: (1, {})} | custom-call | flops 20000000 | tf_op jit(solution)/shard_map/pallas_call | solution.py:46
  21.4 1.0 %collective-permute-done.10.far_ref = f32[3,32,128]{2,1,0:T(8,128)S(1)} collective-permute-done((f32[3,32,128]{2,1,0:T(8,128)S(1)}, f32[3,32,128]{2,1,0:T(8,128)S(1)}, u32[]{:S(2)}, u32[]{:S(2)}) %collective-permute-start.10) | collective-permute-done | bytes 49184 | tf_op jit(solution)/shard_map/ppermute | solution.py:541
  22.4 2.4 %shard_map.93.refs_15_ = f32[64,128]{1,0:T(8,128)S(1)} custom-call(f32[3,64,128]{2,1,0:T(8,128)S(1)} %get-tuple-element.118.own_ref.refs_4_, f32[3,64,128]{2,1,0:T(8,128)S(1)} %collective-permute-done.7.near_ref.refs_8_, f32[3,32,128]{2,1,0:T(8,128)S(1)} %collective-permute-done.10.far_ref, f32[96,128]{1,0:T(8,128)S(1)} %get-tuple-element.122.pick_ref, ...), custom_call_target="tpu_custom_call" | custom-call | flops 20000000 | tf_op jit(solution)/shard_map/pallas_call | solution.py:46
  24.8 0.1 shard_map.94
  25.0 0.1 collective-permute-start.12
  25.2 1.6 %collective-permute-start.15 = (f32[3,32,128]{2,1,0:T(8,128)S(1)}, f32[3,32,128]{2,1,0:T(8,128)S(1)}, u32[]{:S(2)}, u32[]{:S(2)}) collective-permute-start(f32[3,32,128]{2,1,0:T(8,128)S(1)} %get-tuple-element.135), channel_id=1, source_target_pairs={{0,1},{1,0},{2,3},{3,2},{4,5},{5,4},{6,7},{7,6},{8,9},{9,8},{10,11... | collective-permute-start | bytes 147464 | tf_op jit(solution)/shard_map/ppermute | solution.py:541
  26.8 0.2 collective-permute-start.13
  26.9 0.5 %collective-permute-start.14 = (f32[3,16,128]{2,1,0:T(8,128)S(1)}, f32[3,16,128]{2,1,0:T(8,128)S(1)}, u32[]{:S(2)}, u32[]{:S(2)}) collective-permute-start(f32[3,16,128]{2,1,0:T(8,128)S(1)} %get-tuple-element.134.refs_6_), channel_id=1, source_target_pairs={{0,3},{1,2},{2,1},{3,0},{4,7},{5,6},{6,5},{7,4},{8,11},{9,10},{10,... | collective-permute-start | bytes 73736 | tf_op jit(solution)/shard_map/ppermute | solution.py:541
  27.4 1.8 %shard_map.95 = (f32[3,16,64,128]{3,2,1,0:T(8,128)S(1)}, f32[3,16,64,128]{3,2,1,0:T(8,128)S(1)}, f32[3,16,128]{2,1,0:T(8,128)S(1)}, f32[3,16,128]{2,1,0:T(8,128)S(1)}) custom-call(f32[3,16,64,128]{3,2,1,0:T(8,128)S(1)} %get-tuple-element.113.refs_0_.u_in, ...), custom_call_target="tpu_custom_call", output_to_operand_aliasing={{0}: (0, {}), {1}: (1, {})} | custom-call | flops 20000000 | tf_op jit(solution)/shard_map/pallas_call | solution.py:46
  29.2 1.5 %collective-permute-done.15.far_ref = f32[3,32,128]{2,1,0:T(8,128)S(1)} collective-permute-done((f32[3,32,128]{2,1,0:T(8,128)S(1)}, f32[3,32,128]{2,1,0:T(8,128)S(1)}, u32[]{:S(2)}, u32[]{:S(2)}) %collective-permute-start.15) | collective-permute-done | bytes 49184 | tf_op jit(solution)/shard_map/ppermute | solution.py:541
  30.7 2.4 %shard_map.96.refs_15_ = f32[64,128]{1,0:T(8,128)S(1)} custom-call(f32[3,64,128]{2,1,0:T(8,128)S(1)} %get-tuple-element.132.own_ref.refs_4_, f32[3,64,128]{2,1,0:T(8,128)S(1)} %collective-permute-done.12.near_ref.refs_8_, f32[3,32,128]{2,1,0:T(8,128)S(1)} %collective-permute-done.15.far_ref, f32[96,128]{1,0:T(8,128)S(1)} %get-tuple-element.122.pick_ref, ...), custom_call_target="tpu_custom_call" | custom-call | flops 20000000 | tf_op jit(solution)/shard_map/pallas_call | solution.py:46
  33.2 0.2 shard_map.97
  33.3 0.3 collective-permute-start.16
  33.6 1.6 %collective-permute-start.17 = (f32[3,32,128]{2,1,0:T(8,128)S(1)}, f32[3,32,128]{2,1,0:T(8,128)S(1)}, u32[]{:S(2)}, u32[]{:S(2)}) collective-permute-start(f32[3,32,128]{2,1,0:T(8,128)S(1)} %get-tuple-element.143), channel_id=1, source_target_pairs={{0,1},{1,0},{2,3},{3,2},{4,5},{5,4},{6,7},{7,6},{8,9},{9,8},{10,11... | collective-permute-start | bytes 147464 | tf_op jit(solution)/shard_map/ppermute | solution.py:541
  35.3 1.6 %collective-permute-start.20 = (f32[3,16,128]{2,1,0:T(8,128)S(1)}, f32[3,16,128]{2,1,0:T(8,128)S(1)}, u32[]{:S(2)}, u32[]{:S(2)}) collective-permute-start(f32[3,16,128]{2,1,0:T(8,128)S(1)} %get-tuple-element.148.refs_7_), channel_id=1, source_target_pairs={{0,3},{1,2},{2,1},{3,0},{4,7},{5,6},{6,5},{7,4},{8,11},{9,10},{10,... | collective-permute-start | bytes 73736 | tf_op jit(solution)/shard_map/ppermute | solution.py:541
  36.8 2.5 %shard_map.98 = (f32[3,16,64,128]{3,2,1,0:T(8,128)S(1)}, f32[3,16,64,128]{3,2,1,0:T(8,128)S(1)}, f32[3,16,128]{2,1,0:T(8,128)}, f32[3,16,128]{2,1,0:T(8,128)}) custom-call(f32[3,16,64,128]{3,2,1,0:T(8,128)S(1)} %get-tuple-element.127.refs_0_.u_in, f32[3,16,64,128]{3,2,1,0:T(8,128)S(1)} %get-tuple-element.128.w_in, ...), custom_call_target="tpu_custom_call", output_to_operand_aliasing={{0}: (0, {}), {1}: (1, {})} | custom-call | flops 20000000 | tf_op jit(solution)/shard_map/pallas_call | solution.py:46
  39.3 2.5 %shard_map.99 = (f32[3,16,64,128]{3,2,1,0:T(8,128)}, f32[3,16,64,128]{3,2,1,0:T(8,128)}, f32[64,128]{1,0:T(8,128)S(1)}) custom-call(f32[3,64,128]{2,1,0:T(8,128)S(1)} %get-tuple-element.142.own_ref.refs_5_, f32[3,64,128]{2,1,0:T(8,128)S(1)} %collective-permute-done.16.near_ref.refs_9_, f32[3,32,128]{2,1,0:T(8,128)S(1)} %collective-permute-done.17.far_ref, ...), custom_call_target="tpu_custom_call" | custom-call | flops 20000000 | tf_op jit(solution)/shard_map/pallas_call | solution.py:46
  41.8 1.1 %shard_map.100 = (f32[3,16,64,128]{3,2,1,0:T(8,128)}, f32[3,16,64,128]{3,2,1,0:T(8,128)}) custom-call(f32[3,16,64,128]{3,2,1,0:T(8,128)S(1)} %get-tuple-element.140.u_ref.refs_0_, f32[3,16,64,128]{3,2,1,0:T(8,128)S(1)} %get-tuple-element.141.w_ref.refs_1_, ...), custom_call_target="tpu_custom_call", output_to_operand_aliasing={{0}: (2, {}), {1}: (3, {})} | custom-call | tf_op jit(solution)/shard_map/pallas_call | solution.py:46
  (37 shorter events, 0.2 us)
Async XLA Ops:
  0.6 5.8 %copy-start.1 = (s32[1,16,64,128]{3,2,1,0:T(8,128)S(1)}, s32[1,16,64,128]{3,2,1,0:T(8,128)}, u32[]{:S(2)}) copy-start(s32[1,16,64,128]{3,2,1,0:T(8,128)} %param.9) | copy-start | bytes 1572868
  0.6 5.8 %copy-start.2 = (f32[8]{0:T(128)S(1)}, f32[8]{0:T(128)}, u32[]{:S(2)}) copy-start(f32[8]{0:T(128)} %moduli_ref.3) | copy-start | bytes 100
  0.7 5.8 %copy-start.4 = (s32[256]{0:T(256)S(1)}, s32[256]{0:T(256)}, u32[]{:S(2)}) copy-start(s32[256]{0:T(256)} %active_ref.1) | copy-start | bytes 3076
  0.7 5.7 %copy-start.3 = (s32[256]{0:T(256)S(1)}, s32[256]{0:T(256)}, u32[]{:S(2)}) copy-start(s32[256]{0:T(256)} %partner_ref.1) | copy-start | bytes 3076
  0.7 5.7 %copy-start.5 = (f32[8]{0:T(128)S(1)}, f32[8]{0:T(128)}, u32[]{:S(2)}) copy-start(f32[8]{0:T(128)} %density_ref.1) | copy-start | bytes 100
  2.1 7.3 %copy-start = (f32[1,3,16,64,128]{4,3,2,1,0:T(8,128)S(1)}, f32[1,3,16,64,128]{4,3,2,1,0:T(8,128)}, u32[]{:S(2)}) copy-start(f32[1,3,16,64,128]{4,3,2,1,0:T(8,128)} %param.7) | copy-start | bytes 4718596
  2.1 9.4 %collective-permute-start.1 = (f32[4,64,128]{2,1,0:T(8,128)S(1)}, f32[4,64,128]{2,1,0:T(8,128)S(1)}, u32[]{:S(2)}, u32[]{:S(2)}) collective-permute-start(f32[4,64,128]{2,1,0:T(8,128)S(1)} %get-tuple-element.85.sb_ref.own_ref.refs_6_), channel_id=1, source_target_pairs={{0,1},{1,0},{2,3},{3,2},{4,8},{5,9},{6,10},{7,11},{8,4},{9,5},{10,... | collective-permute-start | bytes 393224 | tf_op jit(solution)/shard_map/ppermute | solution.py:541
  3.4 11.1 %collective-permute-start = (f32[4,64,128]{2,1,0:T(8,128)S(1)}, f32[4,64,128]{2,1,0:T(8,128)S(1)}, u32[]{:S(2)}, u32[]{:S(2)}) collective-permute-start(f32[4,64,128]{2,1,0:T(8,128)S(1)} %get-tuple-element.84.sa_ref.refs_5_), channel_id=1, source_target_pairs={{0,4},{1,5},{2,6},{3,7},{4,0},{5,1},{6,2},{7,3},{8,12},{9,13},{10,... | collective-permute-start | bytes 393224 | tf_op jit(solution)/shard_map/ppermute | solution.py:541
  3.4 8.1 %collective-permute-start.5 = (f32[3,64,128]{2,1,0:T(8,128)S(1)}, f32[3,64,128]{2,1,0:T(8,128)S(1)}, u32[]{:S(2)}, u32[]{:S(2)}) collective-permute-start(f32[3,64,128]{2,1,0:T(8,128)S(1)} %get-tuple-element.105), channel_id=1, source_target_pairs={{0,1},{1,0},{2,3},{3,2},{4,5},{5,4},{6,7},{7,6},{8,9},{9,8},{10,11... | collective-permute-start | bytes 294920 | tf_op jit(solution)/shard_map/ppermute | solution.py:541
  5.8 8.7 %collective-permute-start.2 = (f32[4,16,128]{2,1,0:T(8,128)S(1)}, f32[4,16,128]{2,1,0:T(8,128)S(1)}, u32[]{:S(2)}, u32[]{:S(2)}) collective-permute-start(f32[4,16,128]{2,1,0:T(8,128)S(1)} %get-tuple-element.86.sc_ref.refs_7_), channel_id=1, source_target_pairs={{0,1},{1,0},{2,3},{3,2},{4,5},{5,4},{6,7},{7,6},{8,9},{9,8},{10,11... | collective-permute-start | bytes 98312 | tf_op jit(solution)/shard_map/ppermute | solution.py:541
  5.8 8.7 %collective-permute-start.3 = (f32[4,16,128]{2,1,0:T(8,128)S(1)}, f32[4,16,128]{2,1,0:T(8,128)S(1)}, u32[]{:S(2)}, u32[]{:S(2)}) collective-permute-start(f32[4,16,128]{2,1,0:T(8,128)S(1)} %get-tuple-element.87.sd_ref.refs_8_), channel_id=1, source_target_pairs={{0,3},{1,2},{2,1},{3,0},{4,7},{5,6},{6,5},{7,4},{8,11},{9,10},{10,... | collective-permute-start | bytes 98312 | tf_op jit(solution)/shard_map/ppermute | solution.py:541
  11.4 3.0 %collective-permute-start.4 = (f32[1,128]{1,0:T(1,128)S(1)}, f32[1,128]{1,0:T(1,128)S(1)}, u32[]{:S(2)}, u32[]{:S(2)}) collective-permute-start(f32[1,128]{1,0:T(1,128)S(1)} %get-tuple-element.91), channel_id=1, source_target_pairs={{0,5},{1,6},{2,7},{3,4},{4,9},{5,10},{6,11},{7,8},{8,13},{9,14},{1... | collective-permute-start | bytes 1544 | tf_op jit(solution)/shard_map/ppermute | solution.py:541
  15.4 7.0 %collective-permute-start.7 = (f32[3,64,128]{2,1,0:T(8,128)S(1)}, f32[3,64,128]{2,1,0:T(8,128)S(1)}, u32[]{:S(2)}, u32[]{:S(2)}) collective-permute-start(f32[3,64,128]{2,1,0:T(8,128)S(1)} %get-tuple-element.118.own_ref.refs_4_), channel_id=1, source_target_pairs={{0,1},{1,0},{2,3},{3,2},{4,8},{5,9},{6,10},{7,11},{8,4},{9,5},{10,... | collective-permute-start | bytes 294920 | tf_op jit(solution)/shard_map/ppermute | solution.py:541
  16.3 8.5 %collective-permute-start.6 = (f32[3,64,128]{2,1,0:T(8,128)S(1)}, f32[3,64,128]{2,1,0:T(8,128)S(1)}, u32[]{:S(2)}, u32[]{:S(2)}) collective-permute-start(f32[3,64,128]{2,1,0:T(8,128)S(1)} %get-tuple-element.117.refs_3_), channel_id=1, source_target_pairs={{0,4},{1,5},{2,6},{3,7},{4,0},{5,1},{6,2},{7,3},{8,12},{9,13},{10,... | collective-permute-start | bytes 294920 | tf_op jit(solution)/shard_map/ppermute | solution.py:541
  16.3 6.0 %collective-permute-start.10 = (f32[3,32,128]{2,1,0:T(8,128)S(1)}, f32[3,32,128]{2,1,0:T(8,128)S(1)}, u32[]{:S(2)}, u32[]{:S(2)}) collective-permute-start(f32[3,32,128]{2,1,0:T(8,128)S(1)} %get-tuple-element.121), channel_id=1, source_target_pairs={{0,1},{1,0},{2,3},{3,2},{4,5},{5,4},{6,7},{7,6},{8,9},{9,8},{10,11... | collective-permute-start | bytes 147464 | tf_op jit(solution)/shard_map/ppermute | solution.py:541
  18.9 5.9 %collective-permute-start.8 = (f32[3,16,128]{2,1,0:T(8,128)S(1)}, f32[3,16,128]{2,1,0:T(8,128)S(1)}, u32[]{:S(2)}, u32[]{:S(2)}) collective-permute-start(f32[3,16,128]{2,1,0:T(8,128)S(1)} %get-tuple-element.119.refs_5_), channel_id=1, source_target_pairs={{0,1},{1,0},{2,3},{3,2},{4,5},{5,4},{6,7},{7,6},{8,9},{9,8},{10,11... | collective-permute-start | bytes 73736 | tf_op jit(solution)/shard_map/ppermute | solution.py:541
  18.9 5.9 %collective-permute-start.9 = (f32[3,16,128]{2,1,0:T(8,128)S(1)}, f32[3,16,128]{2,1,0:T(8,128)S(1)}, u32[]{:S(2)}, u32[]{:S(2)}) collective-permute-start(f32[3,16,128]{2,1,0:T(8,128)S(1)} %get-tuple-element.120.refs_6_), channel_id=1, source_target_pairs={{0,3},{1,2},{2,1},{3,0},{4,7},{5,6},{6,5},{7,4},{8,11},{9,10},{10,... | collective-permute-start | bytes 73736 | tf_op jit(solution)/shard_map/ppermute | solution.py:541
  25.0 5.7 %collective-permute-start.12 = (f32[3,64,128]{2,1,0:T(8,128)S(1)}, f32[3,64,128]{2,1,0:T(8,128)S(1)}, u32[]{:S(2)}, u32[]{:S(2)}) collective-permute-start(f32[3,64,128]{2,1,0:T(8,128)S(1)} %get-tuple-element.132.own_ref.refs_4_), channel_id=1, source_target_pairs={{0,1},{1,0},{2,3},{3,2},{4,8},{5,9},{6,10},{7,11},{8,4},{9,5},{10,... | collective-permute-start | bytes 294920 | tf_op jit(solution)/shard_map/ppermute | solution.py:541
  25.1 8.1 %collective-permute-start.11 = (f32[3,64,128]{2,1,0:T(8,128)S(1)}, f32[3,64,128]{2,1,0:T(8,128)S(1)}, u32[]{:S(2)}, u32[]{:S(2)}) collective-permute-start(f32[3,64,128]{2,1,0:T(8,128)S(1)} %get-tuple-element.131.refs_3_), channel_id=1, source_target_pairs={{0,4},{1,5},{2,6},{3,7},{4,0},{5,1},{6,2},{7,3},{8,12},{9,13},{10,... | collective-permute-start | bytes 294920 | tf_op jit(solution)/shard_map/ppermute | solution.py:541
  25.2 5.6 %collective-permute-start.15 = (f32[3,32,128]{2,1,0:T(8,128)S(1)}, f32[3,32,128]{2,1,0:T(8,128)S(1)}, u32[]{:S(2)}, u32[]{:S(2)}) collective-permute-start(f32[3,32,128]{2,1,0:T(8,128)S(1)} %get-tuple-element.135), channel_id=1, source_target_pairs={{0,1},{1,0},{2,3},{3,2},{4,5},{5,4},{6,7},{7,6},{8,9},{9,8},{10,11... | collective-permute-start | bytes 147464 | tf_op jit(solution)/shard_map/ppermute | solution.py:541
  26.8 6.4 %collective-permute-start.13 = (f32[3,16,128]{2,1,0:T(8,128)S(1)}, f32[3,16,128]{2,1,0:T(8,128)S(1)}, u32[]{:S(2)}, u32[]{:S(2)}) collective-permute-start(f32[3,16,128]{2,1,0:T(8,128)S(1)} %get-tuple-element.133.refs_5_), channel_id=1, source_target_pairs={{0,1},{1,0},{2,3},{3,2},{4,5},{5,4},{6,7},{7,6},{8,9},{9,8},{10,11... | collective-permute-start | bytes 73736 | tf_op jit(solution)/shard_map/ppermute | solution.py:541
  26.9 6.2 %collective-permute-start.14 = (f32[3,16,128]{2,1,0:T(8,128)S(1)}, f32[3,16,128]{2,1,0:T(8,128)S(1)}, u32[]{:S(2)}, u32[]{:S(2)}) collective-permute-start(f32[3,16,128]{2,1,0:T(8,128)S(1)} %get-tuple-element.134.refs_6_), channel_id=1, source_target_pairs={{0,3},{1,2},{2,1},{3,0},{4,7},{5,6},{6,5},{7,4},{8,11},{9,10},{10,... | collective-permute-start | bytes 73736 | tf_op jit(solution)/shard_map/ppermute | solution.py:541
  33.3 6.0 %collective-permute-start.16 = (f32[3,64,128]{2,1,0:T(8,128)S(1)}, f32[3,64,128]{2,1,0:T(8,128)S(1)}, u32[]{:S(2)}, u32[]{:S(2)}) collective-permute-start(f32[3,64,128]{2,1,0:T(8,128)S(1)} %get-tuple-element.142.own_ref.refs_5_), channel_id=1, source_target_pairs={{0,1},{1,0},{2,3},{3,2},{4,8},{5,9},{6,10},{7,11},{8,4},{9,5},{10,... | collective-permute-start | bytes 294920 | tf_op jit(solution)/shard_map/ppermute | solution.py:541
  33.6 8.2 %collective-permute-start.18 = (f32[3,64,128]{2,1,0:T(8,128)S(1)}, f32[3,64,128]{2,1,0:T(8,128)S(1)}, u32[]{:S(2)}, u32[]{:S(2)}) collective-permute-start(f32[3,64,128]{2,1,0:T(8,128)S(1)} %get-tuple-element.146.refs_4_), channel_id=1, source_target_pairs={{0,4},{1,5},{2,6},{3,7},{4,0},{5,1},{6,2},{7,3},{8,12},{9,13},{10,... | collective-permute-start | bytes 294920 | tf_op jit(solution)/shard_map/ppermute | solution.py:541
  33.6 5.7 %collective-permute-start.17 = (f32[3,32,128]{2,1,0:T(8,128)S(1)}, f32[3,32,128]{2,1,0:T(8,128)S(1)}, u32[]{:S(2)}, u32[]{:S(2)}) collective-permute-start(f32[3,32,128]{2,1,0:T(8,128)S(1)} %get-tuple-element.143), channel_id=1, source_target_pairs={{0,1},{1,0},{2,3},{3,2},{4,5},{5,4},{6,7},{7,6},{8,9},{9,8},{10,11... | collective-permute-start | bytes 147464 | tf_op jit(solution)/shard_map/ppermute | solution.py:541
  35.2 6.6 %collective-permute-start.19 = (f32[3,16,128]{2,1,0:T(8,128)S(1)}, f32[3,16,128]{2,1,0:T(8,128)S(1)}, u32[]{:S(2)}, u32[]{:S(2)}) collective-permute-start(f32[3,16,128]{2,1,0:T(8,128)S(1)} %get-tuple-element.147.refs_6_), channel_id=1, source_target_pairs={{0,1},{1,0},{2,3},{3,2},{4,5},{5,4},{6,7},{7,6},{8,9},{9,8},{10,11... | collective-permute-start | bytes 73736 | tf_op jit(solution)/shard_map/ppermute | solution.py:541
  35.3 6.5 %collective-permute-start.20 = (f32[3,16,128]{2,1,0:T(8,128)S(1)}, f32[3,16,128]{2,1,0:T(8,128)S(1)}, u32[]{:S(2)}, u32[]{:S(2)}) collective-permute-start(f32[3,16,128]{2,1,0:T(8,128)S(1)} %get-tuple-element.148.refs_7_), channel_id=1, source_target_pairs={{0,3},{1,2},{2,1},{3,0},{4,7},{5,6},{6,5},{7,4},{8,11},{9,10},{10,... | collective-permute-start | bytes 73736 | tf_op jit(solution)/shard_map/ppermute | solution.py:541

commit v5 on v4

--- a/solution.py
+++ b/solution.py
@@ -130,30 +130,33 @@
 
         lax.fori_loop(0, partner_ref.shape[0], invert, 0, unroll=8)
 
-        def arrive(q, slot):
-            q = other + q
-            r = jnp.where(body == 0, inverse_ref[q], partner_ref[q]) - start
-            here = (r >= 0) & (r < rows)
-            slot_ref[jnp.where(here, r, rows)] = rows + slot
-            return slot + here.astype(jnp.int32)
-
-        lax.fori_loop(0, rows, arrive, jnp.int32(0), unroll=4)
+        def arrive(q, slots):
+            new = []
+            for n, (first, slot) in enumerate(zip((start, other), slots)):
+                r = jnp.where(body == 0, inverse_ref[first + q], partner_ref[first + q]) - start
+                here = (r >= 0) & (r < rows)
+                slot_ref[jnp.where(here, r, rows)] = slot
+                new.append(slot + here.astype(jnp.int32))
+            return tuple(new)
+
+        lax.fori_loop(0, rows, arrive, (jnp.int32(0), jnp.int32(rows // 2)), unroll=4)
         lane = lax.broadcasted_iota(jnp.int32, (1, turned_ref.shape[2]), 1)
 
-        def leave(r, count):
+        def leave(r, counts):
             q = jnp.where(body == 0, partner_ref[start + r], inverse_ref[start + r])
             beside = (q >= start) & (q < start + rows)
             whole = jnp.where(beside, q - start, rows + q - other)
-            half = jnp.where(beside, q - start, slot_ref[r])
+            half = slot_ref[r]
             for n in range(turned_ref.shape[1] // rows):
                 turned_ref[0, pl.ds(n * rows + r, 1)] = jnp.where(lane == whole, 1.0, 0.0)
                 turned_ref[1, pl.ds(n * rows + r, 1)] = jnp.where(lane == half, 1.0, 0.0)
             live = active_ref[jnp.where(body == 0, start + r, q)].astype(jnp.float32)
             push_ref[pl.ds(r, 1)] = jnp.where(lane[:, :cols] >= 0, live * (-PRESSURE_SCALE), 0.0)
-            chosen_ref[jnp.where(beside, rows, count)] = r
-            return count + 1 - beside.astype(jnp.int32)
-
-        lax.fori_loop(0, rows, leave, jnp.int32(0), unroll=4)
+            near, far = counts
+            chosen_ref[jnp.where(beside, near, far)] = r
+            return near + beside.astype(jnp.int32), far + 1 - beside.astype(jnp.int32)
+
+        lax.fori_loop(0, rows, leave, (jnp.int32(0), jnp.int32(rows // 2)), unroll=4)
         pick_ref[...] = turned_ref[0].T
         half_ref[...] = turned_ref[1].T[: half_ref.shape[0]]
 
@@ -167,7 +170,7 @@
             chosen_ref[r] = 0
             return 0
 
-        lax.fori_loop(0, rows + 1, any_row, 0, unroll=8)
+        lax.fori_loop(0, chosen_ref.shape[0], any_row, 0, unroll=8)
 
     def plane(i, earlier):
         kinds = kinds_ref[i]
@@ -421,7 +424,8 @@
 def link_moves(scale, extra, sent, got, edges, push_ref, c):
     moves = []
     for n in range(4):
-        stretch = got[n][c] - sent[n][c]
+        arrived = jnp.concatenate([half[c] for half in got[n]], axis=0) if isinstance(got[n], tuple) else got[n][c]
+        stretch = arrived - sent[n][c]
         if scale != 1.0:
             stretch = stretch * scale
         moves.append(edges[n][...] * jnp.tanh(stretch))
@@ -436,11 +440,19 @@
     return moves
 
 
-def boundary_kernel(scale, n_extra, *refs):
+def arrivals(refs, n_got):
+    sent, got, edges, refs = refs[:4], refs[4 : 4 + n_got], refs[4 + n_got : 8 + n_got], refs[8 + n_got :]
+    if n_got == 5:
+        got = [got[0], tuple(got[1:3]), *got[3:]]
+    return sent, got, edges, refs
+
+
+def boundary_kernel(scale, n_extra, n_got, *refs):
     extra, refs = refs[:n_extra], refs[n_extra:]
     u_ref, yc_ref, yd_ref, *refs = refs
-    sent, got, edges, refs = refs[:4], refs[4:8], refs[8:12], refs[12:]
-    push_ref, chosen_ref, na_ref, nb_ref, nc_ref, nd_ref, ne_ref, xl_ref, xh_ref, yl_ref, yh_ref = refs
+    sent, got, edges, refs = arrivals(refs, n_got)
+    push_ref, chosen_ref, na_ref, nb_ref, nc_ref, nd_ref, *refs = refs
+    half_ref, rest_ref, xl_ref, xh_ref, yl_ref, yh_ref = refs
     _, planes, rows, cols = u_ref.shape
     even_x, even_y = lax.axis_index("gx") % 2 == 0, lax.axis_index("yz") % 2 == 0
     for c in range(3):
@@ -455,15 +467,26 @@
         d_low, d_high = (jnp.where(even_y, x, y) for x, y in zip(first, last))
         nc_ref[c] = with_sides(yc_ref[c] + jnp.where(even_y, yh, yl), c_low, c_high)
         nd_ref[c] = with_sides(yd_ref[c] + jnp.where(even_y, yl, yh), d_low, d_high)
-    for r in range(ne_ref.shape[1]):
-        at = chosen_ref[r]
+    half = rows // 2
+    is_face = lax.axis_index("gx") == lax.axis_size("gx") - 1
+
+    @pl.when(is_face)
+    def _():
+        for n, ref in enumerate((half_ref, rest_ref)):
+            for r in range(half):
+                at = chosen_ref[n * half + r]
+                for c in range(3):
+                    ref[c, r : r + 1] = nb_ref[c, pl.ds(at, 1)]
+
+    @pl.when(jnp.logical_not(is_face))
+    def _():
         for c in range(3):
-            ne_ref[c, r : r + 1] = nb_ref[c, pl.ds(at, 1)]
+            half_ref[c], rest_ref[c] = nb_ref[c, :half], nb_ref[c, half:]
 
 
 def finish_kernel(*refs):
     u_ref, w_ref, _, _, *refs = refs
-    sent, got, edges, refs = refs[:4], refs[4:8], refs[8:12], refs[12:]
+    sent, got, edges, refs = arrivals(refs, 5)
     push_ref, d_ref, v_ref, planes_ref, rows_ref, sems = refs
     _, planes, rows, cols = u_ref.shape
     tile = rows_ref.shape[4]
@@ -520,6 +543,7 @@
     return {
         "a": pairs(lambda b, g, y: (b, g ^ 1, y)),
         "b": pairs(outer_x),
+        "rest": pairs(lambda b, g, y: diagonal(b, g, y) if g == count_x - 1 else outer_x(b, g, y)),
         "c": pairs(lambda b, g, y: (b, g, y ^ 1)),
         "d": pairs(lambda b, g, y: (b, g, (y + 1 if y % 2 else y - 1) % count_y)),
         "e": pairs(diagonal),
@@ -557,7 +581,7 @@
     kx, ky, kz, kick, row_kick, high_ky, push_scale, pick, pick_half, chosen, v = call(
         setup_kernel,
         [vmem(block)] * 4 + [vmem((2, *side)), vmem(side), vmem(face)]
-        + [vmem((lanes, lanes)), vmem((rows + rows // 2, lanes)), pltpu.SMEM((rows + 1,), jnp.int32)]
+        + [vmem((lanes, lanes)), vmem((rows, lanes)), pltpu.SMEM((rows + rows // 2,), jnp.int32)]
         + [vmem(state)],
         [kinds, v, moduli, density, partner, active],
         [None, hbm] + [smem] * 4,
@@ -574,17 +598,17 @@
         first, last = step == 0, step == STEPS - 1
         scale = U_SCALE if first else 1.0
         if first:
+            corner, kick = lax.optimization_barrier((corner, kick))
+            corner = passed(corner, "corner")
             u, w, yc, yd = call(
                 first_kernel,
                 [vmem(state)] * 2 + [vmem(side3)] * 2,
                 [d, v, kx, ky, kz, kick],
-                flops=20_000_000,
-            )
-            corner, push_scale, yc = lax.optimization_barrier((corner, push_scale, yc))
-            corner = passed(corner, "corner")
+            )
+            push_scale, yc = lax.optimization_barrier((push_scale, yc))
         else:
-            got_e = passed(spare, "e")
-            got = [passed(block, name) for block, name in zip(sent, "abcd")]
+            got_e, got_half = passed(rest, "rest"), passed(half, "b")
+            got = [passed(sent[0], "a"), got_half, got_e, passed(sent[2], "c"), passed(sent[3], "d")]
             u, w, yc, yd = call(
                 functools.partial(interior_kernel, *((1.0 / U_SCALE, 1.0 / W_SCALE) if last else (1.0, 1.0))),
                 [vmem(state)] * 2 + [vmem(side3)] * 2,
@@ -617,19 +641,19 @@
                 aliases={12: 0, 13: 1, 14: 2},
             )
             edges, extra = rest[:4], rest[4:]
-        *sent, spare, xl, xh, yl, yh = call(
-            functools.partial(boundary_kernel, scale, len(extra)),
-            [vmem(face3)] * 2 + [vmem(side3)] * 2 + [vmem((3, rows // 2, cols))]
+        *sent, half, rest, xl, xh, yl, yh = call(
+            functools.partial(boundary_kernel, scale, len(extra), len(got)),
+            [vmem(face3)] * 2 + [vmem(side3)] * 2 + [vmem((3, rows // 2, cols))] * 2
             + [vmem(face3)] * 2 + [vmem(side3)] * 2,
             [*extra, u, yc, yd, *sent, *got, *edges, push, chosen],
-            [None] * (16 + len(extra)) + [smem],
+            [None] * (12 + len(got) + len(extra)) + [smem],
         )
         moves = [xl, xh, yl, yh]
     d, v = call(
         finish_kernel,
         [jax.ShapeDtypeStruct(state, jnp.float32)] * 2,
         [u, w, d, v, *sent, *got, *edges, push],
-        [None, None, hbm, hbm] + [None] * 13,
+        [None, None, hbm, hbm] + [None] * 14,
         aliases={2: 0, 3: 1},
         scratch=[vmem((2, 2, *face3)), vmem((2, 2, 3, planes - 2, tile, cols)), pltpu.SemaphoreType.DMA((8,))],
         hbm_outs=2,

time: 43.1 us -> 41.9 us (0.972)
  the two profiles are of different devices: /device:TPU:25 before, /device:TPU:8 now
where the time goes in v5:
time: 41.9 us; the launch traced here: 41.4 us
  starting transfers between devices  23.2 us (55%)
  Pallas kernels  15.4 us (37%)
  waiting for transfers between devices  1.88 us (4%)
  between operations  0.92 us (2%)
    ppermute x21, starting transfers between devices, passed(): return lax.ppermute(block, AXES, route[name])  23.2 us
    pallas_call x15, Pallas kernels, call(): pl.pallas_call(kernel, out_shape=outs, in_specs=specs, out_specs=[pl.Bloc...  15.4 us
    ppermute x21, waiting for transfers between devices, passed(): return lax.ppermute(block, AXES, route[name])  1.88 us
  transfers between devices with their start and end apart: 21, of which 3 were waited for; matrix products, arithmetic and copies ran while one was open for 0% of the time, Pallas kernels for 29%

profile of v5, /device:TPU:8, one launch (start us, length us, event | category | flops | bytes accessed | tf_op | source)
XLA Modules:
  0.0 41.4 jit_solution(1857473968311464329)
XLA Ops:
  0.7 1.4 %shard_map.87 = (f32[4,64,128]{2,1,0:T(8,128)S(1)}, f32[4,64,128]{2,1,0:T(8,128)S(1)}, f32[4,16,128]{2,1,0:T(8,128)S(1)}, f32[4,16,128]{2,1,0:T(8,128)S(1)}, f32...) custom-call(f32[3,16,64,128]{3,2,1,0:T(8,128)} %bitcast.5, s32[16,64,128]{2,1,0:T(8,128)} %bitcast.7), custom_call_target="tpu_custom_call" | custom-call | tf_op jit(solution)/shard_map/pallas_call | solution.py:46
  2.1 1.6 %collective-permute-start.1 = (f32[4,64,128]{2,1,0:T(8,128)S(1)}, f32[4,64,128]{2,1,0:T(8,128)S(1)}, u32[]{:S(2)}, u32[]{:S(2)}) collective-permute-start(f32[4,64,128]{2,1,0:T(8,128)S(1)} %get-tuple-element.91.sb_ref.own_ref.refs_6_), channel_id=1, source_target_pairs={{0,1},{1,0},{2,3},{3,2},{4,8},{5,9},{6,10},{7,11},{8,4},{9,5},{10,... | collective-permute-start | bytes 393224 | tf_op jit(solution)/shard_map/ppermute | solution.py:565
  3.7 0.5 %collective-permute-start.2 = (f32[4,16,128]{2,1,0:T(8,128)S(1)}, f32[4,16,128]{2,1,0:T(8,128)S(1)}, u32[]{:S(2)}, u32[]{:S(2)}) collective-permute-start(f32[4,16,128]{2,1,0:T(8,128)S(1)} %get-tuple-element.92.sc_ref.refs_7_), channel_id=1, source_target_pairs={{0,1},{1,0},{2,3},{3,2},{4,5},{5,4},{6,7},{7,6},{8,9},{9,8},{10,11... | collective-permute-start | bytes 98312 | tf_op jit(solution)/shard_map/ppermute | solution.py:565
  4.2 1.1 %collective-permute-start.3 = (f32[4,16,128]{2,1,0:T(8,128)S(1)}, f32[4,16,128]{2,1,0:T(8,128)S(1)}, u32[]{:S(2)}, u32[]{:S(2)}) collective-permute-start(f32[4,16,128]{2,1,0:T(8,128)S(1)} %get-tuple-element.93.sd_ref.refs_8_), channel_id=1, source_target_pairs={{0,3},{1,2},{2,1},{3,0},{4,7},{5,6},{6,5},{7,4},{8,11},{9,10},{10,... | collective-permute-start | bytes 98312 | tf_op jit(solution)/shard_map/ppermute | solution.py:565
  5.4 2.0 %shard_map.86 = (f32[16,64,128]{2,1,0:T(8,128)S(1)}, f32[16,64,128]{2,1,0:T(8,128)S(1)}, f32[16,64,128]{2,1,0:T(8,128)S(1)}, f32[16,64,128]{2,1,0:T(8,128)S(1)},...) custom-call(s32[16,64,128]{2,1,0:T(8,128)S(1)} %bitcast.8, ...), custom_call_target="tpu_custom_call" | custom-call | flops 8000000 | tf_op jit(solution)/shard_map/pallas_call | solution.py:46
  7.4 3.2 %collective-permute-start.4 = (f32[1,128]{1,0:T(1,128)S(1)}, f32[1,128]{1,0:T(1,128)S(1)}, u32[]{:S(2)}, u32[]{:S(2)}) collective-permute-start(f32[1,128]{1,0:T(1,128)S(1)} %get-tuple-element.94), channel_id=1, source_target_pairs={{0,5},{1,6},{2,7},{3,4},{4,9},{5,10},{6,11},{7,8},{8,13},{9,14},{1... | collective-permute-start | bytes 1544 | tf_op jit(solution)/shard_map/ppermute | solution.py:565
  10.6 2.0 %shard_map.88 = (f32[3,16,64,128]{3,2,1,0:T(8,128)S(1)}, f32[3,16,64,128]{3,2,1,0:T(8,128)S(1)}, f32[3,16,128]{2,1,0:T(8,128)S(1)}, f32[3,16,128]{2,1,0:T(8,128)S(1)}) custom-call(f32[3,16,64,128]{3,2,1,0:T(8,128)S(1)} %bitcast.6, f32[3,16,64,128]{3,2,1,0:T(8,128)S(1)} %get-tuple-element.81.v_ref, f32[16,64,128]{2,1,0:T(8,128)S(1)} %get-tuple-element.82.kx_ref.kx_in, ...), custom_call_target="tpu_custom_call" | custom-call | tf_op jit(solution)/shard_map/pallas_call | solution.py:46
  12.7 0.7 %shard_map.89 = (f32[16,64,128]{2,1,0:T(8,128)S(1)}, f32[16,64,128]{2,1,0:T(8,128)S(1)}, f32[16,64,128]{2,1,0:T(8,128)S(1)}, f32[64,128]{1,0:T(8,128)S(1)}, f32[...) custom-call(f32[4,64,128]{2,1,0:T(8,128)S(1)} %get-tuple-element.90., ...), custom_call_target="tpu_custom_call", output_to_operand_aliasing={{0}: (12, {}), {1}: (13, {}), {2}: (14, {})} | custom-call | tf_op jit(solution)/shard_map/pallas_call | solution.py:46
  13.5 0.1 shard_map.91
  13.6 2.6 %collective-permute-start.6 = (f32[3,64,128]{2,1,0:T(8,128)S(1)}, f32[3,64,128]{2,1,0:T(8,128)S(1)}, u32[]{:S(2)}, u32[]{:S(2)}) collective-permute-start(f32[3,64,128]{2,1,0:T(8,128)S(1)} %get-tuple-element.122.refs_3_), channel_id=1, source_target_pairs={{0,4},{1,5},{2,6},{3,7},{4,0},{5,1},{6,2},{7,3},{8,12},{9,13},{10,... | collective-permute-start | bytes 294920 | tf_op jit(solution)/shard_map/ppermute | solution.py:565
  16.2 1.9 %collective-permute-start.7 = (f32[3,32,128]{2,1,0:T(8,128)S(1)}, f32[3,32,128]{2,1,0:T(8,128)S(1)}, u32[]{:S(2)}, u32[]{:S(2)}) collective-permute-start(f32[3,32,128]{2,1,0:T(8,128)S(1)} %get-tuple-element.126), channel_id=1, source_target_pairs={{0,1},{1,0},{2,3},{3,2},{4,8},{5,9},{6,10},{7,11},{8,4},{9,5},{10,... | collective-permute-start | bytes 147464 | tf_op jit(solution)/shard_map/ppermute | solution.py:565
  18.1 0.2 collective-permute-start.8
  18.3 0.2 collective-permute-start.9
  18.5 1.2 %collective-permute-start.10 = (f32[3,16,128]{2,1,0:T(8,128)S(1)}, f32[3,16,128]{2,1,0:T(8,128)S(1)}, u32[]{:S(2)}, u32[]{:S(2)}) collective-permute-start(f32[3,16,128]{2,1,0:T(8,128)S(1)} %get-tuple-element.125.refs_6_), channel_id=1, source_target_pairs={{0,3},{1,2},{2,1},{3,0},{4,7},{5,6},{6,5},{7,4},{8,11},{9,10},{10,... | collective-permute-start | bytes 73736 | tf_op jit(solution)/shard_map/ppermute | solution.py:565
  19.7 1.8 %shard_map.92 = (f32[3,16,64,128]{3,2,1,0:T(8,128)S(1)}, f32[3,16,64,128]{3,2,1,0:T(8,128)S(1)}, f32[3,16,128]{2,1,0:T(8,128)S(1)}, f32[3,16,128]{2,1,0:T(8,128)S(1)}) custom-call(f32[3,16,64,128]{3,2,1,0:T(8,128)S(1)} %get-tuple-element.88.refs_2_.u_in, ...), custom_call_target="tpu_custom_call", output_to_operand_aliasing={{0}: (0, {}), {1}: (1, {})} | custom-call | flops 20000000 | tf_op jit(solution)/shard_map/pallas_call | solution.py:46
  21.5 0.7 %collective-permute-done.8.far_ref.refs_9_ = f32[3,32,128]{2,1,0:T(8,128)S(1)} collective-permute-done((f32[3,32,128]{2,1,0:T(8,128)S(1)}, f32[3,32,128]{2,1,0:T(8,128)S(1)}, u32[]{:S(2)}, u32[]{:S(2)}) %collective-permute-start.8) | collective-permute-done | bytes 49184 | tf_op jit(solution)/shard_map/ppermute | solution.py:565
  22.2 0.1 shard_map.94
  22.3 0.1 collective-permute-start.11
  22.4 3.6 %collective-permute-start.12 = (f32[3,32,128]{2,1,0:T(8,128)S(1)}, f32[3,32,128]{2,1,0:T(8,128)S(1)}, u32[]{:S(2)}, u32[]{:S(2)}) collective-permute-start(f32[3,32,128]{2,1,0:T(8,128)S(1)} %get-tuple-element.141), channel_id=1, source_target_pairs={{0,1},{1,0},{2,3},{3,2},{4,8},{5,9},{6,10},{7,11},{8,4},{9,5},{10,... | collective-permute-start | bytes 147464 | tf_op jit(solution)/shard_map/ppermute | solution.py:565
  26.0 0.0 collective-permute-start.13
  26.0 0.5 %collective-permute-start.14 = (f32[3,16,128]{2,1,0:T(8,128)S(1)}, f32[3,16,128]{2,1,0:T(8,128)S(1)}, u32[]{:S(2)}, u32[]{:S(2)}) collective-permute-start(f32[3,16,128]{2,1,0:T(8,128)S(1)} %get-tuple-element.139.refs_5_), channel_id=1, source_target_pairs={{0,1},{1,0},{2,3},{3,2},{4,5},{5,4},{6,7},{7,6},{8,9},{9,8},{10,11... | collective-permute-start | bytes 73736 | tf_op jit(solution)/shard_map/ppermute | solution.py:565
  26.5 1.1 %collective-permute-start.15 = (f32[3,16,128]{2,1,0:T(8,128)S(1)}, f32[3,16,128]{2,1,0:T(8,128)S(1)}, u32[]{:S(2)}, u32[]{:S(2)}) collective-permute-start(f32[3,16,128]{2,1,0:T(8,128)S(1)} %get-tuple-element.140.refs_6_), channel_id=1, source_target_pairs={{0,3},{1,2},{2,1},{3,0},{4,7},{5,6},{6,5},{7,4},{8,11},{9,10},{10,... | collective-permute-start | bytes 73736 | tf_op jit(solution)/shard_map/ppermute | solution.py:565
  27.6 1.8 %shard_map.95 = (f32[3,16,64,128]{3,2,1,0:T(8,128)S(1)}, f32[3,16,64,128]{3,2,1,0:T(8,128)S(1)}, f32[3,16,128]{2,1,0:T(8,128)S(1)}, f32[3,16,128]{2,1,0:T(8,128)S(1)}) custom-call(f32[3,16,64,128]{3,2,1,0:T(8,128)S(1)} %get-tuple-element.118.refs_0_.u_in, ...), custom_call_target="tpu_custom_call", output_to_operand_aliasing={{0}: (0, {}), {1}: (1, {})} | custom-call | flops 20000000 | tf_op jit(solution)/shard_map/pallas_call | solution.py:46
  29.5 0.7 %collective-permute-done.13.far_ref.refs_9_ = f32[3,32,128]{2,1,0:T(8,128)S(1)} collective-permute-done((f32[3,32,128]{2,1,0:T(8,128)S(1)}, f32[3,32,128]{2,1,0:T(8,128)S(1)}, u32[]{:S(2)}, u32[]{:S(2)}) %collective-permute-start.13) | collective-permute-done | bytes 49184 | tf_op jit(solution)/shard_map/ppermute | solution.py:565
  30.1 0.1 shard_map.97
  30.3 0.1 collective-permute-start.18
  30.3 4.1 %collective-permute-start.16 = (f32[3,32,128]{2,1,0:T(8,128)S(1)}, f32[3,32,128]{2,1,0:T(8,128)S(1)}, u32[]{:S(2)}, u32[]{:S(2)}) collective-permute-start(f32[3,32,128]{2,1,0:T(8,128)S(1)} %get-tuple-element.150), channel_id=1, source_target_pairs={{0,1},{1,0},{2,3},{3,2},{4,8},{5,9},{6,10},{7,11},{8,4},{9,5},{10,... | collective-permute-start | bytes 147464 | tf_op jit(solution)/shard_map/ppermute | solution.py:565
  34.5 1.0 %collective-permute-start.20 = (f32[3,16,128]{2,1,0:T(8,128)S(1)}, f32[3,16,128]{2,1,0:T(8,128)S(1)}, u32[]{:S(2)}, u32[]{:S(2)}) collective-permute-start(f32[3,16,128]{2,1,0:T(8,128)S(1)} %get-tuple-element.156.refs_7_), channel_id=1, source_target_pairs={{0,3},{1,2},{2,1},{3,0},{4,7},{5,6},{6,5},{7,4},{8,11},{9,10},{10,... | collective-permute-start | bytes 73736 | tf_op jit(solution)/shard_map/ppermute | solution.py:565
  35.5 2.5 %shard_map.98 = (f32[3,16,64,128]{3,2,1,0:T(8,128)S(1)}, f32[3,16,64,128]{3,2,1,0:T(8,128)S(1)}, f32[3,16,128]{2,1,0:T(8,128)}, f32[3,16,128]{2,1,0:T(8,128)}) custom-call(f32[3,16,64,128]{3,2,1,0:T(8,128)S(1)} %get-tuple-element.133.refs_0_.u_in, f32[3,16,64,128]{3,2,1,0:T(8,128)S(1)} %get-tuple-element.134.w_in, ...), custom_call_target="tpu_custom_call", output_to_operand_aliasing={{0}: (0, {}), {1}: (1, {})} | custom-call | flops 20000000 | tf_op jit(solution)/shard_map/pallas_call | solution.py:46
  38.0 0.5 %collective-permute-done.17.far_ref.refs_10_ = f32[3,32,128]{2,1,0:T(8,128)S(1)} collective-permute-done((f32[3,32,128]{2,1,0:T(8,128)S(1)}, f32[3,32,128]{2,1,0:T(8,128)S(1)}, u32[]{:S(2)}, u32[]{:S(2)}) %collective-permute-start.17) | collective-permute-done | bytes 49184 | tf_op jit(solution)/shard_map/ppermute | solution.py:565
  38.6 1.7 %shard_map.99 = (f32[3,16,64,128]{3,2,1,0:T(8,128)}, f32[3,16,64,128]{3,2,1,0:T(8,128)}, f32[64,128]{1,0:T(8,128)S(1)}) custom-call(f32[3,64,128]{2,1,0:T(8,128)S(1)} %get-tuple-element.149.own_ref.refs_5_, f32[3,32,128]{2,1,0:T(8,128)S(1)} %collective-permute-done.16.near_ref.refs_9_, f32[3,32,128]{2,1,0:T(8,128)S(1)} %collective-permute-done.17.far_ref.refs_10_, ...), custom_call_target="tpu_custom_call" | custom-call | flops 20000000 | tf_op jit(solution)/shard_map/pallas_call | solution.py:46
  40.3 1.1 %shard_map.100 = (f32[3,16,64,128]{3,2,1,0:T(8,128)}, f32[3,16,64,128]{3,2,1,0:T(8,128)}) custom-call(f32[3,16,64,128]{3,2,1,0:T(8,128)S(1)} %get-tuple-element.147.u_ref.refs_0_, f32[3,16,64,128]{3,2,1,0:T(8,128)S(1)} %get-tuple-element.148.w_ref.refs_1_, ...), custom_call_target="tpu_custom_call", output_to_operand_aliasing={{0}: (2, {}), {1}: (3, {})} | custom-call | tf_op jit(solution)/shard_map/pallas_call | solution.py:46
  (37 shorter events, 0.1 us)
Async XLA Ops:
  0.6 4.7 %copy-start.1 = (s32[1,16,64,128]{3,2,1,0:T(8,128)S(1)}, s32[1,16,64,128]{3,2,1,0:T(8,128)}, u32[]{:S(2)}) copy-start(s32[1,16,64,128]{3,2,1,0:T(8,128)} %param.9) | copy-start | bytes 1572868
  0.6 4.7 %copy-start.2 = (f32[8]{0:T(128)S(1)}, f32[8]{0:T(128)}, u32[]{:S(2)}) copy-start(f32[8]{0:T(128)} %moduli_ref.3) | copy-start | bytes 100
  0.7 4.7 %copy-start.4 = (s32[256]{0:T(256)S(1)}, s32[256]{0:T(256)}, u32[]{:S(2)}) copy-start(s32[256]{0:T(256)} %active_ref.1) | copy-start | bytes 3076
  0.7 4.7 %copy-start.3 = (s32[256]{0:T(256)S(1)}, s32[256]{0:T(256)}, u32[]{:S(2)}) copy-start(s32[256]{0:T(256)} %partner_ref.1) | copy-start | bytes 3076
  0.7 4.7 %copy-start.5 = (f32[8]{0:T(128)S(1)}, f32[8]{0:T(128)}, u32[]{:S(2)}) copy-start(f32[8]{0:T(128)} %density_ref.1) | copy-start | bytes 100
  2.1 8.6 %copy-start = (f32[1,3,16,64,128]{4,3,2,1,0:T(8,128)S(1)}, f32[1,3,16,64,128]{4,3,2,1,0:T(8,128)}, u32[]{:S(2)}) copy-start(f32[1,3,16,64,128]{4,3,2,1,0:T(8,128)} %param.7) | copy-start | bytes 4718596
  2.1 10.6 %collective-permute-start.1 = (f32[4,64,128]{2,1,0:T(8,128)S(1)}, f32[4,64,128]{2,1,0:T(8,128)S(1)}, u32[]{:S(2)}, u32[]{:S(2)}) collective-permute-start(f32[4,64,128]{2,1,0:T(8,128)S(1)} %get-tuple-element.91.sb_ref.own_ref.refs_6_), channel_id=1, source_target_pairs={{0,1},{1,0},{2,3},{3,2},{4,8},{5,9},{6,10},{7,11},{8,4},{9,5},{10,... | collective-permute-start | bytes 393224 | tf_op jit(solution)/shard_map/ppermute | solution.py:565
  3.7 9.0 %collective-permute-start = (f32[4,64,128]{2,1,0:T(8,128)S(1)}, f32[4,64,128]{2,1,0:T(8,128)S(1)}, u32[]{:S(2)}, u32[]{:S(2)}) collective-permute-start(f32[4,64,128]{2,1,0:T(8,128)S(1)} %get-tuple-element.90.sa_ref.refs_5_), channel_id=1, source_target_pairs={{0,4},{1,5},{2,6},{3,7},{4,0},{5,1},{6,2},{7,3},{8,12},{9,13},{10,... | collective-permute-start | bytes 393224 | tf_op jit(solution)/shard_map/ppermute | solution.py:565
  3.7 3.7 %collective-permute-start.5 = (f32[3,64,128]{2,1,0:T(8,128)S(1)}, f32[3,64,128]{2,1,0:T(8,128)S(1)}, u32[]{:S(2)}, u32[]{:S(2)}) collective-permute-start(f32[3,64,128]{2,1,0:T(8,128)S(1)} %get-tuple-element.110), channel_id=1, source_target_pairs={{0,1},{1,0},{2,3},{3,2},{4,5},{5,4},{6,7},{7,6},{8,9},{9,8},{10,11... | collective-permute-start | bytes 294920 | tf_op jit(solution)/shard_map/ppermute | solution.py:565
  3.7 9.0 %collective-permute-start.2 = (f32[4,16,128]{2,1,0:T(8,128)S(1)}, f32[4,16,128]{2,1,0:T(8,128)S(1)}, u32[]{:S(2)}, u32[]{:S(2)}) collective-permute-start(f32[4,16,128]{2,1,0:T(8,128)S(1)} %get-tuple-element.92.sc_ref.refs_7_), channel_id=1, source_target_pairs={{0,1},{1,0},{2,3},{3,2},{4,5},{5,4},{6,7},{7,6},{8,9},{9,8},{10,11... | collective-permute-start | bytes 98312 | tf_op jit(solution)/shard_map/ppermute | solution.py:565
  4.2 8.5 %collective-permute-start.3 = (f32[4,16,128]{2,1,0:T(8,128)S(1)}, f32[4,16,128]{2,1,0:T(8,128)S(1)}, u32[]{:S(2)}, u32[]{:S(2)}) collective-permute-start(f32[4,16,128]{2,1,0:T(8,128)S(1)} %get-tuple-element.93.sd_ref.refs_8_), channel_id=1, source_target_pairs={{0,3},{1,2},{2,1},{3,0},{4,7},{5,6},{6,5},{7,4},{8,11},{9,10},{10,... | collective-permute-start | bytes 98312 | tf_op jit(solution)/shard_map/ppermute | solution.py:565
  7.4 5.3 %collective-permute-start.4 = (f32[1,128]{1,0:T(1,128)S(1)}, f32[1,128]{1,0:T(1,128)S(1)}, u32[]{:S(2)}, u32[]{:S(2)}) collective-permute-start(f32[1,128]{1,0:T(1,128)S(1)} %get-tuple-element.94), channel_id=1, source_target_pairs={{0,5},{1,6},{2,7},{3,4},{4,9},{5,10},{6,11},{7,8},{8,13},{9,14},{1... | collective-permute-start | bytes 1544 | tf_op jit(solution)/shard_map/ppermute | solution.py:565
  13.6 8.6 %collective-permute-start.6 = (f32[3,64,128]{2,1,0:T(8,128)S(1)}, f32[3,64,128]{2,1,0:T(8,128)S(1)}, u32[]{:S(2)}, u32[]{:S(2)}) collective-permute-start(f32[3,64,128]{2,1,0:T(8,128)S(1)} %get-tuple-element.122.refs_3_), channel_id=1, source_target_pairs={{0,4},{1,5},{2,6},{3,7},{4,0},{5,1},{6,2},{7,3},{8,12},{9,13},{10,... | collective-permute-start | bytes 294920 | tf_op jit(solution)/shard_map/ppermute | solution.py:565
  16.2 5.3 %collective-permute-start.7 = (f32[3,32,128]{2,1,0:T(8,128)S(1)}, f32[3,32,128]{2,1,0:T(8,128)S(1)}, u32[]{:S(2)}, u32[]{:S(2)}) collective-permute-start(f32[3,32,128]{2,1,0:T(8,128)S(1)} %get-tuple-element.126), channel_id=1, source_target_pairs={{0,1},{1,0},{2,3},{3,2},{4,8},{5,9},{6,10},{7,11},{8,4},{9,5},{10,... | collective-permute-start | bytes 147464 | tf_op jit(solution)/shard_map/ppermute | solution.py:565
  18.1 4.1 %collective-permute-start.8 = (f32[3,32,128]{2,1,0:T(8,128)S(1)}, f32[3,32,128]{2,1,0:T(8,128)S(1)}, u32[]{:S(2)}, u32[]{:S(2)}) collective-permute-start(f32[3,32,128]{2,1,0:T(8,128)S(1)} %get-tuple-element.127), channel_id=1, source_target_pairs={{0,1},{1,0},{2,3},{3,2},{4,8},{5,9},{6,10},{7,11},{8,4},{9,5},{10,... | collective-permute-start | bytes 147464 | tf_op jit(solution)/shard_map/ppermute | solution.py:565
  18.3 3.9 %collective-permute-start.9 = (f32[3,16,128]{2,1,0:T(8,128)S(1)}, f32[3,16,128]{2,1,0:T(8,128)S(1)}, u32[]{:S(2)}, u32[]{:S(2)}) collective-permute-start(f32[3,16,128]{2,1,0:T(8,128)S(1)} %get-tuple-element.124.refs_5_), channel_id=1, source_target_pairs={{0,1},{1,0},{2,3},{3,2},{4,5},{5,4},{6,7},{7,6},{8,9},{9,8},{10,11... | collective-permute-start | bytes 73736 | tf_op jit(solution)/shard_map/ppermute | solution.py:565
  18.5 3.7 %collective-permute-start.10 = (f32[3,16,128]{2,1,0:T(8,128)S(1)}, f32[3,16,128]{2,1,0:T(8,128)S(1)}, u32[]{:S(2)}, u32[]{:S(2)}) collective-permute-start(f32[3,16,128]{2,1,0:T(8,128)S(1)} %get-tuple-element.125.refs_6_), channel_id=1, source_target_pairs={{0,3},{1,2},{2,1},{3,0},{4,7},{5,6},{6,5},{7,4},{8,11},{9,10},{10,... | collective-permute-start | bytes 73736 | tf_op jit(solution)/shard_map/ppermute | solution.py:565
  22.3 7.8 %collective-permute-start.11 = (f32[3,64,128]{2,1,0:T(8,128)S(1)}, f32[3,64,128]{2,1,0:T(8,128)S(1)}, u32[]{:S(2)}, u32[]{:S(2)}) collective-permute-start(f32[3,64,128]{2,1,0:T(8,128)S(1)} %get-tuple-element.137.refs_3_), channel_id=1, source_target_pairs={{0,4},{1,5},{2,6},{3,7},{4,0},{5,1},{6,2},{7,3},{8,12},{9,13},{10,... | collective-permute-start | bytes 294920 | tf_op jit(solution)/shard_map/ppermute | solution.py:565
  22.4 7.0 %collective-permute-start.12 = (f32[3,32,128]{2,1,0:T(8,128)S(1)}, f32[3,32,128]{2,1,0:T(8,128)S(1)}, u32[]{:S(2)}, u32[]{:S(2)}) collective-permute-start(f32[3,32,128]{2,1,0:T(8,128)S(1)} %get-tuple-element.141), channel_id=1, source_target_pairs={{0,1},{1,0},{2,3},{3,2},{4,8},{5,9},{6,10},{7,11},{8,4},{9,5},{10,... | collective-permute-start | bytes 147464 | tf_op jit(solution)/shard_map/ppermute | solution.py:565
  26.0 4.1 %collective-permute-start.13 = (f32[3,32,128]{2,1,0:T(8,128)S(1)}, f32[3,32,128]{2,1,0:T(8,128)S(1)}, u32[]{:S(2)}, u32[]{:S(2)}) collective-permute-start(f32[3,32,128]{2,1,0:T(8,128)S(1)} %get-tuple-element.142), channel_id=1, source_target_pairs={{0,1},{1,0},{2,3},{3,2},{4,8},{5,9},{6,10},{7,11},{8,4},{9,5},{10,... | collective-permute-start | bytes 147464 | tf_op jit(solution)/shard_map/ppermute | solution.py:565
  26.0 4.1 %collective-permute-start.14 = (f32[3,16,128]{2,1,0:T(8,128)S(1)}, f32[3,16,128]{2,1,0:T(8,128)S(1)}, u32[]{:S(2)}, u32[]{:S(2)}) collective-permute-start(f32[3,16,128]{2,1,0:T(8,128)S(1)} %get-tuple-element.139.refs_5_), channel_id=1, source_target_pairs={{0,1},{1,0},{2,3},{3,2},{4,5},{5,4},{6,7},{7,6},{8,9},{9,8},{10,11... | collective-permute-start | bytes 73736 | tf_op jit(solution)/shard_map/ppermute | solution.py:565
  26.5 3.6 %collective-permute-start.15 = (f32[3,16,128]{2,1,0:T(8,128)S(1)}, f32[3,16,128]{2,1,0:T(8,128)S(1)}, u32[]{:S(2)}, u32[]{:S(2)}) collective-permute-start(f32[3,16,128]{2,1,0:T(8,128)S(1)} %get-tuple-element.140.refs_6_), channel_id=1, source_target_pairs={{0,3},{1,2},{2,1},{3,0},{4,7},{5,6},{6,5},{7,4},{8,11},{9,10},{10,... | collective-permute-start | bytes 73736 | tf_op jit(solution)/shard_map/ppermute | solution.py:565
  30.3 10.0 %collective-permute-start.18 = (f32[3,64,128]{2,1,0:T(8,128)S(1)}, f32[3,64,128]{2,1,0:T(8,128)S(1)}, u32[]{:S(2)}, u32[]{:S(2)}) collective-permute-start(f32[3,64,128]{2,1,0:T(8,128)S(1)} %get-tuple-element.154.refs_4_), channel_id=1, source_target_pairs={{0,4},{1,5},{2,6},{3,7},{4,0},{5,1},{6,2},{7,3},{8,12},{9,13},{10,... | collective-permute-start | bytes 294920 | tf_op jit(solution)/shard_map/ppermute | solution.py:565
  30.3 7.7 %collective-permute-start.16 = (f32[3,32,128]{2,1,0:T(8,128)S(1)}, f32[3,32,128]{2,1,0:T(8,128)S(1)}, u32[]{:S(2)}, u32[]{:S(2)}) collective-permute-start(f32[3,32,128]{2,1,0:T(8,128)S(1)} %get-tuple-element.150), channel_id=1, source_target_pairs={{0,1},{1,0},{2,3},{3,2},{4,8},{5,9},{6,10},{7,11},{8,4},{9,5},{10,... | collective-permute-start | bytes 147464 | tf_op jit(solution)/shard_map/ppermute | solution.py:565
  34.5 4.1 %collective-permute-start.17 = (f32[3,32,128]{2,1,0:T(8,128)S(1)}, f32[3,32,128]{2,1,0:T(8,128)S(1)}, u32[]{:S(2)}, u32[]{:S(2)}) collective-permute-start(f32[3,32,128]{2,1,0:T(8,128)S(1)} %get-tuple-element.151), channel_id=1, source_target_pairs={{0,1},{1,0},{2,3},{3,2},{4,8},{5,9},{6,10},{7,11},{8,4},{9,5},{10,... | collective-permute-start | bytes 147464 | tf_op jit(solution)/shard_map/ppermute | solution.py:565
  34.5 5.7 %collective-permute-start.19 = (f32[3,16,128]{2,1,0:T(8,128)S(1)}, f32[3,16,128]{2,1,0:T(8,128)S(1)}, u32[]{:S(2)}, u32[]{:S(2)}) collective-permute-start(f32[3,16,128]{2,1,0:T(8,128)S(1)} %get-tuple-element.155.refs_6_), channel_id=1, source_target_pairs={{0,1},{1,0},{2,3},{3,2},{4,5},{5,4},{6,7},{7,6},{8,9},{9,8},{10,11... | collective-permute-start | bytes 73736 | tf_op jit(solution)/shard_map/ppermute | solution.py:565
  34.5 5.8 %collective-permute-start.20 = (f32[3,16,128]{2,1,0:T(8,128)S(1)}, f32[3,16,128]{2,1,0:T(8,128)S(1)}, u32[]{:S(2)}, u32[]{:S(2)}) collective-permute-start(f32[3,16,128]{2,1,0:T(8,128)S(1)} %get-tuple-element.156.refs_7_), channel_id=1, source_target_pairs={{0,3},{1,2},{2,1},{3,0},{4,7},{5,6},{6,5},{7,4},{8,11},{9,10},{10,... | collective-permute-start | bytes 73736 | tf_op jit(solution)/shard_map/ppermute | solution.py:565

commit v6 on v5

--- a/solution.py
+++ b/solution.py
@@ -103,9 +103,9 @@
 
 
 def setup_kernel(
-    kinds_ref, v_ref, moduli_ref, density_ref, partner_ref, active_ref,
-    kx_ref, ky_ref, kz_ref, kick_ref, row_kick_ref, high_ky_ref, push_ref, pick_ref, half_ref, chosen_ref, held_ref,
-    turned_ref, inverse_ref, slot_ref, sem,
+    kinds_ref, rc_in, v_ref, moduli_ref, density_ref, partner_ref, active_ref,
+    kx_ref, ky_ref, kz_ref, kick_ref, row_kick_ref, high_ky_ref, push_ref, pick_ref, chosen_ref, rc_ref, held_ref,
+    turned_ref, live_ref, sem,
 ):
     planes, rows, cols = kinds_ref.shape
     place = here_in_mesh()
@@ -124,47 +124,32 @@
 
     @pl.when(last_x)
     def _():
-        def invert(b, _):
-            inverse_ref[partner_ref[b]] = b
-            return 0
-
-        lax.fori_loop(0, partner_ref.shape[0], invert, 0, unroll=8)
-
-        def arrive(q, slots):
+        lane = lax.broadcasted_iota(jnp.int32, (1, turned_ref.shape[1]), 1)
+
+        def meet(i, counts):
             new = []
-            for n, (first, slot) in enumerate(zip((start, other), slots)):
-                r = jnp.where(body == 0, inverse_ref[first + q], partner_ref[first + q]) - start
-                here = (r >= 0) & (r < rows)
-                slot_ref[jnp.where(here, r, rows)] = slot
-                new.append(slot + here.astype(jnp.int32))
+            for n, (block, count) in enumerate(zip((start, other), counts)):
+                b = jnp.where(body == 0, start, block) + i
+                p = partner_ref[b]
+                at = p - jnp.where(body == 0, block, start)
+                mine = (at >= 0) & (at < rows)
+                r = jnp.where(body == 0, i, at)
+                row = pl.ds(jnp.where(mine, r, rows), 1)
+                turned_ref[row] = jnp.where(lane == jnp.where(body == 0, at, i) + n * rows, 1.0, 0.0)
+                live_ref[row] = jnp.where(lane[:, :cols] >= 0, active_ref[b].astype(jnp.float32), 0.0)
+                chosen_ref[jnp.where(mine, count, rows)] = r
+                new.append(count + mine.astype(jnp.int32))
             return tuple(new)
 
-        lax.fori_loop(0, rows, arrive, (jnp.int32(0), jnp.int32(rows // 2)), unroll=4)
-        lane = lax.broadcasted_iota(jnp.int32, (1, turned_ref.shape[2]), 1)
-
-        def leave(r, counts):
-            q = jnp.where(body == 0, partner_ref[start + r], inverse_ref[start + r])
-            beside = (q >= start) & (q < start + rows)
-            whole = jnp.where(beside, q - start, rows + q - other)
-            half = slot_ref[r]
-            for n in range(turned_ref.shape[1] // rows):
-                turned_ref[0, pl.ds(n * rows + r, 1)] = jnp.where(lane == whole, 1.0, 0.0)
-                turned_ref[1, pl.ds(n * rows + r, 1)] = jnp.where(lane == half, 1.0, 0.0)
-            live = active_ref[jnp.where(body == 0, start + r, q)].astype(jnp.float32)
-            push_ref[pl.ds(r, 1)] = jnp.where(lane[:, :cols] >= 0, live * (-PRESSURE_SCALE), 0.0)
-            near, far = counts
-            chosen_ref[jnp.where(beside, near, far)] = r
-            return near + beside.astype(jnp.int32), far + 1 - beside.astype(jnp.int32)
-
-        lax.fori_loop(0, rows, leave, (jnp.int32(0), jnp.int32(rows // 2)), unroll=4)
-        pick_ref[...] = turned_ref[0].T
-        half_ref[...] = turned_ref[1].T[: half_ref.shape[0]]
+        lax.fori_loop(0, rows, meet, (jnp.int32(0), jnp.int32(rows // 2)), unroll=4)
+        turned = turned_ref[0:rows]
+        pick_ref[...] = jnp.concatenate([turned] * (pick_ref.shape[1] // rows), axis=0).T
+        push_ref[...] = live_ref[0:rows] * (-PRESSURE_SCALE)
 
     @pl.when(jnp.logical_not(last_x))
     def _():
         push_ref[...] = jnp.zeros_like(push_ref)
         pick_ref[...] = jnp.zeros_like(pick_ref)
-        half_ref[...] = jnp.zeros_like(half_ref)
 
         def any_row(r, _):
             chosen_ref[r] = 0
@@ -212,7 +197,7 @@
         return tuple(
             advance_plane(
                 c, i, d_ref[c, i] * U_SCALE, ahead and d_ref[c, i + 1] * U_SCALE, v_ref[c, i] * W_SCALE, carried[c],
-                kx_ref[i], ky_ref[i], kz_ref[i], kick_ref[i], u_ref, w_ref, yc_ref, yd_ref, even_y,
+                kx_ref[i], ky_ref[i], kz_ref[i], kick_ref[i], u_ref, w_ref, (yc_ref, yd_ref), even_y,
             )
             for c in range(3)
         )
@@ -288,8 +273,7 @@
 
 
 def interior_kernel(
-    u_scale, w_scale, u_in, w_in, kx_ref, ky_ref, kz_ref, kick_ref, xl_ref, xh_ref, yl_ref, yh_ref,
-    u_ref, w_ref, yc_ref, yd_ref,
+    last, u_in, w_in, kx_ref, ky_ref, kz_ref, kick_ref, xl_ref, xh_ref, yl_ref, yh_ref, u_ref, w_ref, *side_refs
 ):
     _, planes, rows, cols = u_ref.shape
     even_y = lax.axis_index("yz") % 2 == 0
@@ -305,7 +289,7 @@
         return tuple(
             advance_plane(
                 c, i, fixed(u_ref, c, i), ahead and fixed(u_ref, c, i + 1), fixed(w_ref, c, i), carried[c],
-                kx_ref[i], ky_ref[i], kz_ref[i], kick_ref[i], u_ref, w_ref, yc_ref, yd_ref, even_y, u_scale, w_scale,
+                kx_ref[i], ky_ref[i], kz_ref[i], kick_ref[i], u_ref, w_ref, side_refs, even_y, last,
             )
             for c in range(3)
         )
@@ -329,7 +313,7 @@
 
 
 def advance_plane(
-    c, i, here, ahead, w, carried, kx, ky, kz, kick, u_ref, w_ref, yc_ref, yd_ref, even_y, u_scale=1.0, w_scale=1.0
+    c, i, here, ahead, w, carried, kx, ky, kz, kick, u_ref, w_ref, side_refs, even_y, last=False
 ):
     rows, cols = here.shape
     force = -carried
@@ -343,80 +327,111 @@
     force = force + (pull_z - pltpu.roll(pull_z, 1, 1))
     w = w + kick * force
     u = here + w
-    if u_scale != 1.0:
-        u, w = u * u_scale, w * w_scale
+    if last:
+        u_ref[c, i] = u * (1.0 / U_SCALE)
+        w_ref[c, i] = w * (1.0 / W_SCALE)
+        return pull_x
     w_ref[c, i] = w
     u_ref[c, i] = u
-    first, last = u[0:1], u[rows - 1 : rows]
-    yc_ref[c, pl.ds(i, 1)] = jnp.where(even_y, last, first)
-    yd_ref[c, pl.ds(i, 1)] = jnp.where(even_y, first, last)
+    low, high = u[0:1], u[rows - 1 : rows]
+    yc_ref, yd_ref = side_refs
+    yc_ref[c, pl.ds(i, 1)] = jnp.where(even_y, high, low)
+    yd_ref[c, pl.ds(i, 1)] = jnp.where(even_y, low, high)
     return pull_x
 
 
-def contact_kernel(
-    scale, own_ref, near_ref, far_ref, pick_ref, push_ref, out_ref, fp_ref, fy_ref, fz_ref,
-):
-    rows, cols = out_ref.shape
-    lanes = pick_ref.shape[1]
-    parts = lanes // rows
-    deep = cols // parts
-    is_face = lax.axis_index("gx") == lax.axis_size("gx") - 1
-
-    @pl.when(jnp.logical_not(is_face))
-    def _():
-        out_ref[...] = jnp.zeros_like(out_ref)
-
-    @pl.when(is_face)
-    def _():
-        pick = pick_ref[...]
-
+def contact_kernel(own_ref, near_ref, far_ref, pick_ref, push_ref, out_ref, *scratch):
+    @pl.when(on_face())
+    def _():
         def matched(c):
             pool = jnp.concatenate([near_ref[c], far_ref[c]], axis=0)
             return lax.dot_general(
-                pool, pick, (((0,), (0,)), ((), ())),
+                pool, pick_ref[...], (((0,), (0,)), ((), ())),
                 precision=lax.Precision.HIGHEST, preferred_element_type=jnp.float32,
             )
 
+        out_ref[...] = pressures(U_SCALE, lambda c: own_ref[c], matched, out_ref.shape, *scratch) * push_ref[...]
+
+    @pl.when(jnp.logical_not(on_face()))
+    def _():
+        out_ref[...] = jnp.zeros_like(out_ref)
+
+
+def listed_contact_kernel(
+    own_half_ref, own_rest_ref, half_ref, rest_ref, push_ref, chosen_ref, out_ref, list_ref, *scratch
+):
+    rows, cols = out_ref.shape
+
+    @pl.when(on_face())
+    def _():
+        def matched(c):
+            turned = jnp.concatenate([half_ref[c], rest_ref[c]], axis=0).T
+            return jnp.concatenate([turned] * (scratch[0].shape[1] // rows), axis=1)
+
         def own(c):
-            turned = own_ref[c].T
-            return jnp.concatenate([turned[h * deep : (h + 1) * deep] for h in range(parts)], axis=1)
-
-        gap = scale * GAP_SCALE
-        along = scale * YIELD_SPAN * SPAN
-        fp_ref[...] = jnp.exp2(matched(0) * gap - BIAS / 2.0)
-        fy_ref[...] = matched(1) * along
-        spot = lax.broadcasted_iota(jnp.int32, (cols, lanes), 0).astype(jnp.float32)
-        fz_ref[...] = matched(2) * along + spot * SPAN
-        lane = lax.broadcasted_iota(jnp.int32, (deep, lanes), 1)
-        depth = lax.broadcasted_iota(jnp.int32, (deep, lanes), 0)
-        mine = (depth + lane // rows * deep).astype(jnp.float32)
-        op = jnp.exp2(own(0) * gap - BIAS / 2.0)
-        oy = own(1) * along
-        oz = own(2) * along + mine * SPAN
-
-        def term(m, total):
-            at = pl.ds(m, 1)
-            dy = oy - fy_ref[at]
-            dz = oz - fz_ref[at]
+            return jnp.concatenate([own_half_ref[c], own_rest_ref[c]], axis=0)
+
+        list_ref[...] = pressures(1.0, own, matched, out_ref.shape, *scratch)
+        for r in range(rows):
+            out_ref[pl.ds(chosen_ref[r], 1)] = list_ref[r : r + 1]
+        out_ref[...] = out_ref[...] * push_ref[...]
+
+    @pl.when(jnp.logical_not(on_face()))
+    def _():
+        out_ref[...] = jnp.zeros_like(out_ref)
+
+
+def on_face():
+    return lax.axis_index("gx") == lax.axis_size("gx") - 1
+
+
+def pressures(scale, own_rows, matched, shape, fp_ref, fy_ref, fz_ref, total_ref):
+    rows, cols = shape
+    lanes = fp_ref.shape[1]
+    parts = lanes // rows
+    deep = cols // parts
+
+    def own(c):
+        turned = own_rows(c).T
+        return jnp.concatenate([turned[h * deep : (h + 1) * deep] for h in range(parts)], axis=1)
+
+    gap = scale * GAP_SCALE
+    along = scale * YIELD_SPAN * SPAN
+    fp_ref[...] = jnp.exp2(matched(0) * gap - BIAS / 2.0)
+    fy_ref[...] = matched(1) * along
+    spot = lax.broadcasted_iota(jnp.int32, (cols, lanes), 0).astype(jnp.float32)
+    fz_ref[...] = matched(2) * along + spot * SPAN
+    lane = lax.broadcasted_iota(jnp.int32, (deep, lanes), 1)
+    depth = lax.broadcasted_iota(jnp.int32, (deep, lanes), 0)
+    mine = (depth + lane // rows * deep).astype(jnp.float32)
+    op = jnp.exp2(own(0) * gap - BIAS / 2.0)
+    oy = own(1) * along
+    oz = own(2) * along + mine * SPAN
+
+    width = math.gcd(16, deep)
+    for s in range(0, deep, width):
+        some = slice(s, s + width)
+        total = jnp.zeros((width, lanes), jnp.float32)
+        for m in range(cols):
+            dy = oy[some] - fy_ref[m : m + 1]
+            dz = oz[some] - fz_ref[m : m + 1]
             weight = jnp.exp2(-(dy * dy + dz * dz))
-            soft = jnp.log2(op * fp_ref[at] + 2.0**-BIAS) + BIAS
-            return total + weight * soft
-
-        total = lax.fori_loop(0, cols, term, jnp.zeros((deep, lanes), jnp.float32), unroll=math.gcd(16, cols))
-        turned = jnp.concatenate([total[:, h * rows : (h + 1) * rows] for h in range(parts)], axis=0)
-        out_ref[...] = turned.T * push_ref[...]
-
-
-def last_contact_kernel(
-    own_ref, near_ref, far_ref, pick_ref, push_ref, u_ref, w_ref, d_ref, v_ref, out_ref, fp_ref, fy_ref, fz_ref, sems,
-):
+            soft = jnp.log2(op[some] * fp_ref[m : m + 1] + 2.0**-BIAS) + BIAS
+            total = total + weight * soft
+        total_ref[some] = total
+    total = total_ref[...]
+    return jnp.concatenate([total[:, h * rows : (h + 1) * rows] for h in range(parts)], axis=0).T
+
+
+def last_contact_kernel(*refs):
+    meet, (u_ref, w_ref, d_ref, v_ref, out_ref, *scratch, sems) = refs[:6], refs[6:]
     copies = [
         pltpu.make_async_copy(u_ref, d_ref, sems.at[0]),
         pltpu.make_async_copy(w_ref, v_ref, sems.at[1]),
     ]
     for copy in copies:
         copy.start()
-    contact_kernel(1.0, own_ref, near_ref, far_ref, pick_ref, push_ref, out_ref, fp_ref, fy_ref, fz_ref)
+    listed_contact_kernel(*meet, out_ref, *scratch)
     for copy in copies:
         copy.wait()
 
@@ -468,9 +483,8 @@
         nc_ref[c] = with_sides(yc_ref[c] + jnp.where(even_y, yh, yl), c_low, c_high)
         nd_ref[c] = with_sides(yd_ref[c] + jnp.where(even_y, yl, yh), d_low, d_high)
     half = rows // 2
-    is_face = lax.axis_index("gx") == lax.axis_size("gx") - 1
-
-    @pl.when(is_face)
+
+    @pl.when(on_face())
     def _():
         for n, ref in enumerate((half_ref, rest_ref)):
             for r in range(half):
@@ -478,7 +492,7 @@
                 for c in range(3):
                     ref[c, r : r + 1] = nb_ref[c, pl.ds(at, 1)]
 
-    @pl.when(jnp.logical_not(is_face))
+    @pl.when(jnp.logical_not(on_face()))
     def _():
         for c in range(3):
             half_ref[c], rest_ref[c] = nb_ref[c, :half], nb_ref[c, half:]
@@ -578,59 +592,65 @@
     )
     got_e = passed(spare, "e")
     got = [passed(block, name) for block, name in zip(sent, "abcd")]
-    kx, ky, kz, kick, row_kick, high_ky, push_scale, pick, pick_half, chosen, v = call(
+    kx, ky, kz, kick, row_kick, high_ky, push_scale, pick, chosen, got[2], v = call(
         setup_kernel,
-        [vmem(block)] * 4 + [vmem((2, *side)), vmem(side), vmem(face)]
-        + [vmem((lanes, lanes)), vmem((rows, lanes)), pltpu.SMEM((rows + rows // 2,), jnp.int32)]
-        + [vmem(state)],
-        [kinds, v, moduli, density, partner, active],
-        [None, hbm] + [smem] * 4,
-        scratch=[
-            vmem((2, lanes, lanes)),
-            pltpu.SMEM(partner.shape, jnp.int32),
-            pltpu.SMEM((rows + 1,), jnp.int32),
-            pltpu.SemaphoreType.DMA,
-        ],
+        [vmem(block)] * 4 + [vmem((2, *side)), vmem(side), vmem(face), vmem((lanes, lanes))]
+        + [pltpu.SMEM((rows + 1,), jnp.int32), vmem((4, *side)), vmem(state)],
+        [kinds, got[2], v, moduli, density, partner, active],
+        [None, None, hbm] + [smem] * 4,
+        aliases={1: 9},
+        scratch=[vmem((rows + tile, lanes)), vmem((rows + tile, cols)), pltpu.SemaphoreType.DMA],
         flops=8_000_000,
     )
-    pair_scratch = [vmem((cols, lanes))] * 3
+    pair_scratch = [vmem((cols, lanes))] * 3 + [vmem((cols * rows // lanes, lanes))]
     for step in range(STEPS):
         first, last = step == 0, step == STEPS - 1
         scale = U_SCALE if first else 1.0
         if first:
             corner, kick = lax.optimization_barrier((corner, kick))
             corner = passed(corner, "corner")
-            u, w, yc, yd = call(
+            u, w, *sides = call(
                 first_kernel,
                 [vmem(state)] * 2 + [vmem(side3)] * 2,
                 [d, v, kx, ky, kz, kick],
             )
-            push_scale, yc = lax.optimization_barrier((push_scale, yc))
+            push_scale, sides[0] = lax.optimization_barrier((push_scale, sides[0]))
         else:
             got_e, got_half = passed(rest, "rest"), passed(half, "b")
             got = [passed(sent[0], "a"), got_half, got_e, passed(sent[2], "c"), passed(sent[3], "d")]
-            u, w, yc, yd = call(
-                functools.partial(interior_kernel, *((1.0 / U_SCALE, 1.0 / W_SCALE) if last else (1.0, 1.0))),
-                [vmem(state)] * 2 + [vmem(side3)] * 2,
+            u, w, *sides = call(
+                functools.partial(interior_kernel, last),
+                [vmem(state)] * 2 + [vmem(side3)] * (0 if last else 2),
                 [u, w, kx, ky, kz, kick, *moves],
                 aliases={0: 0, 1: 1},
                 flops=20_000_000,
             )
-        meet = [sent[1], got[1], got_e, pick if first else pick_half, push_scale]
+        if not first:
+            meet = [half, rest, got_half, got_e, push_scale, chosen]
         if last:
             d, v, push = call(
                 last_contact_kernel,
                 [jax.ShapeDtypeStruct(state, jnp.float32)] * 2 + [vmem(face)],
                 [*meet, u, w],
-                scratch=pair_scratch + [pltpu.SemaphoreType.DMA((2,))],
+                [None] * 5 + [smem] + [None] * 2,
+                scratch=[vmem(face), *pair_scratch, pltpu.SemaphoreType.DMA((2,))],
                 hbm_outs=2,
                 flops=20_000_000,
             )
             break
-        (push,) = call(
-            functools.partial(contact_kernel, scale), [vmem(face)], meet, scratch=pair_scratch,
-            flops=0 if first else 20_000_000,
-        )
+        if first:
+            (push,) = call(
+                contact_kernel, [vmem(face)], [sent[1], got[1], got_e, pick, push_scale], scratch=pair_scratch
+            )
+        else:
+            (push,) = call(
+                listed_contact_kernel,
+                [vmem(face)],
+                meet,
+                [None] * 5 + [smem],
+                scratch=[vmem(face), *pair_scratch],
+                flops=20_000_000,
+            )
         extra = []
         if first:
             kx, ky, kz, *rest = call(
@@ -645,7 +665,7 @@
             functools.partial(boundary_kernel, scale, len(extra), len(got)),
             [vmem(face3)] * 2 + [vmem(side3)] * 2 + [vmem((3, rows // 2, cols))] * 2
             + [vmem(face3)] * 2 + [vmem(side3)] * 2,
-            [*extra, u, yc, yd, *sent, *got, *edges, push, chosen],
+            [*extra, u, *sides, *sent, *got, *edges, push, chosen],
             [None] * (12 + len(got) + len(extra)) + [smem],
         )
         moves = [xl, xh, yl, yh]

time: 41.9 us -> 41.4 us (0.988)
  waiting for transfers between devices: 1.88 us -> 3.26 us
  starting transfers between devices: 23.2 us -> 22 us
  Pallas kernels: 15.4 us -> 14.8 us
    ppermute x21, waiting for transfers between devices: 1.88 us -> 3.26 us  [passed(): return lax.ppermute(block, AXES, route[name])]
    ppermute x21, starting transfers between devices: 23.2 us -> 22 us  [passed(): return lax.ppermute(block, AXES, route[name])]
    pallas_call x15, Pallas kernels: 15.4 us -> 14.8 us  [call(): pl.pallas_call(kernel, out_shape=outs, in_specs=specs, out_specs=[pl.Bloc...]
  transfers between devices with their start and end apart: 21 -> 21, of which waited for: 3 -> 3; matrix products, arithmetic and copies ran while one was open for 0% -> 0% of each run, Pallas kernels for 29% -> 27%
where the time goes in v6:
time: 41.4 us; the launch traced here: 41.2 us
  starting transfers between devices  22 us (53%)
  Pallas kernels  14.8 us (36%)
  waiting for transfers between devices  3.26 us (8%)
  between operations  1.1 us (3%)
    ppermute x21, starting transfers between devices, passed(): return lax.ppermute(block, AXES, route[name])  22 us
    pallas_call x15, Pallas kernels, call(): pl.pallas_call(kernel, out_shape=outs, in_specs=specs, out_specs=[pl.Bloc...  14.8 us
    ppermute x21, waiting for transfers between devices, passed(): return lax.ppermute(block, AXES, route[name])  3.26 us
  transfers between devices with their start and end apart: 21, of which 3 were waited for; matrix products, arithmetic and copies ran while one was open for 0% of the time, Pallas kernels for 27%

profile of v6, /device:TPU:8, one launch (start us, length us, event | category | flops | bytes accessed | tf_op | source)
XLA Modules:
  0.0 41.2 jit_solution(771589261501088564)
XLA Ops:
  0.7 1.4 %shard_map.86 = (f32[4,64,128]{2,1,0:T(8,128)S(1)}, f32[4,64,128]{2,1,0:T(8,128)S(1)}, f32[4,16,128]{2,1,0:T(8,128)S(1)}, f32[4,16,128]{2,1,0:T(8,128)S(1)}, f32...) custom-call(f32[3,16,64,128]{3,2,1,0:T(8,128)} %bitcast.5, s32[16,64,128]{2,1,0:T(8,128)} %bitcast.7), custom_call_target="tpu_custom_call" | custom-call | tf_op jit(solution)/shard_map/pallas_call | solution.py:46
  2.1 1.6 %collective-permute-start.2 = (f32[4,64,128]{2,1,0:T(8,128)S(1)}, f32[4,64,128]{2,1,0:T(8,128)S(1)}, u32[]{:S(2)}, u32[]{:S(2)}) collective-permute-start(f32[4,64,128]{2,1,0:T(8,128)S(1)} %get-tuple-element.92.sb_ref.own_ref.refs_6_), channel_id=1, source_target_pairs={{0,1},{1,0},{2,3},{3,2},{4,8},{5,9},{6,10},{7,11},{8,4},{9,5},{10,... | collective-permute-start | bytes 393224 | tf_op jit(solution)/shard_map/ppermute | solution.py:579
  3.7 0.5 %collective-permute-start = (f32[4,16,128]{2,1,0:T(8,128)S(1)}, f32[4,16,128]{2,1,0:T(8,128)S(1)}, u32[]{:S(2)}, u32[]{:S(2)}) collective-permute-start(f32[4,16,128]{2,1,0:T(8,128)S(1)} %get-tuple-element.81.sc_ref.refs_7_), channel_id=1, source_target_pairs={{0,1},{1,0},{2,3},{3,2},{4,5},{5,4},{6,7},{7,6},{8,9},{9,8},{10,11... | collective-permute-start | bytes 98312 | tf_op jit(solution)/shard_map/ppermute | solution.py:579
  4.2 1.1 %collective-permute-start.3 = (f32[4,16,128]{2,1,0:T(8,128)S(1)}, f32[4,16,128]{2,1,0:T(8,128)S(1)}, u32[]{:S(2)}, u32[]{:S(2)}) collective-permute-start(f32[4,16,128]{2,1,0:T(8,128)S(1)} %get-tuple-element.93.sd_ref.refs_8_), channel_id=1, source_target_pairs={{0,3},{1,2},{2,1},{3,0},{4,7},{5,6},{6,5},{7,4},{8,11},{9,10},{10,... | collective-permute-start | bytes 98312 | tf_op jit(solution)/shard_map/ppermute | solution.py:579
  5.4 2.0 %shard_map.87 = (f32[16,64,128]{2,1,0:T(8,128)S(1)}, f32[16,64,128]{2,1,0:T(8,128)S(1)}, f32[16,64,128]{2,1,0:T(8,128)S(1)}, f32[16,64,128]{2,1,0:T(8,128)S(1)},...) custom-call(s32[16,64,128]{2,1,0:T(8,128)S(1)} %bitcast.8, ...), custom_call_target="tpu_custom_call", output_to_operand_aliasing={{9}: (1, {})} | custom-call | flops 8000000 | tf_op jit(solution)/shard_map/pallas_call | solution.py:46
  7.4 3.2 %collective-permute-start.4 = (f32[1,128]{1,0:T(1,128)S(1)}, f32[1,128]{1,0:T(1,128)S(1)}, u32[]{:S(2)}, u32[]{:S(2)}) collective-permute-start(f32[1,128]{1,0:T(1,128)S(1)} %get-tuple-element.95), channel_id=1, source_target_pairs={{0,5},{1,6},{2,7},{3,4},{4,9},{5,10},{6,11},{7,8},{8,13},{9,14},{1... | collective-permute-start | bytes 1544 | tf_op jit(solution)/shard_map/ppermute | solution.py:579
  10.6 2.1 %shard_map.88 = (f32[3,16,64,128]{3,2,1,0:T(8,128)S(1)}, f32[3,16,64,128]{3,2,1,0:T(8,128)S(1)}, f32[3,16,128]{2,1,0:T(8,128)S(1)}, f32[3,16,128]{2,1,0:T(8,128)S(1)}) custom-call(f32[3,16,64,128]{3,2,1,0:T(8,128)S(1)} %bitcast.6, f32[3,16,64,128]{3,2,1,0:T(8,128)S(1)} %get-tuple-element.82.v_ref, f32[16,64,128]{2,1,0:T(8,128)S(1)} %get-tuple-element.83.kx_ref.kx_in, ...), custom_call_target="tpu_custom_call" | custom-call | tf_op jit(solution)/shard_map/pallas_call | solution.py:46
  12.8 0.8 %shard_map.89 = (f32[16,64,128]{2,1,0:T(8,128)S(1)}, f32[16,64,128]{2,1,0:T(8,128)S(1)}, f32[16,64,128]{2,1,0:T(8,128)S(1)}, f32[64,128]{1,0:T(8,128)S(1)}, f32[...) custom-call(f32[4,64,128]{2,1,0:T(8,128)S(1)} %get-tuple-element.91., ...), custom_call_target="tpu_custom_call", output_to_operand_aliasing={{0}: (12, {}), {1}: (13, {}), {2}: (14, {})} | custom-call | tf_op jit(solution)/shard_map/pallas_call | solution.py:46
  13.5 0.1 shard_map.91
  13.7 2.4 %collective-permute-start.6 = (f32[3,64,128]{2,1,0:T(8,128)S(1)}, f32[3,64,128]{2,1,0:T(8,128)S(1)}, u32[]{:S(2)}, u32[]{:S(2)}) collective-permute-start(f32[3,64,128]{2,1,0:T(8,128)S(1)} %get-tuple-element.123.refs_3_), channel_id=1, source_target_pairs={{0,4},{1,5},{2,6},{3,7},{4,0},{5,1},{6,2},{7,3},{8,12},{9,13},{10,... | collective-permute-start | bytes 294920 | tf_op jit(solution)/shard_map/ppermute | solution.py:579
  16.1 1.9 %collective-permute-start.7 = (f32[3,32,128]{2,1,0:T(8,128)S(1)}, f32[3,32,128]{2,1,0:T(8,128)S(1)}, u32[]{:S(2)}, u32[]{:S(2)}) collective-permute-start(f32[3,32,128]{2,1,0:T(8,128)S(1)} %get-tuple-element.127.own_half_ref), channel_id=1, source_target_pairs={{0,1},{1,0},{2,3},{3,2},{4,8},{5,9},{6,10},{7,11},{8,4},{9,5},{10,... | collective-permute-start | bytes 147464 | tf_op jit(solution)/shard_map/ppermute | solution.py:579
  18.0 0.1 collective-permute-start.8
  18.1 0.1 collective-permute-start.9
  18.2 1.3 %collective-permute-start.10 = (f32[3,16,128]{2,1,0:T(8,128)S(1)}, f32[3,16,128]{2,1,0:T(8,128)S(1)}, u32[]{:S(2)}, u32[]{:S(2)}) collective-permute-start(f32[3,16,128]{2,1,0:T(8,128)S(1)} %get-tuple-element.126.refs_6_), channel_id=1, source_target_pairs={{0,3},{1,2},{2,1},{3,0},{4,7},{5,6},{6,5},{7,4},{8,11},{9,10},{10,... | collective-permute-start | bytes 73736 | tf_op jit(solution)/shard_map/ppermute | solution.py:579
  19.5 1.8 %shard_map.92 = (f32[3,16,64,128]{3,2,1,0:T(8,128)S(1)}, f32[3,16,64,128]{3,2,1,0:T(8,128)S(1)}, f32[3,16,128]{2,1,0:T(8,128)S(1)}, f32[3,16,128]{2,1,0:T(8,128)S(1)}) custom-call(f32[3,16,64,128]{3,2,1,0:T(8,128)S(1)} %get-tuple-element.89.refs_2_.u_in, ...), custom_call_target="tpu_custom_call", output_to_operand_aliasing={{0}: (0, {}), {1}: (1, {})} | custom-call | flops 20000000 | tf_op jit(solution)/shard_map/pallas_call | solution.py:46
  21.3 0.8 %collective-permute-done.8.rest_ref.refs_9_ = f32[3,32,128]{2,1,0:T(8,128)S(1)} collective-permute-done((f32[3,32,128]{2,1,0:T(8,128)S(1)}, f32[3,32,128]{2,1,0:T(8,128)S(1)}, u32[]{:S(2)}, u32[]{:S(2)}) %collective-permute-start.8) | collective-permute-done | bytes 49184 | tf_op jit(solution)/shard_map/ppermute | solution.py:579
  22.2 0.1 shard_map.94
  22.3 0.1 collective-permute-start.11
  22.4 3.4 %collective-permute-start.12 = (f32[3,32,128]{2,1,0:T(8,128)S(1)}, f32[3,32,128]{2,1,0:T(8,128)S(1)}, u32[]{:S(2)}, u32[]{:S(2)}) collective-permute-start(f32[3,32,128]{2,1,0:T(8,128)S(1)} %get-tuple-element.141.own_half_ref), channel_id=1, source_target_pairs={{0,1},{1,0},{2,3},{3,2},{4,8},{5,9},{6,10},{7,11},{8,4},{9,5},{10,... | collective-permute-start | bytes 147464 | tf_op jit(solution)/shard_map/ppermute | solution.py:579
  25.8 0.8 %collective-permute-start.14 = (f32[3,16,128]{2,1,0:T(8,128)S(1)}, f32[3,16,128]{2,1,0:T(8,128)S(1)}, u32[]{:S(2)}, u32[]{:S(2)}) collective-permute-start(f32[3,16,128]{2,1,0:T(8,128)S(1)} %get-tuple-element.139.refs_5_), channel_id=1, source_target_pairs={{0,1},{1,0},{2,3},{3,2},{4,5},{5,4},{6,7},{7,6},{8,9},{9,8},{10,11... | collective-permute-start | bytes 73736 | tf_op jit(solution)/shard_map/ppermute | solution.py:579
  26.6 0.4 %collective-permute-start.15 = (f32[3,16,128]{2,1,0:T(8,128)S(1)}, f32[3,16,128]{2,1,0:T(8,128)S(1)}, u32[]{:S(2)}, u32[]{:S(2)}) collective-permute-start(f32[3,16,128]{2,1,0:T(8,128)S(1)} %get-tuple-element.140.refs_6_), channel_id=1, source_target_pairs={{0,3},{1,2},{2,1},{3,0},{4,7},{5,6},{6,5},{7,4},{8,11},{9,10},{10,... | collective-permute-start | bytes 73736 | tf_op jit(solution)/shard_map/ppermute | solution.py:579
  27.0 1.8 %shard_map.95 = (f32[3,16,64,128]{3,2,1,0:T(8,128)S(1)}, f32[3,16,64,128]{3,2,1,0:T(8,128)S(1)}, f32[3,16,128]{2,1,0:T(8,128)S(1)}, f32[3,16,128]{2,1,0:T(8,128)S(1)}) custom-call(f32[3,16,64,128]{3,2,1,0:T(8,128)S(1)} %get-tuple-element.119.refs_0_.u_in, ...), custom_call_target="tpu_custom_call", output_to_operand_aliasing={{0}: (0, {}), {1}: (1, {})} | custom-call | flops 20000000 | tf_op jit(solution)/shard_map/pallas_call | solution.py:46
  28.8 1.4 %collective-permute-done.13.rest_ref.refs_9_ = f32[3,32,128]{2,1,0:T(8,128)S(1)} collective-permute-done((f32[3,32,128]{2,1,0:T(8,128)S(1)}, f32[3,32,128]{2,1,0:T(8,128)S(1)}, u32[]{:S(2)}, u32[]{:S(2)}) %collective-permute-start.13) | collective-permute-done | bytes 49184 | tf_op jit(solution)/shard_map/ppermute | solution.py:579
  30.2 0.1 shard_map.97
  30.3 0.1 collective-permute-start.18
  30.4 3.7 %collective-permute-start.16 = (f32[3,32,128]{2,1,0:T(8,128)S(1)}, f32[3,32,128]{2,1,0:T(8,128)S(1)}, u32[]{:S(2)}, u32[]{:S(2)}) collective-permute-start(f32[3,32,128]{2,1,0:T(8,128)S(1)} %get-tuple-element.149.refs_0_), channel_id=1, source_target_pairs={{0,1},{1,0},{2,3},{3,2},{4,8},{5,9},{6,10},{7,11},{8,4},{9,5},{10,... | collective-permute-start | bytes 147464 | tf_op jit(solution)/shard_map/ppermute | solution.py:579
  34.2 0.0 collective-permute-start.19
  34.2 1.1 %collective-permute-start.20 = (f32[3,16,128]{2,1,0:T(8,128)S(1)}, f32[3,16,128]{2,1,0:T(8,128)S(1)}, u32[]{:S(2)}, u32[]{:S(2)}) collective-permute-start(f32[3,16,128]{2,1,0:T(8,128)S(1)} %get-tuple-element.156.refs_7_), channel_id=1, source_target_pairs={{0,3},{1,2},{2,1},{3,0},{4,7},{5,6},{6,5},{7,4},{8,11},{9,10},{10,... | collective-permute-start | bytes 73736 | tf_op jit(solution)/shard_map/ppermute | solution.py:579
  35.3 1.9 %shard_map.98 = (f32[3,16,64,128]{3,2,1,0:T(8,128)S(1)}, f32[3,16,64,128]{3,2,1,0:T(8,128)S(1)}) custom-call(f32[3,16,64,128]{3,2,1,0:T(8,128)S(1)} %get-tuple-element.133.refs_0_.u_in, f32[3,16,64,128]{3,2,1,0:T(8,128)S(1)} %get-tuple-element.134.w_in, f32[16,64,128]{2,1,0:T(8,128)S(1)} %get-tuple-element.98.kx_ref, ...), custom_call_target="tpu_custom_call", output_to_operand_aliasing={{0}: (0, {}), {1}: (1, {})} | custom-call | flops 20000000 | tf_op jit(solution)/shard_map/pallas_call | solution.py:46
  37.2 1.0 %collective-permute-done.17.refs_3_.refs_10_ = f32[3,32,128]{2,1,0:T(8,128)S(1)} collective-permute-done((f32[3,32,128]{2,1,0:T(8,128)S(1)}, f32[3,32,128]{2,1,0:T(8,128)S(1)}, u32[]{:S(2)}, u32[]{:S(2)}) %collective-permute-start.17) | collective-permute-done | bytes 49184 | tf_op jit(solution)/shard_map/ppermute | solution.py:579
  38.2 1.7 %shard_map.99 = (f32[3,16,64,128]{3,2,1,0:T(8,128)}, f32[3,16,64,128]{3,2,1,0:T(8,128)}, f32[64,128]{1,0:T(8,128)S(1)}) custom-call(f32[3,32,128]{2,1,0:T(8,128)S(1)} %get-tuple-element.149.refs_0_, f32[3,32,128]{2,1,0:T(8,128)S(1)} %get-tuple-element.150.refs_1_, f32[3,32,128]{2,1,0:T(8,128)S(1)} %collective-permute-done.16.refs_2_.refs_9_, ...), custom_call_target="tpu_custom_call" | custom-call | flops 20000000 | tf_op jit(solution)/shard_map/pallas_call | solution.py:46
  39.9 1.1 %shard_map.100 = (f32[3,16,64,128]{3,2,1,0:T(8,128)}, f32[3,16,64,128]{3,2,1,0:T(8,128)}) custom-call(f32[3,16,64,128]{3,2,1,0:T(8,128)S(1)} %get-tuple-element.147.refs_6_.refs_0_, f32[3,16,64,128]{3,2,1,0:T(8,128)S(1)} %get-tuple-element.148.refs_7_.refs_1_, ...), custom_call_target="tpu_custom_call", output_to_operand_aliasing={{0}: (2, {}), {1}: (3, {})} | custom-call | tf_op jit(solution)/shard_map/pallas_call | solution.py:46
  (37 shorter events, 0.2 us)
Async XLA Ops:
  0.6 4.7 %copy-start.1 = (s32[1,16,64,128]{3,2,1,0:T(8,128)S(1)}, s32[1,16,64,128]{3,2,1,0:T(8,128)}, u32[]{:S(2)}) copy-start(s32[1,16,64,128]{3,2,1,0:T(8,128)} %param.9) | copy-start | bytes 1572868
  0.6 4.7 %copy-start.2 = (f32[8]{0:T(128)S(1)}, f32[8]{0:T(128)}, u32[]{:S(2)}) copy-start(f32[8]{0:T(128)} %moduli_ref.3) | copy-start | bytes 100
  0.7 4.7 %copy-start.4 = (s32[256]{0:T(256)S(1)}, s32[256]{0:T(256)}, u32[]{:S(2)}) copy-start(s32[256]{0:T(256)} %active_ref.1) | copy-start | bytes 3076
  0.7 4.7 %copy-start.3 = (s32[256]{0:T(256)S(1)}, s32[256]{0:T(256)}, u32[]{:S(2)}) copy-start(s32[256]{0:T(256)} %partner_ref.1) | copy-start | bytes 3076
  0.7 4.7 %copy-start.5 = (f32[8]{0:T(128)S(1)}, f32[8]{0:T(128)}, u32[]{:S(2)}) copy-start(f32[8]{0:T(128)} %density_ref.1) | copy-start | bytes 100
  2.1 8.6 %copy-start = (f32[1,3,16,64,128]{4,3,2,1,0:T(8,128)S(1)}, f32[1,3,16,64,128]{4,3,2,1,0:T(8,128)}, u32[]{:S(2)}) copy-start(f32[1,3,16,64,128]{4,3,2,1,0:T(8,128)} %param.7) | copy-start | bytes 4718596
  2.1 10.6 %collective-permute-start.2 = (f32[4,64,128]{2,1,0:T(8,128)S(1)}, f32[4,64,128]{2,1,0:T(8,128)S(1)}, u32[]{:S(2)}, u32[]{:S(2)}) collective-permute-start(f32[4,64,128]{2,1,0:T(8,128)S(1)} %get-tuple-element.92.sb_ref.own_ref.refs_6_), channel_id=1, source_target_pairs={{0,1},{1,0},{2,3},{3,2},{4,8},{5,9},{6,10},{7,11},{8,4},{9,5},{10,... | collective-permute-start | bytes 393224 | tf_op jit(solution)/shard_map/ppermute | solution.py:579
  3.7 9.1 %collective-permute-start.1 = (f32[4,64,128]{2,1,0:T(8,128)S(1)}, f32[4,64,128]{2,1,0:T(8,128)S(1)}, u32[]{:S(2)}, u32[]{:S(2)}) collective-permute-start(f32[4,64,128]{2,1,0:T(8,128)S(1)} %get-tuple-element.91.sa_ref.refs_5_), channel_id=1, source_target_pairs={{0,4},{1,5},{2,6},{3,7},{4,0},{5,1},{6,2},{7,3},{8,12},{9,13},{10,... | collective-permute-start | bytes 393224 | tf_op jit(solution)/shard_map/ppermute | solution.py:579
  3.7 9.0 %collective-permute-start.5 = (f32[3,64,128]{2,1,0:T(8,128)S(1)}, f32[3,64,128]{2,1,0:T(8,128)S(1)}, u32[]{:S(2)}, u32[]{:S(2)}) collective-permute-start(f32[3,64,128]{2,1,0:T(8,128)S(1)} %get-tuple-element.111), channel_id=1, source_target_pairs={{0,1},{1,0},{2,3},{3,2},{4,5},{5,4},{6,7},{7,6},{8,9},{9,8},{10,11... | collective-permute-start | bytes 294920 | tf_op jit(solution)/shard_map/ppermute | solution.py:579
  3.7 1.6 %collective-permute-start = (f32[4,16,128]{2,1,0:T(8,128)S(1)}, f32[4,16,128]{2,1,0:T(8,128)S(1)}, u32[]{:S(2)}, u32[]{:S(2)}) collective-permute-start(f32[4,16,128]{2,1,0:T(8,128)S(1)} %get-tuple-element.81.sc_ref.refs_7_), channel_id=1, source_target_pairs={{0,1},{1,0},{2,3},{3,2},{4,5},{5,4},{6,7},{7,6},{8,9},{9,8},{10,11... | collective-permute-start | bytes 98312 | tf_op jit(solution)/shard_map/ppermute | solution.py:579
  4.2 8.5 %collective-permute-start.3 = (f32[4,16,128]{2,1,0:T(8,128)S(1)}, f32[4,16,128]{2,1,0:T(8,128)S(1)}, u32[]{:S(2)}, u32[]{:S(2)}) collective-permute-start(f32[4,16,128]{2,1,0:T(8,128)S(1)} %get-tuple-element.93.sd_ref.refs_8_), channel_id=1, source_target_pairs={{0,3},{1,2},{2,1},{3,0},{4,7},{5,6},{6,5},{7,4},{8,11},{9,10},{10,... | collective-permute-start | bytes 98312 | tf_op jit(solution)/shard_map/ppermute | solution.py:579
  7.4 5.4 %collective-permute-start.4 = (f32[1,128]{1,0:T(1,128)S(1)}, f32[1,128]{1,0:T(1,128)S(1)}, u32[]{:S(2)}, u32[]{:S(2)}) collective-permute-start(f32[1,128]{1,0:T(1,128)S(1)} %get-tuple-element.95), channel_id=1, source_target_pairs={{0,5},{1,6},{2,7},{3,4},{4,9},{5,10},{6,11},{7,8},{8,13},{9,14},{1... | collective-permute-start | bytes 1544 | tf_op jit(solution)/shard_map/ppermute | solution.py:579
  13.7 8.5 %collective-permute-start.6 = (f32[3,64,128]{2,1,0:T(8,128)S(1)}, f32[3,64,128]{2,1,0:T(8,128)S(1)}, u32[]{:S(2)}, u32[]{:S(2)}) collective-permute-start(f32[3,64,128]{2,1,0:T(8,128)S(1)} %get-tuple-element.123.refs_3_), channel_id=1, source_target_pairs={{0,4},{1,5},{2,6},{3,7},{4,0},{5,1},{6,2},{7,3},{8,12},{9,13},{10,... | collective-permute-start | bytes 294920 | tf_op jit(solution)/shard_map/ppermute | solution.py:579
  16.1 5.2 %collective-permute-start.7 = (f32[3,32,128]{2,1,0:T(8,128)S(1)}, f32[3,32,128]{2,1,0:T(8,128)S(1)}, u32[]{:S(2)}, u32[]{:S(2)}) collective-permute-start(f32[3,32,128]{2,1,0:T(8,128)S(1)} %get-tuple-element.127.own_half_ref), channel_id=1, source_target_pairs={{0,1},{1,0},{2,3},{3,2},{4,8},{5,9},{6,10},{7,11},{8,4},{9,5},{10,... | collective-permute-start | bytes 147464 | tf_op jit(solution)/shard_map/ppermute | solution.py:579
  18.0 4.1 %collective-permute-start.8 = (f32[3,32,128]{2,1,0:T(8,128)S(1)}, f32[3,32,128]{2,1,0:T(8,128)S(1)}, u32[]{:S(2)}, u32[]{:S(2)}) collective-permute-start(f32[3,32,128]{2,1,0:T(8,128)S(1)} %get-tuple-element.128.own_rest_ref), channel_id=1, source_target_pairs={{0,1},{1,0},{2,3},{3,2},{4,8},{5,9},{6,10},{7,11},{8,4},{9,5},{10,... | collective-permute-start | bytes 147464 | tf_op jit(solution)/shard_map/ppermute | solution.py:579
  18.1 4.0 %collective-permute-start.9 = (f32[3,16,128]{2,1,0:T(8,128)S(1)}, f32[3,16,128]{2,1,0:T(8,128)S(1)}, u32[]{:S(2)}, u32[]{:S(2)}) collective-permute-start(f32[3,16,128]{2,1,0:T(8,128)S(1)} %get-tuple-element.125.refs_5_), channel_id=1, source_target_pairs={{0,1},{1,0},{2,3},{3,2},{4,5},{5,4},{6,7},{7,6},{8,9},{9,8},{10,11... | collective-permute-start | bytes 73736 | tf_op jit(solution)/shard_map/ppermute | solution.py:579
  18.2 3.9 %collective-permute-start.10 = (f32[3,16,128]{2,1,0:T(8,128)S(1)}, f32[3,16,128]{2,1,0:T(8,128)S(1)}, u32[]{:S(2)}, u32[]{:S(2)}) collective-permute-start(f32[3,16,128]{2,1,0:T(8,128)S(1)} %get-tuple-element.126.refs_6_), channel_id=1, source_target_pairs={{0,3},{1,2},{2,1},{3,0},{4,7},{5,6},{6,5},{7,4},{8,11},{9,10},{10,... | collective-permute-start | bytes 73736 | tf_op jit(solution)/shard_map/ppermute | solution.py:579
  22.3 7.9 %collective-permute-start.11 = (f32[3,64,128]{2,1,0:T(8,128)S(1)}, f32[3,64,128]{2,1,0:T(8,128)S(1)}, u32[]{:S(2)}, u32[]{:S(2)}) collective-permute-start(f32[3,64,128]{2,1,0:T(8,128)S(1)} %get-tuple-element.137.refs_3_), channel_id=1, source_target_pairs={{0,4},{1,5},{2,6},{3,7},{4,0},{5,1},{6,2},{7,3},{8,12},{9,13},{10,... | collective-permute-start | bytes 294920 | tf_op jit(solution)/shard_map/ppermute | solution.py:579
  22.4 6.4 %collective-permute-start.12 = (f32[3,32,128]{2,1,0:T(8,128)S(1)}, f32[3,32,128]{2,1,0:T(8,128)S(1)}, u32[]{:S(2)}, u32[]{:S(2)}) collective-permute-start(f32[3,32,128]{2,1,0:T(8,128)S(1)} %get-tuple-element.141.own_half_ref), channel_id=1, source_target_pairs={{0,1},{1,0},{2,3},{3,2},{4,8},{5,9},{6,10},{7,11},{8,4},{9,5},{10,... | collective-permute-start | bytes 147464 | tf_op jit(solution)/shard_map/ppermute | solution.py:579
  25.7 4.4 %collective-permute-start.13 = (f32[3,32,128]{2,1,0:T(8,128)S(1)}, f32[3,32,128]{2,1,0:T(8,128)S(1)}, u32[]{:S(2)}, u32[]{:S(2)}) collective-permute-start(f32[3,32,128]{2,1,0:T(8,128)S(1)} %get-tuple-element.142.own_rest_ref), channel_id=1, source_target_pairs={{0,1},{1,0},{2,3},{3,2},{4,8},{5,9},{6,10},{7,11},{8,4},{9,5},{10,... | collective-permute-start | bytes 147464 | tf_op jit(solution)/shard_map/ppermute | solution.py:579
  25.8 4.4 %collective-permute-start.14 = (f32[3,16,128]{2,1,0:T(8,128)S(1)}, f32[3,16,128]{2,1,0:T(8,128)S(1)}, u32[]{:S(2)}, u32[]{:S(2)}) collective-permute-start(f32[3,16,128]{2,1,0:T(8,128)S(1)} %get-tuple-element.139.refs_5_), channel_id=1, source_target_pairs={{0,1},{1,0},{2,3},{3,2},{4,5},{5,4},{6,7},{7,6},{8,9},{9,8},{10,11... | collective-permute-start | bytes 73736 | tf_op jit(solution)/shard_map/ppermute | solution.py:579
  26.6 3.6 %collective-permute-start.15 = (f32[3,16,128]{2,1,0:T(8,128)S(1)}, f32[3,16,128]{2,1,0:T(8,128)S(1)}, u32[]{:S(2)}, u32[]{:S(2)}) collective-permute-start(f32[3,16,128]{2,1,0:T(8,128)S(1)} %get-tuple-element.140.refs_6_), channel_id=1, source_target_pairs={{0,3},{1,2},{2,1},{3,0},{4,7},{5,6},{6,5},{7,4},{8,11},{9,10},{10,... | collective-permute-start | bytes 73736 | tf_op jit(solution)/shard_map/ppermute | solution.py:579
  30.3 9.6 %collective-permute-start.18 = (f32[3,64,128]{2,1,0:T(8,128)S(1)}, f32[3,64,128]{2,1,0:T(8,128)S(1)}, u32[]{:S(2)}, u32[]{:S(2)}) collective-permute-start(f32[3,64,128]{2,1,0:T(8,128)S(1)} %get-tuple-element.153.refs_4_), channel_id=1, source_target_pairs={{0,4},{1,5},{2,6},{3,7},{4,0},{5,1},{6,2},{7,3},{8,12},{9,13},{10,... | collective-permute-start | bytes 294920 | tf_op jit(solution)/shard_map/ppermute | solution.py:579
  30.4 6.8 %collective-permute-start.16 = (f32[3,32,128]{2,1,0:T(8,128)S(1)}, f32[3,32,128]{2,1,0:T(8,128)S(1)}, u32[]{:S(2)}, u32[]{:S(2)}) collective-permute-start(f32[3,32,128]{2,1,0:T(8,128)S(1)} %get-tuple-element.149.refs_0_), channel_id=1, source_target_pairs={{0,1},{1,0},{2,3},{3,2},{4,8},{5,9},{6,10},{7,11},{8,4},{9,5},{10,... | collective-permute-start | bytes 147464 | tf_op jit(solution)/shard_map/ppermute | solution.py:579
  34.1 4.1 %collective-permute-start.17 = (f32[3,32,128]{2,1,0:T(8,128)S(1)}, f32[3,32,128]{2,1,0:T(8,128)S(1)}, u32[]{:S(2)}, u32[]{:S(2)}) collective-permute-start(f32[3,32,128]{2,1,0:T(8,128)S(1)} %get-tuple-element.150.refs_1_), channel_id=1, source_target_pairs={{0,1},{1,0},{2,3},{3,2},{4,8},{5,9},{6,10},{7,11},{8,4},{9,5},{10,... | collective-permute-start | bytes 147464 | tf_op jit(solution)/shard_map/ppermute | solution.py:579
  34.2 5.7 %collective-permute-start.19 = (f32[3,16,128]{2,1,0:T(8,128)S(1)}, f32[3,16,128]{2,1,0:T(8,128)S(1)}, u32[]{:S(2)}, u32[]{:S(2)}) collective-permute-start(f32[3,16,128]{2,1,0:T(8,128)S(1)} %get-tuple-element.155.refs_6_), channel_id=1, source_target_pairs={{0,1},{1,0},{2,3},{3,2},{4,5},{5,4},{6,7},{7,6},{8,9},{9,8},{10,11... | collective-permute-start | bytes 73736 | tf_op jit(solution)/shard_map/ppermute | solution.py:579
  34.2 5.7 %collective-permute-start.20 = (f32[3,16,128]{2,1,0:T(8,128)S(1)}, f32[3,16,128]{2,1,0:T(8,128)S(1)}, u32[]{:S(2)}, u32[]{:S(2)}) collective-permute-start(f32[3,16,128]{2,1,0:T(8,128)S(1)} %get-tuple-element.156.refs_7_), channel_id=1, source_target_pairs={{0,3},{1,2},{2,1},{3,0},{4,7},{5,6},{6,5},{7,4},{8,11},{9,10},{10,... | collective-permute-start | bytes 73736 | tf_op jit(solution)/shard_map/ppermute | solution.py:579

commit v7 on v6

--- a/solution.py
+++ b/solution.py
@@ -103,9 +103,9 @@
 
 
 def setup_kernel(
-    kinds_ref, rc_in, v_ref, moduli_ref, density_ref, partner_ref, active_ref,
-    kx_ref, ky_ref, kz_ref, kick_ref, row_kick_ref, high_ky_ref, push_ref, pick_ref, chosen_ref, rc_ref, held_ref,
-    turned_ref, live_ref, sem,
+    kinds_ref, rc_in, d_ref, moduli_ref, density_ref, partner_ref, active_ref,
+    kx_ref, ky_ref, kz_ref, kick_ref, row_kick_ref, high_ky_ref, push_ref, pick_ref, chosen_ref, rc_ref,
+    turned_ref, live_ref,
 ):
     planes, rows, cols = kinds_ref.shape
     place = here_in_mesh()
@@ -115,8 +115,7 @@
     col = lax.broadcasted_iota(jnp.int32, (rows, cols), 1)
     inside = (col < cols - 1) & ((row < rows - 1) | jnp.logical_not(last_y))
 
-    velocities = pltpu.make_async_copy(v_ref, held_ref, sem)
-    velocities.start()
+    del rc_in, d_ref
 
     body, blocks = place[4], place[3]
     start = place[2] * rows
@@ -180,9 +179,8 @@
         kz_ref[i] = both + rows_behind(both, row)
         return here
 
-    lax.fori_loop(0, planes, plane, jnp.zeros((rows, cols), jnp.float32), unroll=math.gcd(4, planes))
+    lax.fori_loop(0, planes, plane, jnp.zeros((rows, cols), jnp.float32), unroll=math.gcd(16, planes))
     push_ref[...] = push_ref[...] * kick_ref[planes - 1]
-    velocities.wait()
 
 
 def rows_behind(value, row, first=0.0):
@@ -458,7 +456,8 @@
 def arrivals(refs, n_got):
     sent, got, edges, refs = refs[:4], refs[4 : 4 + n_got], refs[4 + n_got : 8 + n_got], refs[8 + n_got :]
     if n_got == 5:
-        got = [got[0], tuple(got[1:3]), *got[3:]]
+        a, half, rest, c, d = got
+        got = [a, (half, rest), c, d]
     return sent, got, edges, refs
 
 
@@ -592,14 +591,14 @@
     )
     got_e = passed(spare, "e")
     got = [passed(block, name) for block, name in zip(sent, "abcd")]
-    kx, ky, kz, kick, row_kick, high_ky, push_scale, pick, chosen, got[2], v = call(
+    kx, ky, kz, kick, row_kick, high_ky, push_scale, pick, chosen, got[2] = call(
         setup_kernel,
         [vmem(block)] * 4 + [vmem((2, *side)), vmem(side), vmem(face), vmem((lanes, lanes))]
-        + [pltpu.SMEM((rows + 1,), jnp.int32), vmem((4, *side)), vmem(state)],
-        [kinds, got[2], v, moduli, density, partner, active],
-        [None, None, hbm] + [smem] * 4,
+        + [pltpu.SMEM((rows + 1,), jnp.int32), vmem((4, *side))],
+        [kinds, got[2], d, moduli, density, partner, active],
+        [None, None, None] + [smem] * 4,
         aliases={1: 9},
-        scratch=[vmem((rows + tile, lanes)), vmem((rows + tile, cols)), pltpu.SemaphoreType.DMA],
+        scratch=[vmem((rows + tile, lanes)), vmem((rows + tile, cols))],
         flops=8_000_000,
     )
     pair_scratch = [vmem((cols, lanes))] * 3 + [vmem((cols * rows // lanes, lanes))]
@@ -616,7 +615,7 @@
             )
             push_scale, sides[0] = lax.optimization_barrier((push_scale, sides[0]))
         else:
-            got_e, got_half = passed(rest, "rest"), passed(half, "b")
+            got_half, got_e = passed(half, "b"), passed(rest, "rest")
             got = [passed(sent[0], "a"), got_half, got_e, passed(sent[2], "c"), passed(sent[3], "d")]
             u, w, *sides = call(
                 functools.partial(interior_kernel, last),

time: 41.4 us -> 41.2 us (level)
  waiting for transfers between devices: 3.26 us -> 3.73 us
    ppermute x21, waiting for transfers between devices: 3.26 us -> 3.73 us  [passed(): return lax.ppermute(block, AXES, route[name])]
  transfers between devices with their start and end apart: 21 -> 21, of which waited for: 3 -> 3; matrix products, arithmetic and copies ran while one was open for 0% -> 0% of each run, Pallas kernels for 27% -> 26%
where the time goes in v7:
time: 41.2 us; the launch traced here: 41.1 us
  starting transfers between devices  21.8 us (53%)
  Pallas kernels  14.4 us (35%)
  waiting for transfers between devices  3.73 us (9%)
  between operations  1.11 us (3%)
    ppermute x21, starting transfers between devices, passed(): return lax.ppermute(block, AXES, route[name])  21.8 us
    pallas_call x15, Pallas kernels, call(): pl.pallas_call(kernel, out_shape=outs, in_specs=specs, out_specs=[pl.Bloc...  14.4 us
    ppermute x21, waiting for transfers between devices, passed(): return lax.ppermute(block, AXES, route[name])  3.73 us
  transfers between devices with their start and end apart: 21, of which 3 were waited for; matrix products, arithmetic and copies ran while one was open for 0% of the time, Pallas kernels for 26%

profile of v7, /device:TPU:8, one launch (start us, length us, event | category | flops | bytes accessed | tf_op | source)
XLA Modules:
  0.0 41.1 jit_solution(13877880250156266284)
XLA Ops:
  0.7 1.5 %shard_map.86 = (f32[4,64,128]{2,1,0:T(8,128)S(1)}, f32[4,64,128]{2,1,0:T(8,128)S(1)}, f32[4,16,128]{2,1,0:T(8,128)S(1)}, f32[4,16,128]{2,1,0:T(8,128)S(1)}, f32...) custom-call(f32[3,16,64,128]{3,2,1,0:T(8,128)} %bitcast.5, s32[16,64,128]{2,1,0:T(8,128)} %bitcast.8), custom_call_target="tpu_custom_call" | custom-call | tf_op jit(solution)/shard_map/pallas_call | solution.py:46
  2.2 1.6 %collective-permute-start.2 = (f32[4,64,128]{2,1,0:T(8,128)S(1)}, f32[4,64,128]{2,1,0:T(8,128)S(1)}, u32[]{:S(2)}, u32[]{:S(2)}) collective-permute-start(f32[4,64,128]{2,1,0:T(8,128)S(1)} %get-tuple-element.90.sb_ref.own_ref.refs_6_), channel_id=1, source_target_pairs={{0,1},{1,0},{2,3},{3,2},{4,8},{5,9},{6,10},{7,11},{8,4},{9,5},{10,... | collective-permute-start | bytes 393224 | tf_op jit(solution)/shard_map/ppermute | solution.py:578
  3.8 0.5 %collective-permute-start = (f32[4,16,128]{2,1,0:T(8,128)S(1)}, f32[4,16,128]{2,1,0:T(8,128)S(1)}, u32[]{:S(2)}, u32[]{:S(2)}) collective-permute-start(f32[4,16,128]{2,1,0:T(8,128)S(1)} %get-tuple-element.80.sc_ref.refs_7_), channel_id=1, source_target_pairs={{0,1},{1,0},{2,3},{3,2},{4,5},{5,4},{6,7},{7,6},{8,9},{9,8},{10,11... | collective-permute-start | bytes 98312 | tf_op jit(solution)/shard_map/ppermute | solution.py:578
  4.3 1.1 %collective-permute-start.3 = (f32[4,16,128]{2,1,0:T(8,128)S(1)}, f32[4,16,128]{2,1,0:T(8,128)S(1)}, u32[]{:S(2)}, u32[]{:S(2)}) collective-permute-start(f32[4,16,128]{2,1,0:T(8,128)S(1)} %get-tuple-element.91.sd_ref.refs_8_), channel_id=1, source_target_pairs={{0,3},{1,2},{2,1},{3,0},{4,7},{5,6},{6,5},{7,4},{8,11},{9,10},{10,... | collective-permute-start | bytes 98312 | tf_op jit(solution)/shard_map/ppermute | solution.py:578
  5.5 1.4 %shard_map.87 = (f32[16,64,128]{2,1,0:T(8,128)S(1)}, f32[16,64,128]{2,1,0:T(8,128)S(1)}, f32[16,64,128]{2,1,0:T(8,128)S(1)}, f32[16,64,128]{2,1,0:T(8,128)S(1)},...) custom-call(s32[16,64,128]{2,1,0:T(8,128)S(1)} %bitcast.9, ...), custom_call_target="tpu_custom_call", output_to_operand_aliasing={{9}: (1, {})} | custom-call | flops 8000000 | tf_op jit(solution)/shard_map/pallas_call | solution.py:46
  6.9 3.2 %collective-permute-start.4 = (f32[1,128]{1,0:T(1,128)S(1)}, f32[1,128]{1,0:T(1,128)S(1)}, u32[]{:S(2)}, u32[]{:S(2)}) collective-permute-start(f32[1,128]{1,0:T(1,128)S(1)} %get-tuple-element.93), channel_id=1, source_target_pairs={{0,5},{1,6},{2,7},{3,4},{4,9},{5,10},{6,11},{7,8},{8,13},{9,14},{1... | collective-permute-start | bytes 1544 | tf_op jit(solution)/shard_map/ppermute | solution.py:578
  10.1 2.0 %shard_map.88 = (f32[3,16,64,128]{3,2,1,0:T(8,128)S(1)}, f32[3,16,64,128]{3,2,1,0:T(8,128)S(1)}, f32[3,16,128]{2,1,0:T(8,128)S(1)}, f32[3,16,128]{2,1,0:T(8,128)S(1)}) custom-call(f32[3,16,64,128]{3,2,1,0:T(8,128)S(1)} %bitcast.7, f32[3,16,64,128]{3,2,1,0:T(8,128)S(1)} %bitcast.10, f32[16,64,128]{2,1,0:T(8,128)S(1)} %get-tuple-element.81.kx_ref.kx_in, ...), custom_call_target="tpu_custom_call" | custom-call | tf_op jit(solution)/shard_map/pallas_call | solution.py:46
  12.2 0.7 %shard_map.89 = (f32[16,64,128]{2,1,0:T(8,128)S(1)}, f32[16,64,128]{2,1,0:T(8,128)S(1)}, f32[16,64,128]{2,1,0:T(8,128)S(1)}, f32[64,128]{1,0:T(8,128)S(1)}, f32[...) custom-call(f32[4,64,128]{2,1,0:T(8,128)S(1)} %get-tuple-element.89., ...), custom_call_target="tpu_custom_call", output_to_operand_aliasing={{0}: (12, {}), {1}: (13, {}), {2}: (14, {})} | custom-call | tf_op jit(solution)/shard_map/pallas_call | solution.py:46
  13.0 0.1 shard_map.91
  13.1 2.5 %collective-permute-start.6 = (f32[3,64,128]{2,1,0:T(8,128)S(1)}, f32[3,64,128]{2,1,0:T(8,128)S(1)}, u32[]{:S(2)}, u32[]{:S(2)}) collective-permute-start(f32[3,64,128]{2,1,0:T(8,128)S(1)} %get-tuple-element.121.refs_3_), channel_id=1, source_target_pairs={{0,4},{1,5},{2,6},{3,7},{4,0},{5,1},{6,2},{7,3},{8,12},{9,13},{10,... | collective-permute-start | bytes 294920 | tf_op jit(solution)/shard_map/ppermute | solution.py:578
  15.6 2.1 %collective-permute-start.7 = (f32[3,32,128]{2,1,0:T(8,128)S(1)}, f32[3,32,128]{2,1,0:T(8,128)S(1)}, u32[]{:S(2)}, u32[]{:S(2)}) collective-permute-start(f32[3,32,128]{2,1,0:T(8,128)S(1)} %get-tuple-element.125.own_half_ref), channel_id=1, source_target_pairs={{0,1},{1,0},{2,3},{3,2},{4,8},{5,9},{6,10},{7,11},{8,4},{9,5},{10,... | collective-permute-start | bytes 147464 | tf_op jit(solution)/shard_map/ppermute | solution.py:578
  17.7 0.0 collective-permute-start.8
  17.7 1.2 %collective-permute-start.10 = (f32[3,16,128]{2,1,0:T(8,128)S(1)}, f32[3,16,128]{2,1,0:T(8,128)S(1)}, u32[]{:S(2)}, u32[]{:S(2)}) collective-permute-start(f32[3,16,128]{2,1,0:T(8,128)S(1)} %get-tuple-element.124.refs_6_), channel_id=1, source_target_pairs={{0,3},{1,2},{2,1},{3,0},{4,7},{5,6},{6,5},{7,4},{8,11},{9,10},{10,... | collective-permute-start | bytes 73736 | tf_op jit(solution)/shard_map/ppermute | solution.py:578
  19.0 1.8 %shard_map.92 = (f32[3,16,64,128]{3,2,1,0:T(8,128)S(1)}, f32[3,16,64,128]{3,2,1,0:T(8,128)S(1)}, f32[3,16,128]{2,1,0:T(8,128)S(1)}, f32[3,16,128]{2,1,0:T(8,128)S(1)}) custom-call(f32[3,16,64,128]{3,2,1,0:T(8,128)S(1)} %get-tuple-element.87.refs_2_.u_in, ...), custom_call_target="tpu_custom_call", output_to_operand_aliasing={{0}: (0, {}), {1}: (1, {})} | custom-call | flops 20000000 | tf_op jit(solution)/shard_map/pallas_call | solution.py:46
  20.8 1.0 %collective-permute-done.8.rest_ref.refs_9_ = f32[3,32,128]{2,1,0:T(8,128)S(1)} collective-permute-done((f32[3,32,128]{2,1,0:T(8,128)S(1)}, f32[3,32,128]{2,1,0:T(8,128)S(1)}, u32[]{:S(2)}, u32[]{:S(2)}) %collective-permute-start.8) | collective-permute-done | bytes 49184 | tf_op jit(solution)/shard_map/ppermute | solution.py:578
  21.8 0.1 shard_map.94
  21.9 0.1 collective-permute-start.11
  22.0 3.4 %collective-permute-start.12 = (f32[3,32,128]{2,1,0:T(8,128)S(1)}, f32[3,32,128]{2,1,0:T(8,128)S(1)}, u32[]{:S(2)}, u32[]{:S(2)}) collective-permute-start(f32[3,32,128]{2,1,0:T(8,128)S(1)} %get-tuple-element.139.own_half_ref), channel_id=1, source_target_pairs={{0,1},{1,0},{2,3},{3,2},{4,8},{5,9},{6,10},{7,11},{8,4},{9,5},{10,... | collective-permute-start | bytes 147464 | tf_op jit(solution)/shard_map/ppermute | solution.py:578
  25.4 0.0 collective-permute-start.13
  25.4 0.6 %collective-permute-start.14 = (f32[3,16,128]{2,1,0:T(8,128)S(1)}, f32[3,16,128]{2,1,0:T(8,128)S(1)}, u32[]{:S(2)}, u32[]{:S(2)}) collective-permute-start(f32[3,16,128]{2,1,0:T(8,128)S(1)} %get-tuple-element.137.refs_5_), channel_id=1, source_target_pairs={{0,1},{1,0},{2,3},{3,2},{4,5},{5,4},{6,7},{7,6},{8,9},{9,8},{10,11... | collective-permute-start | bytes 73736 | tf_op jit(solution)/shard_map/ppermute | solution.py:578
  26.0 0.4 collective-permute-start.15
  26.4 1.8 %shard_map.95 = (f32[3,16,64,128]{3,2,1,0:T(8,128)S(1)}, f32[3,16,64,128]{3,2,1,0:T(8,128)S(1)}, f32[3,16,128]{2,1,0:T(8,128)S(1)}, f32[3,16,128]{2,1,0:T(8,128)S(1)}) custom-call(f32[3,16,64,128]{3,2,1,0:T(8,128)S(1)} %get-tuple-element.117.refs_0_.u_in, ...), custom_call_target="tpu_custom_call", output_to_operand_aliasing={{0}: (0, {}), {1}: (1, {})} | custom-call | flops 20000000 | tf_op jit(solution)/shard_map/pallas_call | solution.py:46
  28.2 1.4 %collective-permute-done.13.rest_ref.refs_9_ = f32[3,32,128]{2,1,0:T(8,128)S(1)} collective-permute-done((f32[3,32,128]{2,1,0:T(8,128)S(1)}, f32[3,32,128]{2,1,0:T(8,128)S(1)}, u32[]{:S(2)}, u32[]{:S(2)}) %collective-permute-start.13) | collective-permute-done | bytes 49184 | tf_op jit(solution)/shard_map/ppermute | solution.py:578
  29.7 0.3 shard_map.97
  30.0 0.1 collective-permute-start.18
  30.0 4.0 %collective-permute-start.16 = (f32[3,32,128]{2,1,0:T(8,128)S(1)}, f32[3,32,128]{2,1,0:T(8,128)S(1)}, u32[]{:S(2)}, u32[]{:S(2)}) collective-permute-start(f32[3,32,128]{2,1,0:T(8,128)S(1)} %get-tuple-element.147.refs_0_), channel_id=1, source_target_pairs={{0,1},{1,0},{2,3},{3,2},{4,8},{5,9},{6,10},{7,11},{8,4},{9,5},{10,... | collective-permute-start | bytes 147464 | tf_op jit(solution)/shard_map/ppermute | solution.py:578
  34.0 0.0 collective-permute-start.17
  34.0 0.9 %collective-permute-start.20 = (f32[3,16,128]{2,1,0:T(8,128)S(1)}, f32[3,16,128]{2,1,0:T(8,128)S(1)}, u32[]{:S(2)}, u32[]{:S(2)}) collective-permute-start(f32[3,16,128]{2,1,0:T(8,128)S(1)} %get-tuple-element.154.refs_7_), channel_id=1, source_target_pairs={{0,3},{1,2},{2,1},{3,0},{4,7},{5,6},{6,5},{7,4},{8,11},{9,10},{10,... | collective-permute-start | bytes 73736 | tf_op jit(solution)/shard_map/ppermute | solution.py:578
  34.9 1.9 %shard_map.98 = (f32[3,16,64,128]{3,2,1,0:T(8,128)S(1)}, f32[3,16,64,128]{3,2,1,0:T(8,128)S(1)}) custom-call(f32[3,16,64,128]{3,2,1,0:T(8,128)S(1)} %get-tuple-element.131.refs_0_.u_in, f32[3,16,64,128]{3,2,1,0:T(8,128)S(1)} %get-tuple-element.132.w_in, f32[16,64,128]{2,1,0:T(8,128)S(1)} %get-tuple-element.96.kx_ref, ...), custom_call_target="tpu_custom_call", output_to_operand_aliasing={{0}: (0, {}), {1}: (1, {})} | custom-call | flops 20000000 | tf_op jit(solution)/shard_map/pallas_call | solution.py:46
  36.8 1.3 %collective-permute-done.17.refs_3_.refs_10_ = f32[3,32,128]{2,1,0:T(8,128)S(1)} collective-permute-done((f32[3,32,128]{2,1,0:T(8,128)S(1)}, f32[3,32,128]{2,1,0:T(8,128)S(1)}, u32[]{:S(2)}, u32[]{:S(2)}) %collective-permute-start.17) | collective-permute-done | bytes 49184 | tf_op jit(solution)/shard_map/ppermute | solution.py:578
  38.1 1.7 %shard_map.99 = (f32[3,16,64,128]{3,2,1,0:T(8,128)}, f32[3,16,64,128]{3,2,1,0:T(8,128)}, f32[64,128]{1,0:T(8,128)S(1)}) custom-call(f32[3,32,128]{2,1,0:T(8,128)S(1)} %get-tuple-element.147.refs_0_, f32[3,32,128]{2,1,0:T(8,128)S(1)} %get-tuple-element.148.refs_1_, f32[3,32,128]{2,1,0:T(8,128)S(1)} %collective-permute-done.16.refs_2_.refs_9_, ...), custom_call_target="tpu_custom_call" | custom-call | flops 20000000 | tf_op jit(solution)/shard_map/pallas_call | solution.py:46
  39.8 1.1 %shard_map.100 = (f32[3,16,64,128]{3,2,1,0:T(8,128)}, f32[3,16,64,128]{3,2,1,0:T(8,128)}) custom-call(f32[3,16,64,128]{3,2,1,0:T(8,128)S(1)} %get-tuple-element.145.refs_6_.refs_0_, f32[3,16,64,128]{3,2,1,0:T(8,128)S(1)} %get-tuple-element.146.refs_7_.refs_1_, ...), custom_call_target="tpu_custom_call", output_to_operand_aliasing={{0}: (2, {}), {1}: (3, {})} | custom-call | tf_op jit(solution)/shard_map/pallas_call | solution.py:46
  (39 shorter events, 0.1 us)
Async XLA Ops:
  0.6 4.8 %copy-start.1 = (s32[1,16,64,128]{3,2,1,0:T(8,128)S(1)}, s32[1,16,64,128]{3,2,1,0:T(8,128)}, u32[]{:S(2)}) copy-start(s32[1,16,64,128]{3,2,1,0:T(8,128)} %param.9) | copy-start | bytes 1572868
  0.6 4.8 %copy-start = (f32[1,3,16,64,128]{4,3,2,1,0:T(8,128)S(1)}, f32[1,3,16,64,128]{4,3,2,1,0:T(8,128)}, u32[]{:S(2)}) copy-start(f32[1,3,16,64,128]{4,3,2,1,0:T(8,128)} %param.7) | copy-start | bytes 4718596
  0.7 4.8 %copy-start.3 = (f32[8]{0:T(128)S(1)}, f32[8]{0:T(128)}, u32[]{:S(2)}) copy-start(f32[8]{0:T(128)} %moduli_ref.3) | copy-start | bytes 100
  0.7 4.8 %copy-start.5 = (s32[256]{0:T(256)S(1)}, s32[256]{0:T(256)}, u32[]{:S(2)}) copy-start(s32[256]{0:T(256)} %active_ref.1) | copy-start | bytes 3076
  0.7 4.8 %copy-start.4 = (s32[256]{0:T(256)S(1)}, s32[256]{0:T(256)}, u32[]{:S(2)}) copy-start(s32[256]{0:T(256)} %partner_ref.1) | copy-start | bytes 3076
  0.7 4.8 %copy-start.6 = (f32[8]{0:T(128)S(1)}, f32[8]{0:T(128)}, u32[]{:S(2)}) copy-start(f32[8]{0:T(128)} %density_ref.1) | copy-start | bytes 100
  2.2 8.0 %copy-start.2 = (f32[1,3,16,64,128]{4,3,2,1,0:T(8,128)S(1)}, f32[1,3,16,64,128]{4,3,2,1,0:T(8,128)}, u32[]{:S(2)}) copy-start(f32[1,3,16,64,128]{4,3,2,1,0:T(8,128)} %param.8) | copy-start | bytes 4718596
  2.2 10.0 %collective-permute-start.2 = (f32[4,64,128]{2,1,0:T(8,128)S(1)}, f32[4,64,128]{2,1,0:T(8,128)S(1)}, u32[]{:S(2)}, u32[]{:S(2)}) collective-permute-start(f32[4,64,128]{2,1,0:T(8,128)S(1)} %get-tuple-element.90.sb_ref.own_ref.refs_6_), channel_id=1, source_target_pairs={{0,1},{1,0},{2,3},{3,2},{4,8},{5,9},{6,10},{7,11},{8,4},{9,5},{10,... | collective-permute-start | bytes 393224 | tf_op jit(solution)/shard_map/ppermute | solution.py:578
  3.8 8.4 %collective-permute-start.1 = (f32[4,64,128]{2,1,0:T(8,128)S(1)}, f32[4,64,128]{2,1,0:T(8,128)S(1)}, u32[]{:S(2)}, u32[]{:S(2)}) collective-permute-start(f32[4,64,128]{2,1,0:T(8,128)S(1)} %get-tuple-element.89.sa_ref.refs_5_), channel_id=1, source_target_pairs={{0,4},{1,5},{2,6},{3,7},{4,0},{5,1},{6,2},{7,3},{8,12},{9,13},{10,... | collective-permute-start | bytes 393224 | tf_op jit(solution)/shard_map/ppermute | solution.py:578
  3.8 8.3 %collective-permute-start.5 = (f32[3,64,128]{2,1,0:T(8,128)S(1)}, f32[3,64,128]{2,1,0:T(8,128)S(1)}, u32[]{:S(2)}, u32[]{:S(2)}) collective-permute-start(f32[3,64,128]{2,1,0:T(8,128)S(1)} %get-tuple-element.109), channel_id=1, source_target_pairs={{0,1},{1,0},{2,3},{3,2},{4,5},{5,4},{6,7},{7,6},{8,9},{9,8},{10,11... | collective-permute-start | bytes 294920 | tf_op jit(solution)/shard_map/ppermute | solution.py:578
  3.8 1.6 %collective-permute-start = (f32[4,16,128]{2,1,0:T(8,128)S(1)}, f32[4,16,128]{2,1,0:T(8,128)S(1)}, u32[]{:S(2)}, u32[]{:S(2)}) collective-permute-start(f32[4,16,128]{2,1,0:T(8,128)S(1)} %get-tuple-element.80.sc_ref.refs_7_), channel_id=1, source_target_pairs={{0,1},{1,0},{2,3},{3,2},{4,5},{5,4},{6,7},{7,6},{8,9},{9,8},{10,11... | collective-permute-start | bytes 98312 | tf_op jit(solution)/shard_map/ppermute | solution.py:578
  4.3 7.9 %collective-permute-start.3 = (f32[4,16,128]{2,1,0:T(8,128)S(1)}, f32[4,16,128]{2,1,0:T(8,128)S(1)}, u32[]{:S(2)}, u32[]{:S(2)}) collective-permute-start(f32[4,16,128]{2,1,0:T(8,128)S(1)} %get-tuple-element.91.sd_ref.refs_8_), channel_id=1, source_target_pairs={{0,3},{1,2},{2,1},{3,0},{4,7},{5,6},{6,5},{7,4},{8,11},{9,10},{10,... | collective-permute-start | bytes 98312 | tf_op jit(solution)/shard_map/ppermute | solution.py:578
  6.9 5.3 %collective-permute-start.4 = (f32[1,128]{1,0:T(1,128)S(1)}, f32[1,128]{1,0:T(1,128)S(1)}, u32[]{:S(2)}, u32[]{:S(2)}) collective-permute-start(f32[1,128]{1,0:T(1,128)S(1)} %get-tuple-element.93), channel_id=1, source_target_pairs={{0,5},{1,6},{2,7},{3,4},{4,9},{5,10},{6,11},{7,8},{8,13},{9,14},{1... | collective-permute-start | bytes 1544 | tf_op jit(solution)/shard_map/ppermute | solution.py:578
  13.1 8.7 %collective-permute-start.6 = (f32[3,64,128]{2,1,0:T(8,128)S(1)}, f32[3,64,128]{2,1,0:T(8,128)S(1)}, u32[]{:S(2)}, u32[]{:S(2)}) collective-permute-start(f32[3,64,128]{2,1,0:T(8,128)S(1)} %get-tuple-element.121.refs_3_), channel_id=1, source_target_pairs={{0,4},{1,5},{2,6},{3,7},{4,0},{5,1},{6,2},{7,3},{8,12},{9,13},{10,... | collective-permute-start | bytes 294920 | tf_op jit(solution)/shard_map/ppermute | solution.py:578
  15.6 5.2 %collective-permute-start.7 = (f32[3,32,128]{2,1,0:T(8,128)S(1)}, f32[3,32,128]{2,1,0:T(8,128)S(1)}, u32[]{:S(2)}, u32[]{:S(2)}) collective-permute-start(f32[3,32,128]{2,1,0:T(8,128)S(1)} %get-tuple-element.125.own_half_ref), channel_id=1, source_target_pairs={{0,1},{1,0},{2,3},{3,2},{4,8},{5,9},{6,10},{7,11},{8,4},{9,5},{10,... | collective-permute-start | bytes 147464 | tf_op jit(solution)/shard_map/ppermute | solution.py:578
  17.7 4.1 %collective-permute-start.8 = (f32[3,32,128]{2,1,0:T(8,128)S(1)}, f32[3,32,128]{2,1,0:T(8,128)S(1)}, u32[]{:S(2)}, u32[]{:S(2)}) collective-permute-start(f32[3,32,128]{2,1,0:T(8,128)S(1)} %get-tuple-element.126.own_rest_ref), channel_id=1, source_target_pairs={{0,1},{1,0},{2,3},{3,2},{4,8},{5,9},{6,10},{7,11},{8,4},{9,5},{10,... | collective-permute-start | bytes 147464 | tf_op jit(solution)/shard_map/ppermute | solution.py:578
  17.7 4.1 %collective-permute-start.9 = (f32[3,16,128]{2,1,0:T(8,128)S(1)}, f32[3,16,128]{2,1,0:T(8,128)S(1)}, u32[]{:S(2)}, u32[]{:S(2)}) collective-permute-start(f32[3,16,128]{2,1,0:T(8,128)S(1)} %get-tuple-element.123.refs_5_), channel_id=1, source_target_pairs={{0,1},{1,0},{2,3},{3,2},{4,5},{5,4},{6,7},{7,6},{8,9},{9,8},{10,11... | collective-permute-start | bytes 73736 | tf_op jit(solution)/shard_map/ppermute | solution.py:578
  17.7 4.1 %collective-permute-start.10 = (f32[3,16,128]{2,1,0:T(8,128)S(1)}, f32[3,16,128]{2,1,0:T(8,128)S(1)}, u32[]{:S(2)}, u32[]{:S(2)}) collective-permute-start(f32[3,16,128]{2,1,0:T(8,128)S(1)} %get-tuple-element.124.refs_6_), channel_id=1, source_target_pairs={{0,3},{1,2},{2,1},{3,0},{4,7},{5,6},{6,5},{7,4},{8,11},{9,10},{10,... | collective-permute-start | bytes 73736 | tf_op jit(solution)/shard_map/ppermute | solution.py:578
  21.9 7.7 %collective-permute-start.11 = (f32[3,64,128]{2,1,0:T(8,128)S(1)}, f32[3,64,128]{2,1,0:T(8,128)S(1)}, u32[]{:S(2)}, u32[]{:S(2)}) collective-permute-start(f32[3,64,128]{2,1,0:T(8,128)S(1)} %get-tuple-element.135.refs_3_), channel_id=1, source_target_pairs={{0,4},{1,5},{2,6},{3,7},{4,0},{5,1},{6,2},{7,3},{8,12},{9,13},{10,... | collective-permute-start | bytes 294920 | tf_op jit(solution)/shard_map/ppermute | solution.py:578
  22.0 6.2 %collective-permute-start.12 = (f32[3,32,128]{2,1,0:T(8,128)S(1)}, f32[3,32,128]{2,1,0:T(8,128)S(1)}, u32[]{:S(2)}, u32[]{:S(2)}) collective-permute-start(f32[3,32,128]{2,1,0:T(8,128)S(1)} %get-tuple-element.139.own_half_ref), channel_id=1, source_target_pairs={{0,1},{1,0},{2,3},{3,2},{4,8},{5,9},{6,10},{7,11},{8,4},{9,5},{10,... | collective-permute-start | bytes 147464 | tf_op jit(solution)/shard_map/ppermute | solution.py:578
  25.4 4.2 %collective-permute-start.13 = (f32[3,32,128]{2,1,0:T(8,128)S(1)}, f32[3,32,128]{2,1,0:T(8,128)S(1)}, u32[]{:S(2)}, u32[]{:S(2)}) collective-permute-start(f32[3,32,128]{2,1,0:T(8,128)S(1)} %get-tuple-element.140.own_rest_ref), channel_id=1, source_target_pairs={{0,1},{1,0},{2,3},{3,2},{4,8},{5,9},{6,10},{7,11},{8,4},{9,5},{10,... | collective-permute-start | bytes 147464 | tf_op jit(solution)/shard_map/ppermute | solution.py:578
  25.4 4.2 %collective-permute-start.14 = (f32[3,16,128]{2,1,0:T(8,128)S(1)}, f32[3,16,128]{2,1,0:T(8,128)S(1)}, u32[]{:S(2)}, u32[]{:S(2)}) collective-permute-start(f32[3,16,128]{2,1,0:T(8,128)S(1)} %get-tuple-element.137.refs_5_), channel_id=1, source_target_pairs={{0,1},{1,0},{2,3},{3,2},{4,5},{5,4},{6,7},{7,6},{8,9},{9,8},{10,11... | collective-permute-start | bytes 73736 | tf_op jit(solution)/shard_map/ppermute | solution.py:578
  26.0 3.6 %collective-permute-start.15 = (f32[3,16,128]{2,1,0:T(8,128)S(1)}, f32[3,16,128]{2,1,0:T(8,128)S(1)}, u32[]{:S(2)}, u32[]{:S(2)}) collective-permute-start(f32[3,16,128]{2,1,0:T(8,128)S(1)} %get-tuple-element.138.refs_6_), channel_id=1, source_target_pairs={{0,3},{1,2},{2,1},{3,0},{4,7},{5,6},{6,5},{7,4},{8,11},{9,10},{10,... | collective-permute-start | bytes 73736 | tf_op jit(solution)/shard_map/ppermute | solution.py:578
  30.0 9.8 %collective-permute-start.18 = (f32[3,64,128]{2,1,0:T(8,128)S(1)}, f32[3,64,128]{2,1,0:T(8,128)S(1)}, u32[]{:S(2)}, u32[]{:S(2)}) collective-permute-start(f32[3,64,128]{2,1,0:T(8,128)S(1)} %get-tuple-element.151.refs_4_), channel_id=1, source_target_pairs={{0,4},{1,5},{2,6},{3,7},{4,0},{5,1},{6,2},{7,3},{8,12},{9,13},{10,... | collective-permute-start | bytes 294920 | tf_op jit(solution)/shard_map/ppermute | solution.py:578
  30.0 6.8 %collective-permute-start.16 = (f32[3,32,128]{2,1,0:T(8,128)S(1)}, f32[3,32,128]{2,1,0:T(8,128)S(1)}, u32[]{:S(2)}, u32[]{:S(2)}) collective-permute-start(f32[3,32,128]{2,1,0:T(8,128)S(1)} %get-tuple-element.147.refs_0_), channel_id=1, source_target_pairs={{0,1},{1,0},{2,3},{3,2},{4,8},{5,9},{6,10},{7,11},{8,4},{9,5},{10,... | collective-permute-start | bytes 147464 | tf_op jit(solution)/shard_map/ppermute | solution.py:578
  34.0 4.1 %collective-permute-start.17 = (f32[3,32,128]{2,1,0:T(8,128)S(1)}, f32[3,32,128]{2,1,0:T(8,128)S(1)}, u32[]{:S(2)}, u32[]{:S(2)}) collective-permute-start(f32[3,32,128]{2,1,0:T(8,128)S(1)} %get-tuple-element.148.refs_1_), channel_id=1, source_target_pairs={{0,1},{1,0},{2,3},{3,2},{4,8},{5,9},{6,10},{7,11},{8,4},{9,5},{10,... | collective-permute-start | bytes 147464 | tf_op jit(solution)/shard_map/ppermute | solution.py:578
  34.0 5.7 %collective-permute-start.19 = (f32[3,16,128]{2,1,0:T(8,128)S(1)}, f32[3,16,128]{2,1,0:T(8,128)S(1)}, u32[]{:S(2)}, u32[]{:S(2)}) collective-permute-start(f32[3,16,128]{2,1,0:T(8,128)S(1)} %get-tuple-element.153.refs_6_), channel_id=1, source_target_pairs={{0,1},{1,0},{2,3},{3,2},{4,5},{5,4},{6,7},{7,6},{8,9},{9,8},{10,11... | collective-permute-start | bytes 73736 | tf_op jit(solution)/shard_map/ppermute | solution.py:578
  34.0 5.8 %collective-permute-start.20 = (f32[3,16,128]{2,1,0:T(8,128)S(1)}, f32[3,16,128]{2,1,0:T(8,128)S(1)}, u32[]{:S(2)}, u32[]{:S(2)}) collective-permute-start(f32[3,16,128]{2,1,0:T(8,128)S(1)} %get-tuple-element.154.refs_7_), channel_id=1, source_target_pairs={{0,3},{1,2},{2,1},{3,0},{4,7},{5,6},{6,5},{7,4},{8,11},{9,10},{10,... | collective-permute-start | bytes 73736 | tf_op jit(solution)/shard_map/ppermute | solution.py:578

commit v8 on v7

--- a/solution.py
+++ b/solution.py
@@ -363,8 +363,7 @@
     @pl.when(on_face())
     def _():
         def matched(c):
-            turned = jnp.concatenate([half_ref[c], rest_ref[c]], axis=0).T
-            return jnp.concatenate([turned] * (scratch[0].shape[1] // rows), axis=1)
+            return jnp.concatenate([half_ref[c], rest_ref[c]] * (scratch[0].shape[1] // rows), axis=0).T
 
         def own(c):
             return jnp.concatenate([own_half_ref[c], own_rest_ref[c]], axis=0)
@@ -389,9 +388,15 @@
     parts = lanes // rows
     deep = cols // parts
 
+    lane = lax.broadcasted_iota(jnp.int32, (deep, lanes), 1)
+    depth = lax.broadcasted_iota(jnp.int32, (deep, lanes), 0)
+
     def own(c):
-        turned = own_rows(c).T
-        return jnp.concatenate([turned[h * deep : (h + 1) * deep] for h in range(parts)], axis=1)
+        turned = jnp.concatenate([own_rows(c)] * parts, axis=0).T
+        value = turned[0:deep]
+        for h in range(1, parts):
+            value = jnp.where(lane >= h * rows, turned[h * deep : (h + 1) * deep], value)
+        return value
 
     gap = scale * GAP_SCALE
     along = scale * YIELD_SPAN * SPAN
@@ -399,8 +404,6 @@
     fy_ref[...] = matched(1) * along
     spot = lax.broadcasted_iota(jnp.int32, (cols, lanes), 0).astype(jnp.float32)
     fz_ref[...] = matched(2) * along + spot * SPAN
-    lane = lax.broadcasted_iota(jnp.int32, (deep, lanes), 1)
-    depth = lax.broadcasted_iota(jnp.int32, (deep, lanes), 0)
     mine = (depth + lane // rows * deep).astype(jnp.float32)
     op = jnp.exp2(own(0) * gap - BIAS / 2.0)
     oy = own(1) * along
@@ -417,8 +420,12 @@
             soft = jnp.log2(op[some] * fp_ref[m : m + 1] + 2.0**-BIAS) + BIAS
             total = total + weight * soft
         total_ref[some] = total
-    total = total_ref[...]
-    return jnp.concatenate([total[:, h * rows : (h + 1) * rows] for h in range(parts)], axis=0).T
+    turned = jnp.concatenate([total_ref[...]] * parts, axis=0).T
+    column = lax.broadcasted_iota(jnp.int32, (rows, cols), 1)
+    value = turned[0:rows]
+    for h in range(1, parts):
+        value = jnp.where(column >= h * deep, turned[h * rows : (h + 1) * rows], value)
+    return value
 
 
 def last_contact_kernel(*refs):

time: 41.2 us -> 40.8 us (level)
  no operation moved by 1% of the time
where the time goes in v8:
time: 40.8 us; the launch traced here: 40.6 us
  starting transfers between devices  21.4 us (52%)
  Pallas kernels  14.4 us (35%)
  waiting for transfers between devices  3.69 us (9%)
  between operations  1.11 us (3%)
    ppermute x21, starting transfers between devices, passed(): return lax.ppermute(block, AXES, route[name])  21.4 us
    pallas_call x15, Pallas kernels, call(): pl.pallas_call(kernel, out_shape=outs, in_specs=specs, out_specs=[pl.Bloc...  14.4 us
    ppermute x21, waiting for transfers between devices, passed(): return lax.ppermute(block, AXES, route[name])  3.69 us
  transfers between devices with their start and end apart: 21, of which 3 were waited for; matrix products, arithmetic and copies ran while one was open for 0% of the time, Pallas kernels for 26%

profile of v8, /device:TPU:8, one launch (start us, length us, event | category | flops | bytes accessed | tf_op | source)
XLA Modules:
  0.0 40.6 jit_solution(4182489096490634796)
XLA Ops:
  0.7 1.5 %shard_map.86 = (f32[4,64,128]{2,1,0:T(8,128)S(1)}, f32[4,64,128]{2,1,0:T(8,128)S(1)}, f32[4,16,128]{2,1,0:T(8,128)S(1)}, f32[4,16,128]{2,1,0:T(8,128)S(1)}, f32...) custom-call(f32[3,16,64,128]{3,2,1,0:T(8,128)} %bitcast.5, s32[16,64,128]{2,1,0:T(8,128)} %bitcast.8), custom_call_target="tpu_custom_call" | custom-call | tf_op jit(solution)/shard_map/pallas_call | solution.py:46
  2.2 1.6 %collective-permute-start.2 = (f32[4,64,128]{2,1,0:T(8,128)S(1)}, f32[4,64,128]{2,1,0:T(8,128)S(1)}, u32[]{:S(2)}, u32[]{:S(2)}) collective-permute-start(f32[4,64,128]{2,1,0:T(8,128)S(1)} %get-tuple-element.90.sb_ref.own_ref.refs_6_), channel_id=1, source_target_pairs={{0,1},{1,0},{2,3},{3,2},{4,8},{5,9},{6,10},{7,11},{8,4},{9,5},{10,... | collective-permute-start | bytes 393224 | tf_op jit(solution)/shard_map/ppermute | solution.py:585
  3.8 0.5 %collective-permute-start = (f32[4,16,128]{2,1,0:T(8,128)S(1)}, f32[4,16,128]{2,1,0:T(8,128)S(1)}, u32[]{:S(2)}, u32[]{:S(2)}) collective-permute-start(f32[4,16,128]{2,1,0:T(8,128)S(1)} %get-tuple-element.80.sc_ref.refs_7_), channel_id=1, source_target_pairs={{0,1},{1,0},{2,3},{3,2},{4,5},{5,4},{6,7},{7,6},{8,9},{9,8},{10,11... | collective-permute-start | bytes 98312 | tf_op jit(solution)/shard_map/ppermute | solution.py:585
  4.3 1.1 %collective-permute-start.3 = (f32[4,16,128]{2,1,0:T(8,128)S(1)}, f32[4,16,128]{2,1,0:T(8,128)S(1)}, u32[]{:S(2)}, u32[]{:S(2)}) collective-permute-start(f32[4,16,128]{2,1,0:T(8,128)S(1)} %get-tuple-element.91.sd_ref.refs_8_), channel_id=1, source_target_pairs={{0,3},{1,2},{2,1},{3,0},{4,7},{5,6},{6,5},{7,4},{8,11},{9,10},{10,... | collective-permute-start | bytes 98312 | tf_op jit(solution)/shard_map/ppermute | solution.py:585
  5.5 1.4 %shard_map.87 = (f32[16,64,128]{2,1,0:T(8,128)S(1)}, f32[16,64,128]{2,1,0:T(8,128)S(1)}, f32[16,64,128]{2,1,0:T(8,128)S(1)}, f32[16,64,128]{2,1,0:T(8,128)S(1)},...) custom-call(s32[16,64,128]{2,1,0:T(8,128)S(1)} %bitcast.9, ...), custom_call_target="tpu_custom_call", output_to_operand_aliasing={{9}: (1, {})} | custom-call | flops 8000000 | tf_op jit(solution)/shard_map/pallas_call | solution.py:46
  6.9 3.2 %collective-permute-start.4 = (f32[1,128]{1,0:T(1,128)S(1)}, f32[1,128]{1,0:T(1,128)S(1)}, u32[]{:S(2)}, u32[]{:S(2)}) collective-permute-start(f32[1,128]{1,0:T(1,128)S(1)} %get-tuple-element.93), channel_id=1, source_target_pairs={{0,5},{1,6},{2,7},{3,4},{4,9},{5,10},{6,11},{7,8},{8,13},{9,14},{1... | collective-permute-start | bytes 1544 | tf_op jit(solution)/shard_map/ppermute | solution.py:585
  10.1 2.0 %shard_map.88 = (f32[3,16,64,128]{3,2,1,0:T(8,128)S(1)}, f32[3,16,64,128]{3,2,1,0:T(8,128)S(1)}, f32[3,16,128]{2,1,0:T(8,128)S(1)}, f32[3,16,128]{2,1,0:T(8,128)S(1)}) custom-call(f32[3,16,64,128]{3,2,1,0:T(8,128)S(1)} %bitcast.7, f32[3,16,64,128]{3,2,1,0:T(8,128)S(1)} %bitcast.10, f32[16,64,128]{2,1,0:T(8,128)S(1)} %get-tuple-element.81.kx_ref.kx_in, ...), custom_call_target="tpu_custom_call" | custom-call | tf_op jit(solution)/shard_map/pallas_call | solution.py:46
  12.2 0.7 %shard_map.89 = (f32[16,64,128]{2,1,0:T(8,128)S(1)}, f32[16,64,128]{2,1,0:T(8,128)S(1)}, f32[16,64,128]{2,1,0:T(8,128)S(1)}, f32[64,128]{1,0:T(8,128)S(1)}, f32[...) custom-call(f32[4,64,128]{2,1,0:T(8,128)S(1)} %get-tuple-element.89., ...), custom_call_target="tpu_custom_call", output_to_operand_aliasing={{0}: (12, {}), {1}: (13, {}), {2}: (14, {})} | custom-call | tf_op jit(solution)/shard_map/pallas_call | solution.py:46
  13.0 0.1 shard_map.91
  13.1 2.5 %collective-permute-start.6 = (f32[3,64,128]{2,1,0:T(8,128)S(1)}, f32[3,64,128]{2,1,0:T(8,128)S(1)}, u32[]{:S(2)}, u32[]{:S(2)}) collective-permute-start(f32[3,64,128]{2,1,0:T(8,128)S(1)} %get-tuple-element.121.refs_3_), channel_id=1, source_target_pairs={{0,4},{1,5},{2,6},{3,7},{4,0},{5,1},{6,2},{7,3},{8,12},{9,13},{10,... | collective-permute-start | bytes 294920 | tf_op jit(solution)/shard_map/ppermute | solution.py:585
  15.6 2.0 %collective-permute-start.7 = (f32[3,32,128]{2,1,0:T(8,128)S(1)}, f32[3,32,128]{2,1,0:T(8,128)S(1)}, u32[]{:S(2)}, u32[]{:S(2)}) collective-permute-start(f32[3,32,128]{2,1,0:T(8,128)S(1)} %get-tuple-element.125.own_half_ref), channel_id=1, source_target_pairs={{0,1},{1,0},{2,3},{3,2},{4,8},{5,9},{6,10},{7,11},{8,4},{9,5},{10,... | collective-permute-start | bytes 147464 | tf_op jit(solution)/shard_map/ppermute | solution.py:585
  17.6 0.0 collective-permute-start.8
  17.7 1.3 %collective-permute-start.10 = (f32[3,16,128]{2,1,0:T(8,128)S(1)}, f32[3,16,128]{2,1,0:T(8,128)S(1)}, u32[]{:S(2)}, u32[]{:S(2)}) collective-permute-start(f32[3,16,128]{2,1,0:T(8,128)S(1)} %get-tuple-element.124.refs_6_), channel_id=1, source_target_pairs={{0,3},{1,2},{2,1},{3,0},{4,7},{5,6},{6,5},{7,4},{8,11},{9,10},{10,... | collective-permute-start | bytes 73736 | tf_op jit(solution)/shard_map/ppermute | solution.py:585
  19.0 1.8 %shard_map.92 = (f32[3,16,64,128]{3,2,1,0:T(8,128)S(1)}, f32[3,16,64,128]{3,2,1,0:T(8,128)S(1)}, f32[3,16,128]{2,1,0:T(8,128)S(1)}, f32[3,16,128]{2,1,0:T(8,128)S(1)}) custom-call(f32[3,16,64,128]{3,2,1,0:T(8,128)S(1)} %get-tuple-element.87.refs_2_.u_in, ...), custom_call_target="tpu_custom_call", output_to_operand_aliasing={{0}: (0, {}), {1}: (1, {})} | custom-call | flops 20000000 | tf_op jit(solution)/shard_map/pallas_call | solution.py:46
  20.8 1.0 %collective-permute-done.8.rest_ref.refs_9_ = f32[3,32,128]{2,1,0:T(8,128)S(1)} collective-permute-done((f32[3,32,128]{2,1,0:T(8,128)S(1)}, f32[3,32,128]{2,1,0:T(8,128)S(1)}, u32[]{:S(2)}, u32[]{:S(2)}) %collective-permute-start.8) | collective-permute-done | bytes 49184 | tf_op jit(solution)/shard_map/ppermute | solution.py:585
  21.8 0.1 shard_map.94
  21.9 0.1 collective-permute-start.11
  22.0 3.2 %collective-permute-start.12 = (f32[3,32,128]{2,1,0:T(8,128)S(1)}, f32[3,32,128]{2,1,0:T(8,128)S(1)}, u32[]{:S(2)}, u32[]{:S(2)}) collective-permute-start(f32[3,32,128]{2,1,0:T(8,128)S(1)} %get-tuple-element.139.own_half_ref), channel_id=1, source_target_pairs={{0,1},{1,0},{2,3},{3,2},{4,8},{5,9},{6,10},{7,11},{8,4},{9,5},{10,... | collective-permute-start | bytes 147464 | tf_op jit(solution)/shard_map/ppermute | solution.py:585
  25.1 0.0 collective-permute-start.13
  25.2 0.6 %collective-permute-start.14 = (f32[3,16,128]{2,1,0:T(8,128)S(1)}, f32[3,16,128]{2,1,0:T(8,128)S(1)}, u32[]{:S(2)}, u32[]{:S(2)}) collective-permute-start(f32[3,16,128]{2,1,0:T(8,128)S(1)} %get-tuple-element.137.refs_5_), channel_id=1, source_target_pairs={{0,1},{1,0},{2,3},{3,2},{4,5},{5,4},{6,7},{7,6},{8,9},{9,8},{10,11... | collective-permute-start | bytes 73736 | tf_op jit(solution)/shard_map/ppermute | solution.py:585
  25.8 0.4 collective-permute-start.15
  26.2 1.8 %shard_map.95 = (f32[3,16,64,128]{3,2,1,0:T(8,128)S(1)}, f32[3,16,64,128]{3,2,1,0:T(8,128)S(1)}, f32[3,16,128]{2,1,0:T(8,128)S(1)}, f32[3,16,128]{2,1,0:T(8,128)S(1)}) custom-call(f32[3,16,64,128]{3,2,1,0:T(8,128)S(1)} %get-tuple-element.117.refs_0_.u_in, ...), custom_call_target="tpu_custom_call", output_to_operand_aliasing={{0}: (0, {}), {1}: (1, {})} | custom-call | flops 20000000 | tf_op jit(solution)/shard_map/pallas_call | solution.py:46
  28.0 1.4 %collective-permute-done.13.rest_ref.refs_9_ = f32[3,32,128]{2,1,0:T(8,128)S(1)} collective-permute-done((f32[3,32,128]{2,1,0:T(8,128)S(1)}, f32[3,32,128]{2,1,0:T(8,128)S(1)}, u32[]{:S(2)}, u32[]{:S(2)}) %collective-permute-start.13) | collective-permute-done | bytes 49184 | tf_op jit(solution)/shard_map/ppermute | solution.py:585
  29.4 0.3 shard_map.97
  29.7 0.1 collective-permute-start.18
  29.8 3.8 %collective-permute-start.16 = (f32[3,32,128]{2,1,0:T(8,128)S(1)}, f32[3,32,128]{2,1,0:T(8,128)S(1)}, u32[]{:S(2)}, u32[]{:S(2)}) collective-permute-start(f32[3,32,128]{2,1,0:T(8,128)S(1)} %get-tuple-element.147.refs_0_), channel_id=1, source_target_pairs={{0,1},{1,0},{2,3},{3,2},{4,8},{5,9},{6,10},{7,11},{8,4},{9,5},{10,... | collective-permute-start | bytes 147464 | tf_op jit(solution)/shard_map/ppermute | solution.py:585
  33.6 0.0 collective-permute-start.17
  33.6 0.9 %collective-permute-start.20 = (f32[3,16,128]{2,1,0:T(8,128)S(1)}, f32[3,16,128]{2,1,0:T(8,128)S(1)}, u32[]{:S(2)}, u32[]{:S(2)}) collective-permute-start(f32[3,16,128]{2,1,0:T(8,128)S(1)} %get-tuple-element.154.refs_7_), channel_id=1, source_target_pairs={{0,3},{1,2},{2,1},{3,0},{4,7},{5,6},{6,5},{7,4},{8,11},{9,10},{10,... | collective-permute-start | bytes 73736 | tf_op jit(solution)/shard_map/ppermute | solution.py:585
  34.5 1.9 %shard_map.98 = (f32[3,16,64,128]{3,2,1,0:T(8,128)S(1)}, f32[3,16,64,128]{3,2,1,0:T(8,128)S(1)}) custom-call(f32[3,16,64,128]{3,2,1,0:T(8,128)S(1)} %get-tuple-element.131.refs_0_.u_in, f32[3,16,64,128]{3,2,1,0:T(8,128)S(1)} %get-tuple-element.132.w_in, f32[16,64,128]{2,1,0:T(8,128)S(1)} %get-tuple-element.96.kx_ref, ...), custom_call_target="tpu_custom_call", output_to_operand_aliasing={{0}: (0, {}), {1}: (1, {})} | custom-call | flops 20000000 | tf_op jit(solution)/shard_map/pallas_call | solution.py:46
  36.4 1.3 %collective-permute-done.17.refs_3_.refs_10_ = f32[3,32,128]{2,1,0:T(8,128)S(1)} collective-permute-done((f32[3,32,128]{2,1,0:T(8,128)S(1)}, f32[3,32,128]{2,1,0:T(8,128)S(1)}, u32[]{:S(2)}, u32[]{:S(2)}) %collective-permute-start.17) | collective-permute-done | bytes 49184 | tf_op jit(solution)/shard_map/ppermute | solution.py:585
  37.6 1.7 %shard_map.99 = (f32[3,16,64,128]{3,2,1,0:T(8,128)}, f32[3,16,64,128]{3,2,1,0:T(8,128)}, f32[64,128]{1,0:T(8,128)S(1)}) custom-call(f32[3,32,128]{2,1,0:T(8,128)S(1)} %get-tuple-element.147.refs_0_, f32[3,32,128]{2,1,0:T(8,128)S(1)} %get-tuple-element.148.refs_1_, f32[3,32,128]{2,1,0:T(8,128)S(1)} %collective-permute-done.16.refs_2_.refs_9_, ...), custom_call_target="tpu_custom_call" | custom-call | flops 20000000 | tf_op jit(solution)/shard_map/pallas_call | solution.py:46
  39.4 1.1 %shard_map.100 = (f32[3,16,64,128]{3,2,1,0:T(8,128)}, f32[3,16,64,128]{3,2,1,0:T(8,128)}) custom-call(f32[3,16,64,128]{3,2,1,0:T(8,128)S(1)} %get-tuple-element.145.refs_6_.refs_0_, f32[3,16,64,128]{3,2,1,0:T(8,128)S(1)} %get-tuple-element.146.refs_7_.refs_1_, ...), custom_call_target="tpu_custom_call", output_to_operand_aliasing={{0}: (2, {}), {1}: (3, {})} | custom-call | tf_op jit(solution)/shard_map/pallas_call | solution.py:46
  (39 shorter events, 0.1 us)
Async XLA Ops:
  0.6 4.8 %copy-start.1 = (s32[1,16,64,128]{3,2,1,0:T(8,128)S(1)}, s32[1,16,64,128]{3,2,1,0:T(8,128)}, u32[]{:S(2)}) copy-start(s32[1,16,64,128]{3,2,1,0:T(8,128)} %param.9) | copy-start | bytes 1572868
  0.6 4.8 %copy-start = (f32[1,3,16,64,128]{4,3,2,1,0:T(8,128)S(1)}, f32[1,3,16,64,128]{4,3,2,1,0:T(8,128)}, u32[]{:S(2)}) copy-start(f32[1,3,16,64,128]{4,3,2,1,0:T(8,128)} %param.7) | copy-start | bytes 4718596
  0.7 4.8 %copy-start.3 = (f32[8]{0:T(128)S(1)}, f32[8]{0:T(128)}, u32[]{:S(2)}) copy-start(f32[8]{0:T(128)} %moduli_ref.3) | copy-start | bytes 100
  0.7 4.8 %copy-start.5 = (s32[256]{0:T(256)S(1)}, s32[256]{0:T(256)}, u32[]{:S(2)}) copy-start(s32[256]{0:T(256)} %active_ref.1) | copy-start | bytes 3076
  0.7 4.8 %copy-start.4 = (s32[256]{0:T(256)S(1)}, s32[256]{0:T(256)}, u32[]{:S(2)}) copy-start(s32[256]{0:T(256)} %partner_ref.1) | copy-start | bytes 3076
  0.7 4.8 %copy-start.6 = (f32[8]{0:T(128)S(1)}, f32[8]{0:T(128)}, u32[]{:S(2)}) copy-start(f32[8]{0:T(128)} %density_ref.1) | copy-start | bytes 100
  2.2 8.0 %copy-start.2 = (f32[1,3,16,64,128]{4,3,2,1,0:T(8,128)S(1)}, f32[1,3,16,64,128]{4,3,2,1,0:T(8,128)}, u32[]{:S(2)}) copy-start(f32[1,3,16,64,128]{4,3,2,1,0:T(8,128)} %param.8) | copy-start | bytes 4718596
  2.2 10.0 %collective-permute-start.2 = (f32[4,64,128]{2,1,0:T(8,128)S(1)}, f32[4,64,128]{2,1,0:T(8,128)S(1)}, u32[]{:S(2)}, u32[]{:S(2)}) collective-permute-start(f32[4,64,128]{2,1,0:T(8,128)S(1)} %get-tuple-element.90.sb_ref.own_ref.refs_6_), channel_id=1, source_target_pairs={{0,1},{1,0},{2,3},{3,2},{4,8},{5,9},{6,10},{7,11},{8,4},{9,5},{10,... | collective-permute-start | bytes 393224 | tf_op jit(solution)/shard_map/ppermute | solution.py:585
  3.8 8.4 %collective-permute-start.1 = (f32[4,64,128]{2,1,0:T(8,128)S(1)}, f32[4,64,128]{2,1,0:T(8,128)S(1)}, u32[]{:S(2)}, u32[]{:S(2)}) collective-permute-start(f32[4,64,128]{2,1,0:T(8,128)S(1)} %get-tuple-element.89.sa_ref.refs_5_), channel_id=1, source_target_pairs={{0,4},{1,5},{2,6},{3,7},{4,0},{5,1},{6,2},{7,3},{8,12},{9,13},{10,... | collective-permute-start | bytes 393224 | tf_op jit(solution)/shard_map/ppermute | solution.py:585
  3.8 8.3 %collective-permute-start.5 = (f32[3,64,128]{2,1,0:T(8,128)S(1)}, f32[3,64,128]{2,1,0:T(8,128)S(1)}, u32[]{:S(2)}, u32[]{:S(2)}) collective-permute-start(f32[3,64,128]{2,1,0:T(8,128)S(1)} %get-tuple-element.109), channel_id=1, source_target_pairs={{0,1},{1,0},{2,3},{3,2},{4,5},{5,4},{6,7},{7,6},{8,9},{9,8},{10,11... | collective-permute-start | bytes 294920 | tf_op jit(solution)/shard_map/ppermute | solution.py:585
  3.8 1.6 %collective-permute-start = (f32[4,16,128]{2,1,0:T(8,128)S(1)}, f32[4,16,128]{2,1,0:T(8,128)S(1)}, u32[]{:S(2)}, u32[]{:S(2)}) collective-permute-start(f32[4,16,128]{2,1,0:T(8,128)S(1)} %get-tuple-element.80.sc_ref.refs_7_), channel_id=1, source_target_pairs={{0,1},{1,0},{2,3},{3,2},{4,5},{5,4},{6,7},{7,6},{8,9},{9,8},{10,11... | collective-permute-start | bytes 98312 | tf_op jit(solution)/shard_map/ppermute | solution.py:585
  4.3 7.9 %collective-permute-start.3 = (f32[4,16,128]{2,1,0:T(8,128)S(1)}, f32[4,16,128]{2,1,0:T(8,128)S(1)}, u32[]{:S(2)}, u32[]{:S(2)}) collective-permute-start(f32[4,16,128]{2,1,0:T(8,128)S(1)} %get-tuple-element.91.sd_ref.refs_8_), channel_id=1, source_target_pairs={{0,3},{1,2},{2,1},{3,0},{4,7},{5,6},{6,5},{7,4},{8,11},{9,10},{10,... | collective-permute-start | bytes 98312 | tf_op jit(solution)/shard_map/ppermute | solution.py:585
  6.9 5.3 %collective-permute-start.4 = (f32[1,128]{1,0:T(1,128)S(1)}, f32[1,128]{1,0:T(1,128)S(1)}, u32[]{:S(2)}, u32[]{:S(2)}) collective-permute-start(f32[1,128]{1,0:T(1,128)S(1)} %get-tuple-element.93), channel_id=1, source_target_pairs={{0,5},{1,6},{2,7},{3,4},{4,9},{5,10},{6,11},{7,8},{8,13},{9,14},{1... | collective-permute-start | bytes 1544 | tf_op jit(solution)/shard_map/ppermute | solution.py:585
  13.1 8.6 %collective-permute-start.6 = (f32[3,64,128]{2,1,0:T(8,128)S(1)}, f32[3,64,128]{2,1,0:T(8,128)S(1)}, u32[]{:S(2)}, u32[]{:S(2)}) collective-permute-start(f32[3,64,128]{2,1,0:T(8,128)S(1)} %get-tuple-element.121.refs_3_), channel_id=1, source_target_pairs={{0,4},{1,5},{2,6},{3,7},{4,0},{5,1},{6,2},{7,3},{8,12},{9,13},{10,... | collective-permute-start | bytes 294920 | tf_op jit(solution)/shard_map/ppermute | solution.py:585
  15.6 5.2 %collective-permute-start.7 = (f32[3,32,128]{2,1,0:T(8,128)S(1)}, f32[3,32,128]{2,1,0:T(8,128)S(1)}, u32[]{:S(2)}, u32[]{:S(2)}) collective-permute-start(f32[3,32,128]{2,1,0:T(8,128)S(1)} %get-tuple-element.125.own_half_ref), channel_id=1, source_target_pairs={{0,1},{1,0},{2,3},{3,2},{4,8},{5,9},{6,10},{7,11},{8,4},{9,5},{10,... | collective-permute-start | bytes 147464 | tf_op jit(solution)/shard_map/ppermute | solution.py:585
  17.6 4.1 %collective-permute-start.8 = (f32[3,32,128]{2,1,0:T(8,128)S(1)}, f32[3,32,128]{2,1,0:T(8,128)S(1)}, u32[]{:S(2)}, u32[]{:S(2)}) collective-permute-start(f32[3,32,128]{2,1,0:T(8,128)S(1)} %get-tuple-element.126.own_rest_ref), channel_id=1, source_target_pairs={{0,1},{1,0},{2,3},{3,2},{4,8},{5,9},{6,10},{7,11},{8,4},{9,5},{10,... | collective-permute-start | bytes 147464 | tf_op jit(solution)/shard_map/ppermute | solution.py:585
  17.7 4.1 %collective-permute-start.9 = (f32[3,16,128]{2,1,0:T(8,128)S(1)}, f32[3,16,128]{2,1,0:T(8,128)S(1)}, u32[]{:S(2)}, u32[]{:S(2)}) collective-permute-start(f32[3,16,128]{2,1,0:T(8,128)S(1)} %get-tuple-element.123.refs_5_), channel_id=1, source_target_pairs={{0,1},{1,0},{2,3},{3,2},{4,5},{5,4},{6,7},{7,6},{8,9},{9,8},{10,11... | collective-permute-start | bytes 73736 | tf_op jit(solution)/shard_map/ppermute | solution.py:585
  17.7 4.1 %collective-permute-start.10 = (f32[3,16,128]{2,1,0:T(8,128)S(1)}, f32[3,16,128]{2,1,0:T(8,128)S(1)}, u32[]{:S(2)}, u32[]{:S(2)}) collective-permute-start(f32[3,16,128]{2,1,0:T(8,128)S(1)} %get-tuple-element.124.refs_6_), channel_id=1, source_target_pairs={{0,3},{1,2},{2,1},{3,0},{4,7},{5,6},{6,5},{7,4},{8,11},{9,10},{10,... | collective-permute-start | bytes 73736 | tf_op jit(solution)/shard_map/ppermute | solution.py:585
  21.9 7.5 %collective-permute-start.11 = (f32[3,64,128]{2,1,0:T(8,128)S(1)}, f32[3,64,128]{2,1,0:T(8,128)S(1)}, u32[]{:S(2)}, u32[]{:S(2)}) collective-permute-start(f32[3,64,128]{2,1,0:T(8,128)S(1)} %get-tuple-element.135.refs_3_), channel_id=1, source_target_pairs={{0,4},{1,5},{2,6},{3,7},{4,0},{5,1},{6,2},{7,3},{8,12},{9,13},{10,... | collective-permute-start | bytes 294920 | tf_op jit(solution)/shard_map/ppermute | solution.py:585
  22.0 6.0 %collective-permute-start.12 = (f32[3,32,128]{2,1,0:T(8,128)S(1)}, f32[3,32,128]{2,1,0:T(8,128)S(1)}, u32[]{:S(2)}, u32[]{:S(2)}) collective-permute-start(f32[3,32,128]{2,1,0:T(8,128)S(1)} %get-tuple-element.139.own_half_ref), channel_id=1, source_target_pairs={{0,1},{1,0},{2,3},{3,2},{4,8},{5,9},{6,10},{7,11},{8,4},{9,5},{10,... | collective-permute-start | bytes 147464 | tf_op jit(solution)/shard_map/ppermute | solution.py:585
  25.1 4.2 %collective-permute-start.13 = (f32[3,32,128]{2,1,0:T(8,128)S(1)}, f32[3,32,128]{2,1,0:T(8,128)S(1)}, u32[]{:S(2)}, u32[]{:S(2)}) collective-permute-start(f32[3,32,128]{2,1,0:T(8,128)S(1)} %get-tuple-element.140.own_rest_ref), channel_id=1, source_target_pairs={{0,1},{1,0},{2,3},{3,2},{4,8},{5,9},{6,10},{7,11},{8,4},{9,5},{10,... | collective-permute-start | bytes 147464 | tf_op jit(solution)/shard_map/ppermute | solution.py:585
  25.2 4.2 %collective-permute-start.14 = (f32[3,16,128]{2,1,0:T(8,128)S(1)}, f32[3,16,128]{2,1,0:T(8,128)S(1)}, u32[]{:S(2)}, u32[]{:S(2)}) collective-permute-start(f32[3,16,128]{2,1,0:T(8,128)S(1)} %get-tuple-element.137.refs_5_), channel_id=1, source_target_pairs={{0,1},{1,0},{2,3},{3,2},{4,5},{5,4},{6,7},{7,6},{8,9},{9,8},{10,11... | collective-permute-start | bytes 73736 | tf_op jit(solution)/shard_map/ppermute | solution.py:585
  25.8 3.6 %collective-permute-start.15 = (f32[3,16,128]{2,1,0:T(8,128)S(1)}, f32[3,16,128]{2,1,0:T(8,128)S(1)}, u32[]{:S(2)}, u32[]{:S(2)}) collective-permute-start(f32[3,16,128]{2,1,0:T(8,128)S(1)} %get-tuple-element.138.refs_6_), channel_id=1, source_target_pairs={{0,3},{1,2},{2,1},{3,0},{4,7},{5,6},{6,5},{7,4},{8,11},{9,10},{10,... | collective-permute-start | bytes 73736 | tf_op jit(solution)/shard_map/ppermute | solution.py:585
  29.7 9.6 %collective-permute-start.18 = (f32[3,64,128]{2,1,0:T(8,128)S(1)}, f32[3,64,128]{2,1,0:T(8,128)S(1)}, u32[]{:S(2)}, u32[]{:S(2)}) collective-permute-start(f32[3,64,128]{2,1,0:T(8,128)S(1)} %get-tuple-element.151.refs_4_), channel_id=1, source_target_pairs={{0,4},{1,5},{2,6},{3,7},{4,0},{5,1},{6,2},{7,3},{8,12},{9,13},{10,... | collective-permute-start | bytes 294920 | tf_op jit(solution)/shard_map/ppermute | solution.py:585
  29.8 6.6 %collective-permute-start.16 = (f32[3,32,128]{2,1,0:T(8,128)S(1)}, f32[3,32,128]{2,1,0:T(8,128)S(1)}, u32[]{:S(2)}, u32[]{:S(2)}) collective-permute-start(f32[3,32,128]{2,1,0:T(8,128)S(1)} %get-tuple-element.147.refs_0_), channel_id=1, source_target_pairs={{0,1},{1,0},{2,3},{3,2},{4,8},{5,9},{6,10},{7,11},{8,4},{9,5},{10,... | collective-permute-start | bytes 147464 | tf_op jit(solution)/shard_map/ppermute | solution.py:585
  33.6 4.1 %collective-permute-start.17 = (f32[3,32,128]{2,1,0:T(8,128)S(1)}, f32[3,32,128]{2,1,0:T(8,128)S(1)}, u32[]{:S(2)}, u32[]{:S(2)}) collective-permute-start(f32[3,32,128]{2,1,0:T(8,128)S(1)} %get-tuple-element.148.refs_1_), channel_id=1, source_target_pairs={{0,1},{1,0},{2,3},{3,2},{4,8},{5,9},{6,10},{7,11},{8,4},{9,5},{10,... | collective-permute-start | bytes 147464 | tf_op jit(solution)/shard_map/ppermute | solution.py:585
  33.6 5.7 %collective-permute-start.19 = (f32[3,16,128]{2,1,0:T(8,128)S(1)}, f32[3,16,128]{2,1,0:T(8,128)S(1)}, u32[]{:S(2)}, u32[]{:S(2)}) collective-permute-start(f32[3,16,128]{2,1,0:T(8,128)S(1)} %get-tuple-element.153.refs_6_), channel_id=1, source_target_pairs={{0,1},{1,0},{2,3},{3,2},{4,5},{5,4},{6,7},{7,6},{8,9},{9,8},{10,11... | collective-permute-start | bytes 73736 | tf_op jit(solution)/shard_map/ppermute | solution.py:585
  33.6 5.8 %collective-permute-start.20 = (f32[3,16,128]{2,1,0:T(8,128)S(1)}, f32[3,16,128]{2,1,0:T(8,128)S(1)}, u32[]{:S(2)}, u32[]{:S(2)}) collective-permute-start(f32[3,16,128]{2,1,0:T(8,128)S(1)} %get-tuple-element.154.refs_7_), channel_id=1, source_target_pairs={{0,3},{1,2},{2,1},{3,0},{4,7},{5,6},{6,5},{7,4},{8,11},{9,10},{10,... | collective-permute-start | bytes 73736 | tf_op jit(solution)/shard_map/ppermute | solution.py:585

commit v9 on v8

--- a/solution.py
+++ b/solution.py
@@ -24,6 +24,7 @@
 PRESSURE_SCALE = PENALTY * SOFT_WIDTH / LOG2E
 STIFF = 0.25 * YIELD_SPAN
 BIAS = 32.0
+SHIFT = 64.0
 
 AXES = ("body", "gx", "yz")
 VMEM_LIMIT = 48 * 1024 * 1024
@@ -382,7 +383,7 @@
     return lax.axis_index("gx") == lax.axis_size("gx") - 1
 
 
-def pressures(scale, own_rows, matched, shape, fp_ref, fy_ref, fz_ref, total_ref):
+def pressures(scale, own_rows, matched, shape, fp_ref, fy_ref, fz_ref, base_ref, total_ref):
     rows, cols = shape
     lanes = fp_ref.shape[1]
     parts = lanes // rows
@@ -401,24 +402,33 @@
     gap = scale * GAP_SCALE
     along = scale * YIELD_SPAN * SPAN
     fp_ref[...] = jnp.exp2(matched(0) * gap - BIAS / 2.0)
-    fy_ref[...] = matched(1) * along
+    fy = matched(1) * along
+    fy_ref[...] = fy
     spot = lax.broadcasted_iota(jnp.int32, (cols, lanes), 0).astype(jnp.float32)
-    fz_ref[...] = matched(2) * along + spot * SPAN
-    mine = (depth + lane // rows * deep).astype(jnp.float32)
+    fz = matched(2) * along
+    fy_square = fy * fy + SHIFT
+    width = math.gcd(32, deep)
+    middle = (lax.broadcasted_iota(jnp.int32, (cols, lanes), 1) // rows * deep + width // 2).astype(jnp.float32)
+    for k in range(deep // width):
+        z = fz + (spot - (middle + k * width)) * SPAN
+        fz_ref[k] = z
+        base_ref[k] = -(z * z + fy_square)
+    mine = (depth % width - width // 2).astype(jnp.float32)
     op = jnp.exp2(own(0) * gap - BIAS / 2.0)
     oy = own(1) * along
     oz = own(2) * along + mine * SPAN
 
-    width = math.gcd(16, deep)
-    for s in range(0, deep, width):
-        some = slice(s, s + width)
+    own_power = jnp.exp2(SHIFT - (oy * oy + oz * oz))
+    oy, oz = oy * 2.0, oz * 2.0
+    for k in range(deep // width):
+        some = slice(k * width, (k + 1) * width)
         total = jnp.zeros((width, lanes), jnp.float32)
         for m in range(cols):
-            dy = oy[some] - fy_ref[m : m + 1]
-            dz = oz[some] - fz_ref[m : m + 1]
-            weight = jnp.exp2(-(dy * dy + dz * dz))
-            soft = jnp.log2(op[some] * fp_ref[m : m + 1] + 2.0**-BIAS) + BIAS
+            at = slice(m, m + 1)
+            weight = jnp.exp2(oz[some] * fz_ref[k, at] + (oy[some] * fy_ref[at] + base_ref[k, at]))
+            soft = jnp.log2(op[some] * fp_ref[at] + 2.0**-BIAS) + BIAS
             total = total + weight * soft
+        total = total * own_power[some]
         total_ref[some] = total
     turned = jnp.concatenate([total_ref[...]] * parts, axis=0).T
     column = lax.broadcasted_iota(jnp.int32, (rows, cols), 1)
@@ -608,7 +618,8 @@
         scratch=[vmem((rows + tile, lanes)), vmem((rows + tile, cols))],
         flops=8_000_000,
     )
-    pair_scratch = [vmem((cols, lanes))] * 3 + [vmem((cols * rows // lanes, lanes))]
+    deep = cols * rows // lanes
+    pair_scratch = [vmem((cols, lanes))] * 2 + [vmem((deep // math.gcd(32, deep), cols, lanes))] * 2 + [vmem((deep, lanes))]
     for step in range(STEPS):
         first, last = step == 0, step == STEPS - 1
         scale = U_SCALE if first else 1.0

time: 40.8 us -> 39.8 us (0.975)
  starting transfers between devices: 21.4 us -> 20.9 us
    ppermute x21, starting transfers between devices: 21.4 us -> 20.9 us  [passed(): return lax.ppermute(block, AXES, route[name])]
  transfers between devices with their start and end apart: 21 -> 21, of which waited for: 3 -> 3; matrix products, arithmetic and copies ran while one was open for 0% -> 0% of each run, Pallas kernels for 26% -> 27%
where the time goes in v9:
time: 39.8 us; the launch traced here: 39.7 us
  starting transfers between devices  20.9 us (53%)
  Pallas kernels  14.2 us (36%)
  waiting for transfers between devices  3.5 us (9%)
  between operations  0.95 us (2%)
    ppermute x21, starting transfers between devices, passed(): return lax.ppermute(block, AXES, route[name])  20.9 us
    pallas_call x15, Pallas kernels, call(): pl.pallas_call(kernel, out_shape=outs, in_specs=specs, out_specs=[pl.Bloc...  14.2 us
    ppermute x21, waiting for transfers between devices, passed(): return lax.ppermute(block, AXES, route[name])  3.5 us
  transfers between devices with their start and end apart: 21, of which 3 were waited for; matrix products, arithmetic and copies ran while one was open for 0% of the time, Pallas kernels for 27%

profile of v9, /device:TPU:8, one launch (start us, length us, event | category | flops | bytes accessed | tf_op | source)
XLA Modules:
  0.0 39.7 jit_solution(14841712074734146957)
XLA Ops:
  0.7 1.5 %shard_map.86 = (f32[4,64,128]{2,1,0:T(8,128)S(1)}, f32[4,64,128]{2,1,0:T(8,128)S(1)}, f32[4,16,128]{2,1,0:T(8,128)S(1)}, f32[4,16,128]{2,1,0:T(8,128)S(1)}, f32...) custom-call(f32[3,16,64,128]{3,2,1,0:T(8,128)} %bitcast.5, s32[16,64,128]{2,1,0:T(8,128)} %bitcast.8), custom_call_target="tpu_custom_call" | custom-call | tf_op jit(solution)/shard_map/pallas_call | solution.py:47
  2.2 1.6 %collective-permute-start.2 = (f32[4,64,128]{2,1,0:T(8,128)S(1)}, f32[4,64,128]{2,1,0:T(8,128)S(1)}, u32[]{:S(2)}, u32[]{:S(2)}) collective-permute-start(f32[4,64,128]{2,1,0:T(8,128)S(1)} %get-tuple-element.90.sb_ref.own_ref.refs_6_), channel_id=1, source_target_pairs={{0,1},{1,0},{2,3},{3,2},{4,8},{5,9},{6,10},{7,11},{8,4},{9,5},{10,... | collective-permute-start | bytes 393224 | tf_op jit(solution)/shard_map/ppermute | solution.py:595
  3.8 0.5 %collective-permute-start = (f32[4,16,128]{2,1,0:T(8,128)S(1)}, f32[4,16,128]{2,1,0:T(8,128)S(1)}, u32[]{:S(2)}, u32[]{:S(2)}) collective-permute-start(f32[4,16,128]{2,1,0:T(8,128)S(1)} %get-tuple-element.80.sc_ref.refs_7_), channel_id=1, source_target_pairs={{0,1},{1,0},{2,3},{3,2},{4,5},{5,4},{6,7},{7,6},{8,9},{9,8},{10,11... | collective-permute-start | bytes 98312 | tf_op jit(solution)/shard_map/ppermute | solution.py:595
  4.3 1.1 %collective-permute-start.3 = (f32[4,16,128]{2,1,0:T(8,128)S(1)}, f32[4,16,128]{2,1,0:T(8,128)S(1)}, u32[]{:S(2)}, u32[]{:S(2)}) collective-permute-start(f32[4,16,128]{2,1,0:T(8,128)S(1)} %get-tuple-element.91.sd_ref.refs_8_), channel_id=1, source_target_pairs={{0,3},{1,2},{2,1},{3,0},{4,7},{5,6},{6,5},{7,4},{8,11},{9,10},{10,... | collective-permute-start | bytes 98312 | tf_op jit(solution)/shard_map/ppermute | solution.py:595
  5.5 1.4 %shard_map.87 = (f32[16,64,128]{2,1,0:T(8,128)S(1)}, f32[16,64,128]{2,1,0:T(8,128)S(1)}, f32[16,64,128]{2,1,0:T(8,128)S(1)}, f32[16,64,128]{2,1,0:T(8,128)S(1)},...) custom-call(s32[16,64,128]{2,1,0:T(8,128)S(1)} %bitcast.9, ...), custom_call_target="tpu_custom_call", output_to_operand_aliasing={{9}: (1, {})} | custom-call | flops 8000000 | tf_op jit(solution)/shard_map/pallas_call | solution.py:47
  6.9 3.2 %collective-permute-start.4 = (f32[1,128]{1,0:T(1,128)S(1)}, f32[1,128]{1,0:T(1,128)S(1)}, u32[]{:S(2)}, u32[]{:S(2)}) collective-permute-start(f32[1,128]{1,0:T(1,128)S(1)} %get-tuple-element.93), channel_id=1, source_target_pairs={{0,5},{1,6},{2,7},{3,4},{4,9},{5,10},{6,11},{7,8},{8,13},{9,14},{1... | collective-permute-start | bytes 1544 | tf_op jit(solution)/shard_map/ppermute | solution.py:595
  10.1 2.0 %shard_map.88 = (f32[3,16,64,128]{3,2,1,0:T(8,128)S(1)}, f32[3,16,64,128]{3,2,1,0:T(8,128)S(1)}, f32[3,16,128]{2,1,0:T(8,128)S(1)}, f32[3,16,128]{2,1,0:T(8,128)S(1)}) custom-call(f32[3,16,64,128]{3,2,1,0:T(8,128)S(1)} %bitcast.7, f32[3,16,64,128]{3,2,1,0:T(8,128)S(1)} %bitcast.10, f32[16,64,128]{2,1,0:T(8,128)S(1)} %get-tuple-element.81.kx_ref.kx_in, ...), custom_call_target="tpu_custom_call" | custom-call | tf_op jit(solution)/shard_map/pallas_call | solution.py:47
  12.2 0.7 %shard_map.89 = (f32[16,64,128]{2,1,0:T(8,128)S(1)}, f32[16,64,128]{2,1,0:T(8,128)S(1)}, f32[16,64,128]{2,1,0:T(8,128)S(1)}, f32[64,128]{1,0:T(8,128)S(1)}, f32[...) custom-call(f32[4,64,128]{2,1,0:T(8,128)S(1)} %get-tuple-element.89., ...), custom_call_target="tpu_custom_call", output_to_operand_aliasing={{0}: (12, {}), {1}: (13, {}), {2}: (14, {})} | custom-call | tf_op jit(solution)/shard_map/pallas_call | solution.py:47
  13.0 0.1 shard_map.91
  13.1 2.5 %collective-permute-start.6 = (f32[3,64,128]{2,1,0:T(8,128)S(1)}, f32[3,64,128]{2,1,0:T(8,128)S(1)}, u32[]{:S(2)}, u32[]{:S(2)}) collective-permute-start(f32[3,64,128]{2,1,0:T(8,128)S(1)} %get-tuple-element.121.refs_3_), channel_id=1, source_target_pairs={{0,4},{1,5},{2,6},{3,7},{4,0},{5,1},{6,2},{7,3},{8,12},{9,13},{10,... | collective-permute-start | bytes 294920 | tf_op jit(solution)/shard_map/ppermute | solution.py:595
  15.6 2.0 %collective-permute-start.7 = (f32[3,32,128]{2,1,0:T(8,128)S(1)}, f32[3,32,128]{2,1,0:T(8,128)S(1)}, u32[]{:S(2)}, u32[]{:S(2)}) collective-permute-start(f32[3,32,128]{2,1,0:T(8,128)S(1)} %get-tuple-element.125.own_half_ref), channel_id=1, source_target_pairs={{0,1},{1,0},{2,3},{3,2},{4,8},{5,9},{6,10},{7,11},{8,4},{9,5},{10,... | collective-permute-start | bytes 147464 | tf_op jit(solution)/shard_map/ppermute | solution.py:595
  17.6 0.0 collective-permute-start.8
  17.7 1.3 %collective-permute-start.10 = (f32[3,16,128]{2,1,0:T(8,128)S(1)}, f32[3,16,128]{2,1,0:T(8,128)S(1)}, u32[]{:S(2)}, u32[]{:S(2)}) collective-permute-start(f32[3,16,128]{2,1,0:T(8,128)S(1)} %get-tuple-element.124.refs_6_), channel_id=1, source_target_pairs={{0,3},{1,2},{2,1},{3,0},{4,7},{5,6},{6,5},{7,4},{8,11},{9,10},{10,... | collective-permute-start | bytes 73736 | tf_op jit(solution)/shard_map/ppermute | solution.py:595
  19.0 1.8 %shard_map.92 = (f32[3,16,64,128]{3,2,1,0:T(8,128)S(1)}, f32[3,16,64,128]{3,2,1,0:T(8,128)S(1)}, f32[3,16,128]{2,1,0:T(8,128)S(1)}, f32[3,16,128]{2,1,0:T(8,128)S(1)}) custom-call(f32[3,16,64,128]{3,2,1,0:T(8,128)S(1)} %get-tuple-element.87.refs_2_.u_in, ...), custom_call_target="tpu_custom_call", output_to_operand_aliasing={{0}: (0, {}), {1}: (1, {})} | custom-call | flops 20000000 | tf_op jit(solution)/shard_map/pallas_call | solution.py:47
  20.8 0.9 %collective-permute-done.8.rest_ref.refs_9_ = f32[3,32,128]{2,1,0:T(8,128)S(1)} collective-permute-done((f32[3,32,128]{2,1,0:T(8,128)S(1)}, f32[3,32,128]{2,1,0:T(8,128)S(1)}, u32[]{:S(2)}, u32[]{:S(2)}) %collective-permute-start.8) | collective-permute-done | bytes 49184 | tf_op jit(solution)/shard_map/ppermute | solution.py:595
  21.8 0.1 shard_map.94
  21.9 0.1 collective-permute-start.11
  22.0 3.0 %collective-permute-start.12 = (f32[3,32,128]{2,1,0:T(8,128)S(1)}, f32[3,32,128]{2,1,0:T(8,128)S(1)}, u32[]{:S(2)}, u32[]{:S(2)}) collective-permute-start(f32[3,32,128]{2,1,0:T(8,128)S(1)} %get-tuple-element.139.own_half_ref), channel_id=1, source_target_pairs={{0,1},{1,0},{2,3},{3,2},{4,8},{5,9},{6,10},{7,11},{8,4},{9,5},{10,... | collective-permute-start | bytes 147464 | tf_op jit(solution)/shard_map/ppermute | solution.py:595
  24.9 0.0 collective-permute-start.13
  24.9 0.6 %collective-permute-start.14 = (f32[3,16,128]{2,1,0:T(8,128)S(1)}, f32[3,16,128]{2,1,0:T(8,128)S(1)}, u32[]{:S(2)}, u32[]{:S(2)}) collective-permute-start(f32[3,16,128]{2,1,0:T(8,128)S(1)} %get-tuple-element.137.refs_5_), channel_id=1, source_target_pairs={{0,1},{1,0},{2,3},{3,2},{4,5},{5,4},{6,7},{7,6},{8,9},{9,8},{10,11... | collective-permute-start | bytes 73736 | tf_op jit(solution)/shard_map/ppermute | solution.py:595
  25.5 0.4 %collective-permute-start.15 = (f32[3,16,128]{2,1,0:T(8,128)S(1)}, f32[3,16,128]{2,1,0:T(8,128)S(1)}, u32[]{:S(2)}, u32[]{:S(2)}) collective-permute-start(f32[3,16,128]{2,1,0:T(8,128)S(1)} %get-tuple-element.138.refs_6_), channel_id=1, source_target_pairs={{0,3},{1,2},{2,1},{3,0},{4,7},{5,6},{6,5},{7,4},{8,11},{9,10},{10,... | collective-permute-start | bytes 73736 | tf_op jit(solution)/shard_map/ppermute | solution.py:595
  25.9 1.8 %shard_map.95 = (f32[3,16,64,128]{3,2,1,0:T(8,128)S(1)}, f32[3,16,64,128]{3,2,1,0:T(8,128)S(1)}, f32[3,16,128]{2,1,0:T(8,128)S(1)}, f32[3,16,128]{2,1,0:T(8,128)S(1)}) custom-call(f32[3,16,64,128]{3,2,1,0:T(8,128)S(1)} %get-tuple-element.117.refs_0_.u_in, ...), custom_call_target="tpu_custom_call", output_to_operand_aliasing={{0}: (0, {}), {1}: (1, {})} | custom-call | flops 20000000 | tf_op jit(solution)/shard_map/pallas_call | solution.py:47
  27.8 1.4 %collective-permute-done.13.rest_ref.refs_9_ = f32[3,32,128]{2,1,0:T(8,128)S(1)} collective-permute-done((f32[3,32,128]{2,1,0:T(8,128)S(1)}, f32[3,32,128]{2,1,0:T(8,128)S(1)}, u32[]{:S(2)}, u32[]{:S(2)}) %collective-permute-start.13) | collective-permute-done | bytes 49184 | tf_op jit(solution)/shard_map/ppermute | solution.py:595
  29.2 0.1 shard_map.97
  29.3 0.1 collective-permute-start.18
  29.4 3.4 %collective-permute-start.16 = (f32[3,32,128]{2,1,0:T(8,128)S(1)}, f32[3,32,128]{2,1,0:T(8,128)S(1)}, u32[]{:S(2)}, u32[]{:S(2)}) collective-permute-start(f32[3,32,128]{2,1,0:T(8,128)S(1)} %get-tuple-element.147.refs_0_), channel_id=1, source_target_pairs={{0,1},{1,0},{2,3},{3,2},{4,8},{5,9},{6,10},{7,11},{8,4},{9,5},{10,... | collective-permute-start | bytes 147464 | tf_op jit(solution)/shard_map/ppermute | solution.py:595
  32.7 0.0 collective-permute-start.17
  32.8 1.0 %collective-permute-start.20 = (f32[3,16,128]{2,1,0:T(8,128)S(1)}, f32[3,16,128]{2,1,0:T(8,128)S(1)}, u32[]{:S(2)}, u32[]{:S(2)}) collective-permute-start(f32[3,16,128]{2,1,0:T(8,128)S(1)} %get-tuple-element.154.refs_7_), channel_id=1, source_target_pairs={{0,3},{1,2},{2,1},{3,0},{4,7},{5,6},{6,5},{7,4},{8,11},{9,10},{10,... | collective-permute-start | bytes 73736 | tf_op jit(solution)/shard_map/ppermute | solution.py:595
  33.8 1.9 %shard_map.98 = (f32[3,16,64,128]{3,2,1,0:T(8,128)S(1)}, f32[3,16,64,128]{3,2,1,0:T(8,128)S(1)}) custom-call(f32[3,16,64,128]{3,2,1,0:T(8,128)S(1)} %get-tuple-element.131.refs_0_.u_in, f32[3,16,64,128]{3,2,1,0:T(8,128)S(1)} %get-tuple-element.132.w_in, f32[16,64,128]{2,1,0:T(8,128)S(1)} %get-tuple-element.96.kx_ref, ...), custom_call_target="tpu_custom_call", output_to_operand_aliasing={{0}: (0, {}), {1}: (1, {})} | custom-call | flops 20000000 | tf_op jit(solution)/shard_map/pallas_call | solution.py:47
  35.7 1.1 %collective-permute-done.17.refs_3_.refs_10_ = f32[3,32,128]{2,1,0:T(8,128)S(1)} collective-permute-done((f32[3,32,128]{2,1,0:T(8,128)S(1)}, f32[3,32,128]{2,1,0:T(8,128)S(1)}, u32[]{:S(2)}, u32[]{:S(2)}) %collective-permute-start.17) | collective-permute-done | bytes 49184 | tf_op jit(solution)/shard_map/ppermute | solution.py:595
  36.8 1.7 %shard_map.99 = (f32[3,16,64,128]{3,2,1,0:T(8,128)}, f32[3,16,64,128]{3,2,1,0:T(8,128)}, f32[64,128]{1,0:T(8,128)S(1)}) custom-call(f32[3,32,128]{2,1,0:T(8,128)S(1)} %get-tuple-element.147.refs_0_, f32[3,32,128]{2,1,0:T(8,128)S(1)} %get-tuple-element.148.refs_1_, f32[3,32,128]{2,1,0:T(8,128)S(1)} %collective-permute-done.16.refs_2_.refs_9_, ...), custom_call_target="tpu_custom_call" | custom-call | flops 20000000 | tf_op jit(solution)/shard_map/pallas_call | solution.py:47
  38.5 1.1 %shard_map.100 = (f32[3,16,64,128]{3,2,1,0:T(8,128)}, f32[3,16,64,128]{3,2,1,0:T(8,128)}) custom-call(f32[3,16,64,128]{3,2,1,0:T(8,128)S(1)} %get-tuple-element.145.refs_6_.refs_0_, f32[3,16,64,128]{3,2,1,0:T(8,128)S(1)} %get-tuple-element.146.refs_7_.refs_1_, ...), custom_call_target="tpu_custom_call", output_to_operand_aliasing={{0}: (2, {}), {1}: (3, {})} | custom-call | tf_op jit(solution)/shard_map/pallas_call | solution.py:47
  (39 shorter events, 0.1 us)
Async XLA Ops:
  0.6 4.8 %copy-start.1 = (s32[1,16,64,128]{3,2,1,0:T(8,128)S(1)}, s32[1,16,64,128]{3,2,1,0:T(8,128)}, u32[]{:S(2)}) copy-start(s32[1,16,64,128]{3,2,1,0:T(8,128)} %param.9) | copy-start | bytes 1572868
  0.6 4.8 %copy-start = (f32[1,3,16,64,128]{4,3,2,1,0:T(8,128)S(1)}, f32[1,3,16,64,128]{4,3,2,1,0:T(8,128)}, u32[]{:S(2)}) copy-start(f32[1,3,16,64,128]{4,3,2,1,0:T(8,128)} %param.7) | copy-start | bytes 4718596
  0.7 4.8 %copy-start.3 = (f32[8]{0:T(128)S(1)}, f32[8]{0:T(128)}, u32[]{:S(2)}) copy-start(f32[8]{0:T(128)} %moduli_ref.3) | copy-start | bytes 100
  0.7 4.8 %copy-start.5 = (s32[256]{0:T(256)S(1)}, s32[256]{0:T(256)}, u32[]{:S(2)}) copy-start(s32[256]{0:T(256)} %active_ref.1) | copy-start | bytes 3076
  0.7 4.8 %copy-start.4 = (s32[256]{0:T(256)S(1)}, s32[256]{0:T(256)}, u32[]{:S(2)}) copy-start(s32[256]{0:T(256)} %partner_ref.1) | copy-start | bytes 3076
  0.7 4.8 %copy-start.6 = (f32[8]{0:T(128)S(1)}, f32[8]{0:T(128)}, u32[]{:S(2)}) copy-start(f32[8]{0:T(128)} %density_ref.1) | copy-start | bytes 100
  2.2 8.0 %copy-start.2 = (f32[1,3,16,64,128]{4,3,2,1,0:T(8,128)S(1)}, f32[1,3,16,64,128]{4,3,2,1,0:T(8,128)}, u32[]{:S(2)}) copy-start(f32[1,3,16,64,128]{4,3,2,1,0:T(8,128)} %param.8) | copy-start | bytes 4718596
  2.2 10.0 %collective-permute-start.2 = (f32[4,64,128]{2,1,0:T(8,128)S(1)}, f32[4,64,128]{2,1,0:T(8,128)S(1)}, u32[]{:S(2)}, u32[]{:S(2)}) collective-permute-start(f32[4,64,128]{2,1,0:T(8,128)S(1)} %get-tuple-element.90.sb_ref.own_ref.refs_6_), channel_id=1, source_target_pairs={{0,1},{1,0},{2,3},{3,2},{4,8},{5,9},{6,10},{7,11},{8,4},{9,5},{10,... | collective-permute-start | bytes 393224 | tf_op jit(solution)/shard_map/ppermute | solution.py:595
  3.8 8.4 %collective-permute-start.1 = (f32[4,64,128]{2,1,0:T(8,128)S(1)}, f32[4,64,128]{2,1,0:T(8,128)S(1)}, u32[]{:S(2)}, u32[]{:S(2)}) collective-permute-start(f32[4,64,128]{2,1,0:T(8,128)S(1)} %get-tuple-element.89.sa_ref.refs_5_), channel_id=1, source_target_pairs={{0,4},{1,5},{2,6},{3,7},{4,0},{5,1},{6,2},{7,3},{8,12},{9,13},{10,... | collective-permute-start | bytes 393224 | tf_op jit(solution)/shard_map/ppermute | solution.py:595
  3.8 8.3 %collective-permute-start.5 = (f32[3,64,128]{2,1,0:T(8,128)S(1)}, f32[3,64,128]{2,1,0:T(8,128)S(1)}, u32[]{:S(2)}, u32[]{:S(2)}) collective-permute-start(f32[3,64,128]{2,1,0:T(8,128)S(1)} %get-tuple-element.109), channel_id=1, source_target_pairs={{0,1},{1,0},{2,3},{3,2},{4,5},{5,4},{6,7},{7,6},{8,9},{9,8},{10,11... | collective-permute-start | bytes 294920 | tf_op jit(solution)/shard_map/ppermute | solution.py:595
  3.8 1.6 %collective-permute-start = (f32[4,16,128]{2,1,0:T(8,128)S(1)}, f32[4,16,128]{2,1,0:T(8,128)S(1)}, u32[]{:S(2)}, u32[]{:S(2)}) collective-permute-start(f32[4,16,128]{2,1,0:T(8,128)S(1)} %get-tuple-element.80.sc_ref.refs_7_), channel_id=1, source_target_pairs={{0,1},{1,0},{2,3},{3,2},{4,5},{5,4},{6,7},{7,6},{8,9},{9,8},{10,11... | collective-permute-start | bytes 98312 | tf_op jit(solution)/shard_map/ppermute | solution.py:595
  4.3 7.9 %collective-permute-start.3 = (f32[4,16,128]{2,1,0:T(8,128)S(1)}, f32[4,16,128]{2,1,0:T(8,128)S(1)}, u32[]{:S(2)}, u32[]{:S(2)}) collective-permute-start(f32[4,16,128]{2,1,0:T(8,128)S(1)} %get-tuple-element.91.sd_ref.refs_8_), channel_id=1, source_target_pairs={{0,3},{1,2},{2,1},{3,0},{4,7},{5,6},{6,5},{7,4},{8,11},{9,10},{10,... | collective-permute-start | bytes 98312 | tf_op jit(solution)/shard_map/ppermute | solution.py:595
  6.9 5.3 %collective-permute-start.4 = (f32[1,128]{1,0:T(1,128)S(1)}, f32[1,128]{1,0:T(1,128)S(1)}, u32[]{:S(2)}, u32[]{:S(2)}) collective-permute-start(f32[1,128]{1,0:T(1,128)S(1)} %get-tuple-element.93), channel_id=1, source_target_pairs={{0,5},{1,6},{2,7},{3,4},{4,9},{5,10},{6,11},{7,8},{8,13},{9,14},{1... | collective-permute-start | bytes 1544 | tf_op jit(solution)/shard_map/ppermute | solution.py:595
  13.1 8.6 %collective-permute-start.6 = (f32[3,64,128]{2,1,0:T(8,128)S(1)}, f32[3,64,128]{2,1,0:T(8,128)S(1)}, u32[]{:S(2)}, u32[]{:S(2)}) collective-permute-start(f32[3,64,128]{2,1,0:T(8,128)S(1)} %get-tuple-element.121.refs_3_), channel_id=1, source_target_pairs={{0,4},{1,5},{2,6},{3,7},{4,0},{5,1},{6,2},{7,3},{8,12},{9,13},{10,... | collective-permute-start | bytes 294920 | tf_op jit(solution)/shard_map/ppermute | solution.py:595
  15.6 5.2 %collective-permute-start.7 = (f32[3,32,128]{2,1,0:T(8,128)S(1)}, f32[3,32,128]{2,1,0:T(8,128)S(1)}, u32[]{:S(2)}, u32[]{:S(2)}) collective-permute-start(f32[3,32,128]{2,1,0:T(8,128)S(1)} %get-tuple-element.125.own_half_ref), channel_id=1, source_target_pairs={{0,1},{1,0},{2,3},{3,2},{4,8},{5,9},{6,10},{7,11},{8,4},{9,5},{10,... | collective-permute-start | bytes 147464 | tf_op jit(solution)/shard_map/ppermute | solution.py:595
  17.6 4.1 %collective-permute-start.8 = (f32[3,32,128]{2,1,0:T(8,128)S(1)}, f32[3,32,128]{2,1,0:T(8,128)S(1)}, u32[]{:S(2)}, u32[]{:S(2)}) collective-permute-start(f32[3,32,128]{2,1,0:T(8,128)S(1)} %get-tuple-element.126.own_rest_ref), channel_id=1, source_target_pairs={{0,1},{1,0},{2,3},{3,2},{4,8},{5,9},{6,10},{7,11},{8,4},{9,5},{10,... | collective-permute-start | bytes 147464 | tf_op jit(solution)/shard_map/ppermute | solution.py:595
  17.7 4.1 %collective-permute-start.9 = (f32[3,16,128]{2,1,0:T(8,128)S(1)}, f32[3,16,128]{2,1,0:T(8,128)S(1)}, u32[]{:S(2)}, u32[]{:S(2)}) collective-permute-start(f32[3,16,128]{2,1,0:T(8,128)S(1)} %get-tuple-element.123.refs_5_), channel_id=1, source_target_pairs={{0,1},{1,0},{2,3},{3,2},{4,5},{5,4},{6,7},{7,6},{8,9},{9,8},{10,11... | collective-permute-start | bytes 73736 | tf_op jit(solution)/shard_map/ppermute | solution.py:595
  17.7 4.1 %collective-permute-start.10 = (f32[3,16,128]{2,1,0:T(8,128)S(1)}, f32[3,16,128]{2,1,0:T(8,128)S(1)}, u32[]{:S(2)}, u32[]{:S(2)}) collective-permute-start(f32[3,16,128]{2,1,0:T(8,128)S(1)} %get-tuple-element.124.refs_6_), channel_id=1, source_target_pairs={{0,3},{1,2},{2,1},{3,0},{4,7},{5,6},{6,5},{7,4},{8,11},{9,10},{10,... | collective-permute-start | bytes 73736 | tf_op jit(solution)/shard_map/ppermute | solution.py:595
  21.9 7.3 %collective-permute-start.11 = (f32[3,64,128]{2,1,0:T(8,128)S(1)}, f32[3,64,128]{2,1,0:T(8,128)S(1)}, u32[]{:S(2)}, u32[]{:S(2)}) collective-permute-start(f32[3,64,128]{2,1,0:T(8,128)S(1)} %get-tuple-element.135.refs_3_), channel_id=1, source_target_pairs={{0,4},{1,5},{2,6},{3,7},{4,0},{5,1},{6,2},{7,3},{8,12},{9,13},{10,... | collective-permute-start | bytes 294920 | tf_op jit(solution)/shard_map/ppermute | solution.py:595
  22.0 5.8 %collective-permute-start.12 = (f32[3,32,128]{2,1,0:T(8,128)S(1)}, f32[3,32,128]{2,1,0:T(8,128)S(1)}, u32[]{:S(2)}, u32[]{:S(2)}) collective-permute-start(f32[3,32,128]{2,1,0:T(8,128)S(1)} %get-tuple-element.139.own_half_ref), channel_id=1, source_target_pairs={{0,1},{1,0},{2,3},{3,2},{4,8},{5,9},{6,10},{7,11},{8,4},{9,5},{10,... | collective-permute-start | bytes 147464 | tf_op jit(solution)/shard_map/ppermute | solution.py:595
  24.9 4.2 %collective-permute-start.13 = (f32[3,32,128]{2,1,0:T(8,128)S(1)}, f32[3,32,128]{2,1,0:T(8,128)S(1)}, u32[]{:S(2)}, u32[]{:S(2)}) collective-permute-start(f32[3,32,128]{2,1,0:T(8,128)S(1)} %get-tuple-element.140.own_rest_ref), channel_id=1, source_target_pairs={{0,1},{1,0},{2,3},{3,2},{4,8},{5,9},{6,10},{7,11},{8,4},{9,5},{10,... | collective-permute-start | bytes 147464 | tf_op jit(solution)/shard_map/ppermute | solution.py:595
  24.9 4.2 %collective-permute-start.14 = (f32[3,16,128]{2,1,0:T(8,128)S(1)}, f32[3,16,128]{2,1,0:T(8,128)S(1)}, u32[]{:S(2)}, u32[]{:S(2)}) collective-permute-start(f32[3,16,128]{2,1,0:T(8,128)S(1)} %get-tuple-element.137.refs_5_), channel_id=1, source_target_pairs={{0,1},{1,0},{2,3},{3,2},{4,5},{5,4},{6,7},{7,6},{8,9},{9,8},{10,11... | collective-permute-start | bytes 73736 | tf_op jit(solution)/shard_map/ppermute | solution.py:595
  25.5 3.6 %collective-permute-start.15 = (f32[3,16,128]{2,1,0:T(8,128)S(1)}, f32[3,16,128]{2,1,0:T(8,128)S(1)}, u32[]{:S(2)}, u32[]{:S(2)}) collective-permute-start(f32[3,16,128]{2,1,0:T(8,128)S(1)} %get-tuple-element.138.refs_6_), channel_id=1, source_target_pairs={{0,3},{1,2},{2,1},{3,0},{4,7},{5,6},{6,5},{7,4},{8,11},{9,10},{10,... | collective-permute-start | bytes 73736 | tf_op jit(solution)/shard_map/ppermute | solution.py:595
  29.3 9.2 %collective-permute-start.18 = (f32[3,64,128]{2,1,0:T(8,128)S(1)}, f32[3,64,128]{2,1,0:T(8,128)S(1)}, u32[]{:S(2)}, u32[]{:S(2)}) collective-permute-start(f32[3,64,128]{2,1,0:T(8,128)S(1)} %get-tuple-element.151.refs_4_), channel_id=1, source_target_pairs={{0,4},{1,5},{2,6},{3,7},{4,0},{5,1},{6,2},{7,3},{8,12},{9,13},{10,... | collective-permute-start | bytes 294920 | tf_op jit(solution)/shard_map/ppermute | solution.py:595
  29.4 6.3 %collective-permute-start.16 = (f32[3,32,128]{2,1,0:T(8,128)S(1)}, f32[3,32,128]{2,1,0:T(8,128)S(1)}, u32[]{:S(2)}, u32[]{:S(2)}) collective-permute-start(f32[3,32,128]{2,1,0:T(8,128)S(1)} %get-tuple-element.147.refs_0_), channel_id=1, source_target_pairs={{0,1},{1,0},{2,3},{3,2},{4,8},{5,9},{6,10},{7,11},{8,4},{9,5},{10,... | collective-permute-start | bytes 147464 | tf_op jit(solution)/shard_map/ppermute | solution.py:595
  32.7 4.1 %collective-permute-start.17 = (f32[3,32,128]{2,1,0:T(8,128)S(1)}, f32[3,32,128]{2,1,0:T(8,128)S(1)}, u32[]{:S(2)}, u32[]{:S(2)}) collective-permute-start(f32[3,32,128]{2,1,0:T(8,128)S(1)} %get-tuple-element.148.refs_1_), channel_id=1, source_target_pairs={{0,1},{1,0},{2,3},{3,2},{4,8},{5,9},{6,10},{7,11},{8,4},{9,5},{10,... | collective-permute-start | bytes 147464 | tf_op jit(solution)/shard_map/ppermute | solution.py:595
  32.8 5.7 %collective-permute-start.19 = (f32[3,16,128]{2,1,0:T(8,128)S(1)}, f32[3,16,128]{2,1,0:T(8,128)S(1)}, u32[]{:S(2)}, u32[]{:S(2)}) collective-permute-start(f32[3,16,128]{2,1,0:T(8,128)S(1)} %get-tuple-element.153.refs_6_), channel_id=1, source_target_pairs={{0,1},{1,0},{2,3},{3,2},{4,5},{5,4},{6,7},{7,6},{8,9},{9,8},{10,11... | collective-permute-start | bytes 73736 | tf_op jit(solution)/shard_map/ppermute | solution.py:595
  32.8 5.7 %collective-permute-start.20 = (f32[3,16,128]{2,1,0:T(8,128)S(1)}, f32[3,16,128]{2,1,0:T(8,128)S(1)}, u32[]{:S(2)}, u32[]{:S(2)}) collective-permute-start(f32[3,16,128]{2,1,0:T(8,128)S(1)} %get-tuple-element.154.refs_7_), channel_id=1, source_target_pairs={{0,3},{1,2},{2,1},{3,0},{4,7},{5,6},{6,5},{7,4},{8,11},{9,10},{10,... | collective-permute-start | bytes 73736 | tf_op jit(solution)/shard_map/ppermute | solution.py:595

commit v10 on v9

--- a/solution.py
+++ b/solution.py
@@ -71,16 +71,13 @@
     planes, rows, cols = mat_ref.shape
     place = here_in_mesh()
     ia, ib, jc, jd = links(place, planes, rows)
-    tile = rows_ref.shape[3]
-    tile_c, tile_d = jc // tile * tile, jd // tile * tile
     copies = []
     for n, (ref, i) in enumerate(((sa_ref, ia), (sb_ref, ib))):
         copies.append(pltpu.make_async_copy(d_ref.at[:, i], ref.at[0:3], sems.at[n]))
         copies.append(pltpu.make_async_copy(mat_ref.at[i], plane_ref.at[n], sems.at[2 + n]))
-    for n, at in enumerate((tile_c, tile_d)):
-        some = pl.ds(pl.multiple_of(at, tile), tile)
-        copies.append(pltpu.make_async_copy(d_ref.at[:, :, some], rows_ref.at[n], sems.at[4 + n]))
-        copies.append(pltpu.make_async_copy(mat_ref.at[:, some], kinds_ref.at[n], sems.at[6 + n]))
+    for n, j in enumerate((jc, jd)):
+        copies.append(pltpu.make_async_copy(d_ref.at[:, :, pl.ds(j, 1)], rows_ref.at[n], sems.at[4 + n]))
+        copies.append(pltpu.make_async_copy(mat_ref.at[:, pl.ds(j, 1)], kinds_ref.at[n], sems.at[6 + n]))
     for copy in copies:
         copy.start()
     for copy in copies:
@@ -90,11 +87,11 @@
     for c in range(3):
         se_ref[c] = sb_ref[c]
     corner_ref[...] = jnp.where(place[0] % 2 == 0, kinds_a[rows - 1 :], kinds_b[rows - 1 :])
-    for n, (ref, j) in enumerate(((sc_ref, jc - tile_c), (sd_ref, jd - tile_d))):
+    for n, ref in enumerate((sc_ref, sd_ref)):
         for i in range(planes):
             for c in range(3):
-                ref[c, i : i + 1] = rows_ref[n, c, i, pl.ds(j, 1)]
-            ref[3, i : i + 1] = kinds_ref[n, i, pl.ds(j, 1)].astype(jnp.float32)
+                ref[c, i : i + 1] = rows_ref[n, c, i]
+            ref[3, i : i + 1] = kinds_ref[n, i].astype(jnp.float32)
 
 
 def links(place, planes, rows):
@@ -601,8 +598,8 @@
         [hbm, hbm],
         scratch=[
             pltpu.VMEM((2, *face), jnp.int32),
-            vmem((2, 3, planes, tile, cols)),
-            pltpu.VMEM((2, planes, tile, cols), jnp.int32),
+            vmem((2, 3, planes, 1, cols)),
+            pltpu.VMEM((2, planes, 1, cols), jnp.int32),
             pltpu.SemaphoreType.DMA((8,)),
         ],
     )

time: 39.8 us -> 39.6 us (level)
  no operation moved by 1% of the time
where the time goes in v10:
time: 39.6 us; the launch traced here: 39.4 us
  starting transfers between devices  20.9 us (53%)
  Pallas kernels  14 us (35%)
  waiting for transfers between devices  3.52 us (9%)
  between operations  0.95 us (2%)
    ppermute x21, starting transfers between devices, passed(): return lax.ppermute(block, AXES, route[name])  20.9 us
    pallas_call x15, Pallas kernels, call(): pl.pallas_call(kernel, out_shape=outs, in_specs=specs, out_specs=[pl.Bloc...  14 us
    ppermute x21, waiting for transfers between devices, passed(): return lax.ppermute(block, AXES, route[name])  3.52 us
  transfers between devices with their start and end apart: 21, of which 3 were waited for; matrix products, arithmetic and copies ran while one was open for 0% of the time, Pallas kernels for 27%

profile of v10, /device:TPU:8, one launch (start us, length us, event | category | flops | bytes accessed | tf_op | source)
XLA Modules:
  0.0 39.4 jit_solution(3492586669599394401)
XLA Ops:
  0.7 1.2 %shard_map.86 = (f32[4,64,128]{2,1,0:T(8,128)S(1)}, f32[4,64,128]{2,1,0:T(8,128)S(1)}, f32[4,16,128]{2,1,0:T(8,128)S(1)}, f32[4,16,128]{2,1,0:T(8,128)S(1)}, f32...) custom-call(f32[3,16,64,128]{3,2,1,0:T(8,128)} %bitcast.5, s32[16,64,128]{2,1,0:T(8,128)} %bitcast.8), custom_call_target="tpu_custom_call" | custom-call | tf_op jit(solution)/shard_map/pallas_call | solution.py:47
  1.9 1.6 %collective-permute-start.2 = (f32[4,64,128]{2,1,0:T(8,128)S(1)}, f32[4,64,128]{2,1,0:T(8,128)S(1)}, u32[]{:S(2)}, u32[]{:S(2)}) collective-permute-start(f32[4,64,128]{2,1,0:T(8,128)S(1)} %get-tuple-element.90.sb_ref.own_ref.refs_6_), channel_id=1, source_target_pairs={{0,1},{1,0},{2,3},{3,2},{4,8},{5,9},{6,10},{7,11},{8,4},{9,5},{10,... | collective-permute-start | bytes 393224 | tf_op jit(solution)/shard_map/ppermute | solution.py:592
  3.6 0.5 %collective-permute-start = (f32[4,16,128]{2,1,0:T(8,128)S(1)}, f32[4,16,128]{2,1,0:T(8,128)S(1)}, u32[]{:S(2)}, u32[]{:S(2)}) collective-permute-start(f32[4,16,128]{2,1,0:T(8,128)S(1)} %get-tuple-element.80.sc_ref.refs_7_), channel_id=1, source_target_pairs={{0,1},{1,0},{2,3},{3,2},{4,5},{5,4},{6,7},{7,6},{8,9},{9,8},{10,11... | collective-permute-start | bytes 98312 | tf_op jit(solution)/shard_map/ppermute | solution.py:592
  4.1 1.1 %collective-permute-start.3 = (f32[4,16,128]{2,1,0:T(8,128)S(1)}, f32[4,16,128]{2,1,0:T(8,128)S(1)}, u32[]{:S(2)}, u32[]{:S(2)}) collective-permute-start(f32[4,16,128]{2,1,0:T(8,128)S(1)} %get-tuple-element.91.sd_ref.refs_8_), channel_id=1, source_target_pairs={{0,3},{1,2},{2,1},{3,0},{4,7},{5,6},{6,5},{7,4},{8,11},{9,10},{10,... | collective-permute-start | bytes 98312 | tf_op jit(solution)/shard_map/ppermute | solution.py:592
  5.3 1.4 %shard_map.87 = (f32[16,64,128]{2,1,0:T(8,128)S(1)}, f32[16,64,128]{2,1,0:T(8,128)S(1)}, f32[16,64,128]{2,1,0:T(8,128)S(1)}, f32[16,64,128]{2,1,0:T(8,128)S(1)},...) custom-call(s32[16,64,128]{2,1,0:T(8,128)S(1)} %bitcast.9, ...), custom_call_target="tpu_custom_call", output_to_operand_aliasing={{9}: (1, {})} | custom-call | flops 8000000 | tf_op jit(solution)/shard_map/pallas_call | solution.py:47
  6.7 3.2 %collective-permute-start.4 = (f32[1,128]{1,0:T(1,128)S(1)}, f32[1,128]{1,0:T(1,128)S(1)}, u32[]{:S(2)}, u32[]{:S(2)}) collective-permute-start(f32[1,128]{1,0:T(1,128)S(1)} %get-tuple-element.93), channel_id=1, source_target_pairs={{0,5},{1,6},{2,7},{3,4},{4,9},{5,10},{6,11},{7,8},{8,13},{9,14},{1... | collective-permute-start | bytes 1544 | tf_op jit(solution)/shard_map/ppermute | solution.py:592
  9.9 2.0 %shard_map.88 = (f32[3,16,64,128]{3,2,1,0:T(8,128)S(1)}, f32[3,16,64,128]{3,2,1,0:T(8,128)S(1)}, f32[3,16,128]{2,1,0:T(8,128)S(1)}, f32[3,16,128]{2,1,0:T(8,128)S(1)}) custom-call(f32[3,16,64,128]{3,2,1,0:T(8,128)S(1)} %bitcast.7, f32[3,16,64,128]{3,2,1,0:T(8,128)S(1)} %bitcast.10, f32[16,64,128]{2,1,0:T(8,128)S(1)} %get-tuple-element.81.kx_ref.kx_in, ...), custom_call_target="tpu_custom_call" | custom-call | tf_op jit(solution)/shard_map/pallas_call | solution.py:47
  12.0 0.7 %shard_map.89 = (f32[16,64,128]{2,1,0:T(8,128)S(1)}, f32[16,64,128]{2,1,0:T(8,128)S(1)}, f32[16,64,128]{2,1,0:T(8,128)S(1)}, f32[64,128]{1,0:T(8,128)S(1)}, f32[...) custom-call(f32[4,64,128]{2,1,0:T(8,128)S(1)} %get-tuple-element.89., ...), custom_call_target="tpu_custom_call", output_to_operand_aliasing={{0}: (12, {}), {1}: (13, {}), {2}: (14, {})} | custom-call | tf_op jit(solution)/shard_map/pallas_call | solution.py:47
  12.7 0.1 shard_map.91
  12.9 2.5 %collective-permute-start.6 = (f32[3,64,128]{2,1,0:T(8,128)S(1)}, f32[3,64,128]{2,1,0:T(8,128)S(1)}, u32[]{:S(2)}, u32[]{:S(2)}) collective-permute-start(f32[3,64,128]{2,1,0:T(8,128)S(1)} %get-tuple-element.121.refs_3_), channel_id=1, source_target_pairs={{0,4},{1,5},{2,6},{3,7},{4,0},{5,1},{6,2},{7,3},{8,12},{9,13},{10,... | collective-permute-start | bytes 294920 | tf_op jit(solution)/shard_map/ppermute | solution.py:592
  15.3 2.0 %collective-permute-start.7 = (f32[3,32,128]{2,1,0:T(8,128)S(1)}, f32[3,32,128]{2,1,0:T(8,128)S(1)}, u32[]{:S(2)}, u32[]{:S(2)}) collective-permute-start(f32[3,32,128]{2,1,0:T(8,128)S(1)} %get-tuple-element.125.own_half_ref), channel_id=1, source_target_pairs={{0,1},{1,0},{2,3},{3,2},{4,8},{5,9},{6,10},{7,11},{8,4},{9,5},{10,... | collective-permute-start | bytes 147464 | tf_op jit(solution)/shard_map/ppermute | solution.py:592
  17.4 0.0 collective-permute-start.8
  17.4 1.3 %collective-permute-start.10 = (f32[3,16,128]{2,1,0:T(8,128)S(1)}, f32[3,16,128]{2,1,0:T(8,128)S(1)}, u32[]{:S(2)}, u32[]{:S(2)}) collective-permute-start(f32[3,16,128]{2,1,0:T(8,128)S(1)} %get-tuple-element.124.refs_6_), channel_id=1, source_target_pairs={{0,3},{1,2},{2,1},{3,0},{4,7},{5,6},{6,5},{7,4},{8,11},{9,10},{10,... | collective-permute-start | bytes 73736 | tf_op jit(solution)/shard_map/ppermute | solution.py:592
  18.7 1.8 %shard_map.92 = (f32[3,16,64,128]{3,2,1,0:T(8,128)S(1)}, f32[3,16,64,128]{3,2,1,0:T(8,128)S(1)}, f32[3,16,128]{2,1,0:T(8,128)S(1)}, f32[3,16,128]{2,1,0:T(8,128)S(1)}) custom-call(f32[3,16,64,128]{3,2,1,0:T(8,128)S(1)} %get-tuple-element.87.refs_2_.u_in, ...), custom_call_target="tpu_custom_call", output_to_operand_aliasing={{0}: (0, {}), {1}: (1, {})} | custom-call | flops 20000000 | tf_op jit(solution)/shard_map/pallas_call | solution.py:47
  20.5 0.9 %collective-permute-done.8.rest_ref.refs_9_ = f32[3,32,128]{2,1,0:T(8,128)S(1)} collective-permute-done((f32[3,32,128]{2,1,0:T(8,128)S(1)}, f32[3,32,128]{2,1,0:T(8,128)S(1)}, u32[]{:S(2)}, u32[]{:S(2)}) %collective-permute-start.8) | collective-permute-done | bytes 49184 | tf_op jit(solution)/shard_map/ppermute | solution.py:592
  21.5 0.1 shard_map.94
  21.6 0.1 collective-permute-start.11
  21.7 3.0 %collective-permute-start.12 = (f32[3,32,128]{2,1,0:T(8,128)S(1)}, f32[3,32,128]{2,1,0:T(8,128)S(1)}, u32[]{:S(2)}, u32[]{:S(2)}) collective-permute-start(f32[3,32,128]{2,1,0:T(8,128)S(1)} %get-tuple-element.139.own_half_ref), channel_id=1, source_target_pairs={{0,1},{1,0},{2,3},{3,2},{4,8},{5,9},{6,10},{7,11},{8,4},{9,5},{10,... | collective-permute-start | bytes 147464 | tf_op jit(solution)/shard_map/ppermute | solution.py:592
  24.7 0.0 collective-permute-start.13
  24.7 0.6 %collective-permute-start.14 = (f32[3,16,128]{2,1,0:T(8,128)S(1)}, f32[3,16,128]{2,1,0:T(8,128)S(1)}, u32[]{:S(2)}, u32[]{:S(2)}) collective-permute-start(f32[3,16,128]{2,1,0:T(8,128)S(1)} %get-tuple-element.137.refs_5_), channel_id=1, source_target_pairs={{0,1},{1,0},{2,3},{3,2},{4,5},{5,4},{6,7},{7,6},{8,9},{9,8},{10,11... | collective-permute-start | bytes 73736 | tf_op jit(solution)/shard_map/ppermute | solution.py:592
  25.3 0.4 %collective-permute-start.15 = (f32[3,16,128]{2,1,0:T(8,128)S(1)}, f32[3,16,128]{2,1,0:T(8,128)S(1)}, u32[]{:S(2)}, u32[]{:S(2)}) collective-permute-start(f32[3,16,128]{2,1,0:T(8,128)S(1)} %get-tuple-element.138.refs_6_), channel_id=1, source_target_pairs={{0,3},{1,2},{2,1},{3,0},{4,7},{5,6},{6,5},{7,4},{8,11},{9,10},{10,... | collective-permute-start | bytes 73736 | tf_op jit(solution)/shard_map/ppermute | solution.py:592
  25.7 1.8 %shard_map.95 = (f32[3,16,64,128]{3,2,1,0:T(8,128)S(1)}, f32[3,16,64,128]{3,2,1,0:T(8,128)S(1)}, f32[3,16,128]{2,1,0:T(8,128)S(1)}, f32[3,16,128]{2,1,0:T(8,128)S(1)}) custom-call(f32[3,16,64,128]{3,2,1,0:T(8,128)S(1)} %get-tuple-element.117.refs_0_.u_in, ...), custom_call_target="tpu_custom_call", output_to_operand_aliasing={{0}: (0, {}), {1}: (1, {})} | custom-call | flops 20000000 | tf_op jit(solution)/shard_map/pallas_call | solution.py:47
  27.5 1.4 %collective-permute-done.13.rest_ref.refs_9_ = f32[3,32,128]{2,1,0:T(8,128)S(1)} collective-permute-done((f32[3,32,128]{2,1,0:T(8,128)S(1)}, f32[3,32,128]{2,1,0:T(8,128)S(1)}, u32[]{:S(2)}, u32[]{:S(2)}) %collective-permute-start.13) | collective-permute-done | bytes 49184 | tf_op jit(solution)/shard_map/ppermute | solution.py:592
  28.9 0.1 shard_map.97
  29.0 0.1 collective-permute-start.18
  29.1 3.4 %collective-permute-start.16 = (f32[3,32,128]{2,1,0:T(8,128)S(1)}, f32[3,32,128]{2,1,0:T(8,128)S(1)}, u32[]{:S(2)}, u32[]{:S(2)}) collective-permute-start(f32[3,32,128]{2,1,0:T(8,128)S(1)} %get-tuple-element.147.refs_0_), channel_id=1, source_target_pairs={{0,1},{1,0},{2,3},{3,2},{4,8},{5,9},{6,10},{7,11},{8,4},{9,5},{10,... | collective-permute-start | bytes 147464 | tf_op jit(solution)/shard_map/ppermute | solution.py:592
  32.5 0.0 collective-permute-start.17
  32.5 1.0 %collective-permute-start.20 = (f32[3,16,128]{2,1,0:T(8,128)S(1)}, f32[3,16,128]{2,1,0:T(8,128)S(1)}, u32[]{:S(2)}, u32[]{:S(2)}) collective-permute-start(f32[3,16,128]{2,1,0:T(8,128)S(1)} %get-tuple-element.154.refs_7_), channel_id=1, source_target_pairs={{0,3},{1,2},{2,1},{3,0},{4,7},{5,6},{6,5},{7,4},{8,11},{9,10},{10,... | collective-permute-start | bytes 73736 | tf_op jit(solution)/shard_map/ppermute | solution.py:592
  33.6 1.9 %shard_map.98 = (f32[3,16,64,128]{3,2,1,0:T(8,128)S(1)}, f32[3,16,64,128]{3,2,1,0:T(8,128)S(1)}) custom-call(f32[3,16,64,128]{3,2,1,0:T(8,128)S(1)} %get-tuple-element.131.refs_0_.u_in, f32[3,16,64,128]{3,2,1,0:T(8,128)S(1)} %get-tuple-element.132.w_in, f32[16,64,128]{2,1,0:T(8,128)S(1)} %get-tuple-element.96.kx_ref, ...), custom_call_target="tpu_custom_call", output_to_operand_aliasing={{0}: (0, {}), {1}: (1, {})} | custom-call | flops 20000000 | tf_op jit(solution)/shard_map/pallas_call | solution.py:47
  35.5 1.1 %collective-permute-done.17.refs_3_.refs_10_ = f32[3,32,128]{2,1,0:T(8,128)S(1)} collective-permute-done((f32[3,32,128]{2,1,0:T(8,128)S(1)}, f32[3,32,128]{2,1,0:T(8,128)S(1)}, u32[]{:S(2)}, u32[]{:S(2)}) %collective-permute-start.17) | collective-permute-done | bytes 49184 | tf_op jit(solution)/shard_map/ppermute | solution.py:592
  36.6 1.7 %shard_map.99 = (f32[3,16,64,128]{3,2,1,0:T(8,128)}, f32[3,16,64,128]{3,2,1,0:T(8,128)}, f32[64,128]{1,0:T(8,128)S(1)}) custom-call(f32[3,32,128]{2,1,0:T(8,128)S(1)} %get-tuple-element.147.refs_0_, f32[3,32,128]{2,1,0:T(8,128)S(1)} %get-tuple-element.148.refs_1_, f32[3,32,128]{2,1,0:T(8,128)S(1)} %collective-permute-done.16.refs_2_.refs_9_, ...), custom_call_target="tpu_custom_call" | custom-call | flops 20000000 | tf_op jit(solution)/shard_map/pallas_call | solution.py:47
  38.3 1.1 %shard_map.100 = (f32[3,16,64,128]{3,2,1,0:T(8,128)}, f32[3,16,64,128]{3,2,1,0:T(8,128)}) custom-call(f32[3,16,64,128]{3,2,1,0:T(8,128)S(1)} %get-tuple-element.145.refs_6_.refs_0_, f32[3,16,64,128]{3,2,1,0:T(8,128)S(1)} %get-tuple-element.146.refs_7_.refs_1_, ...), custom_call_target="tpu_custom_call", output_to_operand_aliasing={{0}: (2, {}), {1}: (3, {})} | custom-call | tf_op jit(solution)/shard_map/pallas_call | solution.py:47
  (39 shorter events, 0.1 us)
Async XLA Ops:
  0.6 4.6 %copy-start.1 = (s32[1,16,64,128]{3,2,1,0:T(8,128)S(1)}, s32[1,16,64,128]{3,2,1,0:T(8,128)}, u32[]{:S(2)}) copy-start(s32[1,16,64,128]{3,2,1,0:T(8,128)} %param.9) | copy-start | bytes 1572868
  0.6 4.6 %copy-start = (f32[1,3,16,64,128]{4,3,2,1,0:T(8,128)S(1)}, f32[1,3,16,64,128]{4,3,2,1,0:T(8,128)}, u32[]{:S(2)}) copy-start(f32[1,3,16,64,128]{4,3,2,1,0:T(8,128)} %param.7) | copy-start | bytes 4718596
  0.7 4.6 %copy-start.3 = (f32[8]{0:T(128)S(1)}, f32[8]{0:T(128)}, u32[]{:S(2)}) copy-start(f32[8]{0:T(128)} %moduli_ref.3) | copy-start | bytes 100
  0.7 4.6 %copy-start.5 = (s32[256]{0:T(256)S(1)}, s32[256]{0:T(256)}, u32[]{:S(2)}) copy-start(s32[256]{0:T(256)} %active_ref.1) | copy-start | bytes 3076
  0.7 4.6 %copy-start.4 = (s32[256]{0:T(256)S(1)}, s32[256]{0:T(256)}, u32[]{:S(2)}) copy-start(s32[256]{0:T(256)} %partner_ref.1) | copy-start | bytes 3076
  0.7 4.6 %copy-start.6 = (f32[8]{0:T(128)S(1)}, f32[8]{0:T(128)}, u32[]{:S(2)}) copy-start(f32[8]{0:T(128)} %density_ref.1) | copy-start | bytes 100
  1.9 8.0 %copy-start.2 = (f32[1,3,16,64,128]{4,3,2,1,0:T(8,128)S(1)}, f32[1,3,16,64,128]{4,3,2,1,0:T(8,128)}, u32[]{:S(2)}) copy-start(f32[1,3,16,64,128]{4,3,2,1,0:T(8,128)} %param.8) | copy-start | bytes 4718596
  1.9 10.0 %collective-permute-start.2 = (f32[4,64,128]{2,1,0:T(8,128)S(1)}, f32[4,64,128]{2,1,0:T(8,128)S(1)}, u32[]{:S(2)}, u32[]{:S(2)}) collective-permute-start(f32[4,64,128]{2,1,0:T(8,128)S(1)} %get-tuple-element.90.sb_ref.own_ref.refs_6_), channel_id=1, source_target_pairs={{0,1},{1,0},{2,3},{3,2},{4,8},{5,9},{6,10},{7,11},{8,4},{9,5},{10,... | collective-permute-start | bytes 393224 | tf_op jit(solution)/shard_map/ppermute | solution.py:592
  3.6 8.4 %collective-permute-start.1 = (f32[4,64,128]{2,1,0:T(8,128)S(1)}, f32[4,64,128]{2,1,0:T(8,128)S(1)}, u32[]{:S(2)}, u32[]{:S(2)}) collective-permute-start(f32[4,64,128]{2,1,0:T(8,128)S(1)} %get-tuple-element.89.sa_ref.refs_5_), channel_id=1, source_target_pairs={{0,4},{1,5},{2,6},{3,7},{4,0},{5,1},{6,2},{7,3},{8,12},{9,13},{10,... | collective-permute-start | bytes 393224 | tf_op jit(solution)/shard_map/ppermute | solution.py:592
  3.6 8.3 %collective-permute-start.5 = (f32[3,64,128]{2,1,0:T(8,128)S(1)}, f32[3,64,128]{2,1,0:T(8,128)S(1)}, u32[]{:S(2)}, u32[]{:S(2)}) collective-permute-start(f32[3,64,128]{2,1,0:T(8,128)S(1)} %get-tuple-element.109), channel_id=1, source_target_pairs={{0,1},{1,0},{2,3},{3,2},{4,5},{5,4},{6,7},{7,6},{8,9},{9,8},{10,11... | collective-permute-start | bytes 294920 | tf_op jit(solution)/shard_map/ppermute | solution.py:592
  3.6 1.6 %collective-permute-start = (f32[4,16,128]{2,1,0:T(8,128)S(1)}, f32[4,16,128]{2,1,0:T(8,128)S(1)}, u32[]{:S(2)}, u32[]{:S(2)}) collective-permute-start(f32[4,16,128]{2,1,0:T(8,128)S(1)} %get-tuple-element.80.sc_ref.refs_7_), channel_id=1, source_target_pairs={{0,1},{1,0},{2,3},{3,2},{4,5},{5,4},{6,7},{7,6},{8,9},{9,8},{10,11... | collective-permute-start | bytes 98312 | tf_op jit(solution)/shard_map/ppermute | solution.py:592
  4.1 7.9 %collective-permute-start.3 = (f32[4,16,128]{2,1,0:T(8,128)S(1)}, f32[4,16,128]{2,1,0:T(8,128)S(1)}, u32[]{:S(2)}, u32[]{:S(2)}) collective-permute-start(f32[4,16,128]{2,1,0:T(8,128)S(1)} %get-tuple-element.91.sd_ref.refs_8_), channel_id=1, source_target_pairs={{0,3},{1,2},{2,1},{3,0},{4,7},{5,6},{6,5},{7,4},{8,11},{9,10},{10,... | collective-permute-start | bytes 98312 | tf_op jit(solution)/shard_map/ppermute | solution.py:592
  6.7 5.3 %collective-permute-start.4 = (f32[1,128]{1,0:T(1,128)S(1)}, f32[1,128]{1,0:T(1,128)S(1)}, u32[]{:S(2)}, u32[]{:S(2)}) collective-permute-start(f32[1,128]{1,0:T(1,128)S(1)} %get-tuple-element.93), channel_id=1, source_target_pairs={{0,5},{1,6},{2,7},{3,4},{4,9},{5,10},{6,11},{7,8},{8,13},{9,14},{1... | collective-permute-start | bytes 1544 | tf_op jit(solution)/shard_map/ppermute | solution.py:592
  12.9 8.6 %collective-permute-start.6 = (f32[3,64,128]{2,1,0:T(8,128)S(1)}, f32[3,64,128]{2,1,0:T(8,128)S(1)}, u32[]{:S(2)}, u32[]{:S(2)}) collective-permute-start(f32[3,64,128]{2,1,0:T(8,128)S(1)} %get-tuple-element.121.refs_3_), channel_id=1, source_target_pairs={{0,4},{1,5},{2,6},{3,7},{4,0},{5,1},{6,2},{7,3},{8,12},{9,13},{10,... | collective-permute-start | bytes 294920 | tf_op jit(solution)/shard_map/ppermute | solution.py:592
  15.3 5.2 %collective-permute-start.7 = (f32[3,32,128]{2,1,0:T(8,128)S(1)}, f32[3,32,128]{2,1,0:T(8,128)S(1)}, u32[]{:S(2)}, u32[]{:S(2)}) collective-permute-start(f32[3,32,128]{2,1,0:T(8,128)S(1)} %get-tuple-element.125.own_half_ref), channel_id=1, source_target_pairs={{0,1},{1,0},{2,3},{3,2},{4,8},{5,9},{6,10},{7,11},{8,4},{9,5},{10,... | collective-permute-start | bytes 147464 | tf_op jit(solution)/shard_map/ppermute | solution.py:592
  17.4 4.1 %collective-permute-start.8 = (f32[3,32,128]{2,1,0:T(8,128)S(1)}, f32[3,32,128]{2,1,0:T(8,128)S(1)}, u32[]{:S(2)}, u32[]{:S(2)}) collective-permute-start(f32[3,32,128]{2,1,0:T(8,128)S(1)} %get-tuple-element.126.own_rest_ref), channel_id=1, source_target_pairs={{0,1},{1,0},{2,3},{3,2},{4,8},{5,9},{6,10},{7,11},{8,4},{9,5},{10,... | collective-permute-start | bytes 147464 | tf_op jit(solution)/shard_map/ppermute | solution.py:592
  17.4 4.1 %collective-permute-start.9 = (f32[3,16,128]{2,1,0:T(8,128)S(1)}, f32[3,16,128]{2,1,0:T(8,128)S(1)}, u32[]{:S(2)}, u32[]{:S(2)}) collective-permute-start(f32[3,16,128]{2,1,0:T(8,128)S(1)} %get-tuple-element.123.refs_5_), channel_id=1, source_target_pairs={{0,1},{1,0},{2,3},{3,2},{4,5},{5,4},{6,7},{7,6},{8,9},{9,8},{10,11... | collective-permute-start | bytes 73736 | tf_op jit(solution)/shard_map/ppermute | solution.py:592
  17.4 4.1 %collective-permute-start.10 = (f32[3,16,128]{2,1,0:T(8,128)S(1)}, f32[3,16,128]{2,1,0:T(8,128)S(1)}, u32[]{:S(2)}, u32[]{:S(2)}) collective-permute-start(f32[3,16,128]{2,1,0:T(8,128)S(1)} %get-tuple-element.124.refs_6_), channel_id=1, source_target_pairs={{0,3},{1,2},{2,1},{3,0},{4,7},{5,6},{6,5},{7,4},{8,11},{9,10},{10,... | collective-permute-start | bytes 73736 | tf_op jit(solution)/shard_map/ppermute | solution.py:592
  21.6 7.3 %collective-permute-start.11 = (f32[3,64,128]{2,1,0:T(8,128)S(1)}, f32[3,64,128]{2,1,0:T(8,128)S(1)}, u32[]{:S(2)}, u32[]{:S(2)}) collective-permute-start(f32[3,64,128]{2,1,0:T(8,128)S(1)} %get-tuple-element.135.refs_3_), channel_id=1, source_target_pairs={{0,4},{1,5},{2,6},{3,7},{4,0},{5,1},{6,2},{7,3},{8,12},{9,13},{10,... | collective-permute-start | bytes 294920 | tf_op jit(solution)/shard_map/ppermute | solution.py:592
  21.7 5.8 %collective-permute-start.12 = (f32[3,32,128]{2,1,0:T(8,128)S(1)}, f32[3,32,128]{2,1,0:T(8,128)S(1)}, u32[]{:S(2)}, u32[]{:S(2)}) collective-permute-start(f32[3,32,128]{2,1,0:T(8,128)S(1)} %get-tuple-element.139.own_half_ref), channel_id=1, source_target_pairs={{0,1},{1,0},{2,3},{3,2},{4,8},{5,9},{6,10},{7,11},{8,4},{9,5},{10,... | collective-permute-start | bytes 147464 | tf_op jit(solution)/shard_map/ppermute | solution.py:592
  24.7 4.2 %collective-permute-start.13 = (f32[3,32,128]{2,1,0:T(8,128)S(1)}, f32[3,32,128]{2,1,0:T(8,128)S(1)}, u32[]{:S(2)}, u32[]{:S(2)}) collective-permute-start(f32[3,32,128]{2,1,0:T(8,128)S(1)} %get-tuple-element.140.own_rest_ref), channel_id=1, source_target_pairs={{0,1},{1,0},{2,3},{3,2},{4,8},{5,9},{6,10},{7,11},{8,4},{9,5},{10,... | collective-permute-start | bytes 147464 | tf_op jit(solution)/shard_map/ppermute | solution.py:592
  24.7 4.2 %collective-permute-start.14 = (f32[3,16,128]{2,1,0:T(8,128)S(1)}, f32[3,16,128]{2,1,0:T(8,128)S(1)}, u32[]{:S(2)}, u32[]{:S(2)}) collective-permute-start(f32[3,16,128]{2,1,0:T(8,128)S(1)} %get-tuple-element.137.refs_5_), channel_id=1, source_target_pairs={{0,1},{1,0},{2,3},{3,2},{4,5},{5,4},{6,7},{7,6},{8,9},{9,8},{10,11... | collective-permute-start | bytes 73736 | tf_op jit(solution)/shard_map/ppermute | solution.py:592
  25.3 3.6 %collective-permute-start.15 = (f32[3,16,128]{2,1,0:T(8,128)S(1)}, f32[3,16,128]{2,1,0:T(8,128)S(1)}, u32[]{:S(2)}, u32[]{:S(2)}) collective-permute-start(f32[3,16,128]{2,1,0:T(8,128)S(1)} %get-tuple-element.138.refs_6_), channel_id=1, source_target_pairs={{0,3},{1,2},{2,1},{3,0},{4,7},{5,6},{6,5},{7,4},{8,11},{9,10},{10,... | collective-permute-start | bytes 73736 | tf_op jit(solution)/shard_map/ppermute | solution.py:592
  29.0 9.2 %collective-permute-start.18 = (f32[3,64,128]{2,1,0:T(8,128)S(1)}, f32[3,64,128]{2,1,0:T(8,128)S(1)}, u32[]{:S(2)}, u32[]{:S(2)}) collective-permute-start(f32[3,64,128]{2,1,0:T(8,128)S(1)} %get-tuple-element.151.refs_4_), channel_id=1, source_target_pairs={{0,4},{1,5},{2,6},{3,7},{4,0},{5,1},{6,2},{7,3},{8,12},{9,13},{10,... | collective-permute-start | bytes 294920 | tf_op jit(solution)/shard_map/ppermute | solution.py:592
  29.1 6.3 %collective-permute-start.16 = (f32[3,32,128]{2,1,0:T(8,128)S(1)}, f32[3,32,128]{2,1,0:T(8,128)S(1)}, u32[]{:S(2)}, u32[]{:S(2)}) collective-permute-start(f32[3,32,128]{2,1,0:T(8,128)S(1)} %get-tuple-element.147.refs_0_), channel_id=1, source_target_pairs={{0,1},{1,0},{2,3},{3,2},{4,8},{5,9},{6,10},{7,11},{8,4},{9,5},{10,... | collective-permute-start | bytes 147464 | tf_op jit(solution)/shard_map/ppermute | solution.py:592
  32.5 4.1 %collective-permute-start.17 = (f32[3,32,128]{2,1,0:T(8,128)S(1)}, f32[3,32,128]{2,1,0:T(8,128)S(1)}, u32[]{:S(2)}, u32[]{:S(2)}) collective-permute-start(f32[3,32,128]{2,1,0:T(8,128)S(1)} %get-tuple-element.148.refs_1_), channel_id=1, source_target_pairs={{0,1},{1,0},{2,3},{3,2},{4,8},{5,9},{6,10},{7,11},{8,4},{9,5},{10,... | collective-permute-start | bytes 147464 | tf_op jit(solution)/shard_map/ppermute | solution.py:592
  32.5 5.7 %collective-permute-start.19 = (f32[3,16,128]{2,1,0:T(8,128)S(1)}, f32[3,16,128]{2,1,0:T(8,128)S(1)}, u32[]{:S(2)}, u32[]{:S(2)}) collective-permute-start(f32[3,16,128]{2,1,0:T(8,128)S(1)} %get-tuple-element.153.refs_6_), channel_id=1, source_target_pairs={{0,1},{1,0},{2,3},{3,2},{4,5},{5,4},{6,7},{7,6},{8,9},{9,8},{10,11... | collective-permute-start | bytes 73736 | tf_op jit(solution)/shard_map/ppermute | solution.py:592
  32.5 5.8 %collective-permute-start.20 = (f32[3,16,128]{2,1,0:T(8,128)S(1)}, f32[3,16,128]{2,1,0:T(8,128)S(1)}, u32[]{:S(2)}, u32[]{:S(2)}) collective-permute-start(f32[3,16,128]{2,1,0:T(8,128)S(1)} %get-tuple-element.154.refs_7_), channel_id=1, source_target_pairs={{0,3},{1,2},{2,1},{3,0},{4,7},{5,6},{6,5},{7,4},{8,11},{9,10},{10,... | collective-permute-start | bytes 73736 | tf_op jit(solution)/shard_map/ppermute | solution.py:592

commit v11 on v10

--- a/solution.py
+++ b/solution.py
@@ -516,24 +516,18 @@
     sent, got, edges, refs = arrivals(refs, 5)
     push_ref, d_ref, v_ref, planes_ref, rows_ref, sems = refs
     _, planes, rows, cols = u_ref.shape
-    tile = rows_ref.shape[4]
     inner = slice(1, planes - 1)
     copies = []
     moves = [link_moves(1.0, (), sent, got, edges, push_ref, c) for c in range(3)]
     results = ((u_ref, d_ref, 1.0 / U_SCALE), (w_ref, v_ref, 1.0 / W_SCALE))
     for n, (ref, out, scale) in enumerate(results):
-        for side, at in ((0, 0), (1, rows - tile)):
+        for side, at in ((0, 0), (1, rows - 1)):
             for c in range(3):
                 fix = moves[c][2 + side] * scale
                 for i in range(1, planes - 1):
-                    value = ref[c, i, at : at + tile]
-                    line = fix[i : i + 1]
-                    row = lax.broadcasted_iota(jnp.int32, (tile, cols), 0)
-                    rows_ref[n, side, c, i - 1] = value + jnp.where(row == (tile - 1 if side else 0), line, 0.0)
+                    rows_ref[n, side, c, i - 1] = ref[c, i, at : at + 1] + fix[i : i + 1]
             copies.append(
-                pltpu.make_async_copy(
-                    rows_ref.at[n, side], out.at[:, inner, at : at + tile], sems.at[len(copies)]
-                )
+                pltpu.make_async_copy(rows_ref.at[n, side], out.at[:, inner, at : at + 1], sems.at[len(copies)])
             )
             copies[-1].start()
     for n, (ref, out, scale) in enumerate(results):
@@ -689,7 +683,7 @@
         [u, w, d, v, *sent, *got, *edges, push],
         [None, None, hbm, hbm] + [None] * 14,
         aliases={2: 0, 3: 1},
-        scratch=[vmem((2, 2, *face3)), vmem((2, 2, 3, planes - 2, tile, cols)), pltpu.SemaphoreType.DMA((8,))],
+        scratch=[vmem((2, 2, *face3)), vmem((2, 2, 3, planes - 2, 1, cols)), pltpu.SemaphoreType.DMA((8,))],
         hbm_outs=2,
     )
     return d[None], v[None]

time: 39.6 us -> 39.5 us (level)
  no operation moved by 1% of the time
where the time goes in v11:
time: 39.5 us; the launch traced here: 39.3 us
  starting transfers between devices  20.9 us (53%)
  Pallas kernels  13.9 us (35%)
  waiting for transfers between devices  3.52 us (9%)
  between operations  0.95 us (2%)
    ppermute x21, starting transfers between devices, passed(): return lax.ppermute(block, AXES, route[name])  20.9 us
    pallas_call x15, Pallas kernels, call(): pl.pallas_call(kernel, out_shape=outs, in_specs=specs, out_specs=[pl.Bloc...  13.9 us
    ppermute x21, waiting for transfers between devices, passed(): return lax.ppermute(block, AXES, route[name])  3.52 us
  transfers between devices with their start and end apart: 21, of which 3 were waited for; matrix products, arithmetic and copies ran while one was open for 0% of the time, Pallas kernels for 27%

profile of v11, /device:TPU:8, one launch (start us, length us, event | category | flops | bytes accessed | tf_op | source)
XLA Modules:
  0.0 39.3 jit_solution(7586379288627122504)
XLA Ops:
  0.7 1.2 %shard_map.86 = (f32[4,64,128]{2,1,0:T(8,128)S(1)}, f32[4,64,128]{2,1,0:T(8,128)S(1)}, f32[4,16,128]{2,1,0:T(8,128)S(1)}, f32[4,16,128]{2,1,0:T(8,128)S(1)}, f32...) custom-call(f32[3,16,64,128]{3,2,1,0:T(8,128)} %bitcast.5, s32[16,64,128]{2,1,0:T(8,128)} %bitcast.8), custom_call_target="tpu_custom_call" | custom-call | tf_op jit(solution)/shard_map/pallas_call | solution.py:47
  1.9 1.6 %collective-permute-start.2 = (f32[4,64,128]{2,1,0:T(8,128)S(1)}, f32[4,64,128]{2,1,0:T(8,128)S(1)}, u32[]{:S(2)}, u32[]{:S(2)}) collective-permute-start(f32[4,64,128]{2,1,0:T(8,128)S(1)} %get-tuple-element.90.sb_ref.own_ref.refs_6_), channel_id=1, source_target_pairs={{0,1},{1,0},{2,3},{3,2},{4,8},{5,9},{6,10},{7,11},{8,4},{9,5},{10,... | collective-permute-start | bytes 393224 | tf_op jit(solution)/shard_map/ppermute | solution.py:586
  3.6 0.5 %collective-permute-start = (f32[4,16,128]{2,1,0:T(8,128)S(1)}, f32[4,16,128]{2,1,0:T(8,128)S(1)}, u32[]{:S(2)}, u32[]{:S(2)}) collective-permute-start(f32[4,16,128]{2,1,0:T(8,128)S(1)} %get-tuple-element.80.sc_ref.refs_7_), channel_id=1, source_target_pairs={{0,1},{1,0},{2,3},{3,2},{4,5},{5,4},{6,7},{7,6},{8,9},{9,8},{10,11... | collective-permute-start | bytes 98312 | tf_op jit(solution)/shard_map/ppermute | solution.py:586
  4.1 1.1 %collective-permute-start.3 = (f32[4,16,128]{2,1,0:T(8,128)S(1)}, f32[4,16,128]{2,1,0:T(8,128)S(1)}, u32[]{:S(2)}, u32[]{:S(2)}) collective-permute-start(f32[4,16,128]{2,1,0:T(8,128)S(1)} %get-tuple-element.91.sd_ref.refs_8_), channel_id=1, source_target_pairs={{0,3},{1,2},{2,1},{3,0},{4,7},{5,6},{6,5},{7,4},{8,11},{9,10},{10,... | collective-permute-start | bytes 98312 | tf_op jit(solution)/shard_map/ppermute | solution.py:586
  5.3 1.4 %shard_map.87 = (f32[16,64,128]{2,1,0:T(8,128)S(1)}, f32[16,64,128]{2,1,0:T(8,128)S(1)}, f32[16,64,128]{2,1,0:T(8,128)S(1)}, f32[16,64,128]{2,1,0:T(8,128)S(1)},...) custom-call(s32[16,64,128]{2,1,0:T(8,128)S(1)} %bitcast.9, ...), custom_call_target="tpu_custom_call", output_to_operand_aliasing={{9}: (1, {})} | custom-call | flops 8000000 | tf_op jit(solution)/shard_map/pallas_call | solution.py:47
  6.7 3.2 %collective-permute-start.4 = (f32[1,128]{1,0:T(1,128)S(1)}, f32[1,128]{1,0:T(1,128)S(1)}, u32[]{:S(2)}, u32[]{:S(2)}) collective-permute-start(f32[1,128]{1,0:T(1,128)S(1)} %get-tuple-element.93), channel_id=1, source_target_pairs={{0,5},{1,6},{2,7},{3,4},{4,9},{5,10},{6,11},{7,8},{8,13},{9,14},{1... | collective-permute-start | bytes 1544 | tf_op jit(solution)/shard_map/ppermute | solution.py:586
  9.9 2.0 %shard_map.88 = (f32[3,16,64,128]{3,2,1,0:T(8,128)S(1)}, f32[3,16,64,128]{3,2,1,0:T(8,128)S(1)}, f32[3,16,128]{2,1,0:T(8,128)S(1)}, f32[3,16,128]{2,1,0:T(8,128)S(1)}) custom-call(f32[3,16,64,128]{3,2,1,0:T(8,128)S(1)} %bitcast.7, f32[3,16,64,128]{3,2,1,0:T(8,128)S(1)} %bitcast.10, f32[16,64,128]{2,1,0:T(8,128)S(1)} %get-tuple-element.81.kx_ref.kx_in, ...), custom_call_target="tpu_custom_call" | custom-call | tf_op jit(solution)/shard_map/pallas_call | solution.py:47
  12.0 0.7 %shard_map.89 = (f32[16,64,128]{2,1,0:T(8,128)S(1)}, f32[16,64,128]{2,1,0:T(8,128)S(1)}, f32[16,64,128]{2,1,0:T(8,128)S(1)}, f32[64,128]{1,0:T(8,128)S(1)}, f32[...) custom-call(f32[4,64,128]{2,1,0:T(8,128)S(1)} %get-tuple-element.89., ...), custom_call_target="tpu_custom_call", output_to_operand_aliasing={{0}: (12, {}), {1}: (13, {}), {2}: (14, {})} | custom-call | tf_op jit(solution)/shard_map/pallas_call | solution.py:47
  12.7 0.1 shard_map.91
  12.9 2.5 %collective-permute-start.6 = (f32[3,64,128]{2,1,0:T(8,128)S(1)}, f32[3,64,128]{2,1,0:T(8,128)S(1)}, u32[]{:S(2)}, u32[]{:S(2)}) collective-permute-start(f32[3,64,128]{2,1,0:T(8,128)S(1)} %get-tuple-element.121.refs_3_), channel_id=1, source_target_pairs={{0,4},{1,5},{2,6},{3,7},{4,0},{5,1},{6,2},{7,3},{8,12},{9,13},{10,... | collective-permute-start | bytes 294920 | tf_op jit(solution)/shard_map/ppermute | solution.py:586
  15.3 2.0 %collective-permute-start.7 = (f32[3,32,128]{2,1,0:T(8,128)S(1)}, f32[3,32,128]{2,1,0:T(8,128)S(1)}, u32[]{:S(2)}, u32[]{:S(2)}) collective-permute-start(f32[3,32,128]{2,1,0:T(8,128)S(1)} %get-tuple-element.125.own_half_ref), channel_id=1, source_target_pairs={{0,1},{1,0},{2,3},{3,2},{4,8},{5,9},{6,10},{7,11},{8,4},{9,5},{10,... | collective-permute-start | bytes 147464 | tf_op jit(solution)/shard_map/ppermute | solution.py:586
  17.4 0.0 collective-permute-start.8
  17.4 1.3 %collective-permute-start.10 = (f32[3,16,128]{2,1,0:T(8,128)S(1)}, f32[3,16,128]{2,1,0:T(8,128)S(1)}, u32[]{:S(2)}, u32[]{:S(2)}) collective-permute-start(f32[3,16,128]{2,1,0:T(8,128)S(1)} %get-tuple-element.124.refs_6_), channel_id=1, source_target_pairs={{0,3},{1,2},{2,1},{3,0},{4,7},{5,6},{6,5},{7,4},{8,11},{9,10},{10,... | collective-permute-start | bytes 73736 | tf_op jit(solution)/shard_map/ppermute | solution.py:586
  18.7 1.8 %shard_map.92 = (f32[3,16,64,128]{3,2,1,0:T(8,128)S(1)}, f32[3,16,64,128]{3,2,1,0:T(8,128)S(1)}, f32[3,16,128]{2,1,0:T(8,128)S(1)}, f32[3,16,128]{2,1,0:T(8,128)S(1)}) custom-call(f32[3,16,64,128]{3,2,1,0:T(8,128)S(1)} %get-tuple-element.87.refs_2_.u_in, ...), custom_call_target="tpu_custom_call", output_to_operand_aliasing={{0}: (0, {}), {1}: (1, {})} | custom-call | flops 20000000 | tf_op jit(solution)/shard_map/pallas_call | solution.py:47
  20.5 0.9 %collective-permute-done.8.rest_ref.refs_9_ = f32[3,32,128]{2,1,0:T(8,128)S(1)} collective-permute-done((f32[3,32,128]{2,1,0:T(8,128)S(1)}, f32[3,32,128]{2,1,0:T(8,128)S(1)}, u32[]{:S(2)}, u32[]{:S(2)}) %collective-permute-start.8) | collective-permute-done | bytes 49184 | tf_op jit(solution)/shard_map/ppermute | solution.py:586
  21.5 0.1 shard_map.94
  21.6 0.1 collective-permute-start.11
  21.7 3.0 %collective-permute-start.12 = (f32[3,32,128]{2,1,0:T(8,128)S(1)}, f32[3,32,128]{2,1,0:T(8,128)S(1)}, u32[]{:S(2)}, u32[]{:S(2)}) collective-permute-start(f32[3,32,128]{2,1,0:T(8,128)S(1)} %get-tuple-element.139.own_half_ref), channel_id=1, source_target_pairs={{0,1},{1,0},{2,3},{3,2},{4,8},{5,9},{6,10},{7,11},{8,4},{9,5},{10,... | collective-permute-start | bytes 147464 | tf_op jit(solution)/shard_map/ppermute | solution.py:586
  24.7 0.0 collective-permute-start.13
  24.7 0.6 %collective-permute-start.14 = (f32[3,16,128]{2,1,0:T(8,128)S(1)}, f32[3,16,128]{2,1,0:T(8,128)S(1)}, u32[]{:S(2)}, u32[]{:S(2)}) collective-permute-start(f32[3,16,128]{2,1,0:T(8,128)S(1)} %get-tuple-element.137.refs_5_), channel_id=1, source_target_pairs={{0,1},{1,0},{2,3},{3,2},{4,5},{5,4},{6,7},{7,6},{8,9},{9,8},{10,11... | collective-permute-start | bytes 73736 | tf_op jit(solution)/shard_map/ppermute | solution.py:586
  25.3 0.4 %collective-permute-start.15 = (f32[3,16,128]{2,1,0:T(8,128)S(1)}, f32[3,16,128]{2,1,0:T(8,128)S(1)}, u32[]{:S(2)}, u32[]{:S(2)}) collective-permute-start(f32[3,16,128]{2,1,0:T(8,128)S(1)} %get-tuple-element.138.refs_6_), channel_id=1, source_target_pairs={{0,3},{1,2},{2,1},{3,0},{4,7},{5,6},{6,5},{7,4},{8,11},{9,10},{10,... | collective-permute-start | bytes 73736 | tf_op jit(solution)/shard_map/ppermute | solution.py:586
  25.7 1.8 %shard_map.95 = (f32[3,16,64,128]{3,2,1,0:T(8,128)S(1)}, f32[3,16,64,128]{3,2,1,0:T(8,128)S(1)}, f32[3,16,128]{2,1,0:T(8,128)S(1)}, f32[3,16,128]{2,1,0:T(8,128)S(1)}) custom-call(f32[3,16,64,128]{3,2,1,0:T(8,128)S(1)} %get-tuple-element.117.refs_0_.u_in, ...), custom_call_target="tpu_custom_call", output_to_operand_aliasing={{0}: (0, {}), {1}: (1, {})} | custom-call | flops 20000000 | tf_op jit(solution)/shard_map/pallas_call | solution.py:47
  27.5 1.4 %collective-permute-done.13.rest_ref.refs_9_ = f32[3,32,128]{2,1,0:T(8,128)S(1)} collective-permute-done((f32[3,32,128]{2,1,0:T(8,128)S(1)}, f32[3,32,128]{2,1,0:T(8,128)S(1)}, u32[]{:S(2)}, u32[]{:S(2)}) %collective-permute-start.13) | collective-permute-done | bytes 49184 | tf_op jit(solution)/shard_map/ppermute | solution.py:586
  28.9 0.1 shard_map.97
  29.0 0.1 collective-permute-start.18
  29.1 3.4 %collective-permute-start.16 = (f32[3,32,128]{2,1,0:T(8,128)S(1)}, f32[3,32,128]{2,1,0:T(8,128)S(1)}, u32[]{:S(2)}, u32[]{:S(2)}) collective-permute-start(f32[3,32,128]{2,1,0:T(8,128)S(1)} %get-tuple-element.147.refs_0_), channel_id=1, source_target_pairs={{0,1},{1,0},{2,3},{3,2},{4,8},{5,9},{6,10},{7,11},{8,4},{9,5},{10,... | collective-permute-start | bytes 147464 | tf_op jit(solution)/shard_map/ppermute | solution.py:586
  32.5 0.0 collective-permute-start.17
  32.5 1.0 %collective-permute-start.20 = (f32[3,16,128]{2,1,0:T(8,128)S(1)}, f32[3,16,128]{2,1,0:T(8,128)S(1)}, u32[]{:S(2)}, u32[]{:S(2)}) collective-permute-start(f32[3,16,128]{2,1,0:T(8,128)S(1)} %get-tuple-element.154.refs_7_), channel_id=1, source_target_pairs={{0,3},{1,2},{2,1},{3,0},{4,7},{5,6},{6,5},{7,4},{8,11},{9,10},{10,... | collective-permute-start | bytes 73736 | tf_op jit(solution)/shard_map/ppermute | solution.py:586
  33.6 1.9 %shard_map.98 = (f32[3,16,64,128]{3,2,1,0:T(8,128)S(1)}, f32[3,16,64,128]{3,2,1,0:T(8,128)S(1)}) custom-call(f32[3,16,64,128]{3,2,1,0:T(8,128)S(1)} %get-tuple-element.131.refs_0_.u_in, f32[3,16,64,128]{3,2,1,0:T(8,128)S(1)} %get-tuple-element.132.w_in, f32[16,64,128]{2,1,0:T(8,128)S(1)} %get-tuple-element.96.kx_ref, ...), custom_call_target="tpu_custom_call", output_to_operand_aliasing={{0}: (0, {}), {1}: (1, {})} | custom-call | flops 20000000 | tf_op jit(solution)/shard_map/pallas_call | solution.py:47
  35.5 1.1 %collective-permute-done.17.refs_3_.refs_10_ = f32[3,32,128]{2,1,0:T(8,128)S(1)} collective-permute-done((f32[3,32,128]{2,1,0:T(8,128)S(1)}, f32[3,32,128]{2,1,0:T(8,128)S(1)}, u32[]{:S(2)}, u32[]{:S(2)}) %collective-permute-start.17) | collective-permute-done | bytes 49184 | tf_op jit(solution)/shard_map/ppermute | solution.py:586
  36.6 1.7 %shard_map.99 = (f32[3,16,64,128]{3,2,1,0:T(8,128)}, f32[3,16,64,128]{3,2,1,0:T(8,128)}, f32[64,128]{1,0:T(8,128)S(1)}) custom-call(f32[3,32,128]{2,1,0:T(8,128)S(1)} %get-tuple-element.147.refs_0_, f32[3,32,128]{2,1,0:T(8,128)S(1)} %get-tuple-element.148.refs_1_, f32[3,32,128]{2,1,0:T(8,128)S(1)} %collective-permute-done.16.refs_2_.refs_9_, ...), custom_call_target="tpu_custom_call" | custom-call | flops 20000000 | tf_op jit(solution)/shard_map/pallas_call | solution.py:47
  38.3 1.0 %shard_map.100 = (f32[3,16,64,128]{3,2,1,0:T(8,128)}, f32[3,16,64,128]{3,2,1,0:T(8,128)}) custom-call(f32[3,16,64,128]{3,2,1,0:T(8,128)S(1)} %get-tuple-element.145.refs_6_.refs_0_, f32[3,16,64,128]{3,2,1,0:T(8,128)S(1)} %get-tuple-element.146.refs_7_.refs_1_, ...), custom_call_target="tpu_custom_call", output_to_operand_aliasing={{0}: (2, {}), {1}: (3, {})} | custom-call | tf_op jit(solution)/shard_map/pallas_call | solution.py:47
  (39 shorter events, 0.1 us)
Async XLA Ops:
  0.6 4.6 %copy-start.1 = (s32[1,16,64,128]{3,2,1,0:T(8,128)S(1)}, s32[1,16,64,128]{3,2,1,0:T(8,128)}, u32[]{:S(2)}) copy-start(s32[1,16,64,128]{3,2,1,0:T(8,128)} %param.9) | copy-start | bytes 1572868
  0.6 4.6 %copy-start = (f32[1,3,16,64,128]{4,3,2,1,0:T(8,128)S(1)}, f32[1,3,16,64,128]{4,3,2,1,0:T(8,128)}, u32[]{:S(2)}) copy-start(f32[1,3,16,64,128]{4,3,2,1,0:T(8,128)} %param.7) | copy-start | bytes 4718596
  0.7 4.6 %copy-start.3 = (f32[8]{0:T(128)S(1)}, f32[8]{0:T(128)}, u32[]{:S(2)}) copy-start(f32[8]{0:T(128)} %moduli_ref.3) | copy-start | bytes 100
  0.7 4.6 %copy-start.5 = (s32[256]{0:T(256)S(1)}, s32[256]{0:T(256)}, u32[]{:S(2)}) copy-start(s32[256]{0:T(256)} %active_ref.1) | copy-start | bytes 3076
  0.7 4.6 %copy-start.4 = (s32[256]{0:T(256)S(1)}, s32[256]{0:T(256)}, u32[]{:S(2)}) copy-start(s32[256]{0:T(256)} %partner_ref.1) | copy-start | bytes 3076
  0.7 4.6 %copy-start.6 = (f32[8]{0:T(128)S(1)}, f32[8]{0:T(128)}, u32[]{:S(2)}) copy-start(f32[8]{0:T(128)} %density_ref.1) | copy-start | bytes 100
  1.9 8.0 %copy-start.2 = (f32[1,3,16,64,128]{4,3,2,1,0:T(8,128)S(1)}, f32[1,3,16,64,128]{4,3,2,1,0:T(8,128)}, u32[]{:S(2)}) copy-start(f32[1,3,16,64,128]{4,3,2,1,0:T(8,128)} %param.8) | copy-start | bytes 4718596
  1.9 10.0 %collective-permute-start.2 = (f32[4,64,128]{2,1,0:T(8,128)S(1)}, f32[4,64,128]{2,1,0:T(8,128)S(1)}, u32[]{:S(2)}, u32[]{:S(2)}) collective-permute-start(f32[4,64,128]{2,1,0:T(8,128)S(1)} %get-tuple-element.90.sb_ref.own_ref.refs_6_), channel_id=1, source_target_pairs={{0,1},{1,0},{2,3},{3,2},{4,8},{5,9},{6,10},{7,11},{8,4},{9,5},{10,... | collective-permute-start | bytes 393224 | tf_op jit(solution)/shard_map/ppermute | solution.py:586
  3.6 8.4 %collective-permute-start.1 = (f32[4,64,128]{2,1,0:T(8,128)S(1)}, f32[4,64,128]{2,1,0:T(8,128)S(1)}, u32[]{:S(2)}, u32[]{:S(2)}) collective-permute-start(f32[4,64,128]{2,1,0:T(8,128)S(1)} %get-tuple-element.89.sa_ref.refs_5_), channel_id=1, source_target_pairs={{0,4},{1,5},{2,6},{3,7},{4,0},{5,1},{6,2},{7,3},{8,12},{9,13},{10,... | collective-permute-start | bytes 393224 | tf_op jit(solution)/shard_map/ppermute | solution.py:586
  3.6 8.3 %collective-permute-start.5 = (f32[3,64,128]{2,1,0:T(8,128)S(1)}, f32[3,64,128]{2,1,0:T(8,128)S(1)}, u32[]{:S(2)}, u32[]{:S(2)}) collective-permute-start(f32[3,64,128]{2,1,0:T(8,128)S(1)} %get-tuple-element.109), channel_id=1, source_target_pairs={{0,1},{1,0},{2,3},{3,2},{4,5},{5,4},{6,7},{7,6},{8,9},{9,8},{10,11... | collective-permute-start | bytes 294920 | tf_op jit(solution)/shard_map/ppermute | solution.py:586
  3.6 1.6 %collective-permute-start = (f32[4,16,128]{2,1,0:T(8,128)S(1)}, f32[4,16,128]{2,1,0:T(8,128)S(1)}, u32[]{:S(2)}, u32[]{:S(2)}) collective-permute-start(f32[4,16,128]{2,1,0:T(8,128)S(1)} %get-tuple-element.80.sc_ref.refs_7_), channel_id=1, source_target_pairs={{0,1},{1,0},{2,3},{3,2},{4,5},{5,4},{6,7},{7,6},{8,9},{9,8},{10,11... | collective-permute-start | bytes 98312 | tf_op jit(solution)/shard_map/ppermute | solution.py:586
  4.1 7.9 %collective-permute-start.3 = (f32[4,16,128]{2,1,0:T(8,128)S(1)}, f32[4,16,128]{2,1,0:T(8,128)S(1)}, u32[]{:S(2)}, u32[]{:S(2)}) collective-permute-start(f32[4,16,128]{2,1,0:T(8,128)S(1)} %get-tuple-element.91.sd_ref.refs_8_), channel_id=1, source_target_pairs={{0,3},{1,2},{2,1},{3,0},{4,7},{5,6},{6,5},{7,4},{8,11},{9,10},{10,... | collective-permute-start | bytes 98312 | tf_op jit(solution)/shard_map/ppermute | solution.py:586
  6.7 5.3 %collective-permute-start.4 = (f32[1,128]{1,0:T(1,128)S(1)}, f32[1,128]{1,0:T(1,128)S(1)}, u32[]{:S(2)}, u32[]{:S(2)}) collective-permute-start(f32[1,128]{1,0:T(1,128)S(1)} %get-tuple-element.93), channel_id=1, source_target_pairs={{0,5},{1,6},{2,7},{3,4},{4,9},{5,10},{6,11},{7,8},{8,13},{9,14},{1... | collective-permute-start | bytes 1544 | tf_op jit(solution)/shard_map/ppermute | solution.py:586
  12.9 8.6 %collective-permute-start.6 = (f32[3,64,128]{2,1,0:T(8,128)S(1)}, f32[3,64,128]{2,1,0:T(8,128)S(1)}, u32[]{:S(2)}, u32[]{:S(2)}) collective-permute-start(f32[3,64,128]{2,1,0:T(8,128)S(1)} %get-tuple-element.121.refs_3_), channel_id=1, source_target_pairs={{0,4},{1,5},{2,6},{3,7},{4,0},{5,1},{6,2},{7,3},{8,12},{9,13},{10,... | collective-permute-start | bytes 294920 | tf_op jit(solution)/shard_map/ppermute | solution.py:586
  15.3 5.2 %collective-permute-start.7 = (f32[3,32,128]{2,1,0:T(8,128)S(1)}, f32[3,32,128]{2,1,0:T(8,128)S(1)}, u32[]{:S(2)}, u32[]{:S(2)}) collective-permute-start(f32[3,32,128]{2,1,0:T(8,128)S(1)} %get-tuple-element.125.own_half_ref), channel_id=1, source_target_pairs={{0,1},{1,0},{2,3},{3,2},{4,8},{5,9},{6,10},{7,11},{8,4},{9,5},{10,... | collective-permute-start | bytes 147464 | tf_op jit(solution)/shard_map/ppermute | solution.py:586
  17.4 4.1 %collective-permute-start.8 = (f32[3,32,128]{2,1,0:T(8,128)S(1)}, f32[3,32,128]{2,1,0:T(8,128)S(1)}, u32[]{:S(2)}, u32[]{:S(2)}) collective-permute-start(f32[3,32,128]{2,1,0:T(8,128)S(1)} %get-tuple-element.126.own_rest_ref), channel_id=1, source_target_pairs={{0,1},{1,0},{2,3},{3,2},{4,8},{5,9},{6,10},{7,11},{8,4},{9,5},{10,... | collective-permute-start | bytes 147464 | tf_op jit(solution)/shard_map/ppermute | solution.py:586
  17.4 4.1 %collective-permute-start.9 = (f32[3,16,128]{2,1,0:T(8,128)S(1)}, f32[3,16,128]{2,1,0:T(8,128)S(1)}, u32[]{:S(2)}, u32[]{:S(2)}) collective-permute-start(f32[3,16,128]{2,1,0:T(8,128)S(1)} %get-tuple-element.123.refs_5_), channel_id=1, source_target_pairs={{0,1},{1,0},{2,3},{3,2},{4,5},{5,4},{6,7},{7,6},{8,9},{9,8},{10,11... | collective-permute-start | bytes 73736 | tf_op jit(solution)/shard_map/ppermute | solution.py:586
  17.4 4.1 %collective-permute-start.10 = (f32[3,16,128]{2,1,0:T(8,128)S(1)}, f32[3,16,128]{2,1,0:T(8,128)S(1)}, u32[]{:S(2)}, u32[]{:S(2)}) collective-permute-start(f32[3,16,128]{2,1,0:T(8,128)S(1)} %get-tuple-element.124.refs_6_), channel_id=1, source_target_pairs={{0,3},{1,2},{2,1},{3,0},{4,7},{5,6},{6,5},{7,4},{8,11},{9,10},{10,... | collective-permute-start | bytes 73736 | tf_op jit(solution)/shard_map/ppermute | solution.py:586
  21.6 7.3 %collective-permute-start.11 = (f32[3,64,128]{2,1,0:T(8,128)S(1)}, f32[3,64,128]{2,1,0:T(8,128)S(1)}, u32[]{:S(2)}, u32[]{:S(2)}) collective-permute-start(f32[3,64,128]{2,1,0:T(8,128)S(1)} %get-tuple-element.135.refs_3_), channel_id=1, source_target_pairs={{0,4},{1,5},{2,6},{3,7},{4,0},{5,1},{6,2},{7,3},{8,12},{9,13},{10,... | collective-permute-start | bytes 294920 | tf_op jit(solution)/shard_map/ppermute | solution.py:586
  21.7 5.8 %collective-permute-start.12 = (f32[3,32,128]{2,1,0:T(8,128)S(1)}, f32[3,32,128]{2,1,0:T(8,128)S(1)}, u32[]{:S(2)}, u32[]{:S(2)}) collective-permute-start(f32[3,32,128]{2,1,0:T(8,128)S(1)} %get-tuple-element.139.own_half_ref), channel_id=1, source_target_pairs={{0,1},{1,0},{2,3},{3,2},{4,8},{5,9},{6,10},{7,11},{8,4},{9,5},{10,... | collective-permute-start | bytes 147464 | tf_op jit(solution)/shard_map/ppermute | solution.py:586
  24.7 4.2 %collective-permute-start.13 = (f32[3,32,128]{2,1,0:T(8,128)S(1)}, f32[3,32,128]{2,1,0:T(8,128)S(1)}, u32[]{:S(2)}, u32[]{:S(2)}) collective-permute-start(f32[3,32,128]{2,1,0:T(8,128)S(1)} %get-tuple-element.140.own_rest_ref), channel_id=1, source_target_pairs={{0,1},{1,0},{2,3},{3,2},{4,8},{5,9},{6,10},{7,11},{8,4},{9,5},{10,... | collective-permute-start | bytes 147464 | tf_op jit(solution)/shard_map/ppermute | solution.py:586
  24.7 4.2 %collective-permute-start.14 = (f32[3,16,128]{2,1,0:T(8,128)S(1)}, f32[3,16,128]{2,1,0:T(8,128)S(1)}, u32[]{:S(2)}, u32[]{:S(2)}) collective-permute-start(f32[3,16,128]{2,1,0:T(8,128)S(1)} %get-tuple-element.137.refs_5_), channel_id=1, source_target_pairs={{0,1},{1,0},{2,3},{3,2},{4,5},{5,4},{6,7},{7,6},{8,9},{9,8},{10,11... | collective-permute-start | bytes 73736 | tf_op jit(solution)/shard_map/ppermute | solution.py:586
  25.3 3.6 %collective-permute-start.15 = (f32[3,16,128]{2,1,0:T(8,128)S(1)}, f32[3,16,128]{2,1,0:T(8,128)S(1)}, u32[]{:S(2)}, u32[]{:S(2)}) collective-permute-start(f32[3,16,128]{2,1,0:T(8,128)S(1)} %get-tuple-element.138.refs_6_), channel_id=1, source_target_pairs={{0,3},{1,2},{2,1},{3,0},{4,7},{5,6},{6,5},{7,4},{8,11},{9,10},{10,... | collective-permute-start | bytes 73736 | tf_op jit(solution)/shard_map/ppermute | solution.py:586
  29.0 9.2 %collective-permute-start.18 = (f32[3,64,128]{2,1,0:T(8,128)S(1)}, f32[3,64,128]{2,1,0:T(8,128)S(1)}, u32[]{:S(2)}, u32[]{:S(2)}) collective-permute-start(f32[3,64,128]{2,1,0:T(8,128)S(1)} %get-tuple-element.151.refs_4_), channel_id=1, source_target_pairs={{0,4},{1,5},{2,6},{3,7},{4,0},{5,1},{6,2},{7,3},{8,12},{9,13},{10,... | collective-permute-start | bytes 294920 | tf_op jit(solution)/shard_map/ppermute | solution.py:586
  29.1 6.3 %collective-permute-start.16 = (f32[3,32,128]{2,1,0:T(8,128)S(1)}, f32[3,32,128]{2,1,0:T(8,128)S(1)}, u32[]{:S(2)}, u32[]{:S(2)}) collective-permute-start(f32[3,32,128]{2,1,0:T(8,128)S(1)} %get-tuple-element.147.refs_0_), channel_id=1, source_target_pairs={{0,1},{1,0},{2,3},{3,2},{4,8},{5,9},{6,10},{7,11},{8,4},{9,5},{10,... | collective-permute-start | bytes 147464 | tf_op jit(solution)/shard_map/ppermute | solution.py:586
  32.5 4.1 %collective-permute-start.17 = (f32[3,32,128]{2,1,0:T(8,128)S(1)}, f32[3,32,128]{2,1,0:T(8,128)S(1)}, u32[]{:S(2)}, u32[]{:S(2)}) collective-permute-start(f32[3,32,128]{2,1,0:T(8,128)S(1)} %get-tuple-element.148.refs_1_), channel_id=1, source_target_pairs={{0,1},{1,0},{2,3},{3,2},{4,8},{5,9},{6,10},{7,11},{8,4},{9,5},{10,... | collective-permute-start | bytes 147464 | tf_op jit(solution)/shard_map/ppermute | solution.py:586
  32.5 5.7 %collective-permute-start.19 = (f32[3,16,128]{2,1,0:T(8,128)S(1)}, f32[3,16,128]{2,1,0:T(8,128)S(1)}, u32[]{:S(2)}, u32[]{:S(2)}) collective-permute-start(f32[3,16,128]{2,1,0:T(8,128)S(1)} %get-tuple-element.153.refs_6_), channel_id=1, source_target_pairs={{0,1},{1,0},{2,3},{3,2},{4,5},{5,4},{6,7},{7,6},{8,9},{9,8},{10,11... | collective-permute-start | bytes 73736 | tf_op jit(solution)/shard_map/ppermute | solution.py:586
  32.5 5.8 %collective-permute-start.20 = (f32[3,16,128]{2,1,0:T(8,128)S(1)}, f32[3,16,128]{2,1,0:T(8,128)S(1)}, u32[]{:S(2)}, u32[]{:S(2)}) collective-permute-start(f32[3,16,128]{2,1,0:T(8,128)S(1)} %get-tuple-element.154.refs_7_), channel_id=1, source_target_pairs={{0,3},{1,2},{2,1},{3,0},{4,7},{5,6},{6,5},{7,4},{8,11},{9,10},{10,... | collective-permute-start | bytes 73736 | tf_op jit(solution)/shard_map/ppermute | solution.py:586
